TPU v7x, 128 devices: a whole 4x4x4 slice. The times are simulated.
128 devices in a mesh: visit: 32 (over y, x, core), band: 4 (over z).
Axes of the slice: x: 4, y: 4, z: 4, core: 2. Of those that a mesh axis runs over, the one named last changes fastest.
Arguments:
- exposures: float32 [4, 64, 552, 552], P('band', 'visit'), may hold values from -8 to 8
- variance: float32 [4, 64, 16, 16], P('band', 'visit'), may hold values from 0.3 to 3
- mask_planes: int32 [4, 64, 16, 16], P('band', 'visit'), may hold values from 0 to 4095
- kernel_table: float32 [64, 27], replicated, may hold values from -3 to 3
- kernel_index: int32 [4, 64], P('band', 'visit'), may hold values from 0 to 63
- tile_owner: int32 [4, 1024, 1], P('band', 'visit'), may hold values from 0 to 31; in each aligned block of 32 rows (0 to 31, 32 to 63, ..., all dimensions but the last counted through in order) at most 2 rows name the same one
- tile_slot: int32 [4, 1024], P('band', 'visit'), may hold values from 0 to 7
Outputs:
- coadd_image: float32 [4, 256, 128, 128], P('band', 'visit')
- detection: float32 [256, 128, 128], P('visit')
Inputs may be any that keep to these rules, and one draw needn't show every extreme that they name: `tile_owner`: in each aligned block of 32 items of one band (the items of one device), no owner is named more than 2 times.
All inputs are finite; a program needn't handle non-finite values.
Results may differ from a plain program's by a relative error of at most 0.0003.
Values sent between devices are 32-bit elements; how exact they have to be, the bound alone decides.
No kernel may reach another device: no remote copies, remote signals or barrier semaphores. Data moves between devices by JAX's collectives and lax.ppermute only.
A program may use at most 128 MiB of HBM per device.

v0:
```python
import jax
import jax.numpy as jnp
import numpy as np
from jax import lax
from jax.sharding import PartitionSpec as P

BLOCK = 512
TILE = 128
CELL = 32
KSIZE = 41
OWN_DEV = 8


width_fractions = (0.075, 0.15, 0.3)
family_degrees = (4, 2, 2)
prior_weight = 0.05
reject_planes = 3


def filter_bank(taps):
    half_width = (taps - 1) // 2
    offsets = jnp.arange(taps, dtype=jnp.float32) - half_width
    profiles = []
    for family in range(3):
        gauss_width = width_fractions[family] * half_width
        for degree in range(family_degrees[family] + 1):
            scaled = offsets / gauss_width
            profile = scaled**degree * jnp.exp(-0.5 * scaled * scaled)
            profiles.append(profile / jnp.sqrt(jnp.sum(profile * profile)))
    return jnp.stack(profiles)


def basis_pattern():
    starts = (0, 5, 8)
    planes = []
    for family in range(3):
        for first in range(family_degrees[family] + 1):
            for second in range(family_degrees[family] + 1 - first):
                plane = np.zeros((11, 11), np.float32)
                plane[starts[family] + first, starts[family] + second] = 1.0
                planes.append(plane)
    return np.stack(planes)


def toeplitz(bank, outputs, inputs):
    filters_count, taps = bank.shape
    padded = jnp.concatenate(
        [bank, jnp.zeros((filters_count, inputs + 1 - taps), jnp.float32)], axis=1
    )
    tiled = jnp.tile(padded, (1, outputs))[:, : outputs * inputs]
    return tiled.reshape(filters_count, outputs, inputs)


def weigh_block(pixels, cell_var, cell_bits, mixing, across, down):
    strips = BLOCK // TILE
    highest = lax.Precision.HIGHEST

    def one_strip(strip_index):
        start = strip_index * TILE
        strip = lax.dynamic_slice_in_dim(pixels, start, TILE + KSIZE - 1, 0)
        spread = jnp.einsum("yj,gxj->ygx", strip, across, precision=highest)
        combined = jnp.einsum("gh,yhx->gyx", mixing, spread, precision=highest)
        return jnp.einsum("gay,gyx->ax", down, combined, precision=highest)

    matched = lax.map(one_strip, jnp.arange(strips, dtype=jnp.int32))
    usable = (jnp.bitwise_and(cell_bits, reject_planes) != reject_planes).astype(jnp.float32)
    weight = usable / cell_var
    cells = BLOCK // CELL
    per_tile = TILE // CELL
    pixel_weight = jnp.broadcast_to(weight[:, None, :, None], (cells, CELL, cells, CELL)).reshape(
        strips, TILE, BLOCK
    )
    product = matched * pixel_weight
    tile_values = (
        product.reshape(strips, TILE, strips, TILE)
        .transpose(0, 2, 1, 3)
        .reshape(strips * strips, TILE * TILE)
    )
    tile_cells = (
        weight.reshape(strips, per_tile, strips, per_tile)
        .transpose(0, 2, 1, 3)
        .reshape(strips * strips, per_tile * per_tile)
    )
    return (tile_values, tile_cells)


def finish(total, weight_sum):
    tiles_count = total.shape[0]
    per_tile = TILE // CELL
    spread_weight = (
        jnp.broadcast_to(
            weight_sum.reshape(tiles_count, per_tile, 1, per_tile, 1),
            (tiles_count, per_tile, CELL, per_tile, CELL),
        ).reshape(tiles_count, TILE, TILE)
        + prior_weight
    )
    image = total.reshape(tiles_count, TILE, TILE) / spread_weight
    return (image, image * image * spread_weight)


def local(exposures, variance, mask_planes, kernel_table, kernel_index, tile_owner, tile_slot):
    highest = lax.Precision.HIGHEST
    peers = lax.axis_size("visit")
    owned = OWN_DEV
    bank = filter_bank(KSIZE)
    across = toeplitz(bank, BLOCK, BLOCK + KSIZE - 1)
    down = toeplitz(bank, TILE, TILE + KSIZE - 1)
    pattern = jnp.asarray(basis_pattern()).astype(jnp.float32)
    lookup = (
        kernel_index[0][:, None] == jnp.arange(kernel_table.shape[0], dtype=jnp.int32)[None, :]
    ).astype(jnp.float32)
    chosen = jnp.dot(lookup, kernel_table, precision=highest)
    mixings = jnp.einsum("bk,kgh->bgh", chosen, pattern, precision=highest)

    def per_block(inputs):
        pixels, cell_var, cell_bits, mixing = inputs
        return weigh_block(pixels, cell_var, cell_bits, mixing, across, down)

    tile_values, tile_cells = lax.map(
        per_block, (exposures[0], variance[0], mask_planes[0], mixings)
    )
    tile_values = tile_values.reshape(-1, TILE * TILE)
    tile_cells = tile_cells.reshape(tile_values.shape[0], -1)
    owners = tile_owner[0, :, 0]
    slots = tile_slot[0]
    target = owners * owned + slots
    route = (target[None, :] == jnp.arange(peers * owned, dtype=jnp.int32)[:, None]).astype(
        jnp.float32
    )
    partial_value = jnp.dot(route, tile_values, precision=highest)
    partial_weight = jnp.dot(route, tile_cells, precision=highest)
    total, weight_sum = (
        lax.psum_scatter(partial_value, "visit", scatter_dimension=0, tiled=True),
        lax.psum_scatter(partial_weight, "visit", scatter_dimension=0, tiled=True),
    )
    coadd_image, chi_terms = finish(total, weight_sum)
    detection = lax.psum(chi_terms, "band")
    return (coadd_image[None], detection)


def solution(mesh):
    placed = (
        P("band", "visit", None, None),
        P("band", "visit", None, None),
        P("band", "visit", None, None),
        P(),
        P("band", "visit"),
        P("band", "visit", None),
        P("band", "visit"),
    )
    return jax.shard_map(
        local,
        mesh=mesh,
        in_specs=placed,
        out_specs=(P("band", "visit", None, None), P("visit", None, None)),
        check_vma=False,
    )
```

profile of v0, /device:TPU:0, one launch (start us, length us, event | category | flops | bytes accessed | tf_op | source)
XLA Modules:
  0.0 601.5 jit_solution(4477273009669978374)
XLA Ops:
  27.9 23.3 %tile.9 = f32[11,283136]{1,0:T(8,128)} reshape(f32[11,512,553]{2,1,0:T(8,128)} %tile.8) | data formatting | bytes 24915968 | tf_op jit(solution)/shard_map/tile | solution.py:50
  51.2 12.1 %slice.8 = f32[11,282624]{1,0:T(8,128)} slice(f32[11,283136]{1,0:T(8,128)} %tile.9), slice={[0:11], [0:282624]} | slice | bytes 24870912 | tf_op jit(solution)/shard_map/slice | solution.py:50
  63.3 26.4 %reshape.237 = f32[11,512,552]{2,1,0:T(8,128)} reshape(f32[11,282624]{1,0:T(8,128)} %slice.8) | data formatting | bytes 24870912 | tf_op jit(solution)/shard_map/reshape | solution.py:51
  89.8 14.7 %copy.32 = f32[11,512,552]{1,2,0:T(8,128)} copy(f32[11,512,552]{2,1,0:T(8,128)} %reshape.237) | data formatting | bytes 24870912 | tf_op jit(solution)/shard_map/while | solution.py:119
  111.4 292.8 %while.23 = (s32[]{:T(128)}, f32[2,16,16384]{2,1,0:T(8,128)}, f32[2,16,16]{2,1,0:T(8,128)S(1)}, f32[2,552,552]{2,1,0:T(8,128)}, f32[2,11,11]{2,0,1:T(2,128)S(1)}...) while((s32[]{:T(128)}, f32[2,16,16384]{2,1,0:T(8,128)}, ...), condition=%wide.region_14.15_spmd, body=%wide.region_11.14_spmd.sunk | while | flops 7845954560 | bytes 47409452 | solution.py:119
  113.1 135.5 %while.24 = (s32[]{:T(128)}, f32[4,128,512]{2,1,0:T(8,128)}, s32[4]{0:T(128)S(1)}, f32[552,552]{1,0:T(8,128)S(1)}, f32[11,512,552]{1,2,0:T(8,128)}, /*index=5*/f...) while((s32[]{:T(128)}, f32[4,128,512]{2,1,0:T(8,128)}, ...), condition=%wide.region_13.13_spmd, body=%wide.region_12.12_spmd.sunk | while | flops 7845691392 | bytes 30262416 | solution.py:65
  114.3 13.7 %fusion.54 = f32[168,11,512]{2,0,1:T(8,128)S(1)} fusion(f32[11,512,552]{1,2,0:T(8,128)} %get-tuple-element.299, f32[552,552]{1,0:T(8,128)S(1)} %get-tuple-element.298, s32[]{:T(128)S(6)} %select_n.4), kind=kOutput, calls=%fused_computation.6.clone.1 | convolution fusion | flops 6267469824 | bytes 16650244 | tf_op jit(solution)/shard_map/while/body/eval_jaxpr/while/body/eval_jaxpr/yj,gxj->ygx/dot_general | solution.py:61
  128.0 10.2 %fusion.55 = f32[11,168,512]{2,0,1:T(8,128)S(1)} fusion(f32[168,11,512]{2,0,1:T(8,128)S(1)} %fusion.54, f32[11,11]{1,0:T(8,128)S(1)} %get-tuple-element.300), kind=kOutput, calls=%fused_computation.4.clone.1 | convolution fusion | flops 124895232 | bytes 7569892 | tf_op jit(solution)/shard_map/while/body/eval_jaxpr/while/body/eval_jaxpr/gh,yhx->gyx/dot_general | solution.py:62
  138.2 7.9 %fusion.56 = f32[1,128,512]{1,2,0:T(8,128)S(1)} fusion(f32[11,128,168]{1,2,0:T(8,128)S(1)} %get-tuple-element.301, f32[11,168,512]{2,0,1:T(8,128)S(1)} %fusion.55), kind=kOutput, calls=%fused_computation.5.clone.1 | convolution fusion | flops 1453326336 | bytes 4993024 | tf_op jit(solution)/shard_map/while/body/eval_jaxpr/while/body/eval_jaxpr/gay,gyx->ax/dot_general | solution.py:63
  148.1 13.7 %fusion.54 = f32[168,11,512]{2,0,1:T(8,128)S(1)} fusion(f32[11,512,552]{1,2,0:T(8,128)} %get-tuple-element.299, f32[552,552]{1,0:T(8,128)S(1)} %get-tuple-element.298, s32[]{:T(128)S(6)} %select_n.4), kind=kOutput, calls=%fused_computation.6.clone.1 | convolution fusion | flops 6267469824 | bytes 16650244 | tf_op jit(solution)/shard_map/while/body/eval_jaxpr/while/body/eval_jaxpr/yj,gxj->ygx/dot_general | solution.py:61
  161.9 10.2 %fusion.55 = f32[11,168,512]{2,0,1:T(8,128)S(1)} fusion(f32[168,11,512]{2,0,1:T(8,128)S(1)} %fusion.54, f32[11,11]{1,0:T(8,128)S(1)} %get-tuple-element.300), kind=kOutput, calls=%fused_computation.4.clone.1 | convolution fusion | flops 124895232 | bytes 7569892 | tf_op jit(solution)/shard_map/while/body/eval_jaxpr/while/body/eval_jaxpr/gh,yhx->gyx/dot_general | solution.py:62
  172.1 7.9 %fusion.56 = f32[1,128,512]{1,2,0:T(8,128)S(1)} fusion(f32[11,128,168]{1,2,0:T(8,128)S(1)} %get-tuple-element.301, f32[11,168,512]{2,0,1:T(8,128)S(1)} %fusion.55), kind=kOutput, calls=%fused_computation.5.clone.1 | convolution fusion | flops 1453326336 | bytes 4993024 | tf_op jit(solution)/shard_map/while/body/eval_jaxpr/while/body/eval_jaxpr/gay,gyx->ax/dot_general | solution.py:63
  182.0 13.7 %fusion.54 = f32[168,11,512]{2,0,1:T(8,128)S(1)} fusion(f32[11,512,552]{1,2,0:T(8,128)} %get-tuple-element.299, f32[552,552]{1,0:T(8,128)S(1)} %get-tuple-element.298, s32[]{:T(128)S(6)} %select_n.4), kind=kOutput, calls=%fused_computation.6.clone.1 | convolution fusion | flops 6267469824 | bytes 16650244 | tf_op jit(solution)/shard_map/while/body/eval_jaxpr/while/body/eval_jaxpr/yj,gxj->ygx/dot_general | solution.py:61
  195.7 10.2 %fusion.55 = f32[11,168,512]{2,0,1:T(8,128)S(1)} fusion(f32[168,11,512]{2,0,1:T(8,128)S(1)} %fusion.54, f32[11,11]{1,0:T(8,128)S(1)} %get-tuple-element.300), kind=kOutput, calls=%fused_computation.4.clone.1 | convolution fusion | flops 124895232 | bytes 7569892 | tf_op jit(solution)/shard_map/while/body/eval_jaxpr/while/body/eval_jaxpr/gh,yhx->gyx/dot_general | solution.py:62
  205.9 7.9 %fusion.56 = f32[1,128,512]{1,2,0:T(8,128)S(1)} fusion(f32[11,128,168]{1,2,0:T(8,128)S(1)} %get-tuple-element.301, f32[11,168,512]{2,0,1:T(8,128)S(1)} %fusion.55), kind=kOutput, calls=%fused_computation.5.clone.1 | convolution fusion | flops 1453326336 | bytes 4993024 | tf_op jit(solution)/shard_map/while/body/eval_jaxpr/while/body/eval_jaxpr/gay,gyx->ax/dot_general | solution.py:63
  215.9 13.7 %fusion.54 = f32[168,11,512]{2,0,1:T(8,128)S(1)} fusion(f32[11,512,552]{1,2,0:T(8,128)} %get-tuple-element.299, f32[552,552]{1,0:T(8,128)S(1)} %get-tuple-element.298, s32[]{:T(128)S(6)} %select_n.4), kind=kOutput, calls=%fused_computation.6.clone.1 | convolution fusion | flops 6267469824 | bytes 16650244 | tf_op jit(solution)/shard_map/while/body/eval_jaxpr/while/body/eval_jaxpr/yj,gxj->ygx/dot_general | solution.py:61
  229.6 10.2 %fusion.55 = f32[11,168,512]{2,0,1:T(8,128)S(1)} fusion(f32[168,11,512]{2,0,1:T(8,128)S(1)} %fusion.54, f32[11,11]{1,0:T(8,128)S(1)} %get-tuple-element.300), kind=kOutput, calls=%fused_computation.4.clone.1 | convolution fusion | flops 124895232 | bytes 7569892 | tf_op jit(solution)/shard_map/while/body/eval_jaxpr/while/body/eval_jaxpr/gh,yhx->gyx/dot_general | solution.py:62
  259.3 135.5 %while.24 = (s32[]{:T(128)}, f32[4,128,512]{2,1,0:T(8,128)}, s32[4]{0:T(128)S(1)}, f32[552,552]{1,0:T(8,128)S(1)}, f32[11,512,552]{1,2,0:T(8,128)}, /*index=5*/f...) while((s32[]{:T(128)}, f32[4,128,512]{2,1,0:T(8,128)}, ...), condition=%wide.region_13.13_spmd, body=%wide.region_12.12_spmd.sunk | while | flops 7845691392 | bytes 30262416 | solution.py:65
  260.5 13.7 %fusion.54 = f32[168,11,512]{2,0,1:T(8,128)S(1)} fusion(f32[11,512,552]{1,2,0:T(8,128)} %get-tuple-element.299, f32[552,552]{1,0:T(8,128)S(1)} %get-tuple-element.298, s32[]{:T(128)S(6)} %select_n.4), kind=kOutput, calls=%fused_computation.6.clone.1 | convolution fusion | flops 6267469824 | bytes 16650244 | tf_op jit(solution)/shard_map/while/body/eval_jaxpr/while/body/eval_jaxpr/yj,gxj->ygx/dot_general | solution.py:61
  274.2 10.2 %fusion.55 = f32[11,168,512]{2,0,1:T(8,128)S(1)} fusion(f32[168,11,512]{2,0,1:T(8,128)S(1)} %fusion.54, f32[11,11]{1,0:T(8,128)S(1)} %get-tuple-element.300), kind=kOutput, calls=%fused_computation.4.clone.1 | convolution fusion | flops 124895232 | bytes 7569892 | tf_op jit(solution)/shard_map/while/body/eval_jaxpr/while/body/eval_jaxpr/gh,yhx->gyx/dot_general | solution.py:62
  284.4 7.9 %fusion.56 = f32[1,128,512]{1,2,0:T(8,128)S(1)} fusion(f32[11,128,168]{1,2,0:T(8,128)S(1)} %get-tuple-element.301, f32[11,168,512]{2,0,1:T(8,128)S(1)} %fusion.55), kind=kOutput, calls=%fused_computation.5.clone.1 | convolution fusion | flops 1453326336 | bytes 4993024 | tf_op jit(solution)/shard_map/while/body/eval_jaxpr/while/body/eval_jaxpr/gay,gyx->ax/dot_general | solution.py:63
  294.3 13.7 %fusion.54 = f32[168,11,512]{2,0,1:T(8,128)S(1)} fusion(f32[11,512,552]{1,2,0:T(8,128)} %get-tuple-element.299, f32[552,552]{1,0:T(8,128)S(1)} %get-tuple-element.298, s32[]{:T(128)S(6)} %select_n.4), kind=kOutput, calls=%fused_computation.6.clone.1 | convolution fusion | flops 6267469824 | bytes 16650244 | tf_op jit(solution)/shard_map/while/body/eval_jaxpr/while/body/eval_jaxpr/yj,gxj->ygx/dot_general | solution.py:61
  308.0 10.2 %fusion.55 = f32[11,168,512]{2,0,1:T(8,128)S(1)} fusion(f32[168,11,512]{2,0,1:T(8,128)S(1)} %fusion.54, f32[11,11]{1,0:T(8,128)S(1)} %get-tuple-element.300), kind=kOutput, calls=%fused_computation.4.clone.1 | convolution fusion | flops 124895232 | bytes 7569892 | tf_op jit(solution)/shard_map/while/body/eval_jaxpr/while/body/eval_jaxpr/gh,yhx->gyx/dot_general | solution.py:62
  318.3 7.9 %fusion.56 = f32[1,128,512]{1,2,0:T(8,128)S(1)} fusion(f32[11,128,168]{1,2,0:T(8,128)S(1)} %get-tuple-element.301, f32[11,168,512]{2,0,1:T(8,128)S(1)} %fusion.55), kind=kOutput, calls=%fused_computation.5.clone.1 | convolution fusion | flops 1453326336 | bytes 4993024 | tf_op jit(solution)/shard_map/while/body/eval_jaxpr/while/body/eval_jaxpr/gay,gyx->ax/dot_general | solution.py:63
  328.2 13.7 %fusion.54 = f32[168,11,512]{2,0,1:T(8,128)S(1)} fusion(f32[11,512,552]{1,2,0:T(8,128)} %get-tuple-element.299, f32[552,552]{1,0:T(8,128)S(1)} %get-tuple-element.298, s32[]{:T(128)S(6)} %select_n.4), kind=kOutput, calls=%fused_computation.6.clone.1 | convolution fusion | flops 6267469824 | bytes 16650244 | tf_op jit(solution)/shard_map/while/body/eval_jaxpr/while/body/eval_jaxpr/yj,gxj->ygx/dot_general | solution.py:61
  341.9 10.2 %fusion.55 = f32[11,168,512]{2,0,1:T(8,128)S(1)} fusion(f32[168,11,512]{2,0,1:T(8,128)S(1)} %fusion.54, f32[11,11]{1,0:T(8,128)S(1)} %get-tuple-element.300), kind=kOutput, calls=%fused_computation.4.clone.1 | convolution fusion | flops 124895232 | bytes 7569892 | tf_op jit(solution)/shard_map/while/body/eval_jaxpr/while/body/eval_jaxpr/gh,yhx->gyx/dot_general | solution.py:62
  362.1 13.7 %fusion.54 = f32[168,11,512]{2,0,1:T(8,128)S(1)} fusion(f32[11,512,552]{1,2,0:T(8,128)} %get-tuple-element.299, f32[552,552]{1,0:T(8,128)S(1)} %get-tuple-element.298, s32[]{:T(128)S(6)} %select_n.4), kind=kOutput, calls=%fused_computation.6.clone.1 | convolution fusion | flops 6267469824 | bytes 16650244 | tf_op jit(solution)/shard_map/while/body/eval_jaxpr/while/body/eval_jaxpr/yj,gxj->ygx/dot_general | solution.py:61
  375.8 10.2 %fusion.55 = f32[11,168,512]{2,0,1:T(8,128)S(1)} fusion(f32[168,11,512]{2,0,1:T(8,128)S(1)} %fusion.54, f32[11,11]{1,0:T(8,128)S(1)} %get-tuple-element.300), kind=kOutput, calls=%fused_computation.4.clone.1 | convolution fusion | flops 124895232 | bytes 7569892 | tf_op jit(solution)/shard_map/while/body/eval_jaxpr/while/body/eval_jaxpr/gh,yhx->gyx/dot_general | solution.py:62
  386.0 7.9 %fusion.56 = f32[1,128,512]{1,2,0:T(8,128)S(1)} fusion(f32[11,128,168]{1,2,0:T(8,128)S(1)} %get-tuple-element.301, f32[11,168,512]{2,0,1:T(8,128)S(1)} %fusion.55), kind=kOutput, calls=%fused_computation.5.clone.1 | convolution fusion | flops 1453326336 | bytes 4993024 | tf_op jit(solution)/shard_map/while/body/eval_jaxpr/while/body/eval_jaxpr/gay,gyx->ax/dot_general | solution.py:63
  404.2 11.7 %fusion.18 = f32[256,16384]{1,0:T(8,128)} fusion(f32[32,16384]{1,0:T(8,128)} %bitcast.82, s32[32]{0:T(128)S(1)} %fusion.23), kind=kOutput, calls=%fused_computation.27 | convolution fusion | flops 1610620928 | bytes 18874496 | tf_op jit(solution)/shard_map/dot_general | solution.py:130
  418.0 130.3 %all-reduce.2 = f32[256,16]{1,0:T(8,128)S(1)} all-reduce(f32[256,16]{1,0:T(8,128)S(1)} %fusion.17), channel_id=3, replica_groups=mesh['visit'=32,'band'=4] {'visit'}, use_global_device_ids=true, to_apply=%region_16.17.clone | all-reduce | flops 4096 | bytes 32768
  553.6 38.8 %all-reduce.5.cloned.1.call-done = f32[8,128,128]{2,1,0:T(8,128)} async-done(((f32[8,128,128]{2,1,0:T(8,128)}), f32[8,128,128]{2,1,0:T(8,128)}) %all-reduce.5.cloned.1.call-update) | async-done | bytes 524304 | tf_op jit(solution)/shard_map/psum | solution.py:137
  (128 shorter events, 77.3 us)
Async XLA Ops:
  7.2 103.3 %copy-start = (f32[64,27]{0,1:T(8,128)S(1)}, f32[64,27]{0,1:T(8,128)}, u32[]{:S(2)}) copy-start(f32[64,27]{0,1:T(8,128)} %param.15) | copy-start | bytes 20740
  7.2 542.6 %reduce-scatter.2.cloned.1.call-start = ((), (), s32[]{:S(2)}) async-start(), calls=%async_computation.1 | async-start | bytes 17301504 | tf_op jit(solution)/shard_map/reduce_scatter | solution.py:133
  105.5 5.0 copy-start.6
  105.5 5.2 copy-start.5
  105.5 5.9 copy-start.3
  105.5 5.9 copy-start.4
  111.4 292.8 %copy-start.7 = (s32[1,32]{1,0:T(1,128)S(1)}, s32[1,32]{1,0:T(1,128)}, u32[]{:S(2)}) copy-start(s32[1,32]{1,0:T(1,128)} %param.18) | copy-start | bytes 388
  111.4 292.8 %copy-start.8 = (s32[1,32,1]{1,2,0:T(1,128)S(1)}, s32[1,32,1]{1,2,0:T(1,128)}, u32[]{:S(2)}) copy-start(s32[1,32,1]{1,2,0:T(1,128)} %param.17) | copy-start | bytes 388
  415.9 0.7 copy-start.9
  415.9 176.5 %all-reduce.5.cloned.1.call-start = ((), (), s32[]{:S(2)}) async-start(), calls=%async_computation.2 | async-start | bytes 1048576 | tf_op jit(solution)/shard_map/psum | solution.py:137
  548.9 45.5 %copy-start.1 = (f32[64,27]{0,1:T(8,128)S(1)}, f32[64,27]{0,1:T(8,128)}, u32[]{:S(2)}) copy-start(f32[64,27]{0,1:T(8,128)} %param.15) | copy-start | bytes 20740
  549.8 2.9 copy-start.2
Sparse Core Ops, SparseCore 0:
  416.0 117.9 reduce-scatter.1
  552.0 40.4 all-reduce.4
where the time goes:
time: 608 us; the launch traced here: 602 us
  matrix products  267 us (44%)
  blocking collectives  130 us (21%)
  local copies, waits for them, and re-layouts  124 us (20%)
  waiting for transfers between devices  38.9 us (6%)
  between operations  22.6 us (4%)
  other arithmetic  13 us (2%)
    unnamed x1, blocking collectives  130 us
    dot_general x8, matrix products, one_strip(): spread = jnp.einsum('yj,gxj->ygx', strip, across, precision=highest)  110 us
    dot_general x8, matrix products, one_strip(): combined = jnp.einsum('gh,yhx->gyx', mixing, spread, precision=highest)  81.7 us
    dot_general x8, matrix products, one_strip(): return jnp.einsum('gay,gyx->ax', down, combined, precision=highest)  63.3 us
    psum x1, waiting for transfers between devices, local(): detection = lax.psum(chi_terms, 'band')  38.8 us
    another operation x4, local copies, waits for them, and re-layouts, toeplitz(): tiled = jnp.tile(padded, (1, outputs))[:, :outputs * inputs]  30.4 us
    reshape x2, local copies, waits for them, and re-layouts, toeplitz(): return tiled.reshape(filters_count, outputs, inputs)  29.8 us
    while x2, local copies, waits for them, and re-layouts, local(): lax.map(per_block, (exposures[0], variance[0], mask_planes[0], mixings))  15.1 us
  transfers between devices with their start and end apart: 2, of which 1 were waited for; matrix products, arithmetic and copies ran while one was open for 1% of the time, Pallas kernels for 0%

commit v1 on v0

v1 whole, which is shorter than its diff:
```python
import functools

import jax
import jax.numpy as jnp
import numpy as np
from jax import lax
from jax.experimental import pallas as pl
from jax.experimental.pallas import tpu as pltpu
from jax.sharding import PartitionSpec as P

BLOCK = 512
TILE = 128
CELL = 32
KSIZE = 41
OWN_DEV = 8
PADDED = BLOCK + KSIZE - 1
WIDE = 640
NFILT = 11
VISITS = 32
SIDE = BLOCK // TILE
CELLS = BLOCK // CELL
PER_TILE = TILE // CELL
TILES_BLK = SIDE * SIDE
CHIPS = VISITS // 2
PIECE = TILE // CHIPS
INFO = 8
SPAN = TILE + KSIZE - 1
HALF = SPAN // 2
TALL = 560

width_fractions = (0.075, 0.15, 0.3)
family_degrees = (4, 2, 2)
prior_weight = 0.05
reject_planes = 3

f32 = jnp.float32
bf16 = jnp.bfloat16


def as_halves(matrix):
    high = matrix.astype(np.float32).astype(bf16)
    low = (matrix - high.astype(np.float64)).astype(np.float32).astype(bf16)
    return high, low


def transforms():
    number = np.arange(HALF)
    angle = 2 * np.pi * (number + 0.5) / SPAN
    taps = np.arange(SPAN)
    cosine, sine = np.cos(angle[:, None] * taps), np.sin(angle[:, None] * taps)
    spot = 8 * (number // 4) + number % 4

    by_row = np.zeros((SPAN, SPAN))
    by_row[spot], by_row[spot + 4] = cosine, sine
    by_lane = np.zeros((2 * TILE, SPAN))
    by_lane[:HALF], by_lane[TILE:TILE + HALF] = cosine, sine

    across = np.zeros((2 * TILE, 2 * TILE))
    across[:SPAN] = by_lane.T
    down = np.zeros((SPAN + 8, SPAN))
    down[:SPAN] = by_row
    back_down = by_row.T[:TILE] * (2 / SPAN)
    back_across = by_lane[:, :TILE] * (2 / SPAN)

    def three(matrix):
        high, low = as_halves(matrix)
        rest = np.zeros((matrix.shape[0], 512 - 3 * SPAN), bf16)
        return np.concatenate([high, high, low, rest], axis=1)

    same = np.zeros((SPAN, TILE), np.float32)
    cross = np.zeros((SPAN, TILE), np.float32)
    same[spot, :KSIZE] = same[spot + 4, :KSIZE] = cosine[:, :KSIZE]
    cross[spot, :KSIZE], cross[spot + 4, :KSIZE] = sine[:, :KSIZE], -sine[:, :KSIZE]
    along = np.zeros((TILE, 2 * TILE), np.float32)
    along[:KSIZE, :HALF], along[:KSIZE, TILE:TILE + HALF] = cosine[:, :KSIZE].T, -sine[:, :KSIZE].T
    return (
        np.stack(as_halves(across)),
        three(down),
        three(back_down),
        np.concatenate(as_halves(back_across), axis=1),
        np.stack([same, cross]),
        along,
    )


def filter_terms():
    starts = (0, 5, 8)
    terms = []
    for family in range(3):
        for first in range(family_degrees[family] + 1):
            for second in range(family_degrees[family] + 1 - first):
                terms.append((starts[family] + first, starts[family] + second))
    return terms


def profiles_at(offset):
    half_width = (KSIZE - 1) // 2
    inside = (offset >= 0) & (offset < KSIZE)
    taps = offset.astype(f32) - half_width
    values = []
    for family in range(3):
        scaled = taps / (width_fractions[family] * half_width)
        value = jnp.where(inside, jnp.exp(-0.5 * scaled * scaled), 0.0)
        for degree in range(family_degrees[family] + 1):
            values.append(value)
            value = value * scaled
    return values


def split(value):
    high = value.astype(bf16)
    return high, (value - high.astype(f32)).astype(bf16)


def cell_weights(variance, bits):
    usable = (jnp.bitwise_and(bits, reject_planes) != reject_planes).astype(f32)
    return usable / variance


def item_info(var_ref, bits_ref, owner_ref, slot_ref):
    exact = lax.Precision.HIGHEST
    lane = lax.broadcasted_iota(jnp.int32, (1, TILE), 1)
    row = lax.broadcasted_iota(jnp.int32, (CELLS, TILE), 0)
    item = lane % TILES_BLK
    cell_row = (item // SIDE) * PER_TILE + lane // (2 * TILES_BLK)
    columns = None
    for block in range(2):
        picked = ((row == cell_row) & ((lane // TILES_BLK) % 2 == block)).astype(f32)
        term = lax.dot_general(
            cell_weights(var_ref[block], bits_ref[block]), picked,
            (((0,), (0,)), ((), ())), precision=exact, preferred_element_type=f32,
        )
        columns = term if columns is None else columns + term
    rows = []
    for n in range(PER_TILE):
        chosen = row == (item % SIDE) * PER_TILE + n
        rows.append(jnp.sum(jnp.where(chosen, columns, 0.0), axis=0, keepdims=True))
    target = (owner_ref[...] * OWN_DEV + slot_ref[...]).astype(f32)
    rows.append(jnp.concatenate([target, jnp.zeros((1, TILE - 2 * TILES_BLK), f32)], axis=1))
    rows.append(jnp.zeros((INFO - PER_TILE - 1, TILE), f32))
    return jnp.concatenate(rows, axis=0)


def exact_dot(left, right, sides=((1,), (0,))):
    return lax.dot_general(
        left, right, (sides, ((), ())), precision=lax.Precision.HIGHEST, preferred_element_type=f32
    )


def stacked_halves(value):
    high = value.astype(bf16).astype(f32)
    rest = jnp.zeros((512 - 3 * SPAN, value.shape[1]), f32)
    return jnp.concatenate([high, value - high, high, rest], axis=0).astype(bf16)


def filter_bank():
    taps = lax.broadcasted_iota(jnp.int32, (1, TILE), 1)
    rows = [value / jnp.sqrt(jnp.sum(value * value, axis=1, keepdims=True)) for value in profiles_at(taps)]
    return jnp.concatenate(rows + [jnp.zeros((16 - NFILT, TILE), f32)], axis=0)


def kernel_spectrum(filters, which, table_ref, down_taps_ref, along_ref):
    first = lax.broadcasted_iota(jnp.int32, (16, 16), 0)
    second = lax.broadcasted_iota(jnp.int32, (16, 16), 1)
    mixing = jnp.zeros((16, 16), f32)
    for number, (p, q) in enumerate(filter_terms()):
        mixing = jnp.where((first == p) & (second == q), table_ref[number, which], mixing)
    across = exact_dot(mixing, exact_dot(filters, along_ref[...]))
    return [
        exact_dot(exact_dot(down_taps_ref[part], filters, ((1,), (1,))), across)
        for part in range(2)
    ]


def match_kernel(
    index_hbm, table_hbm, image_hbm, var_hbm, bits_hbm, owner_hbm, slot_hbm,
    across_hbm, down_hbm, back_down_hbm, back_across_hbm, down_taps_hbm, along_hbm, out_hbm,
    index_ref, table_ref, image_ref, var_ref, bits_ref, owner_ref, slot_ref,
    across_ref, down_ref, back_down_ref, back_across_ref, down_taps_ref, along_ref, sems, out_sems,
    tail_ref, high_ref, low_ref, wave_ref, stack_ref, turn_ref, result_ref, rows_ref, factor_ref,
    weight_ref, out_ref,
    *, block,
):
    copies = [
        pltpu.make_async_copy(source, goal, sems.at[number])
        for number, (source, goal) in enumerate((
            (index_hbm, index_ref),
            (table_hbm, table_ref),
            (down_taps_hbm, down_taps_ref),
            (along_hbm, along_ref),
            (image_hbm.at[0, block], image_ref),
            (across_hbm, across_ref),
            (var_hbm.at[0], var_ref),
            (bits_hbm.at[0], bits_ref),
            (owner_hbm, owner_ref),
            (slot_hbm, slot_ref),
            (down_hbm, down_ref),
            (back_down_hbm, back_down_ref),
            (back_across_hbm, back_across_ref),
        ))
    ]
    for copy in copies:
        copy.start()
    tail_ref[...] = jnp.zeros_like(tail_ref)
    filters = filter_bank()
    for copy in copies:
        copy.wait()

    tail_ref[:PADDED, :PADDED - BLOCK] = image_ref[:, BLOCK:]
    whole = TALL - 16
    for columns, source in ((slice(0, BLOCK), image_ref), (slice(BLOCK, WIDE), tail_ref)):
        width = columns.stop - columns.start
        high_ref[:whole, columns], low_ref[:whole, columns] = split(source[:whole, :width])
        last = jnp.concatenate([source[whole:PADDED, :width], jnp.zeros((8, width), f32)], axis=0)
        high_ref[whole:, columns], low_ref[whole:, columns] = split(last)

    forward = jnp.concatenate([across_ref[0], across_ref[0], across_ref[1]], axis=0)
    backward = jnp.concatenate([back_across_ref[...], back_across_ref[...]], axis=0)
    pair = 2 * TILE
    for column in range(SIDE):
        lanes = slice(column * TILE, column * TILE + pair)
        high, low = high_ref[:, lanes], low_ref[:, lanes]
        wave_ref[:, column * pair:(column + 1) * pair] = jnp.dot(
            jnp.concatenate([high, low, high], axis=1), forward, preferred_element_type=f32
        )

    same, cross = kernel_spectrum(filters, index_ref[0, block], table_ref, down_taps_ref, along_ref)
    factor_ref[0] = same.reshape(SPAN // 8, 8, pair)
    factor_ref[1] = cross.reshape(SPAN // 8, 8, pair)

    spread = (
        lax.broadcasted_iota(jnp.int32, (CELLS, BLOCK), 1) // CELL
        == lax.broadcasted_iota(jnp.int32, (CELLS, BLOCK), 0)
    ).astype(f32)
    weight_ref[...] = exact_dot(cell_weights(var_ref[block], bits_ref[block]), spread)
    sends = []
    if block == 0:
        info = item_info(var_ref, bits_ref, owner_ref, slot_ref)
        out_ref[:, TILES_BLK] = jnp.broadcast_to(info[None], (CHIPS, INFO, TILE))
        sends.append(
            pltpu.make_async_copy(out_ref.at[:, TILES_BLK], out_hbm.at[:, TILES_BLK], out_sems.at[TILES_BLK])
        )
        sends[-1].start()

    for line in range(SIDE):
        for column in range(SIDE):
            lanes = slice(column * pair, (column + 1) * pair)
            stack_ref[line, :, lanes] = stacked_halves(
                wave_ref[line * TILE:line * TILE + SPAN, lanes]
            )
        turn_ref[line] = jnp.dot(down_ref[...], stack_ref[line], preferred_element_type=f32)

    for line in range(SIDE):
        for column in range(SIDE):
            lanes = slice(column * pair, (column + 1) * pair)
            wave = turn_ref[line, :SPAN, lanes].reshape(SPAN // 8, 8, pair)
            turned = pltpu.roll(wave, 4, 1)
            wave_c, wave_s = wave[..., :TILE], wave[..., TILE:]
            turned_c, turned_s = turned[..., :TILE], turned[..., TILE:]
            same_c, same_s = factor_ref[0, :, :, :TILE], factor_ref[0, :, :, TILE:]
            cross_c, cross_s = factor_ref[1, :, :, :TILE], factor_ref[1, :, :, TILE:]
            result_c = wave_c * same_c + turned_c * cross_c - wave_s * same_s - turned_s * cross_s
            result_s = wave_s * same_c + turned_s * cross_c + wave_c * same_s + turned_c * cross_s
            result = jnp.concatenate(
                [result_c.reshape(SPAN, TILE), result_s.reshape(SPAN, TILE)], axis=1
            )
            result_ref[line, :, lanes] = stacked_halves(result)
        rows = jnp.dot(back_down_ref[...], result_ref[line], preferred_element_type=f32)
        for column in range(SIDE):
            high, low = split(rows[:, column * pair:(column + 1) * pair])
            rows_ref[column, line * TILE:(line + 1) * TILE, :pair] = high
            rows_ref[column, line * TILE:(line + 1) * TILE, pair:] = low

    for column in range(SIDE):
        matched = jnp.dot(rows_ref[column], backward, preferred_element_type=f32)
        matched = matched[:, :TILE] + matched[:, TILE:]
        weight = weight_ref[:, column * TILE:(column + 1) * TILE]
        weighted = matched.reshape(CELLS, CELL, TILE) * weight[:, None, :]
        weighted = weighted.reshape(SIDE, CHIPS, PIECE, TILE)
        for line in range(SIDE):
            item = line * SIDE + column
            out_ref[:, item] = weighted[line]
            sends.append(
                pltpu.make_async_copy(out_ref.at[:, item], out_hbm.at[:, item], out_sems.at[item])
            )
            sends[-1].start()
    for send in sends:
        send.wait()


def match_block(block, exposures, variance, bits, table, index, owner, slot):
    blocks = exposures.shape[1]
    items = blocks * TILES_BLK
    groups = TILES_BLK + (1 if block == 0 else 0)
    matrices = transforms()
    pieces = pl.pallas_call(
        functools.partial(match_kernel, block=block),
        out_shape=jax.ShapeDtypeStruct((CHIPS, groups, PIECE, TILE), f32),
        in_specs=[pl.BlockSpec(memory_space=pltpu.HBM)] * (7 + len(matrices)),
        out_specs=pl.BlockSpec(memory_space=pltpu.HBM),
        scratch_shapes=[
            pltpu.SMEM((1, blocks), jnp.int32),
            pltpu.SMEM(table.shape, f32),
            pltpu.VMEM((PADDED, PADDED), f32),
            pltpu.VMEM((blocks, CELLS, CELLS), f32),
            pltpu.VMEM((blocks, CELLS, CELLS), jnp.int32),
            pltpu.VMEM((1, items), jnp.int32),
            pltpu.VMEM((1, items), jnp.int32),
            *[pltpu.VMEM(matrix.shape, matrix.dtype) for matrix in matrices],
            pltpu.SemaphoreType.DMA((7 + len(matrices),)),
            pltpu.SemaphoreType.DMA((TILES_BLK + 1,)),
            pltpu.VMEM((TALL, TILE), f32),
            pltpu.VMEM((TALL, WIDE), bf16),
            pltpu.VMEM((TALL, WIDE), bf16),
            pltpu.VMEM((TALL, 2 * BLOCK), f32),
            pltpu.VMEM((SIDE, 512, 2 * BLOCK), bf16),
            pltpu.VMEM((SIDE, SPAN + 8, 2 * BLOCK), f32),
            pltpu.VMEM((SIDE, 512, 2 * BLOCK), bf16),
            pltpu.VMEM((SIDE, BLOCK, 4 * TILE), bf16),
            pltpu.VMEM((2, SPAN // 8, 8, 2 * TILE), f32),
            pltpu.VMEM((CELLS, BLOCK), f32),
            pltpu.VMEM((CHIPS, groups, PIECE, TILE), f32),
        ],
        compiler_params=pltpu.CompilerParams(vmem_limit_bytes=60 << 20),
        cost_estimate=pl.CostEstimate(
            flops=2 * 256 * 256 * 20000, bytes_accessed=3 << 20, transcendentals=0
        ),
        name="match_block",
    )(index, table, exposures, variance, bits, owner, slot, *matrices)
    return pieces.reshape(CHIPS, groups * PIECE, TILE)


def partial_kernel(place_ref, first_ref, second_ref, mine_ref, other_ref):
    core = place_ref[0] % 2
    per_group = TILE // TILES_BLK
    lane = lax.broadcasted_iota(jnp.int32, (INFO, TILE), 1)
    info = [first_ref[source, TILES_BLK * PIECE:, :] for source in range(CHIPS)]
    tables = []
    for block in range(2):
        rows = []
        for m in range(PER_TILE):
            groups = []
            for group in range(CHIPS // per_group):
                total = None
                for member in range(per_group):
                    goal = member * TILES_BLK
                    shift = (goal - (m * 2 + block) * TILES_BLK) % TILE
                    value = info[group * per_group + member]
                    value = pltpu.roll(value, shift, 1) if shift else value
                    here = (lane >= goal) & (lane < goal + TILES_BLK)
                    total = value if total is None else jnp.where(here, value, total)
                groups.append(total)
            rows.append(jnp.concatenate(groups, axis=1))
        tables.append(rows)

    targets = VISITS * OWN_DEV
    owned = targets // 2
    items = CHIPS * TILES_BLK
    row = lax.broadcasted_iota(jnp.int32, (targets, items), 0)
    side = (row // owned + core) % 2
    inner = row % owned
    wanted = ((inner // OWN_DEV) * 2 + side) * OWN_DEV + inner % OWN_DEV
    routes = []
    sums = None
    over_items = (((1,), (1,)), ((), ()))
    for block in range(2):
        target = tables[block][0][PER_TILE:PER_TILE + 1, :].astype(jnp.int32)
        route = jnp.where(wanted == target, 1.0, 0.0).astype(bf16)
        routes.append(route)
        weights = jnp.concatenate(
            tables[block] + [jnp.zeros((TILE - INFO * PER_TILE, items), f32)], axis=0
        )
        for half in split(weights):
            term = lax.dot_general(route, half, over_items, preferred_element_type=f32)
            sums = term if sums is None else sums + term
    mine_ref[owned * PIECE:, :] = sums[:owned]
    other_ref[owned * PIECE:, :] = sums[owned:]
    for line in range(PIECE):
        total = None
        for route, part_ref in zip(routes, (first_ref, second_ref)):
            part = part_ref[:, pl.ds(line, TILES_BLK, PIECE), :].reshape(items, TILE)
            high, low = split(part)
            term = jnp.dot(
                route, jnp.concatenate([high, low], axis=1), preferred_element_type=f32
            )
            total = term if total is None else total + term
        total = total[:, :TILE] + total[:, TILE:]
        mine_ref[pl.ds(line, owned, PIECE), :] = total[:owned]
        other_ref[pl.ds(line, owned, PIECE), :] = total[owned:]


def spread_cells(sums, cell_row):
    pattern = (
        lax.broadcasted_iota(jnp.int32, (TILE, TILE), 1) // CELL + cell_row * INFO
        == lax.broadcasted_iota(jnp.int32, (TILE, TILE), 0)
    ).astype(f32)
    return jnp.dot(sums, pattern, precision=lax.Precision.HIGHEST, preferred_element_type=f32)


def merge_kernel(place_ref, mine_ref, other_ref, out_ref):
    owned = VISITS * OWN_DEV // 2
    cell_row = (place_ref[0] // 2) // (CELL // PIECE)
    sums = mine_ref[owned * PIECE:, :] + other_ref[owned * PIECE:, :]
    scale = 1.0 / (spread_cells(sums, cell_row) + prior_weight)
    total = mine_ref[:owned * PIECE, :] + other_ref[:owned * PIECE, :]
    total = total.reshape(owned, PIECE, TILE) * scale[:, None, :]
    out_ref[...] = total.reshape(owned * PIECE, TILE)


def owner_kernel(place_ref, mine_ref, other_ref, part_ref, image_ref, chi_ref):
    owned = VISITS * OWN_DEV // 2
    rows = pl.ds(pl.multiple_of(owned * PIECE + (place_ref[0] // 2) * OWN_DEV, OWN_DEV), OWN_DEV)
    sums = mine_ref[rows, :] + other_ref[rows, :]
    spread = [spread_cells(sums, cell_row) + prior_weight for cell_row in range(PER_TILE)]
    for slot in range(OWN_DEV):
        image = part_ref[:, slot * PIECE:(slot + 1) * PIECE, :].reshape(TILE, TILE)
        image_ref[slot] = image
        weight = jnp.concatenate(
            [jnp.broadcast_to(spread[m][slot:slot + 1], (CELL, TILE)) for m in range(PER_TILE)],
            axis=0,
        )
        chi_ref[slot] = image * image * weight


def local(exposures, variance, mask_planes, kernel_table, kernel_index, tile_owner, tile_slot):
    place = lax.axis_index("visit").astype(jnp.int32).reshape(1)
    smem = pl.BlockSpec(memory_space=pltpu.SMEM)
    vmem = pl.BlockSpec(memory_space=pltpu.VMEM)
    params = pltpu.CompilerParams(vmem_limit_bytes=32 << 20)
    same_core = [list(range(core, VISITS, 2)) for core in range(2)]
    owned = VISITS * OWN_DEV // 2

    def exchange(pieces):
        return lax.all_to_all(pieces, "visit", 0, 0, axis_index_groups=same_core, tiled=True)

    table = kernel_table.T
    owner = tile_owner.reshape(tile_slot.shape)
    parts = []
    for block in range(exposures.shape[1]):
        pieces = match_block(
            block, exposures, variance, mask_planes, table, kernel_index, owner, tile_slot
        )
        parts.append(exchange(pieces))

    mine, other = pl.pallas_call(
        partial_kernel,
        out_shape=[jax.ShapeDtypeStruct((owned * (PIECE + 1), TILE), f32)] * 2,
        in_specs=[smem, vmem, vmem],
        out_specs=[vmem, vmem],
        compiler_params=params,
        name="partial_sums",
    )(place, *parts)
    other = lax.ppermute(other, "visit", [(device, device ^ 1) for device in range(VISITS)])
    pieces = pl.pallas_call(
        merge_kernel,
        out_shape=jax.ShapeDtypeStruct((owned * PIECE, TILE), f32),
        in_specs=[smem, vmem, vmem],
        out_specs=vmem,
        compiler_params=params,
        name="merge_cores",
    )(place, mine, other)
    pieces = exchange(pieces.reshape(CHIPS, OWN_DEV * PIECE, TILE))
    image, chi = pl.pallas_call(
        owner_kernel,
        out_shape=[jax.ShapeDtypeStruct((OWN_DEV, TILE, TILE), f32)] * 2,
        in_specs=[smem, vmem, vmem, vmem],
        out_specs=[vmem, vmem],
        compiler_params=params,
        name="own",
    )(place, mine, other, pieces)

    pairings = ([(0, 1), (1, 0), (2, 3), (3, 2)], [(0, 3), (3, 0), (1, 2), (2, 1)])
    halves = [chi[:OWN_DEV // 2], chi[OWN_DEV // 2:]]
    for turn in range(2):
        halves = [
            half + lax.ppermute(half, "band", pairings[(turn + number) % 2])
            for number, half in enumerate(halves)
        ]
    return image[None], jnp.concatenate(halves, axis=0)


def solution(mesh):
    placed = (
        P("band", "visit", None, None),
        P("band", "visit", None, None),
        P("band", "visit", None, None),
        P(),
        P("band", "visit"),
        P("band", "visit", None),
        P("band", "visit"),
    )
    return jax.shard_map(
        local,
        mesh=mesh,
        in_specs=placed,
        out_specs=(P("band", "visit", None, None), P("visit", None, None)),
        check_vma=False,
    )
```

time: 608 us -> 93.1 us (0.15)
  matrix products: 267 us -> 0 us
  local copies, waits for them, and re-layouts: 124 us -> 0.03 us
  blocking collectives: 130 us -> 14.7 us
  between operations: 22.6 us -> 0.71 us
  starting transfers between devices: 0.08 us -> 18 us
  Pallas kernels: 0 us -> 17.4 us
  other arithmetic: 13 us -> 0.97 us
    dot_general x28 -> x0, matrix products: 267 us -> none  [the longest x8 110 us: one_strip(): spread = jnp.einsum('yj,gxj->ygx', strip, across, precision=highest)]
    unnamed x1 -> x0, blocking collectives: 130 us -> none
    psum x1 -> x0, waiting for transfers between devices: 38.8 us -> none  [local(): detection = lax.psum(chi_terms, 'band')]
    reshape x6 -> x0, local copies, waits for them, and re-layouts: 37.6 us -> none  [the longest x2 29.8 us: toeplitz(): return tiled.reshape(filters_count, outputs, inputs)]
    another operation x5 -> x0, local copies, waits for them, and re-layouts: 30.4 us -> none  [the longest x4 30.4 us: toeplitz(): tiled = jnp.tile(padded, (1, outputs))[:, :outputs * inputs]]
    all_to_all x0 -> x2, waiting for transfers between devices: none -> 27.1 us  [exchange(): lax.all_to_all(pieces, 'visit', 0, 0, axis_index_groups=same_core, tiled=...]
    pallas_call x0 -> x5, Pallas kernels: none -> 17.4 us  [the longest x2 15.1 us: match_block(): pl.pallas_call(functools.partial(match_kernel, block=block), out_shape=ja...]
    while x2 -> x0, local copies, waits for them, and re-layouts: 15.1 us -> none  [local(): lax.map(per_block, (exposures[0], variance[0], mask_planes[0], mixings))]
  transfers between devices with their start and end apart: 2 -> 7, of which waited for: 1 -> 7; matrix products, arithmetic and copies ran while one was open for 1% -> 0% of each run, Pallas kernels for 0% -> 8%
where the time goes in v1:
time: 93.1 us; the launch traced here: 92.7 us
  waiting for transfers between devices  40.8 us (44%)
  starting transfers between devices  18 us (19%)
  Pallas kernels  17.4 us (19%)
  blocking collectives  14.7 us (16%)
  other arithmetic  0.97 us (1%)
    all_to_all x2, waiting for transfers between devices, exchange(): lax.all_to_all(pieces, 'visit', 0, 0, axis_index_groups=same_core, tiled=...  27.1 us
    pallas_call x2, Pallas kernels, match_block(): pl.pallas_call(functools.partial(match_kernel, block=block), out_shape=ja...  15.1 us
    all_to_all x1, blocking collectives, exchange(): lax.all_to_all(pieces, 'visit', 0, 0, axis_index_groups=same_core, tiled=...  14.7 us
    ppermute x4, waiting for transfers between devices, local(): lax.ppermute(half, 'band', pairings[(turn + number) % 2])  11.7 us
    all_to_all x2, starting transfers between devices, exchange(): lax.all_to_all(pieces, 'visit', 0, 0, axis_index_groups=same_core, tiled=...  10.8 us
    ppermute x4, starting transfers between devices, local(): lax.ppermute(half, 'band', pairings[(turn + number) % 2])  7.12 us
    ppermute x1, waiting for transfers between devices, local(): lax.ppermute(other, 'visit', [(device, device ^ 1) for device in range(VI...  1.99 us
  transfers between devices with their start and end apart: 7, of which 7 were waited for; matrix products, arithmetic and copies ran while one was open for 0% of the time, Pallas kernels for 8%

profile of v1, /device:TPU:0, one launch (start us, length us, event | category | flops | bytes accessed | tf_op | source)
XLA Modules:
  0.0 92.7 jit_solution(16023219342330584536)
XLA Ops:
  0.6 7.5 %match_block.3 = f32[16,16,8,128]{3,2,1,0:T(8,128)} custom-call(s32[1,2]{1,0:T(1,128)} %index_hbm.3, f32[27,64]{1,0:T(8,128)} %bitcast.11, f32[1,2,552,552]{3,2,1,0:T(8,128)} %image_hbm.3, f32[1,2,16,16]{3,2,1,0:T(8,128)} %var_hbm.3, s32[1,2,16,16]{3,2,1,0:T(8,128)} %bits_hbm.3, s32[1,32]{1,0:T(1,128)} %bitcast.13, s32[1,32]{1,0:T(1,128)} %slot_hbm.3, ...), custom_call_target="tpu_custom_call" | custom-call | flops 2621440000 | bytes 3145728 | tf_op jit(solution)/shard_map/match_block/pallas_call | solution.py:296
  8.2 7.1 %all-to-all-start.1 = ((f32[16,128,128]{2,1,0:T(8,128)}), f32[16,128,128]{2,1,0:T(8,128)S(1)}, u32[]{:S(2)}, u32[]{:S(2)}) async-start(f32[16,128,128]{2,1,0:T(8,128)} %bitcast.9), calls=%async_computation.1 | async-start | bytes 2097152 | tf_op jit(solution)/shard_map/all_to_all | solution.py:434
  15.3 7.6 %match_block.2 = f32[16,17,8,128]{3,2,1,0:T(8,128)} custom-call(s32[1,2]{1,0:T(1,128)} %index_hbm.3, f32[27,64]{1,0:T(8,128)} %bitcast.12, f32[1,2,552,552]{3,2,1,0:T(8,128)} %image_hbm.3, f32[1,2,16,16]{3,2,1,0:T(8,128)} %var_hbm.3, s32[1,2,16,16]{3,2,1,0:T(8,128)} %bits_hbm.3, s32[1,32]{1,0:T(1,128)} %bitcast.14, s32[1,32]{1,0:T(1,128)} %slot_hbm.3, ...), custom_call_target="tpu_custom_call" | custom-call | flops 2621440000 | bytes 3145728 | tf_op jit(solution)/shard_map/match_block/pallas_call | solution.py:296
  22.9 10.1 %all-to-all-done.1.second_ref = f32[16,128,128]{2,1,0:T(8,128)S(1)} async-done(((f32[16,128,128]{2,1,0:T(8,128)}), f32[16,128,128]{2,1,0:T(8,128)S(1)}, u32[]{:S(2)}, u32[]{:S(2)}) %all-to-all-start.1) | async-done | bytes 1048608 | tf_op jit(solution)/shard_map/all_to_all | solution.py:434
  33.0 3.7 %all-to-all-start = ((f32[16,136,128]{2,1,0:T(8,128)}), f32[16,136,128]{2,1,0:T(8,128)S(1)}, u32[]{:S(2)}, u32[]{:S(2)}) async-start(f32[16,136,128]{2,1,0:T(8,128)} %bitcast.8), calls=%async_computation | async-start | bytes 2228224 | tf_op jit(solution)/shard_map/all_to_all | solution.py:434
  36.7 17.0 %all-to-all-done.first_ref = f32[16,136,128]{2,1,0:T(8,128)S(1)} async-done(((f32[16,136,128]{2,1,0:T(8,128)}), f32[16,136,128]{2,1,0:T(8,128)S(1)}, u32[]{:S(2)}, u32[]{:S(2)}) %all-to-all-start) | async-done | bytes 1114144 | tf_op jit(solution)/shard_map/all_to_all | solution.py:434
  53.7 1.0 %partial_sums.1 = (f32[1152,128]{1,0:T(8,128)S(1)}, f32[1152,128]{1,0:T(8,128)S(1)}) custom-call(s32[1]{0:T(128)} %bitcast.place_ref, f32[16,136,128]{2,1,0:T(8,128)S(1)} %all-to-all-done.first_ref, f32[16,128,128]{2,1,0:T(8,128)S(1)} %all-to-all-done.1.second_ref), custom_call_target="tpu_custom_call" | custom-call | tf_op jit(solution)/shard_map/partial_sums/pallas_call | solution.py:445
  54.7 0.1 collective-permute-start
  54.8 2.0 %collective-permute-done.other_ref = f32[1152,128]{1,0:T(8,128)S(1)} collective-permute-done((f32[1152,128]{1,0:T(8,128)S(1)}, f32[1152,128]{1,0:T(8,128)S(1)}, u32[]{:S(2)}, u32[]{:S(2)}) %collective-permute-start) | collective-permute-done | bytes 589856 | tf_op jit(solution)/shard_map/ppermute | solution.py:453
  56.8 0.3 merge_cores.1
  57.1 14.7 %all_to_all.15.part_ref = f32[16,64,128]{2,1,0:T(8,128)S(1)} all-to-all(f32[16,64,128]{2,1,0:T(8,128)S(1)} %bitcast.7), channel_id=1, replica_groups={{0,8,16,24,32,40,48,56,64,72,80,88,96,104,112,120},{4,12,20,28,36,44,52..., dimensions={0} | all-to-all | bytes 1048576 | tf_op jit(solution)/shard_map/all_to_all | solution.py:434
  71.8 1.1 %own.1 = (f32[8,128,128]{2,1,0:T(8,128)}, f32[8,128,128]{2,1,0:T(8,128)S(1)}) custom-call(s32[1]{0:T(128)} %bitcast.place_ref, f32[1152,128]{1,0:T(8,128)S(1)} %get-tuple-element.6.mine_ref, f32[1152,128]{1,0:T(8,128)S(1)} %collective-permute-done.other_ref, f32[16,64,128]{2,1,0:T(8,128)S(1)} %all_to_all.15.part_ref), custom_call_target="tpu_custom_call" | custom-call | tf_op jit(solution)/shard_map/own/pallas_call | solution.py:463
  72.9 2.0 %collective-permute-start.1 = (f32[4,128,128]{2,1,0:T(8,128)S(1)}, f32[4,128,128]{2,1,0:T(8,128)S(1)}, u32[]{:S(2)}, u32[]{:S(2)}) collective-permute-start(f32[4,128,128]{2,1,0:T(8,128)S(1)} %get-tuple-element.12), channel_id=1, source_target_pairs={{0,1},{1,0},{2,3},{3,2},{4,5},{5,4},{6,7},{7,6},{8,9},{9,8},{10,11... | collective-permute-start | bytes 786440 | tf_op jit(solution)/shard_map/ppermute | solution.py:476
  74.9 2.5 %collective-permute-start.3 = (f32[4,128,128]{2,1,0:T(8,128)S(1)}, f32[4,128,128]{2,1,0:T(8,128)S(1)}, u32[]{:S(2)}, u32[]{:S(2)}) collective-permute-start(f32[4,128,128]{2,1,0:T(8,128)S(1)} %get-tuple-element.13), channel_id=1, source_target_pairs={{0,3},{3,0},{1,2},{2,1},{4,7},{7,4},{5,6},{6,5},{8,11},{11,8},{9,1... | collective-permute-start | bytes 786440 | tf_op jit(solution)/shard_map/ppermute | solution.py:476
  77.4 2.7 %collective-permute-done.1 = f32[4,128,128]{2,1,0:T(8,128)S(1)} collective-permute-done((f32[4,128,128]{2,1,0:T(8,128)S(1)}, f32[4,128,128]{2,1,0:T(8,128)S(1)}, u32[]{:S(2)}, u32[]{:S(2)}) %collective-permute-start.1) | collective-permute-done | bytes 262176 | tf_op jit(solution)/shard_map/ppermute | solution.py:476
  80.1 2.7 %collective-permute-done.3 = f32[4,128,128]{2,1,0:T(8,128)S(1)} collective-permute-done((f32[4,128,128]{2,1,0:T(8,128)S(1)}, f32[4,128,128]{2,1,0:T(8,128)S(1)}, u32[]{:S(2)}, u32[]{:S(2)}) %collective-permute-start.3) | collective-permute-done | bytes 262176 | tf_op jit(solution)/shard_map/ppermute | solution.py:476
  82.8 0.1 slice_add_fusion.1
  82.9 2.6 %collective-permute-start.2 = (f32[4,128,128]{2,1,0:T(8,128)S(1)}, f32[4,128,128]{2,1,0:T(8,128)S(1)}, u32[]{:S(2)}, u32[]{:S(2)}) collective-permute-start(f32[4,128,128]{2,1,0:T(8,128)S(1)} %get-tuple-element.10), channel_id=1, source_target_pairs={{0,3},{3,0},{1,2},{2,1},{4,7},{7,4},{5,6},{6,5},{8,11},{11,8},{9,1... | collective-permute-start | bytes 786440 | tf_op jit(solution)/shard_map/ppermute | solution.py:476
  85.5 0.0 collective-permute-start.4
  85.5 5.1 %collective-permute-done.2 = f32[4,128,128]{2,1,0:T(8,128)S(1)} collective-permute-done((f32[4,128,128]{2,1,0:T(8,128)S(1)}, f32[4,128,128]{2,1,0:T(8,128)S(1)}, u32[]{:S(2)}, u32[]{:S(2)}) %collective-permute-start.2) | collective-permute-done | bytes 262176 | tf_op jit(solution)/shard_map/ppermute | solution.py:476
  90.6 1.3 %collective-permute-done.4 = f32[4,128,128]{2,1,0:T(8,128)S(1)} collective-permute-done((f32[4,128,128]{2,1,0:T(8,128)S(1)}, f32[4,128,128]{2,1,0:T(8,128)S(1)}, u32[]{:S(2)}, u32[]{:S(2)}) %collective-permute-start.4) | collective-permute-done | bytes 262176 | tf_op jit(solution)/shard_map/ppermute | solution.py:476
  91.9 0.8 pad_maximum_fusion
  (3 shorter events, 0.1 us)
Async XLA Ops:
  8.2 24.8 %all-to-all-start.1 = ((f32[16,128,128]{2,1,0:T(8,128)}), f32[16,128,128]{2,1,0:T(8,128)S(1)}, u32[]{:S(2)}, u32[]{:S(2)}) async-start(f32[16,128,128]{2,1,0:T(8,128)} %bitcast.9), calls=%async_computation.1 | async-start | bytes 2097152 | tf_op jit(solution)/shard_map/all_to_all | solution.py:434
  33.0 20.7 %all-to-all-start = ((f32[16,136,128]{2,1,0:T(8,128)}), f32[16,136,128]{2,1,0:T(8,128)S(1)}, u32[]{:S(2)}, u32[]{:S(2)}) async-start(f32[16,136,128]{2,1,0:T(8,128)} %bitcast.8), calls=%async_computation | async-start | bytes 2228224 | tf_op jit(solution)/shard_map/all_to_all | solution.py:434
  54.7 2.1 %collective-permute-start = (f32[1152,128]{1,0:T(8,128)S(1)}, f32[1152,128]{1,0:T(8,128)S(1)}, u32[]{:S(2)}, u32[]{:S(2)}) collective-permute-start(f32[1152,128]{1,0:T(8,128)S(1)} %get-tuple-element.7), channel_id=1, source_target_pairs={{0,4},{4,0},{8,12},{12,8},{16,20},{20,16},{24,28},{28,24},{32,36},... | collective-permute-start | bytes 1769480 | tf_op jit(solution)/shard_map/ppermute | solution.py:453
  72.9 7.2 %collective-permute-start.1 = (f32[4,128,128]{2,1,0:T(8,128)S(1)}, f32[4,128,128]{2,1,0:T(8,128)S(1)}, u32[]{:S(2)}, u32[]{:S(2)}) collective-permute-start(f32[4,128,128]{2,1,0:T(8,128)S(1)} %get-tuple-element.12), channel_id=1, source_target_pairs={{0,1},{1,0},{2,3},{3,2},{4,5},{5,4},{6,7},{7,6},{8,9},{9,8},{10,11... | collective-permute-start | bytes 786440 | tf_op jit(solution)/shard_map/ppermute | solution.py:476
  74.9 7.9 %collective-permute-start.3 = (f32[4,128,128]{2,1,0:T(8,128)S(1)}, f32[4,128,128]{2,1,0:T(8,128)S(1)}, u32[]{:S(2)}, u32[]{:S(2)}) collective-permute-start(f32[4,128,128]{2,1,0:T(8,128)S(1)} %get-tuple-element.13), channel_id=1, source_target_pairs={{0,3},{3,0},{1,2},{2,1},{4,7},{7,4},{5,6},{6,5},{8,11},{11,8},{9,1... | collective-permute-start | bytes 786440 | tf_op jit(solution)/shard_map/ppermute | solution.py:476
  82.9 7.7 %collective-permute-start.2 = (f32[4,128,128]{2,1,0:T(8,128)S(1)}, f32[4,128,128]{2,1,0:T(8,128)S(1)}, u32[]{:S(2)}, u32[]{:S(2)}) collective-permute-start(f32[4,128,128]{2,1,0:T(8,128)S(1)} %get-tuple-element.10), channel_id=1, source_target_pairs={{0,3},{3,0},{1,2},{2,1},{4,7},{7,4},{5,6},{6,5},{8,11},{11,8},{9,1... | collective-permute-start | bytes 786440 | tf_op jit(solution)/shard_map/ppermute | solution.py:476
  85.5 6.4 %collective-permute-start.4 = (f32[4,128,128]{2,1,0:T(8,128)S(1)}, f32[4,128,128]{2,1,0:T(8,128)S(1)}, u32[]{:S(2)}, u32[]{:S(2)}) collective-permute-start(f32[4,128,128]{2,1,0:T(8,128)S(1)} %get-tuple-element.11), channel_id=1, source_target_pairs={{0,1},{1,0},{2,3},{3,2},{4,5},{5,4},{6,7},{7,6},{8,9},{9,8},{10,11... | collective-permute-start | bytes 786440 | tf_op jit(solution)/shard_map/ppermute | solution.py:476

commit v2 on v1

--- a/solution.py
+++ b/solution.py
@@ -149,8 +149,12 @@
 
 def stacked_halves(value):
     high = value.astype(bf16).astype(f32)
-    rest = jnp.zeros((512 - 3 * SPAN, value.shape[1]), f32)
-    return jnp.concatenate([high, value - high, high, rest], axis=0).astype(bf16)
+    return jnp.concatenate([high, value - high], axis=0).astype(bf16)
+
+
+def against_halves(matrix, halves_ref):
+    rows = jnp.concatenate([halves_ref[...], halves_ref[:SPAN + 8, :]], axis=0)
+    return jnp.dot(matrix, rows, preferred_element_type=f32)
 
 
 def filter_bank():
@@ -179,8 +183,8 @@
     across_ref, down_ref, back_down_ref, back_across_ref, down_taps_ref, along_ref, sems, out_sems,
     tail_ref, high_ref, low_ref, wave_ref, stack_ref, turn_ref, result_ref, rows_ref, factor_ref,
     weight_ref, out_ref,
-    *, block,
 ):
+    blocks = range(2)
     copies = [
         pltpu.make_async_copy(source, goal, sems.at[number])
         for number, (source, goal) in enumerate((
@@ -188,12 +192,13 @@
             (table_hbm, table_ref),
             (down_taps_hbm, down_taps_ref),
             (along_hbm, along_ref),
-            (image_hbm.at[0, block], image_ref),
+            (image_hbm.at[0, 0], image_ref.at[0]),
             (across_hbm, across_ref),
             (var_hbm.at[0], var_ref),
             (bits_hbm.at[0], bits_ref),
             (owner_hbm, owner_ref),
             (slot_hbm, slot_ref),
+            (image_hbm.at[0, 1], image_ref.at[1]),
             (down_hbm, down_ref),
             (back_down_hbm, back_down_ref),
             (back_across_hbm, back_across_ref),
@@ -203,138 +208,166 @@
         copy.start()
     tail_ref[...] = jnp.zeros_like(tail_ref)
     filters = filter_bank()
-    for copy in copies:
-        copy.wait()
-
-    tail_ref[:PADDED, :PADDED - BLOCK] = image_ref[:, BLOCK:]
-    whole = TALL - 16
-    for columns, source in ((slice(0, BLOCK), image_ref), (slice(BLOCK, WIDE), tail_ref)):
-        width = columns.stop - columns.start
-        high_ref[:whole, columns], low_ref[:whole, columns] = split(source[:whole, :width])
-        last = jnp.concatenate([source[whole:PADDED, :width], jnp.zeros((8, width), f32)], axis=0)
-        high_ref[whole:, columns], low_ref[whole:, columns] = split(last)
-
-    forward = jnp.concatenate([across_ref[0], across_ref[0], across_ref[1]], axis=0)
-    backward = jnp.concatenate([back_across_ref[...], back_across_ref[...]], axis=0)
-    pair = 2 * TILE
-    for column in range(SIDE):
-        lanes = slice(column * TILE, column * TILE + pair)
-        high, low = high_ref[:, lanes], low_ref[:, lanes]
-        wave_ref[:, column * pair:(column + 1) * pair] = jnp.dot(
-            jnp.concatenate([high, low, high], axis=1), forward, preferred_element_type=f32
-        )
-
-    same, cross = kernel_spectrum(filters, index_ref[0, block], table_ref, down_taps_ref, along_ref)
-    factor_ref[0] = same.reshape(SPAN // 8, 8, pair)
-    factor_ref[1] = cross.reshape(SPAN // 8, 8, pair)
-
     spread = (
         lax.broadcasted_iota(jnp.int32, (CELLS, BLOCK), 1) // CELL
         == lax.broadcasted_iota(jnp.int32, (CELLS, BLOCK), 0)
     ).astype(f32)
-    weight_ref[...] = exact_dot(cell_weights(var_ref[block], bits_ref[block]), spread)
+    for copy in copies:
+        copy.wait()
+
+    pair = 2 * TILE
+    forward = jnp.concatenate([across_ref[0], across_ref[0], across_ref[1]], axis=0)
+    backward = jnp.concatenate([back_across_ref[...], back_across_ref[...]], axis=0)
     sends = []
-    if block == 0:
-        info = item_info(var_ref, bits_ref, owner_ref, slot_ref)
-        out_ref[:, TILES_BLK] = jnp.broadcast_to(info[None], (CHIPS, INFO, TILE))
-        sends.append(
-            pltpu.make_async_copy(out_ref.at[:, TILES_BLK], out_hbm.at[:, TILES_BLK], out_sems.at[TILES_BLK])
+
+    def send(item):
+        sends.append(pltpu.make_async_copy(out_ref.at[:, item], out_hbm.at[:, item], out_sems.at[item]))
+        sends[-1].start()
+
+    def halve(block):
+        tail_ref[block, :PADDED, :PADDED - BLOCK] = image_ref[block, :, BLOCK:]
+        whole = TALL - 16
+        for first, width, source in ((0, BLOCK, image_ref), (BLOCK, TILE, tail_ref)):
+            lanes = slice(first, first + width)
+            high_ref[block, :whole, lanes], low_ref[block, :whole, lanes] = split(
+                source[block, :whole, :width]
+            )
+            last = jnp.concatenate(
+                [source[block, whole:PADDED, :width], jnp.zeros((8, width), f32)], axis=0
+            )
+            high_ref[block, whole:, lanes], low_ref[block, whole:, lanes] = split(last)
+
+    def transform_across(block, column):
+        lanes = slice(column * TILE, column * TILE + pair)
+        high, low = high_ref[block, :, lanes], low_ref[block, :, lanes]
+        wave_ref[block, :, column * pair:(column + 1) * pair] = jnp.dot(
+            jnp.concatenate([high, low, high], axis=1), forward, preferred_element_type=f32
         )
-        sends[-1].start()
-
-    for line in range(SIDE):
+
+    def prepare(block):
+        same, cross = kernel_spectrum(
+            filters, index_ref[0, block], table_ref, down_taps_ref, along_ref
+        )
+        factor_ref[block, 0] = same.reshape(SPAN // 8, 8, pair)
+        factor_ref[block, 1] = cross.reshape(SPAN // 8, 8, pair)
+        weight_ref[block] = exact_dot(cell_weights(var_ref[block], bits_ref[block]), spread)
+
+    def transform_down(block, line):
         for column in range(SIDE):
             lanes = slice(column * pair, (column + 1) * pair)
-            stack_ref[line, :, lanes] = stacked_halves(
-                wave_ref[line * TILE:line * TILE + SPAN, lanes]
+            stack_ref[block, line, :, lanes] = stacked_halves(
+                wave_ref[block, line * TILE:line * TILE + SPAN, lanes]
             )
-        turn_ref[line] = jnp.dot(down_ref[...], stack_ref[line], preferred_element_type=f32)
-
-    for line in range(SIDE):
+        turn_ref[block, line] = against_halves(down_ref[...], stack_ref.at[block, line])
+
+    def multiply(block, line):
         for column in range(SIDE):
             lanes = slice(column * pair, (column + 1) * pair)
-            wave = turn_ref[line, :SPAN, lanes].reshape(SPAN // 8, 8, pair)
+            wave = turn_ref[block, line, :SPAN, lanes].reshape(SPAN // 8, 8, pair)
             turned = pltpu.roll(wave, 4, 1)
             wave_c, wave_s = wave[..., :TILE], wave[..., TILE:]
             turned_c, turned_s = turned[..., :TILE], turned[..., TILE:]
-            same_c, same_s = factor_ref[0, :, :, :TILE], factor_ref[0, :, :, TILE:]
-            cross_c, cross_s = factor_ref[1, :, :, :TILE], factor_ref[1, :, :, TILE:]
+            same_c, same_s = factor_ref[block, 0, :, :, :TILE], factor_ref[block, 0, :, :, TILE:]
+            cross_c, cross_s = factor_ref[block, 1, :, :, :TILE], factor_ref[block, 1, :, :, TILE:]
             result_c = wave_c * same_c + turned_c * cross_c - wave_s * same_s - turned_s * cross_s
             result_s = wave_s * same_c + turned_s * cross_c + wave_c * same_s + turned_c * cross_s
             result = jnp.concatenate(
                 [result_c.reshape(SPAN, TILE), result_s.reshape(SPAN, TILE)], axis=1
             )
-            result_ref[line, :, lanes] = stacked_halves(result)
-        rows = jnp.dot(back_down_ref[...], result_ref[line], preferred_element_type=f32)
+            result_ref[block, line, :, lanes] = stacked_halves(result)
+
+    def back_down(block, line):
+        rows = against_halves(back_down_ref[...], result_ref.at[block, line])
         for column in range(SIDE):
             high, low = split(rows[:, column * pair:(column + 1) * pair])
-            rows_ref[column, line * TILE:(line + 1) * TILE, :pair] = high
-            rows_ref[column, line * TILE:(line + 1) * TILE, pair:] = low
-
-    for column in range(SIDE):
-        matched = jnp.dot(rows_ref[column], backward, preferred_element_type=f32)
+            rows_ref[block, column, line * TILE:(line + 1) * TILE, :pair] = high
+            rows_ref[block, column, line * TILE:(line + 1) * TILE, pair:] = low
+
+    def back_across(block, column):
+        matched = jnp.dot(rows_ref[block, column], backward, preferred_element_type=f32)
         matched = matched[:, :TILE] + matched[:, TILE:]
-        weight = weight_ref[:, column * TILE:(column + 1) * TILE]
+        weight = weight_ref[block, :, column * TILE:(column + 1) * TILE]
         weighted = matched.reshape(CELLS, CELL, TILE) * weight[:, None, :]
         weighted = weighted.reshape(SIDE, CHIPS, PIECE, TILE)
         for line in range(SIDE):
-            item = line * SIDE + column
+            item = block * TILES_BLK + line * SIDE + column
             out_ref[:, item] = weighted[line]
-            sends.append(
-                pltpu.make_async_copy(out_ref.at[:, item], out_hbm.at[:, item], out_sems.at[item])
-            )
-            sends[-1].start()
-    for send in sends:
-        send.wait()
-
-
-def match_block(block, exposures, variance, bits, table, index, owner, slot):
+            send(item)
+
+    halve(0)
+    for column in range(SIDE):
+        transform_across(0, column)
+    halve(1)
+    for block in blocks:
+        prepare(block)
+    info = item_info(var_ref, bits_ref, owner_ref, slot_ref)
+    out_ref[:, 2 * TILES_BLK] = jnp.broadcast_to(info[None], (CHIPS, INFO, TILE))
+    send(2 * TILES_BLK)
+    for line in range(SIDE):
+        transform_across(1, line)
+        transform_down(0, line)
+    for line in range(SIDE):
+        transform_down(1, line)
+        multiply(0, line)
+    for line in range(SIDE):
+        back_down(0, line)
+        multiply(1, line)
+    for line in range(SIDE):
+        back_across(0, line)
+        back_down(1, line)
+    for line in range(SIDE):
+        back_across(1, line)
+    for copy in sends:
+        copy.wait()
+
+
+def match_blocks(exposures, variance, bits, table, index, owner, slot):
     blocks = exposures.shape[1]
     items = blocks * TILES_BLK
-    groups = TILES_BLK + (1 if block == 0 else 0)
+    groups = items + 1
     matrices = transforms()
     pieces = pl.pallas_call(
-        functools.partial(match_kernel, block=block),
+        match_kernel,
         out_shape=jax.ShapeDtypeStruct((CHIPS, groups, PIECE, TILE), f32),
         in_specs=[pl.BlockSpec(memory_space=pltpu.HBM)] * (7 + len(matrices)),
         out_specs=pl.BlockSpec(memory_space=pltpu.HBM),
         scratch_shapes=[
             pltpu.SMEM((1, blocks), jnp.int32),
             pltpu.SMEM(table.shape, f32),
-            pltpu.VMEM((PADDED, PADDED), f32),
+            pltpu.VMEM((blocks, PADDED, PADDED), f32),
             pltpu.VMEM((blocks, CELLS, CELLS), f32),
             pltpu.VMEM((blocks, CELLS, CELLS), jnp.int32),
             pltpu.VMEM((1, items), jnp.int32),
             pltpu.VMEM((1, items), jnp.int32),
             *[pltpu.VMEM(matrix.shape, matrix.dtype) for matrix in matrices],
-            pltpu.SemaphoreType.DMA((7 + len(matrices),)),
-            pltpu.SemaphoreType.DMA((TILES_BLK + 1,)),
-            pltpu.VMEM((TALL, TILE), f32),
-            pltpu.VMEM((TALL, WIDE), bf16),
-            pltpu.VMEM((TALL, WIDE), bf16),
-            pltpu.VMEM((TALL, 2 * BLOCK), f32),
-            pltpu.VMEM((SIDE, 512, 2 * BLOCK), bf16),
-            pltpu.VMEM((SIDE, SPAN + 8, 2 * BLOCK), f32),
-            pltpu.VMEM((SIDE, 512, 2 * BLOCK), bf16),
-            pltpu.VMEM((SIDE, BLOCK, 4 * TILE), bf16),
-            pltpu.VMEM((2, SPAN // 8, 8, 2 * TILE), f32),
-            pltpu.VMEM((CELLS, BLOCK), f32),
+            pltpu.SemaphoreType.DMA((8 + len(matrices),)),
+            pltpu.SemaphoreType.DMA((groups,)),
+            pltpu.VMEM((blocks, TALL, TILE), f32),
+            pltpu.VMEM((blocks, TALL, WIDE), bf16),
+            pltpu.VMEM((blocks, TALL, WIDE), bf16),
+            pltpu.VMEM((blocks, TALL, 2 * BLOCK), f32),
+            pltpu.VMEM((blocks, SIDE, 2 * SPAN, 2 * BLOCK), bf16),
+            pltpu.VMEM((blocks, SIDE, SPAN + 8, 2 * BLOCK), f32),
+            pltpu.VMEM((blocks, SIDE, 2 * SPAN, 2 * BLOCK), bf16),
+            pltpu.VMEM((blocks, SIDE, BLOCK, 4 * TILE), bf16),
+            pltpu.VMEM((blocks, 2, SPAN // 8, 8, 2 * TILE), f32),
+            pltpu.VMEM((blocks, CELLS, BLOCK), f32),
             pltpu.VMEM((CHIPS, groups, PIECE, TILE), f32),
         ],
         compiler_params=pltpu.CompilerParams(vmem_limit_bytes=60 << 20),
         cost_estimate=pl.CostEstimate(
-            flops=2 * 256 * 256 * 20000, bytes_accessed=3 << 20, transcendentals=0
+            flops=2 * 256 * 256 * 40000, bytes_accessed=6 << 20, transcendentals=0
         ),
-        name="match_block",
+        name="match_blocks",
     )(index, table, exposures, variance, bits, owner, slot, *matrices)
     return pieces.reshape(CHIPS, groups * PIECE, TILE)
 
 
-def partial_kernel(place_ref, first_ref, second_ref, mine_ref, other_ref):
+def partial_kernel(place_ref, part_ref, mine_ref, other_ref):
     core = place_ref[0] % 2
     per_group = TILE // TILES_BLK
     lane = lax.broadcasted_iota(jnp.int32, (INFO, TILE), 1)
-    info = [first_ref[source, TILES_BLK * PIECE:, :] for source in range(CHIPS)]
+    info = [part_ref[source, 2 * TILES_BLK * PIECE:, :] for source in range(CHIPS)]
     tables = []
     for block in range(2):
         rows = []
@@ -377,8 +410,9 @@
     other_ref[owned * PIECE:, :] = sums[owned:]
     for line in range(PIECE):
         total = None
-        for route, part_ref in zip(routes, (first_ref, second_ref)):
-            part = part_ref[:, pl.ds(line, TILES_BLK, PIECE), :].reshape(items, TILE)
+        for block, route in enumerate(routes):
+            rows = pl.ds(block * TILES_BLK * PIECE + line, TILES_BLK, PIECE)
+            part = part_ref[:, rows, :].reshape(items, TILE)
             high, low = split(part)
             term = jnp.dot(
                 route, jnp.concatenate([high, low], axis=1), preferred_element_type=f32
@@ -435,21 +469,17 @@
 
     table = kernel_table.T
     owner = tile_owner.reshape(tile_slot.shape)
-    parts = []
-    for block in range(exposures.shape[1]):
-        pieces = match_block(
-            block, exposures, variance, mask_planes, table, kernel_index, owner, tile_slot
-        )
-        parts.append(exchange(pieces))
-
+    parts = exchange(
+        match_blocks(exposures, variance, mask_planes, table, kernel_index, owner, tile_slot)
+    )
     mine, other = pl.pallas_call(
         partial_kernel,
         out_shape=[jax.ShapeDtypeStruct((owned * (PIECE + 1), TILE), f32)] * 2,
-        in_specs=[smem, vmem, vmem],
+        in_specs=[smem, vmem],
         out_specs=[vmem, vmem],
         compiler_params=params,
         name="partial_sums",
-    )(place, *parts)
+    )(place, parts)
     other = lax.ppermute(other, "visit", [(device, device ^ 1) for device in range(VISITS)])
     pieces = pl.pallas_call(
         merge_kernel,
@@ -469,14 +499,14 @@
         name="own",
     )(place, mine, other, pieces)
 
-    pairings = ([(0, 1), (1, 0), (2, 3), (3, 2)], [(0, 3), (3, 0), (1, 2), (2, 1)])
-    halves = [chi[:OWN_DEV // 2], chi[OWN_DEV // 2:]]
     for turn in range(2):
-        halves = [
-            half + lax.ppermute(half, "band", pairings[(turn + number) % 2])
-            for number, half in enumerate(halves)
+        partners = [
+            (visit * 4 + band, visit * 4 + (band ^ (1 if (visit + turn) % 2 else 3)))
+            for visit in range(VISITS)
+            for band in range(4)
         ]
-    return image[None], jnp.concatenate(halves, axis=0)
+        chi = chi + lax.ppermute(chi, ("visit", "band"), partners)
+    return image[None], chi
 
 
 def solution(mesh):

time: 93.1 us -> 94.3 us (1.013)
  waiting for transfers between devices: 40.8 us -> 50.9 us
  starting transfers between devices: 18 us -> 11.3 us
  Pallas kernels: 17.4 us -> 14.9 us
    all_to_all x2 -> x1, waiting for transfers between devices: 27.1 us -> 32.6 us  [exchange(): lax.all_to_all(pieces, 'visit', 0, 0, axis_index_groups=same_core, tiled=...]
    ppermute x4 -> x2, waiting for transfers between devices: 11.7 us -> 16.3 us  [local(): chi = chi + lax.ppermute(chi, ('visit', 'band'), partners)]
    all_to_all x2 -> x1, starting transfers between devices: 10.8 us -> 7.13 us  [exchange(): lax.all_to_all(pieces, 'visit', 0, 0, axis_index_groups=same_core, tiled=...]
    ppermute x4 -> x2, starting transfers between devices: 7.12 us -> 4.1 us  [local(): chi = chi + lax.ppermute(chi, ('visit', 'band'), partners)]
    pallas_call x2 -> x1, Pallas kernels: 15.1 us -> 12.6 us  [match_blocks(): pl.pallas_call(match_kernel, out_shape=jax.ShapeDtypeStruct((CHIPS, group...]
  transfers between devices with their start and end apart: 7 -> 4, of which waited for: 7 -> 4; matrix products, arithmetic and copies ran while one was open for 0% -> 0% of each run, Pallas kernels for 8% -> 0%
where the time goes in v2:
time: 94.3 us; the launch traced here: 94.1 us
  waiting for transfers between devices  50.9 us (54%)
  blocking collectives  15.3 us (16%)
  Pallas kernels  14.9 us (16%)
  starting transfers between devices  11.3 us (12%)
    all_to_all x1, waiting for transfers between devices, exchange(): lax.all_to_all(pieces, 'visit', 0, 0, axis_index_groups=same_core, tiled=...  32.6 us
    ppermute x2, waiting for transfers between devices, local(): chi = chi + lax.ppermute(chi, ('visit', 'band'), partners)  16.3 us
    all_to_all x1, blocking collectives, exchange(): lax.all_to_all(pieces, 'visit', 0, 0, axis_index_groups=same_core, tiled=...  15.3 us
    pallas_call x1, Pallas kernels, match_blocks(): pl.pallas_call(match_kernel, out_shape=jax.ShapeDtypeStruct((CHIPS, group...  12.6 us
    all_to_all x1, starting transfers between devices, exchange(): lax.all_to_all(pieces, 'visit', 0, 0, axis_index_groups=same_core, tiled=...  7.13 us
    ppermute x2, starting transfers between devices, local(): chi = chi + lax.ppermute(chi, ('visit', 'band'), partners)  4.1 us
    ppermute x1, waiting for transfers between devices, local(): lax.ppermute(other, 'visit', [(device, device ^ 1) for device in range(VI...  1.99 us
  transfers between devices with their start and end apart: 4, of which 4 were waited for; matrix products, arithmetic and copies ran while one was open for 0% of the time, Pallas kernels for 0%

profile of v2, /device:TPU:0, one launch (start us, length us, event | category | flops | bytes accessed | tf_op | source)
XLA Modules:
  0.0 94.1 jit_solution(4285604205486134423)
XLA Ops:
  0.6 12.6 %match_blocks.1 = f32[16,33,8,128]{3,2,1,0:T(8,128)} custom-call(s32[1,2]{1,0:T(1,128)} %index_hbm.1, f32[27,64]{1,0:T(8,128)} %bitcast.9, f32[1,2,552,552]{3,2,1,0:T(8,128)} %image_hbm.1, f32[1,2,16,16]{3,2,1,0:T(8,128)} %var_hbm.1, s32[1,2,16,16]{3,2,1,0:T(8,128)} %bits_hbm.1, s32[1,32]{1,0:T(1,128)} %bitcast.10, s32[1,32]{1,0:T(1,128)} %slot_hbm.1, ...), custom_call_target="tpu_custom_call" | custom-call | flops 5242880000 | bytes 6291456 | tf_op jit(solution)/shard_map/match_blocks/pallas_call | solution.py:329
  13.2 7.1 %all-to-all-start = ((f32[16,264,128]{2,1,0:T(8,128)}), f32[16,264,128]{2,1,0:T(8,128)S(1)}, u32[]{:S(2)}, u32[]{:S(2)}) async-start(f32[16,264,128]{2,1,0:T(8,128)} %bitcast.7), calls=%async_computation | async-start | bytes 4325376 | tf_op jit(solution)/shard_map/all_to_all | solution.py:468
  20.4 32.6 %all-to-all-done.part_ref = f32[16,264,128]{2,1,0:T(8,128)S(1)} async-done(((f32[16,264,128]{2,1,0:T(8,128)}), f32[16,264,128]{2,1,0:T(8,128)S(1)}, u32[]{:S(2)}, u32[]{:S(2)}) %all-to-all-start) | async-done | bytes 2162720 | tf_op jit(solution)/shard_map/all_to_all | solution.py:468
  53.0 1.0 %partial_sums.1 = (f32[1152,128]{1,0:T(8,128)S(1)}, f32[1152,128]{1,0:T(8,128)S(1)}) custom-call(s32[1]{0:T(128)} %bitcast.place_ref, f32[16,264,128]{2,1,0:T(8,128)S(1)} %all-to-all-done.part_ref), custom_call_target="tpu_custom_call" | custom-call | tf_op jit(solution)/shard_map/partial_sums/pallas_call | solution.py:475
  54.0 0.1 collective-permute-start
  54.1 2.0 %collective-permute-done.other_ref = f32[1152,128]{1,0:T(8,128)S(1)} collective-permute-done((f32[1152,128]{1,0:T(8,128)S(1)}, f32[1152,128]{1,0:T(8,128)S(1)}, u32[]{:S(2)}, u32[]{:S(2)}) %collective-permute-start) | collective-permute-done | bytes 589856 | tf_op jit(solution)/shard_map/ppermute | solution.py:483
  56.1 0.3 merge_cores.1
  56.4 15.3 %all_to_all.10.part_ref = f32[16,64,128]{2,1,0:T(8,128)S(1)} all-to-all(f32[16,64,128]{2,1,0:T(8,128)S(1)} %bitcast.6), channel_id=1, replica_groups={{0,8,16,24,32,40,48,56,64,72,80,88,96,104,112,120},{4,12,20,28,36,44,52..., dimensions={0} | all-to-all | bytes 1048576 | tf_op jit(solution)/shard_map/all_to_all | solution.py:468
  71.6 1.1 %own.1 = (f32[8,128,128]{2,1,0:T(8,128)}, f32[8,128,128]{2,1,0:T(8,128)S(1)}) custom-call(s32[1]{0:T(128)} %bitcast.place_ref, f32[1152,128]{1,0:T(8,128)S(1)} %get-tuple-element.6.mine_ref, f32[1152,128]{1,0:T(8,128)S(1)} %collective-permute-done.other_ref, f32[16,64,128]{2,1,0:T(8,128)S(1)} %all_to_all.10.part_ref), custom_call_target="tpu_custom_call" | custom-call | tf_op jit(solution)/shard_map/own/pallas_call | solution.py:493
  72.7 4.0 %collective-permute-start.1 = (f32[8,128,128]{2,1,0:T(8,128)S(1)}, f32[8,128,128]{2,1,0:T(8,128)S(1)}, u32[]{:S(2)}, u32[]{:S(2)}) collective-permute-start(f32[8,128,128]{2,1,0:T(8,128)S(1)} %get-tuple-element.9), channel_id=1, source_target_pairs={{0,3},{1,2},{2,1},{3,0},{4,5},{5,4},{6,7},{7,6},{8,11},{9,10},{10,... | collective-permute-start | bytes 1572872 | tf_op jit(solution)/shard_map/ppermute | solution.py:508
  76.7 7.2 %collective-permute-done.1 = f32[8,128,128]{2,1,0:T(8,128)S(1)} collective-permute-done((f32[8,128,128]{2,1,0:T(8,128)S(1)}, f32[8,128,128]{2,1,0:T(8,128)S(1)}, u32[]{:S(2)}, u32[]{:S(2)}) %collective-permute-start.1) | collective-permute-done | bytes 524320 | tf_op jit(solution)/shard_map/ppermute | solution.py:508
  83.9 0.1 add.6
  84.0 0.1 collective-permute-start.2
  84.0 9.2 %collective-permute-done.2 = f32[8,128,128]{2,1,0:T(8,128)S(1)} collective-permute-done((f32[8,128,128]{2,1,0:T(8,128)S(1)}, f32[8,128,128]{2,1,0:T(8,128)S(1)}, u32[]{:S(2)}, u32[]{:S(2)}) %collective-permute-start.2) | collective-permute-done | bytes 524320 | tf_op jit(solution)/shard_map/ppermute | solution.py:508
  93.2 0.8 add.7
Async XLA Ops:
  13.2 39.8 %all-to-all-start = ((f32[16,264,128]{2,1,0:T(8,128)}), f32[16,264,128]{2,1,0:T(8,128)S(1)}, u32[]{:S(2)}, u32[]{:S(2)}) async-start(f32[16,264,128]{2,1,0:T(8,128)} %bitcast.7), calls=%async_computation | async-start | bytes 4325376 | tf_op jit(solution)/shard_map/all_to_all | solution.py:468
  54.0 2.1 %collective-permute-start = (f32[1152,128]{1,0:T(8,128)S(1)}, f32[1152,128]{1,0:T(8,128)S(1)}, u32[]{:S(2)}, u32[]{:S(2)}) collective-permute-start(f32[1152,128]{1,0:T(8,128)S(1)} %get-tuple-element.7), channel_id=1, source_target_pairs={{0,4},{4,0},{8,12},{12,8},{16,20},{20,16},{24,28},{28,24},{32,36},... | collective-permute-start | bytes 1769480 | tf_op jit(solution)/shard_map/ppermute | solution.py:483
  72.7 11.2 %collective-permute-start.1 = (f32[8,128,128]{2,1,0:T(8,128)S(1)}, f32[8,128,128]{2,1,0:T(8,128)S(1)}, u32[]{:S(2)}, u32[]{:S(2)}) collective-permute-start(f32[8,128,128]{2,1,0:T(8,128)S(1)} %get-tuple-element.9), channel_id=1, source_target_pairs={{0,3},{1,2},{2,1},{3,0},{4,5},{5,4},{6,7},{7,6},{8,11},{9,10},{10,... | collective-permute-start | bytes 1572872 | tf_op jit(solution)/shard_map/ppermute | solution.py:508
  84.0 9.3 %collective-permute-start.2 = (f32[8,128,128]{2,1,0:T(8,128)S(1)}, f32[8,128,128]{2,1,0:T(8,128)S(1)}, u32[]{:S(2)}, u32[]{:S(2)}) collective-permute-start(f32[8,128,128]{2,1,0:T(8,128)S(1)} %add.6), channel_id=1, source_target_pairs={{0,1},{1,0},{2,3},{3,2},{4,7},{5,6},{6,5},{7,4},{8,9},{9,8},{10,11... | collective-permute-start | bytes 1572872 | tf_op jit(solution)/shard_map/ppermute | solution.py:508

commit v3 on v2

--- a/solution.py
+++ b/solution.py
@@ -141,6 +141,41 @@
     return jnp.concatenate(rows, axis=0)
 
 
+def phase_masks(core):
+    return (1, 3) if core == 0 else (3, 1)
+
+
+def way_to(place, piece):
+    core, offset = place % 2, jnp.bitwise_xor(place // 2, piece)
+    first, second = 0, 0
+    for coordinate in (offset // 4, offset % 4):
+        high = coordinate // 2
+        both = jnp.bitwise_xor(high, coordinate % 2)
+        first = 2 * first + jnp.where(core == 0, both, high)
+        second = 2 * second + jnp.where(core == 0, high, both)
+    return 4 * first + second
+
+
+def chip_at(place, first, second):
+    core = place % 2
+    one, two = jnp.where(core == 0, 1, 3), jnp.where(core == 0, 3, 1)
+    offset = 0
+    for bit in (2, 1):
+        step = jnp.bitwise_xor(
+            one if first & bit else 0, two if second & bit else 0
+        )
+        offset = 4 * offset + step
+    return jnp.bitwise_xor(place // 2, offset)
+
+
+def phase_partners(phase, way):
+    partners = []
+    for device in range(VISITS):
+        mask = phase_masks(device % 2)[phase]
+        partners.append((device, device ^ (2 * (4 * mask * (way // 2) + mask * (way % 2)))))
+    return partners
+
+
 def exact_dot(left, right, sides=((1,), (0,))):
     return lax.dot_general(
         left, right, (sides, ((), ())), precision=lax.Precision.HIGHEST, preferred_element_type=f32
@@ -177,8 +212,8 @@
 
 
 def match_kernel(
-    index_hbm, table_hbm, image_hbm, var_hbm, bits_hbm, owner_hbm, slot_hbm,
-    across_hbm, down_hbm, back_down_hbm, back_across_hbm, down_taps_hbm, along_hbm, out_hbm,
+    place_ref, index_hbm, table_hbm, image_hbm, var_hbm, bits_hbm, owner_hbm, slot_hbm,
+    across_hbm, down_hbm, back_down_hbm, back_across_hbm, down_taps_hbm, along_hbm, out_0, out_1, out_2, out_3,
     index_ref, table_ref, image_ref, var_ref, bits_ref, owner_ref, slot_ref,
     across_ref, down_ref, back_down_ref, back_across_ref, down_taps_ref, along_ref, sems, out_sems,
     tail_ref, high_ref, low_ref, wave_ref, stack_ref, turn_ref, result_ref, rows_ref, factor_ref,
@@ -219,10 +254,17 @@
     forward = jnp.concatenate([across_ref[0], across_ref[0], across_ref[1]], axis=0)
     backward = jnp.concatenate([back_across_ref[...], back_across_ref[...]], axis=0)
     sends = []
-
-    def send(item):
-        sends.append(pltpu.make_async_copy(out_ref.at[:, item], out_hbm.at[:, item], out_sems.at[item]))
-        sends[-1].start()
+    spots = [way_to(place_ref[0], piece) for piece in range(CHIPS)]
+
+    def send(part, first, last):
+        for way, out_hbm in enumerate((out_0, out_1, out_2, out_3)):
+            ways = slice(way * 4, way * 4 + 4)
+            sends.append(
+                pltpu.make_async_copy(
+                    out_ref.at[ways, first:last], out_hbm.at[:, first:last], out_sems.at[part, way]
+                )
+            )
+            sends[-1].start()
 
     def halve(block):
         tail_ref[block, :PADDED, :PADDED - BLOCK] = image_ref[block, :, BLOCK:]
@@ -291,8 +333,8 @@
         weighted = weighted.reshape(SIDE, CHIPS, PIECE, TILE)
         for line in range(SIDE):
             item = block * TILES_BLK + line * SIDE + column
-            out_ref[:, item] = weighted[line]
-            send(item)
+            for piece in range(CHIPS):
+                out_ref[spots[piece], item] = weighted[line, piece]
 
     halve(0)
     for column in range(SIDE):
@@ -302,7 +344,6 @@
         prepare(block)
     info = item_info(var_ref, bits_ref, owner_ref, slot_ref)
     out_ref[:, 2 * TILES_BLK] = jnp.broadcast_to(info[None], (CHIPS, INFO, TILE))
-    send(2 * TILES_BLK)
     for line in range(SIDE):
         transform_across(1, line)
         transform_down(0, line)
@@ -315,22 +356,25 @@
     for line in range(SIDE):
         back_across(0, line)
         back_down(1, line)
+    send(0, 0, TILES_BLK)
     for line in range(SIDE):
         back_across(1, line)
+    send(1, TILES_BLK, 2 * TILES_BLK + 1)
     for copy in sends:
         copy.wait()
 
 
-def match_blocks(exposures, variance, bits, table, index, owner, slot):
+def match_blocks(place, exposures, variance, bits, table, index, owner, slot):
     blocks = exposures.shape[1]
     items = blocks * TILES_BLK
     groups = items + 1
     matrices = transforms()
-    pieces = pl.pallas_call(
+    return pl.pallas_call(
         match_kernel,
-        out_shape=jax.ShapeDtypeStruct((CHIPS, groups, PIECE, TILE), f32),
-        in_specs=[pl.BlockSpec(memory_space=pltpu.HBM)] * (7 + len(matrices)),
-        out_specs=pl.BlockSpec(memory_space=pltpu.HBM),
+        out_shape=[jax.ShapeDtypeStruct((4, groups, PIECE, TILE), f32)] * 4,
+        in_specs=[pl.BlockSpec(memory_space=pltpu.SMEM)]
+        + [pl.BlockSpec(memory_space=pltpu.HBM)] * (7 + len(matrices)),
+        out_specs=[pl.BlockSpec(memory_space=pltpu.HBM)] * 4,
         scratch_shapes=[
             pltpu.SMEM((1, blocks), jnp.int32),
             pltpu.SMEM(table.shape, f32),
@@ -341,7 +385,7 @@
             pltpu.VMEM((1, items), jnp.int32),
             *[pltpu.VMEM(matrix.shape, matrix.dtype) for matrix in matrices],
             pltpu.SemaphoreType.DMA((8 + len(matrices),)),
-            pltpu.SemaphoreType.DMA((groups,)),
+            pltpu.SemaphoreType.DMA((2, 4)),
             pltpu.VMEM((blocks, TALL, TILE), f32),
             pltpu.VMEM((blocks, TALL, WIDE), bf16),
             pltpu.VMEM((blocks, TALL, WIDE), bf16),
@@ -359,15 +403,30 @@
             flops=2 * 256 * 256 * 40000, bytes_accessed=6 << 20, transcendentals=0
         ),
         name="match_blocks",
-    )(index, table, exposures, variance, bits, owner, slot, *matrices)
-    return pieces.reshape(CHIPS, groups * PIECE, TILE)
-
-
-def partial_kernel(place_ref, part_ref, mine_ref, other_ref):
+    )(place, index, table, exposures, variance, bits, owner, slot, *matrices)
+
+
+WAYS = (0, 3, 1, 2)
+
+
+def keep_kernel(part_hbm, out_ref, sem):
+    copy = pltpu.make_async_copy(part_hbm, out_ref, sem)
+    copy.start()
+    copy.wait()
+
+
+def turn_kernel(*refs):
+    for first, part_ref in zip(WAYS, refs[:4]):
+        for second, out_ref in enumerate(refs[4:]):
+            out_ref[first] = part_ref[second]
+
+
+def partial_kernel(place_ref, *refs):
+    part_refs, (mine_ref, other_ref) = refs[:4], refs[4:]
     core = place_ref[0] % 2
     per_group = TILE // TILES_BLK
     lane = lax.broadcasted_iota(jnp.int32, (INFO, TILE), 1)
-    info = [part_ref[source, 2 * TILES_BLK * PIECE:, :] for source in range(CHIPS)]
+    info = [part_refs[source // 4][source % 4, 2 * TILES_BLK * PIECE:] for source in range(CHIPS)]
     tables = []
     for block in range(2):
         rows = []
@@ -412,7 +471,9 @@
         total = None
         for block, route in enumerate(routes):
             rows = pl.ds(block * TILES_BLK * PIECE + line, TILES_BLK, PIECE)
-            part = part_ref[:, rows, :].reshape(items, TILE)
+            part = jnp.concatenate(
+                [part_ref[:, rows, :].reshape(items // 4, TILE) for part_ref in part_refs], axis=0
+            )
             high, low = split(part)
             term = jnp.dot(
                 route, jnp.concatenate([high, low], axis=1), preferred_element_type=f32
@@ -431,24 +492,35 @@
     return jnp.dot(sums, pattern, precision=lax.Precision.HIGHEST, preferred_element_type=f32)
 
 
-def merge_kernel(place_ref, mine_ref, other_ref, out_ref):
+def merge_kernel(place_ref, mine_ref, other_ref, *refs):
+    out_refs, scale_ref = refs[:4], refs[4]
     owned = VISITS * OWN_DEV // 2
     cell_row = (place_ref[0] // 2) // (CELL // PIECE)
     sums = mine_ref[owned * PIECE:, :] + other_ref[owned * PIECE:, :]
-    scale = 1.0 / (spread_cells(sums, cell_row) + prior_weight)
-    total = mine_ref[:owned * PIECE, :] + other_ref[:owned * PIECE, :]
-    total = total.reshape(owned, PIECE, TILE) * scale[:, None, :]
-    out_ref[...] = total.reshape(owned * PIECE, TILE)
-
-
-def owner_kernel(place_ref, mine_ref, other_ref, part_ref, image_ref, chi_ref):
+    scale_ref[...] = 1.0 / (spread_cells(sums, cell_row) + prior_weight)
+    height = OWN_DEV * PIECE
+    for first in range(4):
+        for second in range(4):
+            goal = chip_at(place_ref[0], first, second)
+            rows = pl.ds(pl.multiple_of(goal * height, height), height)
+            scale = scale_ref[pl.ds(pl.multiple_of(goal * OWN_DEV, OWN_DEV), OWN_DEV), :]
+            total = (mine_ref[rows, :] + other_ref[rows, :]).reshape(OWN_DEV, PIECE, TILE)
+            out_refs[first][second] = total * scale[:, None, :]
+
+
+def owner_kernel(place_ref, mine_ref, other_ref, *refs):
+    part_refs, (image_ref, chi_ref) = refs[:4], refs[4:]
     owned = VISITS * OWN_DEV // 2
-    rows = pl.ds(pl.multiple_of(owned * PIECE + (place_ref[0] // 2) * OWN_DEV, OWN_DEV), OWN_DEV)
+    chip = place_ref[0] // 2
+    rows = pl.ds(pl.multiple_of(owned * PIECE + chip * OWN_DEV, OWN_DEV), OWN_DEV)
     sums = mine_ref[rows, :] + other_ref[rows, :]
     spread = [spread_cells(sums, cell_row) + prior_weight for cell_row in range(PER_TILE)]
+    for second, part_ref in zip(WAYS, part_refs):
+        for first in range(4):
+            source = chip_at(place_ref[0], first, second)
+            image_ref[:, pl.ds(pl.multiple_of(source * PIECE, PIECE), PIECE), :] = part_ref[first]
     for slot in range(OWN_DEV):
-        image = part_ref[:, slot * PIECE:(slot + 1) * PIECE, :].reshape(TILE, TILE)
-        image_ref[slot] = image
+        image = image_ref[slot]
         weight = jnp.concatenate(
             [jnp.broadcast_to(spread[m][slot:slot + 1], (CELL, TILE)) for m in range(PER_TILE)],
             axis=0,
@@ -461,52 +533,77 @@
     smem = pl.BlockSpec(memory_space=pltpu.SMEM)
     vmem = pl.BlockSpec(memory_space=pltpu.VMEM)
     params = pltpu.CompilerParams(vmem_limit_bytes=32 << 20)
-    same_core = [list(range(core, VISITS, 2)) for core in range(2)]
     owned = VISITS * OWN_DEV // 2
 
-    def exchange(pieces):
-        return lax.all_to_all(pieces, "visit", 0, 0, axis_index_groups=same_core, tiled=True)
+    def exchange(parts):
+        for phase in range(2):
+            parts = [
+                lax.ppermute(parts[way], "visit", phase_partners(phase, way)) if way else parts[0]
+                for way in WAYS
+            ]
+            if phase == 0:
+                parts = pl.pallas_call(
+                    turn_kernel,
+                    out_shape=[jax.ShapeDtypeStruct(parts[0].shape, f32)] * 4,
+                    in_specs=[vmem] * 4,
+                    out_specs=[vmem] * 4,
+                    compiler_params=params,
+                    name="turn",
+                )(*parts)
+        return parts
 
     table = kernel_table.T
     owner = tile_owner.reshape(tile_slot.shape)
-    parts = exchange(
-        match_blocks(exposures, variance, mask_planes, table, kernel_index, owner, tile_slot)
+    parts = match_blocks(
+        place, exposures, variance, mask_planes, table, kernel_index, owner, tile_slot
     )
+    own = pl.pallas_call(
+        keep_kernel,
+        out_shape=jax.ShapeDtypeStruct(parts[0].shape, f32),
+        in_specs=[pl.BlockSpec(memory_space=pltpu.HBM)],
+        out_specs=vmem,
+        scratch_shapes=[pltpu.SemaphoreType.DMA],
+        compiler_params=params,
+        name="keep",
+    )(parts[0])
+    parts = [part.reshape(4, -1, TILE) for part in exchange([own, *parts[1:]])]
+
     mine, other = pl.pallas_call(
         partial_kernel,
         out_shape=[jax.ShapeDtypeStruct((owned * (PIECE + 1), TILE), f32)] * 2,
-        in_specs=[smem, vmem],
+        in_specs=[smem] + [vmem] * 4,
         out_specs=[vmem, vmem],
         compiler_params=params,
         name="partial_sums",
-    )(place, parts)
+    )(place, *parts)
     other = lax.ppermute(other, "visit", [(device, device ^ 1) for device in range(VISITS)])
     pieces = pl.pallas_call(
         merge_kernel,
-        out_shape=jax.ShapeDtypeStruct((owned * PIECE, TILE), f32),
+        out_shape=[jax.ShapeDtypeStruct((4, OWN_DEV, PIECE, TILE), f32)] * 4,
         in_specs=[smem, vmem, vmem],
-        out_specs=vmem,
+        out_specs=[vmem] * 4,
+        scratch_shapes=[pltpu.VMEM((owned, TILE), f32)],
         compiler_params=params,
         name="merge_cores",
     )(place, mine, other)
-    pieces = exchange(pieces.reshape(CHIPS, OWN_DEV * PIECE, TILE))
+    pieces = exchange(pieces)
     image, chi = pl.pallas_call(
         owner_kernel,
         out_shape=[jax.ShapeDtypeStruct((OWN_DEV, TILE, TILE), f32)] * 2,
-        in_specs=[smem, vmem, vmem, vmem],
+        in_specs=[smem, vmem, vmem] + [vmem] * 4,
         out_specs=[vmem, vmem],
         compiler_params=params,
         name="own",
-    )(place, mine, other, pieces)
-
+    )(place, mine, other, *pieces)
+
+    pairings = ([(0, 1), (1, 0), (2, 3), (3, 2)], [(0, 3), (3, 0), (1, 2), (2, 1)])
+    halves = [chi[:OWN_DEV // 2], chi[OWN_DEV // 2:]]
     for turn in range(2):
-        partners = [
-            (visit * 4 + band, visit * 4 + (band ^ (1 if (visit + turn) % 2 else 3)))
-            for visit in range(VISITS)
-            for band in range(4)
+        halves = [
+            half + lax.ppermute(half, "band", pairings[(turn + number) % 2])
+            for number, half in enumerate(halves)
         ]
-        chi = chi + lax.ppermute(chi, ("visit", "band"), partners)
-    return image[None], chi
+    return image[None], jnp.concatenate(halves, axis=0)
 
 
 def solution(mesh):

time: 94.3 us -> 92.2 us (0.978)
  starting transfers between devices: 11.3 us -> 27.2 us
  blocking collectives: 15.3 us -> 0 us
  waiting for transfers between devices: 50.9 us -> 46.8 us
  local copies, waits for them, and re-layouts: 0 us -> 1.08 us
    all_to_all x1 -> x0, waiting for transfers between devices: 32.6 us -> none  [exchange(): lax.all_to_all(pieces, 'visit', 0, 0, axis_index_groups=same_core, tiled=...]
    ppermute x2 -> x16, waiting for transfers between devices: 16.3 us -> 44.8 us  [the longest x12 34 us: exchange(): lax.ppermute(parts[way], 'visit', phase_partners(phase, way))]
    ppermute x2 -> x16, starting transfers between devices: 4.1 us -> 26.9 us  [the longest x12 19.1 us: exchange(): lax.ppermute(parts[way], 'visit', phase_partners(phase, way))]
    all_to_all x1 -> x0, blocking collectives: 15.3 us -> none  [exchange(): lax.all_to_all(pieces, 'visit', 0, 0, axis_index_groups=same_core, tiled=...]
    all_to_all x1 -> x0, starting transfers between devices: 7.13 us -> none  [exchange(): lax.all_to_all(pieces, 'visit', 0, 0, axis_index_groups=same_core, tiled=...]
    unnamed x0 -> x2, local copies, waits for them, and re-layouts: none -> 1.05 us
    pallas_call x2 -> x5, Pallas kernels: 12.8 us -> 13.2 us  [the longest x1 12.7 us: match_blocks(): pl.pallas_call(match_kernel, out_shape=[jax.ShapeDtypeStruct((4, groups,...]
  transfers between devices with their start and end apart: 4 -> 17, of which waited for: 4 -> 14; matrix products, arithmetic and copies ran while one was open for 0% -> 0% of each run, Pallas kernels for 0% -> 0%
where the time goes in v3:
time: 92.2 us; the launch traced here: 92 us
  waiting for transfers between devices  46.8 us (51%)
  starting transfers between devices  27.2 us (30%)
  Pallas kernels  15.2 us (16%)
  local copies, waits for them, and re-layouts  1.08 us (1%)
  other arithmetic  0.95 us (1%)
    ppermute x12, waiting for transfers between devices, exchange(): lax.ppermute(parts[way], 'visit', phase_partners(phase, way))  34 us
    ppermute x12, starting transfers between devices, exchange(): lax.ppermute(parts[way], 'visit', phase_partners(phase, way))  19.1 us
    pallas_call x1, Pallas kernels, match_blocks(): pl.pallas_call(match_kernel, out_shape=[jax.ShapeDtypeStruct((4, groups,...  12.7 us
    ppermute x4, waiting for transfers between devices, local(): lax.ppermute(half, 'band', pairings[(turn + number) % 2])  10.8 us
    ppermute x4, starting transfers between devices, local(): lax.ppermute(half, 'band', pairings[(turn + number) % 2])  7.84 us
    ppermute x1, waiting for transfers between devices, local(): lax.ppermute(other, 'visit', [(device, device ^ 1) for device in range(VI...  1.99 us
  transfers between devices with their start and end apart: 17, of which 14 were waited for; matrix products, arithmetic and copies ran while one was open for 0% of the time, Pallas kernels for 0%

profile of v3, /device:TPU:0, one launch (start us, length us, event | category | flops | bytes accessed | tf_op | source)
XLA Modules:
  0.0 92.0 jit_solution(5910592546558961974)
XLA Ops:
  0.6 12.7 %match_blocks.1 = (f32[4,33,8,128]{3,2,1,0:T(8,128)}, f32[4,33,8,128]{3,2,1,0:T(8,128)}, f32[4,33,8,128]{3,2,1,0:T(8,128)}, f32[4,33,8,128]{3,2,1,0:T(8,128)}) custom-call(s32[1]{0:T(128)} %bitcast.place_ref, s32[1,2]{1,0:T(1,128)} %index_hbm.1, f32[27,64]{1,0:T(8,128)} %bitcast.13, f32[1,2,552,552]{3,2,1,0:T(8,128)} %image_hbm.1, f32[1,2,16,16]{3,2,1,0:T(8,128)} %var_hbm.1, ...), custom_call_target="tpu_custom_call" | custom-call | flops 5242880000 | bytes 6291456 | tf_op jit(solution)/shard_map/match_blocks/pallas_call | solution.py:372
  13.3 2.7 %collective-permute-start = (f32[4,33,8,128]{3,2,1,0:T(8,128)}, f32[4,33,8,128]{3,2,1,0:T(8,128)S(1)}, u32[]{:S(2)}, u32[]{:S(2)}) collective-permute-start(f32[4,33,8,128]{3,2,1,0:T(8,128)} %get-tuple-element.23), channel_id=1, source_target_pairs={{0,40},{4,124},{8,32},{12,116},{16,56},{20,108},{24,48},{28,100},{... | collective-permute-start | bytes 1622024 | tf_op jit(solution)/shard_map/ppermute | solution.py:541
  16.0 0.5 collective-permute-start.1
  16.9 1.0 %copy-done = f32[4,33,8,128]{3,2,1,0:T(8,128)S(1)} copy-done((f32[4,33,8,128]{3,2,1,0:T(8,128)S(1)}, f32[4,33,8,128]{3,2,1,0:T(8,128)}, u32[]{:S(2)}) %copy-start) | copy-done | bytes 540696
  18.0 6.0 %collective-permute-done.refs_1_ = f32[4,33,8,128]{3,2,1,0:T(8,128)S(1)} collective-permute-done((f32[4,33,8,128]{3,2,1,0:T(8,128)}, f32[4,33,8,128]{3,2,1,0:T(8,128)S(1)}, u32[]{:S(2)}, u32[]{:S(2)}) %collective-permute-start) | collective-permute-done | bytes 540704 | tf_op jit(solution)/shard_map/ppermute | solution.py:541
  24.0 5.9 %collective-permute-done.1.refs_2_ = f32[4,33,8,128]{3,2,1,0:T(8,128)S(1)} collective-permute-done((f32[4,33,8,128]{3,2,1,0:T(8,128)}, f32[4,33,8,128]{3,2,1,0:T(8,128)S(1)}, u32[]{:S(2)}, u32[]{:S(2)}) %collective-permute-start.1) | collective-permute-done | bytes 540704 | tf_op jit(solution)/shard_map/ppermute | solution.py:541
  30.1 5.1 %collective-permute-start.3 = (f32[4,33,8,128]{3,2,1,0:T(8,128)S(1)}, f32[4,33,8,128]{3,2,1,0:T(8,128)S(1)}, u32[]{:S(2)}, u32[]{:S(2)}) collective-permute-start(f32[4,33,8,128]{3,2,1,0:T(8,128)S(1)} %get-tuple-element.27), channel_id=1, source_target_pairs={{0,120},{4,44},{8,112},{12,36},{16,104},{20,60},{24,96},{28,52},{3... | collective-permute-start | bytes 1622024 | tf_op jit(solution)/shard_map/ppermute | solution.py:541
  35.2 0.5 collective-permute-start.4
  36.1 6.9 %collective-permute-done.3 = f32[4,33,8,128]{3,2,1,0:T(8,128)S(1)} collective-permute-done((f32[4,33,8,128]{3,2,1,0:T(8,128)S(1)}, f32[4,33,8,128]{3,2,1,0:T(8,128)S(1)}, u32[]{:S(2)}, u32[]{:S(2)}) %collective-permute-start.3) | collective-permute-done | bytes 540704 | tf_op jit(solution)/shard_map/ppermute | solution.py:541
  42.9 5.9 %collective-permute-done.4 = f32[4,33,8,128]{3,2,1,0:T(8,128)S(1)} collective-permute-done((f32[4,33,8,128]{3,2,1,0:T(8,128)S(1)}, f32[4,33,8,128]{3,2,1,0:T(8,128)S(1)}, u32[]{:S(2)}, u32[]{:S(2)}) %collective-permute-start.4) | collective-permute-done | bytes 540704 | tf_op jit(solution)/shard_map/ppermute | solution.py:541
  48.9 1.0 %partial_sums.1 = (f32[1152,128]{1,0:T(8,128)S(1)}, f32[1152,128]{1,0:T(8,128)S(1)}) custom-call(s32[1]{0:T(128)} %bitcast.place_ref, f32[4,264,128]{2,1,0:T(8,128)S(1)} %bitcast.8, f32[4,264,128]{2,1,0:T(8,128)S(1)} %bitcast.9, f32[4,264,128]{2,1,0:T(8,128)S(1)} %bitcast.10, f32[4,264,128]{2,1,0:T(8,128)S(1)} %bitcast.11), custom_call_target="tpu_custom_call" | custom-call | tf_op jit(solution)/shard_map/partial_sums/pallas_call | solution.py:571
  50.1 2.0 %collective-permute-done.6.other_ref = f32[1152,128]{1,0:T(8,128)S(1)} collective-permute-done((f32[1152,128]{1,0:T(8,128)S(1)}, f32[1152,128]{1,0:T(8,128)S(1)}, u32[]{:S(2)}, u32[]{:S(2)}) %collective-permute-start.6) | collective-permute-done | bytes 589856 | tf_op jit(solution)/shard_map/ppermute | solution.py:579
  52.5 1.6 %collective-permute-start.8 = (f32[4,8,8,128]{3,2,1,0:T(8,128)S(1)}, f32[4,8,8,128]{3,2,1,0:T(8,128)S(1)}, u32[]{:S(2)}, u32[]{:S(2)}) collective-permute-start(f32[4,8,8,128]{3,2,1,0:T(8,128)S(1)} %get-tuple-element.34), channel_id=1, source_target_pairs={{0,8},{4,28},{8,0},{12,20},{16,24},{20,12},{24,16},{28,4},{32,40},... | collective-permute-start | bytes 393224 | tf_op jit(solution)/shard_map/ppermute | solution.py:541
  54.1 1.9 %collective-permute-start.9 = (f32[4,8,8,128]{3,2,1,0:T(8,128)S(1)}, f32[4,8,8,128]{3,2,1,0:T(8,128)S(1)}, u32[]{:S(2)}, u32[]{:S(2)}) collective-permute-start(f32[4,8,8,128]{3,2,1,0:T(8,128)S(1)} %get-tuple-element.35), channel_id=1, source_target_pairs={{0,32},{4,100},{8,40},{12,108},{16,48},{20,116},{24,56},{28,124},{... | collective-permute-start | bytes 393224 | tf_op jit(solution)/shard_map/ppermute | solution.py:541
  56.0 2.4 %collective-permute-done.7.refs_1_ = f32[4,8,8,128]{3,2,1,0:T(8,128)S(1)} collective-permute-done((f32[4,8,8,128]{3,2,1,0:T(8,128)S(1)}, f32[4,8,8,128]{3,2,1,0:T(8,128)S(1)}, u32[]{:S(2)}, u32[]{:S(2)}) %collective-permute-start.7) | collective-permute-done | bytes 131104 | tf_op jit(solution)/shard_map/ppermute | solution.py:541
  58.5 1.3 %collective-permute-done.9.refs_3_ = f32[4,8,8,128]{3,2,1,0:T(8,128)S(1)} collective-permute-done((f32[4,8,8,128]{3,2,1,0:T(8,128)S(1)}, f32[4,8,8,128]{3,2,1,0:T(8,128)S(1)}, u32[]{:S(2)}, u32[]{:S(2)}) %collective-permute-start.9) | collective-permute-done | bytes 131104 | tf_op jit(solution)/shard_map/ppermute | solution.py:541
  59.8 4.9 %collective-permute-start.10 = (f32[4,8,8,128]{3,2,1,0:T(8,128)S(1)}, f32[4,8,8,128]{3,2,1,0:T(8,128)S(1)}, u32[]{:S(2)}, u32[]{:S(2)}) collective-permute-start(f32[4,8,8,128]{3,2,1,0:T(8,128)S(1)} %get-tuple-element.37), channel_id=1, source_target_pairs={{0,120},{4,44},{8,112},{12,36},{16,104},{20,60},{24,96},{28,52},{3... | collective-permute-start | bytes 393224 | tf_op jit(solution)/shard_map/ppermute | solution.py:541
  64.7 0.5 collective-permute-start.11
  65.2 0.6 collective-permute-start.12
  65.8 2.4 %collective-permute-done.10.refs_1_ = f32[4,8,8,128]{3,2,1,0:T(8,128)S(1)} collective-permute-done((f32[4,8,8,128]{3,2,1,0:T(8,128)S(1)}, f32[4,8,8,128]{3,2,1,0:T(8,128)S(1)}, u32[]{:S(2)}, u32[]{:S(2)}) %collective-permute-start.10) | collective-permute-done | bytes 131104 | tf_op jit(solution)/shard_map/ppermute | solution.py:541
  68.2 2.7 %collective-permute-done.11.refs_2_ = f32[4,8,8,128]{3,2,1,0:T(8,128)S(1)} collective-permute-done((f32[4,8,8,128]{3,2,1,0:T(8,128)S(1)}, f32[4,8,8,128]{3,2,1,0:T(8,128)S(1)}, u32[]{:S(2)}, u32[]{:S(2)}) %collective-permute-start.11) | collective-permute-done | bytes 131104 | tf_op jit(solution)/shard_map/ppermute | solution.py:541
  70.9 0.5 collective-permute-done.12.refs_3_
  71.4 1.0 %own.1 = (f32[8,128,128]{2,1,0:T(8,128)}, f32[8,128,128]{2,1,0:T(8,128)S(1)}) custom-call(s32[1]{0:T(128)} %bitcast.place_ref, f32[1152,128]{1,0:T(8,128)S(1)} %get-tuple-element.30.mine_ref, f32[1152,128]{1,0:T(8,128)S(1)} %collective-permute-done.6.other_ref, f32[4,8,8,128]{3,2,1,0:T(8,128)S(1)} %get-tuple-element.36.refs_0_, ...), custom_call_target="tpu_custom_call" | custom-call | tf_op jit(solution)/shard_map/own/pallas_call | solution.py:590
  72.4 2.0 %collective-permute-start.13 = (f32[4,128,128]{2,1,0:T(8,128)S(1)}, f32[4,128,128]{2,1,0:T(8,128)S(1)}, u32[]{:S(2)}, u32[]{:S(2)}) collective-permute-start(f32[4,128,128]{2,1,0:T(8,128)S(1)} %get-tuple-element.44), channel_id=1, source_target_pairs={{0,1},{1,0},{2,3},{3,2},{4,5},{5,4},{6,7},{7,6},{8,9},{9,8},{10,11... | collective-permute-start | bytes 786440 | tf_op jit(solution)/shard_map/ppermute | solution.py:603
  74.4 2.5 %collective-permute-start.15 = (f32[4,128,128]{2,1,0:T(8,128)S(1)}, f32[4,128,128]{2,1,0:T(8,128)S(1)}, u32[]{:S(2)}, u32[]{:S(2)}) collective-permute-start(f32[4,128,128]{2,1,0:T(8,128)S(1)} %get-tuple-element.45), channel_id=1, source_target_pairs={{0,3},{3,0},{1,2},{2,1},{4,7},{7,4},{5,6},{6,5},{8,11},{11,8},{9,1... | collective-permute-start | bytes 786440 | tf_op jit(solution)/shard_map/ppermute | solution.py:603
  76.9 1.9 %collective-permute-done.13 = f32[4,128,128]{2,1,0:T(8,128)S(1)} collective-permute-done((f32[4,128,128]{2,1,0:T(8,128)S(1)}, f32[4,128,128]{2,1,0:T(8,128)S(1)}, u32[]{:S(2)}, u32[]{:S(2)}) %collective-permute-start.13) | collective-permute-done | bytes 262176 | tf_op jit(solution)/shard_map/ppermute | solution.py:603
  78.9 3.3 %collective-permute-done.15 = f32[4,128,128]{2,1,0:T(8,128)S(1)} collective-permute-done((f32[4,128,128]{2,1,0:T(8,128)S(1)}, f32[4,128,128]{2,1,0:T(8,128)S(1)}, u32[]{:S(2)}, u32[]{:S(2)}) %collective-permute-start.15) | collective-permute-done | bytes 262176 | tf_op jit(solution)/shard_map/ppermute | solution.py:603
  82.2 2.6 %collective-permute-start.14 = (f32[4,128,128]{2,1,0:T(8,128)S(1)}, f32[4,128,128]{2,1,0:T(8,128)S(1)}, u32[]{:S(2)}, u32[]{:S(2)}) collective-permute-start(f32[4,128,128]{2,1,0:T(8,128)S(1)} %get-tuple-element.42), channel_id=1, source_target_pairs={{0,3},{3,0},{1,2},{2,1},{4,7},{7,4},{5,6},{6,5},{8,11},{11,8},{9,1... | collective-permute-start | bytes 786440 | tf_op jit(solution)/shard_map/ppermute | solution.py:603
  84.8 0.7 collective-permute-start.16
  85.5 4.3 %collective-permute-done.14 = f32[4,128,128]{2,1,0:T(8,128)S(1)} collective-permute-done((f32[4,128,128]{2,1,0:T(8,128)S(1)}, f32[4,128,128]{2,1,0:T(8,128)S(1)}, u32[]{:S(2)}, u32[]{:S(2)}) %collective-permute-start.14) | collective-permute-done | bytes 262176 | tf_op jit(solution)/shard_map/ppermute | solution.py:603
  89.9 1.3 %collective-permute-done.16 = f32[4,128,128]{2,1,0:T(8,128)S(1)} collective-permute-done((f32[4,128,128]{2,1,0:T(8,128)S(1)}, f32[4,128,128]{2,1,0:T(8,128)S(1)}, u32[]{:S(2)}, u32[]{:S(2)}) %collective-permute-start.16) | collective-permute-done | bytes 262176 | tf_op jit(solution)/shard_map/ppermute | solution.py:603
  91.2 0.8 pad_maximum_fusion
  (16 shorter events, 1.8 us)
Async XLA Ops:
  13.3 10.7 %collective-permute-start = (f32[4,33,8,128]{3,2,1,0:T(8,128)}, f32[4,33,8,128]{3,2,1,0:T(8,128)S(1)}, u32[]{:S(2)}, u32[]{:S(2)}) collective-permute-start(f32[4,33,8,128]{3,2,1,0:T(8,128)} %get-tuple-element.23), channel_id=1, source_target_pairs={{0,40},{4,124},{8,32},{12,116},{16,56},{20,108},{24,48},{28,100},{... | collective-permute-start | bytes 1622024 | tf_op jit(solution)/shard_map/ppermute | solution.py:541
  16.0 13.9 %collective-permute-start.1 = (f32[4,33,8,128]{3,2,1,0:T(8,128)}, f32[4,33,8,128]{3,2,1,0:T(8,128)S(1)}, u32[]{:S(2)}, u32[]{:S(2)}) collective-permute-start(f32[4,33,8,128]{3,2,1,0:T(8,128)} %get-tuple-element.24), channel_id=1, source_target_pairs={{0,8},{4,28},{8,0},{12,20},{16,24},{20,12},{24,16},{28,4},{32,40},... | collective-permute-start | bytes 1622024 | tf_op jit(solution)/shard_map/ppermute | solution.py:541
  16.6 13.4 %collective-permute-start.2 = (f32[4,33,8,128]{3,2,1,0:T(8,128)}, f32[4,33,8,128]{3,2,1,0:T(8,128)S(1)}, u32[]{:S(2)}, u32[]{:S(2)}) collective-permute-start(f32[4,33,8,128]{3,2,1,0:T(8,128)} %get-tuple-element.25), channel_id=1, source_target_pairs={{0,32},{4,100},{8,40},{12,108},{16,48},{20,116},{24,56},{28,124},{... | collective-permute-start | bytes 1622024 | tf_op jit(solution)/shard_map/ppermute | solution.py:541
  16.9 1.0 %copy-start = (f32[4,33,8,128]{3,2,1,0:T(8,128)S(1)}, f32[4,33,8,128]{3,2,1,0:T(8,128)}, u32[]{:S(2)}) copy-start(f32[4,33,8,128]{3,2,1,0:T(8,128)} %get-tuple-element.22.part_hbm) | copy-start | bytes 1622020
  30.1 12.9 %collective-permute-start.3 = (f32[4,33,8,128]{3,2,1,0:T(8,128)S(1)}, f32[4,33,8,128]{3,2,1,0:T(8,128)S(1)}, u32[]{:S(2)}, u32[]{:S(2)}) collective-permute-start(f32[4,33,8,128]{3,2,1,0:T(8,128)S(1)} %get-tuple-element.27), channel_id=1, source_target_pairs={{0,120},{4,44},{8,112},{12,36},{16,104},{20,60},{24,96},{28,52},{3... | collective-permute-start | bytes 1622024 | tf_op jit(solution)/shard_map/ppermute | solution.py:541
  35.2 13.7 %collective-permute-start.4 = (f32[4,33,8,128]{3,2,1,0:T(8,128)S(1)}, f32[4,33,8,128]{3,2,1,0:T(8,128)S(1)}, u32[]{:S(2)}, u32[]{:S(2)}) collective-permute-start(f32[4,33,8,128]{3,2,1,0:T(8,128)S(1)} %get-tuple-element.28), channel_id=1, source_target_pairs={{0,24},{4,12},{8,16},{12,4},{16,8},{20,28},{24,0},{28,20},{32,56},... | collective-permute-start | bytes 1622024 | tf_op jit(solution)/shard_map/ppermute | solution.py:541
  35.7 13.2 %collective-permute-start.5 = (f32[4,33,8,128]{3,2,1,0:T(8,128)S(1)}, f32[4,33,8,128]{3,2,1,0:T(8,128)S(1)}, u32[]{:S(2)}, u32[]{:S(2)}) collective-permute-start(f32[4,33,8,128]{3,2,1,0:T(8,128)S(1)} %get-tuple-element.29), channel_id=1, source_target_pairs={{0,96},{4,36},{8,104},{12,44},{16,112},{20,52},{24,120},{28,60},{3... | collective-permute-start | bytes 1622024 | tf_op jit(solution)/shard_map/ppermute | solution.py:541
  49.9 2.3 %collective-permute-start.6 = (f32[1152,128]{1,0:T(8,128)S(1)}, f32[1152,128]{1,0:T(8,128)S(1)}, u32[]{:S(2)}, u32[]{:S(2)}) collective-permute-start(f32[1152,128]{1,0:T(8,128)S(1)} %get-tuple-element.31), channel_id=1, source_target_pairs={{0,4},{4,0},{8,12},{12,8},{16,20},{20,16},{24,28},{28,24},{32,36},... | collective-permute-start | bytes 1769480 | tf_op jit(solution)/shard_map/ppermute | solution.py:579
  52.5 6.0 %collective-permute-start.7 = (f32[4,8,8,128]{3,2,1,0:T(8,128)S(1)}, f32[4,8,8,128]{3,2,1,0:T(8,128)S(1)}, u32[]{:S(2)}, u32[]{:S(2)}) collective-permute-start(f32[4,8,8,128]{3,2,1,0:T(8,128)S(1)} %get-tuple-element.33), channel_id=1, source_target_pairs={{0,40},{4,124},{8,32},{12,116},{16,56},{20,108},{24,48},{28,100},{... | collective-permute-start | bytes 393224 | tf_op jit(solution)/shard_map/ppermute | solution.py:541
  52.5 5.9 %collective-permute-start.8 = (f32[4,8,8,128]{3,2,1,0:T(8,128)S(1)}, f32[4,8,8,128]{3,2,1,0:T(8,128)S(1)}, u32[]{:S(2)}, u32[]{:S(2)}) collective-permute-start(f32[4,8,8,128]{3,2,1,0:T(8,128)S(1)} %get-tuple-element.34), channel_id=1, source_target_pairs={{0,8},{4,28},{8,0},{12,20},{16,24},{20,12},{24,16},{28,4},{32,40},... | collective-permute-start | bytes 393224 | tf_op jit(solution)/shard_map/ppermute | solution.py:541
  54.1 5.7 %collective-permute-start.9 = (f32[4,8,8,128]{3,2,1,0:T(8,128)S(1)}, f32[4,8,8,128]{3,2,1,0:T(8,128)S(1)}, u32[]{:S(2)}, u32[]{:S(2)}) collective-permute-start(f32[4,8,8,128]{3,2,1,0:T(8,128)S(1)} %get-tuple-element.35), channel_id=1, source_target_pairs={{0,32},{4,100},{8,40},{12,108},{16,48},{20,116},{24,56},{28,124},{... | collective-permute-start | bytes 393224 | tf_op jit(solution)/shard_map/ppermute | solution.py:541
  59.8 8.4 %collective-permute-start.10 = (f32[4,8,8,128]{3,2,1,0:T(8,128)S(1)}, f32[4,8,8,128]{3,2,1,0:T(8,128)S(1)}, u32[]{:S(2)}, u32[]{:S(2)}) collective-permute-start(f32[4,8,8,128]{3,2,1,0:T(8,128)S(1)} %get-tuple-element.37), channel_id=1, source_target_pairs={{0,120},{4,44},{8,112},{12,36},{16,104},{20,60},{24,96},{28,52},{3... | collective-permute-start | bytes 393224 | tf_op jit(solution)/shard_map/ppermute | solution.py:541
  64.7 6.2 %collective-permute-start.11 = (f32[4,8,8,128]{3,2,1,0:T(8,128)S(1)}, f32[4,8,8,128]{3,2,1,0:T(8,128)S(1)}, u32[]{:S(2)}, u32[]{:S(2)}) collective-permute-start(f32[4,8,8,128]{3,2,1,0:T(8,128)S(1)} %get-tuple-element.38), channel_id=1, source_target_pairs={{0,24},{4,12},{8,16},{12,4},{16,8},{20,28},{24,0},{28,20},{32,56},... | collective-permute-start | bytes 393224 | tf_op jit(solution)/shard_map/ppermute | solution.py:541
  65.2 6.2 %collective-permute-start.12 = (f32[4,8,8,128]{3,2,1,0:T(8,128)S(1)}, f32[4,8,8,128]{3,2,1,0:T(8,128)S(1)}, u32[]{:S(2)}, u32[]{:S(2)}) collective-permute-start(f32[4,8,8,128]{3,2,1,0:T(8,128)S(1)} %get-tuple-element.39), channel_id=1, source_target_pairs={{0,96},{4,36},{8,104},{12,44},{16,112},{20,52},{24,120},{28,60},{3... | collective-permute-start | bytes 393224 | tf_op jit(solution)/shard_map/ppermute | solution.py:541
  72.4 6.5 %collective-permute-start.13 = (f32[4,128,128]{2,1,0:T(8,128)S(1)}, f32[4,128,128]{2,1,0:T(8,128)S(1)}, u32[]{:S(2)}, u32[]{:S(2)}) collective-permute-start(f32[4,128,128]{2,1,0:T(8,128)S(1)} %get-tuple-element.44), channel_id=1, source_target_pairs={{0,1},{1,0},{2,3},{3,2},{4,5},{5,4},{6,7},{7,6},{8,9},{9,8},{10,11... | collective-permute-start | bytes 786440 | tf_op jit(solution)/shard_map/ppermute | solution.py:603
  74.4 7.7 %collective-permute-start.15 = (f32[4,128,128]{2,1,0:T(8,128)S(1)}, f32[4,128,128]{2,1,0:T(8,128)S(1)}, u32[]{:S(2)}, u32[]{:S(2)}) collective-permute-start(f32[4,128,128]{2,1,0:T(8,128)S(1)} %get-tuple-element.45), channel_id=1, source_target_pairs={{0,3},{3,0},{1,2},{2,1},{4,7},{7,4},{5,6},{6,5},{8,11},{11,8},{9,1... | collective-permute-start | bytes 786440 | tf_op jit(solution)/shard_map/ppermute | solution.py:603
  82.2 7.7 %collective-permute-start.14 = (f32[4,128,128]{2,1,0:T(8,128)S(1)}, f32[4,128,128]{2,1,0:T(8,128)S(1)}, u32[]{:S(2)}, u32[]{:S(2)}) collective-permute-start(f32[4,128,128]{2,1,0:T(8,128)S(1)} %get-tuple-element.42), channel_id=1, source_target_pairs={{0,3},{3,0},{1,2},{2,1},{4,7},{7,4},{5,6},{6,5},{8,11},{11,8},{9,1... | collective-permute-start | bytes 786440 | tf_op jit(solution)/shard_map/ppermute | solution.py:603
  84.8 6.4 %collective-permute-start.16 = (f32[4,128,128]{2,1,0:T(8,128)S(1)}, f32[4,128,128]{2,1,0:T(8,128)S(1)}, u32[]{:S(2)}, u32[]{:S(2)}) collective-permute-start(f32[4,128,128]{2,1,0:T(8,128)S(1)} %get-tuple-element.43), channel_id=1, source_target_pairs={{0,1},{1,0},{2,3},{3,2},{4,5},{5,4},{6,7},{7,6},{8,9},{9,8},{10,11... | collective-permute-start | bytes 786440 | tf_op jit(solution)/shard_map/ppermute | solution.py:603

commit v4 on v1

--- a/solution.py
+++ b/solution.py
@@ -141,6 +141,29 @@
     return jnp.concatenate(rows, axis=0)
 
 
+def phase_masks(core):
+    return (1, 3) if core == 0 else (3, 1)
+
+
+def way_to(place, piece):
+    core, offset = place % 2, jnp.bitwise_xor(place // 2, piece)
+    first, second = 0, 0
+    for coordinate in (offset // 4, offset % 4):
+        high = coordinate // 2
+        both = jnp.bitwise_xor(high, coordinate % 2)
+        first = 2 * first + jnp.where(core == 0, both, high)
+        second = 2 * second + jnp.where(core == 0, high, both)
+    return 4 * first + second
+
+
+def phase_partners(phase, way):
+    partners = []
+    for device in range(VISITS):
+        mask = phase_masks(device % 2)[phase]
+        partners.append((device, device ^ (2 * (4 * mask * (way // 2) + mask * (way % 2)))))
+    return partners
+
+
 def exact_dot(left, right, sides=((1,), (0,))):
     return lax.dot_general(
         left, right, (sides, ((), ())), precision=lax.Precision.HIGHEST, preferred_element_type=f32
@@ -149,8 +172,12 @@
 
 def stacked_halves(value):
     high = value.astype(bf16).astype(f32)
-    rest = jnp.zeros((512 - 3 * SPAN, value.shape[1]), f32)
-    return jnp.concatenate([high, value - high, high, rest], axis=0).astype(bf16)
+    return jnp.concatenate([high, value - high], axis=0).astype(bf16)
+
+
+def against_halves(matrix, halves_ref):
+    rows = jnp.concatenate([halves_ref[...], halves_ref[:SPAN + 8, :]], axis=0)
+    return jnp.dot(matrix, rows, preferred_element_type=f32)
 
 
 def filter_bank():
@@ -173,8 +200,9 @@
 
 
 def match_kernel(
-    index_hbm, table_hbm, image_hbm, var_hbm, bits_hbm, owner_hbm, slot_hbm,
-    across_hbm, down_hbm, back_down_hbm, back_across_hbm, down_taps_hbm, along_hbm, out_hbm,
+    place_ref, index_hbm, table_hbm, image_hbm, var_hbm, bits_hbm, owner_hbm, slot_hbm,
+    across_hbm, down_hbm, back_down_hbm, back_across_hbm, down_taps_hbm, along_hbm,
+    out_0, out_1, out_2, out_3,
     index_ref, table_ref, image_ref, var_ref, bits_ref, owner_ref, slot_ref,
     across_ref, down_ref, back_down_ref, back_across_ref, down_taps_ref, along_ref, sems, out_sems,
     tail_ref, high_ref, low_ref, wave_ref, stack_ref, turn_ref, result_ref, rows_ref, factor_ref,
@@ -203,75 +231,75 @@
         copy.start()
     tail_ref[...] = jnp.zeros_like(tail_ref)
     filters = filter_bank()
-    for copy in copies:
-        copy.wait()
-
-    tail_ref[:PADDED, :PADDED - BLOCK] = image_ref[:, BLOCK:]
-    whole = TALL - 16
-    for columns, source in ((slice(0, BLOCK), image_ref), (slice(BLOCK, WIDE), tail_ref)):
-        width = columns.stop - columns.start
-        high_ref[:whole, columns], low_ref[:whole, columns] = split(source[:whole, :width])
-        last = jnp.concatenate([source[whole:PADDED, :width], jnp.zeros((8, width), f32)], axis=0)
-        high_ref[whole:, columns], low_ref[whole:, columns] = split(last)
-
-    forward = jnp.concatenate([across_ref[0], across_ref[0], across_ref[1]], axis=0)
-    backward = jnp.concatenate([back_across_ref[...], back_across_ref[...]], axis=0)
-    pair = 2 * TILE
-    for column in range(SIDE):
-        lanes = slice(column * TILE, column * TILE + pair)
-        high, low = high_ref[:, lanes], low_ref[:, lanes]
-        wave_ref[:, column * pair:(column + 1) * pair] = jnp.dot(
-            jnp.concatenate([high, low, high], axis=1), forward, preferred_element_type=f32
-        )
-
-    same, cross = kernel_spectrum(filters, index_ref[0, block], table_ref, down_taps_ref, along_ref)
-    factor_ref[0] = same.reshape(SPAN // 8, 8, pair)
-    factor_ref[1] = cross.reshape(SPAN // 8, 8, pair)
-
     spread = (
         lax.broadcasted_iota(jnp.int32, (CELLS, BLOCK), 1) // CELL
         == lax.broadcasted_iota(jnp.int32, (CELLS, BLOCK), 0)
     ).astype(f32)
-    weight_ref[...] = exact_dot(cell_weights(var_ref[block], bits_ref[block]), spread)
-    sends = []
-    if block == 0:
-        info = item_info(var_ref, bits_ref, owner_ref, slot_ref)
-        out_ref[:, TILES_BLK] = jnp.broadcast_to(info[None], (CHIPS, INFO, TILE))
-        sends.append(
-            pltpu.make_async_copy(out_ref.at[:, TILES_BLK], out_hbm.at[:, TILES_BLK], out_sems.at[TILES_BLK])
-        )
-        sends[-1].start()
-
-    for line in range(SIDE):
-        for column in range(SIDE):
-            lanes = slice(column * pair, (column + 1) * pair)
-            stack_ref[line, :, lanes] = stacked_halves(
-                wave_ref[line * TILE:line * TILE + SPAN, lanes]
+    for copy in copies:
+        copy.wait()
+
+    pair = 2 * TILE
+    forward = jnp.concatenate([across_ref[0], across_ref[0], across_ref[1]], axis=0)
+    backward = jnp.concatenate([back_across_ref[...], back_across_ref[...]], axis=0)
+    spots = [way_to(place_ref[0], piece) for piece in range(CHIPS)]
+
+    def halve():
+        tail_ref[:PADDED, :PADDED - BLOCK] = image_ref[:, BLOCK:]
+        whole = TALL - 16
+        for first, width, source in ((0, BLOCK, image_ref), (BLOCK, TILE, tail_ref)):
+            lanes = slice(first, first + width)
+            high_ref[:whole, lanes], low_ref[:whole, lanes] = split(source[:whole, :width])
+            last = jnp.concatenate(
+                [source[whole:PADDED, :width], jnp.zeros((8, width), f32)], axis=0
             )
-        turn_ref[line] = jnp.dot(down_ref[...], stack_ref[line], preferred_element_type=f32)
-
-    for line in range(SIDE):
-        for column in range(SIDE):
-            lanes = slice(column * pair, (column + 1) * pair)
-            wave = turn_ref[line, :SPAN, lanes].reshape(SPAN // 8, 8, pair)
-            turned = pltpu.roll(wave, 4, 1)
-            wave_c, wave_s = wave[..., :TILE], wave[..., TILE:]
-            turned_c, turned_s = turned[..., :TILE], turned[..., TILE:]
-            same_c, same_s = factor_ref[0, :, :, :TILE], factor_ref[0, :, :, TILE:]
-            cross_c, cross_s = factor_ref[1, :, :, :TILE], factor_ref[1, :, :, TILE:]
-            result_c = wave_c * same_c + turned_c * cross_c - wave_s * same_s - turned_s * cross_s
-            result_s = wave_s * same_c + turned_s * cross_c + wave_c * same_s + turned_c * cross_s
-            result = jnp.concatenate(
-                [result_c.reshape(SPAN, TILE), result_s.reshape(SPAN, TILE)], axis=1
-            )
-            result_ref[line, :, lanes] = stacked_halves(result)
-        rows = jnp.dot(back_down_ref[...], result_ref[line], preferred_element_type=f32)
-        for column in range(SIDE):
-            high, low = split(rows[:, column * pair:(column + 1) * pair])
-            rows_ref[column, line * TILE:(line + 1) * TILE, :pair] = high
-            rows_ref[column, line * TILE:(line + 1) * TILE, pair:] = low
-
-    for column in range(SIDE):
+            high_ref[whole:, lanes], low_ref[whole:, lanes] = split(last)
+
+    def transform_across(column):
+        lanes = slice(column * TILE, column * TILE + pair)
+        high, low = high_ref[:, lanes], low_ref[:, lanes]
+        wave_ref[column] = jnp.dot(
+            jnp.concatenate([high, low, high], axis=1), forward, preferred_element_type=f32
+        )
+
+    def prepare():
+        same, cross = kernel_spectrum(
+            filters, index_ref[0, block], table_ref, down_taps_ref, along_ref
+        )
+        factor_ref[0] = same.reshape(SPAN // 8, 8, pair)
+        factor_ref[1] = cross.reshape(SPAN // 8, 8, pair)
+        weight_ref[...] = exact_dot(cell_weights(var_ref[block], bits_ref[block]), spread)
+        if block == 0:
+            info = item_info(var_ref, bits_ref, owner_ref, slot_ref)
+            out_ref[:, TILES_BLK] = jnp.broadcast_to(info[None], (CHIPS, INFO, TILE))
+
+    def stack(tile):
+        column, line = divmod(tile, SIDE)
+        stack_ref[tile] = stacked_halves(wave_ref[column, line * TILE:line * TILE + SPAN, :])
+
+    def transform_down(tile):
+        turn_ref[tile] = against_halves(down_ref[...], stack_ref.at[tile])
+
+    def multiply(tile):
+        wave = turn_ref[tile, :SPAN].reshape(SPAN // 8, 8, pair)
+        turned = pltpu.roll(wave, 4, 1)
+        wave_c, wave_s = wave[..., :TILE], wave[..., TILE:]
+        turned_c, turned_s = turned[..., :TILE], turned[..., TILE:]
+        same_c, same_s = factor_ref[0, :, :, :TILE], factor_ref[0, :, :, TILE:]
+        cross_c, cross_s = factor_ref[1, :, :, :TILE], factor_ref[1, :, :, TILE:]
+        result_c = wave_c * same_c + turned_c * cross_c - wave_s * same_s - turned_s * cross_s
+        result_s = wave_s * same_c + turned_s * cross_c + wave_c * same_s + turned_c * cross_s
+        result = jnp.concatenate(
+            [result_c.reshape(SPAN, TILE), result_s.reshape(SPAN, TILE)], axis=1
+        )
+        result_ref[tile] = stacked_halves(result)
+
+    def back_down(tile):
+        column, line = divmod(tile, SIDE)
+        high, low = split(against_halves(back_down_ref[...], result_ref.at[tile]))
+        rows_ref[column, line * TILE:(line + 1) * TILE, :pair] = high
+        rows_ref[column, line * TILE:(line + 1) * TILE, pair:] = low
+
+    def back_across(column):
         matched = jnp.dot(rows_ref[column], backward, preferred_element_type=f32)
         matched = matched[:, :TILE] + matched[:, TILE:]
         weight = weight_ref[:, column * TILE:(column + 1) * TILE]
@@ -279,25 +307,42 @@
         weighted = weighted.reshape(SIDE, CHIPS, PIECE, TILE)
         for line in range(SIDE):
             item = line * SIDE + column
-            out_ref[:, item] = weighted[line]
-            sends.append(
-                pltpu.make_async_copy(out_ref.at[:, item], out_hbm.at[:, item], out_sems.at[item])
-            )
-            sends[-1].start()
+            for piece in range(CHIPS):
+                out_ref[spots[piece], item] = weighted[line, piece]
+
+    halve()
+    transform_across(0)
+    prepare()
+    for step in range(TILES_BLK + 5):
+        if step % SIDE == 0 and step // SIDE + 1 < SIDE:
+            transform_across(step // SIDE + 1)
+        for delay, stage in enumerate((stack, transform_down, multiply, back_down)):
+            if 0 <= step - delay < TILES_BLK:
+                stage(step - delay)
+        column, rest = divmod(step - 4, SIDE)
+        if rest == SIDE - 1 and 0 <= column < SIDE:
+            back_across(column)
+    sends = [
+        pltpu.make_async_copy(out_ref.at[way * 4:way * 4 + 4], out_hbm, out_sems.at[way])
+        for way, out_hbm in enumerate((out_0, out_1, out_2, out_3))
+    ]
+    for way in (3, 1, 2, 0):
+        sends[way].start()
     for send in sends:
         send.wait()
 
 
-def match_block(block, exposures, variance, bits, table, index, owner, slot):
+def match_block(block, place, exposures, variance, bits, table, index, owner, slot):
     blocks = exposures.shape[1]
     items = blocks * TILES_BLK
     groups = TILES_BLK + (1 if block == 0 else 0)
     matrices = transforms()
-    pieces = pl.pallas_call(
+    return pl.pallas_call(
         functools.partial(match_kernel, block=block),
-        out_shape=jax.ShapeDtypeStruct((CHIPS, groups, PIECE, TILE), f32),
-        in_specs=[pl.BlockSpec(memory_space=pltpu.HBM)] * (7 + len(matrices)),
-        out_specs=pl.BlockSpec(memory_space=pltpu.HBM),
+        out_shape=[jax.ShapeDtypeStruct((4, groups, PIECE, TILE), f32)] * 4,
+        in_specs=[pl.BlockSpec(memory_space=pltpu.SMEM)]
+        + [pl.BlockSpec(memory_space=pltpu.HBM)] * (7 + len(matrices)),
+        out_specs=[pl.BlockSpec(memory_space=pltpu.HBM)] * 4,
         scratch_shapes=[
             pltpu.SMEM((1, blocks), jnp.int32),
             pltpu.SMEM(table.shape, f32),
@@ -308,33 +353,48 @@
             pltpu.VMEM((1, items), jnp.int32),
             *[pltpu.VMEM(matrix.shape, matrix.dtype) for matrix in matrices],
             pltpu.SemaphoreType.DMA((7 + len(matrices),)),
-            pltpu.SemaphoreType.DMA((TILES_BLK + 1,)),
+            pltpu.SemaphoreType.DMA((4,)),
             pltpu.VMEM((TALL, TILE), f32),
             pltpu.VMEM((TALL, WIDE), bf16),
             pltpu.VMEM((TALL, WIDE), bf16),
-            pltpu.VMEM((TALL, 2 * BLOCK), f32),
-            pltpu.VMEM((SIDE, 512, 2 * BLOCK), bf16),
-            pltpu.VMEM((SIDE, SPAN + 8, 2 * BLOCK), f32),
-            pltpu.VMEM((SIDE, 512, 2 * BLOCK), bf16),
+            pltpu.VMEM((SIDE, TALL, 2 * TILE), f32),
+            pltpu.VMEM((TILES_BLK, 2 * SPAN, 2 * TILE), bf16),
+            pltpu.VMEM((TILES_BLK, SPAN + 8, 2 * TILE), f32),
+            pltpu.VMEM((TILES_BLK, 2 * SPAN, 2 * TILE), bf16),
             pltpu.VMEM((SIDE, BLOCK, 4 * TILE), bf16),
             pltpu.VMEM((2, SPAN // 8, 8, 2 * TILE), f32),
             pltpu.VMEM((CELLS, BLOCK), f32),
             pltpu.VMEM((CHIPS, groups, PIECE, TILE), f32),
         ],
-        compiler_params=pltpu.CompilerParams(vmem_limit_bytes=60 << 20),
+        compiler_params=pltpu.CompilerParams(vmem_limit_bytes=59 << 20),
         cost_estimate=pl.CostEstimate(
-            flops=2 * 256 * 256 * 20000, bytes_accessed=3 << 20, transcendentals=0
+            flops=2 * 256 * 256 * 40000, bytes_accessed=3 << 20, transcendentals=0
         ),
         name="match_block",
-    )(index, table, exposures, variance, bits, owner, slot, *matrices)
-    return pieces.reshape(CHIPS, groups * PIECE, TILE)
-
-
-def partial_kernel(place_ref, first_ref, second_ref, mine_ref, other_ref):
+    )(place, index, table, exposures, variance, bits, owner, slot, *matrices)
+
+
+WAYS = (0, 3, 1, 2)
+
+
+def keep_kernel(part_hbm, out_ref, sem):
+    copy = pltpu.make_async_copy(part_hbm, out_ref, sem)
+    copy.start()
+    copy.wait()
+
+
+def turn_kernel(*refs):
+    for first, part_ref in zip(WAYS, refs[:4]):
+        for second, out_ref in enumerate(refs[4:]):
+            out_ref[first] = part_ref[second]
+
+
+def partial_kernel(place_ref, *refs):
+    first_refs, second_refs, (mine_ref, other_ref) = refs[:4], refs[4:8], refs[8:]
     core = place_ref[0] % 2
     per_group = TILE // TILES_BLK
     lane = lax.broadcasted_iota(jnp.int32, (INFO, TILE), 1)
-    info = [first_ref[source, TILES_BLK * PIECE:, :] for source in range(CHIPS)]
+    info = [first_refs[source // 4][source % 4, TILES_BLK * PIECE:] for source in range(CHIPS)]
     tables = []
     for block in range(2):
         rows = []
@@ -377,8 +437,11 @@
     other_ref[owned * PIECE:, :] = sums[owned:]
     for line in range(PIECE):
         total = None
-        for route, part_ref in zip(routes, (first_ref, second_ref)):
-            part = part_ref[:, pl.ds(line, TILES_BLK, PIECE), :].reshape(items, TILE)
+        rows = pl.ds(line, TILES_BLK, PIECE)
+        for route, part_refs in zip(routes, (first_refs, second_refs)):
+            part = jnp.concatenate(
+                [part_ref[:, rows, :].reshape(items // 4, TILE) for part_ref in part_refs], axis=0
+            )
             high, low = split(part)
             term = jnp.dot(
                 route, jnp.concatenate([high, low], axis=1), preferred_element_type=f32
@@ -427,25 +490,48 @@
     smem = pl.BlockSpec(memory_space=pltpu.SMEM)
     vmem = pl.BlockSpec(memory_space=pltpu.VMEM)
     params = pltpu.CompilerParams(vmem_limit_bytes=32 << 20)
-    same_core = [list(range(core, VISITS, 2)) for core in range(2)]
     owned = VISITS * OWN_DEV // 2
 
-    def exchange(pieces):
-        return lax.all_to_all(pieces, "visit", 0, 0, axis_index_groups=same_core, tiled=True)
+    def exchange(parts):
+        for phase in range(2):
+            parts = [
+                lax.ppermute(parts[way], "visit", phase_partners(phase, way)) if way else parts[0]
+                for way in WAYS
+            ]
+            if phase == 0:
+                parts = pl.pallas_call(
+                    turn_kernel,
+                    out_shape=[jax.ShapeDtypeStruct(parts[0].shape, f32)] * 4,
+                    in_specs=[vmem] * 4,
+                    out_specs=[vmem] * 4,
+                    compiler_params=params,
+                    name="turn",
+                )(*parts)
+        return parts
 
     table = kernel_table.T
     owner = tile_owner.reshape(tile_slot.shape)
     parts = []
     for block in range(exposures.shape[1]):
         pieces = match_block(
-            block, exposures, variance, mask_planes, table, kernel_index, owner, tile_slot
-        )
-        parts.append(exchange(pieces))
+            block, place, exposures, variance, mask_planes, table, kernel_index, owner, tile_slot
+        )
+        own = pl.pallas_call(
+            keep_kernel,
+            out_shape=jax.ShapeDtypeStruct(pieces[0].shape, f32),
+            in_specs=[pl.BlockSpec(memory_space=pltpu.HBM)],
+            out_specs=vmem,
+            scratch_shapes=[pltpu.SemaphoreType.DMA],
+            compiler_params=params,
+            name="keep",
+        )(pieces[0])
+        parts.extend(exchange([own, *pieces[1:]]))
+    parts = [part.reshape(4, -1, TILE) for part in parts]
 
     mine, other = pl.pallas_call(
         partial_kernel,
         out_shape=[jax.ShapeDtypeStruct((owned * (PIECE + 1), TILE), f32)] * 2,
-        in_specs=[smem, vmem, vmem],
+        in_specs=[smem] + [vmem] * 8,
         out_specs=[vmem, vmem],
         compiler_params=params,
         name="partial_sums",
@@ -459,7 +545,14 @@
         compiler_params=params,
         name="merge_cores",
     )(place, mine, other)
-    pieces = exchange(pieces.reshape(CHIPS, OWN_DEV * PIECE, TILE))
+    pieces = lax.all_to_all(
+        pieces.reshape(CHIPS, OWN_DEV * PIECE, TILE),
+        "visit",
+        0,
+        0,
+        axis_index_groups=[list(range(core, VISITS, 2)) for core in range(2)],
+        tiled=True,
+    )
     image, chi = pl.pallas_call(
         owner_kernel,
         out_shape=[jax.ShapeDtypeStruct((OWN_DEV, TILE, TILE), f32)] * 2,

time: 93.1 us -> 90.1 us (0.968)
  waiting for transfers between devices: 40.8 us -> 22.9 us
  starting transfers between devices: 18 us -> 30.6 us
  blocking collectives: 14.7 us -> 16.7 us
  local copies, waits for them, and re-layouts: 0.03 us -> 0.99 us
    all_to_all x2 -> x0, waiting for transfers between devices: 27.1 us -> none  [exchange(): lax.all_to_all(pieces, 'visit', 0, 0, axis_index_groups=same_core, tiled=...]
    ppermute x0 -> x12, starting transfers between devices: none -> 23.4 us  [exchange(): lax.ppermute(parts[way], 'visit', phase_partners(phase, way))]
    all_to_all x2 -> x0, starting transfers between devices: 10.8 us -> none  [exchange(): lax.all_to_all(pieces, 'visit', 0, 0, axis_index_groups=same_core, tiled=...]
    ppermute x0 -> x12, waiting for transfers between devices: none -> 9.16 us  [exchange(): lax.ppermute(parts[way], 'visit', phase_partners(phase, way))]
    all_to_all x1, blocking collectives: 14.7 us -> 16.7 us  [local(): lax.all_to_all(pieces.reshape(CHIPS, OWN_DEV * PIECE, TILE), 'visit', 0,...]
    unnamed x0 -> x4, local copies, waits for them, and re-layouts: none -> 0.96 us
    pallas_call x2 -> x6, Pallas kernels: 15.1 us -> 14.6 us  [the longest x2 14.4 us: match_block(): pl.pallas_call(functools.partial(match_kernel, block=block), out_shape=[j...]
  transfers between devices with their start and end apart: 7 -> 17, of which waited for: 7 -> 8; matrix products, arithmetic and copies ran while one was open for 0% -> 0% of each run, Pallas kernels for 8% -> 8%
where the time goes in v4:
time: 90.1 us; the launch traced here: 89.8 us
  starting transfers between devices  30.6 us (34%)
  waiting for transfers between devices  22.9 us (25%)
  Pallas kernels  16.9 us (19%)
  blocking collectives  16.7 us (19%)
  local copies, waits for them, and re-layouts  0.99 us (1%)
  other arithmetic  0.95 us (1%)
    ppermute x12, starting transfers between devices, exchange(): lax.ppermute(parts[way], 'visit', phase_partners(phase, way))  23.4 us
    all_to_all x1, blocking collectives, local(): lax.all_to_all(pieces.reshape(CHIPS, OWN_DEV * PIECE, TILE), 'visit', 0,...  16.7 us
    pallas_call x2, Pallas kernels, match_block(): pl.pallas_call(functools.partial(match_kernel, block=block), out_shape=[j...  14.4 us
    ppermute x4, waiting for transfers between devices, local(): lax.ppermute(half, 'band', pairings[(turn + number) % 2])  11.7 us
    ppermute x12, waiting for transfers between devices, exchange(): lax.ppermute(parts[way], 'visit', phase_partners(phase, way))  9.16 us
    ppermute x4, starting transfers between devices, local(): lax.ppermute(half, 'band', pairings[(turn + number) % 2])  7.14 us
    ppermute x1, waiting for transfers between devices, local(): lax.ppermute(other, 'visit', [(device, device ^ 1) for device in range(VI...  1.99 us
  transfers between devices with their start and end apart: 17, of which 8 were waited for; matrix products, arithmetic and copies ran while one was open for 0% of the time, Pallas kernels for 8%

profile of v4, /device:TPU:0, one launch (start us, length us, event | category | flops | bytes accessed | tf_op | source)
XLA Modules:
  0.0 89.8 jit_solution(14104653706272556909)
XLA Ops:
  0.6 7.0 %match_block.3 = (f32[4,16,8,128]{3,2,1,0:T(8,128)}, f32[4,16,8,128]{3,2,1,0:T(8,128)}, f32[4,16,8,128]{3,2,1,0:T(8,128)}, f32[4,16,8,128]{3,2,1,0:T(8,128)}) custom-call(s32[1]{0:T(128)} %bitcast.place_ref, s32[1,2]{1,0:T(1,128)} %index_hbm.3, f32[27,64]{1,0:T(8,128)} %bitcast.23, f32[1,2,552,552]{3,2,1,0:T(8,128)} %image_hbm.3, f32[1,2,16,16]{3,2,1,0:T(8,128)} %var_hbm.3, ...), custom_call_target="tpu_custom_call" | custom-call | flops 5242880000 | bytes 3145728 | tf_op jit(solution)/shard_map/match_block/pallas_call | solution.py:340
  7.7 2.7 %collective-permute-start.6 = (f32[4,16,8,128]{3,2,1,0:T(8,128)}, f32[4,16,8,128]{3,2,1,0:T(8,128)S(1)}, u32[]{:S(2)}, u32[]{:S(2)}) collective-permute-start(f32[4,16,8,128]{3,2,1,0:T(8,128)} %get-tuple-element.31), channel_id=1, source_target_pairs={{0,40},{4,124},{8,32},{12,116},{16,56},{20,108},{24,48},{28,100},{... | collective-permute-start | bytes 786440 | tf_op jit(solution)/shard_map/ppermute | solution.py:498
  10.3 0.5 collective-permute-start.7
  10.9 0.4 collective-permute-start.8
  11.2 7.4 %match_block.2 = (f32[4,17,8,128]{3,2,1,0:T(8,128)}, f32[4,17,8,128]{3,2,1,0:T(8,128)}, f32[4,17,8,128]{3,2,1,0:T(8,128)}, f32[4,17,8,128]{3,2,1,0:T(8,128)}) custom-call(s32[1]{0:T(128)} %bitcast.place_ref, s32[1,2]{1,0:T(1,128)} %index_hbm.3, f32[27,64]{1,0:T(8,128)} %bitcast.24, f32[1,2,552,552]{3,2,1,0:T(8,128)} %image_hbm.3, f32[1,2,16,16]{3,2,1,0:T(8,128)} %var_hbm.3, ...), custom_call_target="tpu_custom_call" | custom-call | flops 5242880000 | bytes 3145728 | tf_op jit(solution)/shard_map/match_block/pallas_call | solution.py:340
  18.6 2.7 %collective-permute-start = (f32[4,17,8,128]{3,2,1,0:T(8,128)}, f32[4,17,8,128]{3,2,1,0:T(8,128)S(1)}, u32[]{:S(2)}, u32[]{:S(2)}) collective-permute-start(f32[4,17,8,128]{3,2,1,0:T(8,128)} %get-tuple-element.23), channel_id=1, source_target_pairs={{0,40},{4,124},{8,32},{12,116},{16,56},{20,108},{24,48},{28,100},{... | collective-permute-start | bytes 835592 | tf_op jit(solution)/shard_map/ppermute | solution.py:498
  21.2 0.5 collective-permute-start.1
  21.8 0.4 collective-permute-start.2
  22.3 5.4 %collective-permute-start.9 = (f32[4,16,8,128]{3,2,1,0:T(8,128)S(1)}, f32[4,16,8,128]{3,2,1,0:T(8,128)S(1)}, u32[]{:S(2)}, u32[]{:S(2)}) collective-permute-start(f32[4,16,8,128]{3,2,1,0:T(8,128)S(1)} %get-tuple-element.35), channel_id=1, source_target_pairs={{0,120},{4,44},{8,112},{12,36},{16,104},{20,60},{24,96},{28,52},{3... | collective-permute-start | bytes 786440 | tf_op jit(solution)/shard_map/ppermute | solution.py:498
  27.7 1.0 %copy-done = f32[4,17,8,128]{3,2,1,0:T(8,128)S(1)} copy-done((f32[4,17,8,128]{3,2,1,0:T(8,128)S(1)}, f32[4,17,8,128]{3,2,1,0:T(8,128)}, u32[]{:S(2)}) %copy-start) | copy-done | bytes 278552
  28.7 3.7 %collective-permute-done.1.refs_2_ = f32[4,17,8,128]{3,2,1,0:T(8,128)S(1)} collective-permute-done((f32[4,17,8,128]{3,2,1,0:T(8,128)}, f32[4,17,8,128]{3,2,1,0:T(8,128)S(1)}, u32[]{:S(2)}, u32[]{:S(2)}) %collective-permute-start.1) | collective-permute-done | bytes 278560 | tf_op jit(solution)/shard_map/ppermute | solution.py:498
  32.4 4.4 %collective-permute-start.3 = (f32[4,17,8,128]{3,2,1,0:T(8,128)S(1)}, f32[4,17,8,128]{3,2,1,0:T(8,128)S(1)}, u32[]{:S(2)}, u32[]{:S(2)}) collective-permute-start(f32[4,17,8,128]{3,2,1,0:T(8,128)S(1)} %get-tuple-element.27), channel_id=1, source_target_pairs={{0,120},{4,44},{8,112},{12,36},{16,104},{20,60},{24,96},{28,52},{3... | collective-permute-start | bytes 835592 | tf_op jit(solution)/shard_map/ppermute | solution.py:498
  36.8 0.5 collective-permute-start.4
  37.3 1.1 %collective-permute-start.5 = (f32[4,17,8,128]{3,2,1,0:T(8,128)S(1)}, f32[4,17,8,128]{3,2,1,0:T(8,128)S(1)}, u32[]{:S(2)}, u32[]{:S(2)}) collective-permute-start(f32[4,17,8,128]{3,2,1,0:T(8,128)S(1)} %get-tuple-element.29), channel_id=1, source_target_pairs={{0,96},{4,36},{8,104},{12,44},{16,112},{20,52},{24,120},{28,60},{3... | collective-permute-start | bytes 835592 | tf_op jit(solution)/shard_map/ppermute | solution.py:498
  38.4 2.8 %collective-permute-start.10 = (f32[4,16,8,128]{3,2,1,0:T(8,128)S(1)}, f32[4,16,8,128]{3,2,1,0:T(8,128)S(1)}, u32[]{:S(2)}, u32[]{:S(2)}) collective-permute-start(f32[4,16,8,128]{3,2,1,0:T(8,128)S(1)} %get-tuple-element.36), channel_id=1, source_target_pairs={{0,24},{4,12},{8,16},{12,4},{16,8},{20,28},{24,0},{28,20},{32,56},... | collective-permute-start | bytes 786440 | tf_op jit(solution)/shard_map/ppermute | solution.py:498
  41.2 2.1 %collective-permute-start.11 = (f32[4,16,8,128]{3,2,1,0:T(8,128)S(1)}, f32[4,16,8,128]{3,2,1,0:T(8,128)S(1)}, u32[]{:S(2)}, u32[]{:S(2)}) collective-permute-start(f32[4,16,8,128]{3,2,1,0:T(8,128)S(1)} %get-tuple-element.37), channel_id=1, source_target_pairs={{0,96},{4,36},{8,104},{12,44},{16,112},{20,52},{24,120},{28,60},{3... | collective-permute-start | bytes 786440 | tf_op jit(solution)/shard_map/ppermute | solution.py:498
  43.3 4.3 %collective-permute-done.10 = f32[4,16,8,128]{3,2,1,0:T(8,128)S(1)} collective-permute-done((f32[4,16,8,128]{3,2,1,0:T(8,128)S(1)}, f32[4,16,8,128]{3,2,1,0:T(8,128)S(1)}, u32[]{:S(2)}, u32[]{:S(2)}) %collective-permute-start.10) | collective-permute-done | bytes 262176 | tf_op jit(solution)/shard_map/ppermute | solution.py:498
  47.6 1.1 %collective-permute-done.11 = f32[4,16,8,128]{3,2,1,0:T(8,128)S(1)} collective-permute-done((f32[4,16,8,128]{3,2,1,0:T(8,128)S(1)}, f32[4,16,8,128]{3,2,1,0:T(8,128)S(1)}, u32[]{:S(2)}, u32[]{:S(2)}) %collective-permute-start.11) | collective-permute-done | bytes 262176 | tf_op jit(solution)/shard_map/ppermute | solution.py:498
  48.8 1.0 %partial_sums.1 = (f32[1152,128]{1,0:T(8,128)S(1)}, f32[1152,128]{1,0:T(8,128)S(1)}) custom-call(s32[1]{0:T(128)} %bitcast.place_ref, f32[4,136,128]{2,1,0:T(8,128)S(1)} %bitcast.14, f32[4,136,128]{2,1,0:T(8,128)S(1)} %bitcast.15, f32[4,136,128]{2,1,0:T(8,128)S(1)} %bitcast.16, f32[4,136,128]{2,1,0:T(8,128)S(1)} %bitcast.17, f32[4,128,128]{2,1,0:T(8,128)S(1)} %bitcast.18, ...), custom_call_target="tpu_custom_call" | custom-call | tf_op jit(solution)/shard_map/partial_sums/pallas_call | solution.py:531
  49.8 0.1 collective-permute-start.12
  49.9 2.0 %collective-permute-done.12.other_ref = f32[1152,128]{1,0:T(8,128)S(1)} collective-permute-done((f32[1152,128]{1,0:T(8,128)S(1)}, f32[1152,128]{1,0:T(8,128)S(1)}, u32[]{:S(2)}, u32[]{:S(2)}) %collective-permute-start.12) | collective-permute-done | bytes 589856 | tf_op jit(solution)/shard_map/ppermute | solution.py:539
  51.9 0.3 merge_cores.1
  52.2 16.7 %all_to_all.5.part_ref = f32[16,64,128]{2,1,0:T(8,128)S(1)} all-to-all(f32[16,64,128]{2,1,0:T(8,128)S(1)} %bitcast.13), channel_id=1, replica_groups={{0,8,16,24,32,40,48,56,64,72,80,88,96,104,112,120},{4,12,20,28,36,44,52..., dimensions={0} | all-to-all | bytes 1048576 | tf_op jit(solution)/shard_map/all_to_all | solution.py:548
  68.9 1.1 %own.1 = (f32[8,128,128]{2,1,0:T(8,128)}, f32[8,128,128]{2,1,0:T(8,128)S(1)}) custom-call(s32[1]{0:T(128)} %bitcast.place_ref, f32[1152,128]{1,0:T(8,128)S(1)} %get-tuple-element.38.mine_ref, f32[1152,128]{1,0:T(8,128)S(1)} %collective-permute-done.12.other_ref, f32[16,64,128]{2,1,0:T(8,128)S(1)} %all_to_all.5.part_ref), custom_call_target="tpu_custom_call" | custom-call | tf_op jit(solution)/shard_map/own/pallas_call | solution.py:556
  70.0 2.0 %collective-permute-start.13 = (f32[4,128,128]{2,1,0:T(8,128)S(1)}, f32[4,128,128]{2,1,0:T(8,128)S(1)}, u32[]{:S(2)}, u32[]{:S(2)}) collective-permute-start(f32[4,128,128]{2,1,0:T(8,128)S(1)} %get-tuple-element.44), channel_id=1, source_target_pairs={{0,1},{1,0},{2,3},{3,2},{4,5},{5,4},{6,7},{7,6},{8,9},{9,8},{10,11... | collective-permute-start | bytes 786440 | tf_op jit(solution)/shard_map/ppermute | solution.py:569
  72.0 2.5 %collective-permute-start.15 = (f32[4,128,128]{2,1,0:T(8,128)S(1)}, f32[4,128,128]{2,1,0:T(8,128)S(1)}, u32[]{:S(2)}, u32[]{:S(2)}) collective-permute-start(f32[4,128,128]{2,1,0:T(8,128)S(1)} %get-tuple-element.45), channel_id=1, source_target_pairs={{0,3},{3,0},{1,2},{2,1},{4,7},{7,4},{5,6},{6,5},{8,11},{11,8},{9,1... | collective-permute-start | bytes 786440 | tf_op jit(solution)/shard_map/ppermute | solution.py:569
  74.5 2.7 %collective-permute-done.13 = f32[4,128,128]{2,1,0:T(8,128)S(1)} collective-permute-done((f32[4,128,128]{2,1,0:T(8,128)S(1)}, f32[4,128,128]{2,1,0:T(8,128)S(1)}, u32[]{:S(2)}, u32[]{:S(2)}) %collective-permute-start.13) | collective-permute-done | bytes 262176 | tf_op jit(solution)/shard_map/ppermute | solution.py:569
  77.2 2.7 %collective-permute-done.15 = f32[4,128,128]{2,1,0:T(8,128)S(1)} collective-permute-done((f32[4,128,128]{2,1,0:T(8,128)S(1)}, f32[4,128,128]{2,1,0:T(8,128)S(1)}, u32[]{:S(2)}, u32[]{:S(2)}) %collective-permute-start.15) | collective-permute-done | bytes 262176 | tf_op jit(solution)/shard_map/ppermute | solution.py:569
  80.0 2.6 %collective-permute-start.14 = (f32[4,128,128]{2,1,0:T(8,128)S(1)}, f32[4,128,128]{2,1,0:T(8,128)S(1)}, u32[]{:S(2)}, u32[]{:S(2)}) collective-permute-start(f32[4,128,128]{2,1,0:T(8,128)S(1)} %get-tuple-element.42), channel_id=1, source_target_pairs={{0,3},{3,0},{1,2},{2,1},{4,7},{7,4},{5,6},{6,5},{8,11},{11,8},{9,1... | collective-permute-start | bytes 786440 | tf_op jit(solution)/shard_map/ppermute | solution.py:569
  82.6 5.0 %collective-permute-done.14 = f32[4,128,128]{2,1,0:T(8,128)S(1)} collective-permute-done((f32[4,128,128]{2,1,0:T(8,128)S(1)}, f32[4,128,128]{2,1,0:T(8,128)S(1)}, u32[]{:S(2)}, u32[]{:S(2)}) %collective-permute-start.14) | collective-permute-done | bytes 262176 | tf_op jit(solution)/shard_map/ppermute | solution.py:569
  87.7 1.3 %collective-permute-done.16 = f32[4,128,128]{2,1,0:T(8,128)S(1)} collective-permute-done((f32[4,128,128]{2,1,0:T(8,128)S(1)}, f32[4,128,128]{2,1,0:T(8,128)S(1)}, u32[]{:S(2)}, u32[]{:S(2)}) %collective-permute-start.16) | collective-permute-done | bytes 262176 | tf_op jit(solution)/shard_map/ppermute | solution.py:569
  89.0 0.8 pad_maximum_fusion
  (21 shorter events, 0.4 us)
Async XLA Ops:
  7.7 14.1 %collective-permute-start.6 = (f32[4,16,8,128]{3,2,1,0:T(8,128)}, f32[4,16,8,128]{3,2,1,0:T(8,128)S(1)}, u32[]{:S(2)}, u32[]{:S(2)}) collective-permute-start(f32[4,16,8,128]{3,2,1,0:T(8,128)} %get-tuple-element.31), channel_id=1, source_target_pairs={{0,40},{4,124},{8,32},{12,116},{16,56},{20,108},{24,48},{28,100},{... | collective-permute-start | bytes 786440 | tf_op jit(solution)/shard_map/ppermute | solution.py:498
  10.3 11.9 %collective-permute-start.7 = (f32[4,16,8,128]{3,2,1,0:T(8,128)}, f32[4,16,8,128]{3,2,1,0:T(8,128)S(1)}, u32[]{:S(2)}, u32[]{:S(2)}) collective-permute-start(f32[4,16,8,128]{3,2,1,0:T(8,128)} %get-tuple-element.32), channel_id=1, source_target_pairs={{0,8},{4,28},{8,0},{12,20},{16,24},{20,12},{24,16},{28,4},{32,40},... | collective-permute-start | bytes 786440 | tf_op jit(solution)/shard_map/ppermute | solution.py:498
  10.9 11.3 %copy-start.1 = (f32[4,16,8,128]{3,2,1,0:T(8,128)S(1)}, f32[4,16,8,128]{3,2,1,0:T(8,128)}, u32[]{:S(2)}) copy-start(f32[4,16,8,128]{3,2,1,0:T(8,128)} %get-tuple-element.30.part_hbm) | copy-start | bytes 786436
  10.9 11.4 %collective-permute-start.8 = (f32[4,16,8,128]{3,2,1,0:T(8,128)}, f32[4,16,8,128]{3,2,1,0:T(8,128)S(1)}, u32[]{:S(2)}, u32[]{:S(2)}) collective-permute-start(f32[4,16,8,128]{3,2,1,0:T(8,128)} %get-tuple-element.33), channel_id=1, source_target_pairs={{0,32},{4,100},{8,40},{12,108},{16,48},{20,116},{24,56},{28,124},{... | collective-permute-start | bytes 786440 | tf_op jit(solution)/shard_map/ppermute | solution.py:498
  18.6 10.1 %collective-permute-start = (f32[4,17,8,128]{3,2,1,0:T(8,128)}, f32[4,17,8,128]{3,2,1,0:T(8,128)S(1)}, u32[]{:S(2)}, u32[]{:S(2)}) collective-permute-start(f32[4,17,8,128]{3,2,1,0:T(8,128)} %get-tuple-element.23), channel_id=1, source_target_pairs={{0,40},{4,124},{8,32},{12,116},{16,56},{20,108},{24,48},{28,100},{... | collective-permute-start | bytes 835592 | tf_op jit(solution)/shard_map/ppermute | solution.py:498
  21.2 11.1 %collective-permute-start.1 = (f32[4,17,8,128]{3,2,1,0:T(8,128)}, f32[4,17,8,128]{3,2,1,0:T(8,128)S(1)}, u32[]{:S(2)}, u32[]{:S(2)}) collective-permute-start(f32[4,17,8,128]{3,2,1,0:T(8,128)} %get-tuple-element.24), channel_id=1, source_target_pairs={{0,8},{4,28},{8,0},{12,20},{16,24},{20,12},{24,16},{28,4},{32,40},... | collective-permute-start | bytes 835592 | tf_op jit(solution)/shard_map/ppermute | solution.py:498
  21.8 10.6 %collective-permute-start.2 = (f32[4,17,8,128]{3,2,1,0:T(8,128)}, f32[4,17,8,128]{3,2,1,0:T(8,128)S(1)}, u32[]{:S(2)}, u32[]{:S(2)}) collective-permute-start(f32[4,17,8,128]{3,2,1,0:T(8,128)} %get-tuple-element.25), channel_id=1, source_target_pairs={{0,32},{4,100},{8,40},{12,108},{16,48},{20,116},{24,56},{28,124},{... | collective-permute-start | bytes 835592 | tf_op jit(solution)/shard_map/ppermute | solution.py:498
  22.3 18.9 %collective-permute-start.9 = (f32[4,16,8,128]{3,2,1,0:T(8,128)S(1)}, f32[4,16,8,128]{3,2,1,0:T(8,128)S(1)}, u32[]{:S(2)}, u32[]{:S(2)}) collective-permute-start(f32[4,16,8,128]{3,2,1,0:T(8,128)S(1)} %get-tuple-element.35), channel_id=1, source_target_pairs={{0,120},{4,44},{8,112},{12,36},{16,104},{20,60},{24,96},{28,52},{3... | collective-permute-start | bytes 786440 | tf_op jit(solution)/shard_map/ppermute | solution.py:498
  27.7 1.0 %copy-start = (f32[4,17,8,128]{3,2,1,0:T(8,128)S(1)}, f32[4,17,8,128]{3,2,1,0:T(8,128)}, u32[]{:S(2)}) copy-start(f32[4,17,8,128]{3,2,1,0:T(8,128)} %get-tuple-element.22.part_hbm) | copy-start | bytes 835588
  32.4 16.3 %collective-permute-start.3 = (f32[4,17,8,128]{3,2,1,0:T(8,128)S(1)}, f32[4,17,8,128]{3,2,1,0:T(8,128)S(1)}, u32[]{:S(2)}, u32[]{:S(2)}) collective-permute-start(f32[4,17,8,128]{3,2,1,0:T(8,128)S(1)} %get-tuple-element.27), channel_id=1, source_target_pairs={{0,120},{4,44},{8,112},{12,36},{16,104},{20,60},{24,96},{28,52},{3... | collective-permute-start | bytes 835592 | tf_op jit(solution)/shard_map/ppermute | solution.py:498
  36.8 11.9 %collective-permute-start.4 = (f32[4,17,8,128]{3,2,1,0:T(8,128)S(1)}, f32[4,17,8,128]{3,2,1,0:T(8,128)S(1)}, u32[]{:S(2)}, u32[]{:S(2)}) collective-permute-start(f32[4,17,8,128]{3,2,1,0:T(8,128)S(1)} %get-tuple-element.28), channel_id=1, source_target_pairs={{0,24},{4,12},{8,16},{12,4},{16,8},{20,28},{24,0},{28,20},{32,56},... | collective-permute-start | bytes 835592 | tf_op jit(solution)/shard_map/ppermute | solution.py:498
  37.3 11.5 %collective-permute-start.5 = (f32[4,17,8,128]{3,2,1,0:T(8,128)S(1)}, f32[4,17,8,128]{3,2,1,0:T(8,128)S(1)}, u32[]{:S(2)}, u32[]{:S(2)}) collective-permute-start(f32[4,17,8,128]{3,2,1,0:T(8,128)S(1)} %get-tuple-element.29), channel_id=1, source_target_pairs={{0,96},{4,36},{8,104},{12,44},{16,112},{20,52},{24,120},{28,60},{3... | collective-permute-start | bytes 835592 | tf_op jit(solution)/shard_map/ppermute | solution.py:498
  38.4 9.2 %collective-permute-start.10 = (f32[4,16,8,128]{3,2,1,0:T(8,128)S(1)}, f32[4,16,8,128]{3,2,1,0:T(8,128)S(1)}, u32[]{:S(2)}, u32[]{:S(2)}) collective-permute-start(f32[4,16,8,128]{3,2,1,0:T(8,128)S(1)} %get-tuple-element.36), channel_id=1, source_target_pairs={{0,24},{4,12},{8,16},{12,4},{16,8},{20,28},{24,0},{28,20},{32,56},... | collective-permute-start | bytes 786440 | tf_op jit(solution)/shard_map/ppermute | solution.py:498
  41.2 7.6 %collective-permute-start.11 = (f32[4,16,8,128]{3,2,1,0:T(8,128)S(1)}, f32[4,16,8,128]{3,2,1,0:T(8,128)S(1)}, u32[]{:S(2)}, u32[]{:S(2)}) collective-permute-start(f32[4,16,8,128]{3,2,1,0:T(8,128)S(1)} %get-tuple-element.37), channel_id=1, source_target_pairs={{0,96},{4,36},{8,104},{12,44},{16,112},{20,52},{24,120},{28,60},{3... | collective-permute-start | bytes 786440 | tf_op jit(solution)/shard_map/ppermute | solution.py:498
  49.8 2.1 %collective-permute-start.12 = (f32[1152,128]{1,0:T(8,128)S(1)}, f32[1152,128]{1,0:T(8,128)S(1)}, u32[]{:S(2)}, u32[]{:S(2)}) collective-permute-start(f32[1152,128]{1,0:T(8,128)S(1)} %get-tuple-element.39), channel_id=1, source_target_pairs={{0,4},{4,0},{8,12},{12,8},{16,20},{20,16},{24,28},{28,24},{32,36},... | collective-permute-start | bytes 1769480 | tf_op jit(solution)/shard_map/ppermute | solution.py:539
  70.0 7.2 %collective-permute-start.13 = (f32[4,128,128]{2,1,0:T(8,128)S(1)}, f32[4,128,128]{2,1,0:T(8,128)S(1)}, u32[]{:S(2)}, u32[]{:S(2)}) collective-permute-start(f32[4,128,128]{2,1,0:T(8,128)S(1)} %get-tuple-element.44), channel_id=1, source_target_pairs={{0,1},{1,0},{2,3},{3,2},{4,5},{5,4},{6,7},{7,6},{8,9},{9,8},{10,11... | collective-permute-start | bytes 786440 | tf_op jit(solution)/shard_map/ppermute | solution.py:569
  72.0 7.9 %collective-permute-start.15 = (f32[4,128,128]{2,1,0:T(8,128)S(1)}, f32[4,128,128]{2,1,0:T(8,128)S(1)}, u32[]{:S(2)}, u32[]{:S(2)}) collective-permute-start(f32[4,128,128]{2,1,0:T(8,128)S(1)} %get-tuple-element.45), channel_id=1, source_target_pairs={{0,3},{3,0},{1,2},{2,1},{4,7},{7,4},{5,6},{6,5},{8,11},{11,8},{9,1... | collective-permute-start | bytes 786440 | tf_op jit(solution)/shard_map/ppermute | solution.py:569
  80.0 7.7 %collective-permute-start.14 = (f32[4,128,128]{2,1,0:T(8,128)S(1)}, f32[4,128,128]{2,1,0:T(8,128)S(1)}, u32[]{:S(2)}, u32[]{:S(2)}) collective-permute-start(f32[4,128,128]{2,1,0:T(8,128)S(1)} %get-tuple-element.42), channel_id=1, source_target_pairs={{0,3},{3,0},{1,2},{2,1},{4,7},{7,4},{5,6},{6,5},{8,11},{11,8},{9,1... | collective-permute-start | bytes 786440 | tf_op jit(solution)/shard_map/ppermute | solution.py:569
  82.6 6.4 %collective-permute-start.16 = (f32[4,128,128]{2,1,0:T(8,128)S(1)}, f32[4,128,128]{2,1,0:T(8,128)S(1)}, u32[]{:S(2)}, u32[]{:S(2)}) collective-permute-start(f32[4,128,128]{2,1,0:T(8,128)S(1)} %get-tuple-element.43), channel_id=1, source_target_pairs={{0,1},{1,0},{2,3},{3,2},{4,5},{5,4},{6,7},{7,6},{8,9},{9,8},{10,11... | collective-permute-start | bytes 786440 | tf_op jit(solution)/shard_map/ppermute | solution.py:569

commit v5 on v4

--- a/solution.py
+++ b/solution.py
@@ -27,6 +27,7 @@
 SPAN = TILE + KSIZE - 1
 HALF = SPAN // 2
 TALL = 560
+TAPS = 48
 
 width_fractions = (0.075, 0.15, 0.3)
 family_degrees = (4, 2, 2)
@@ -62,23 +63,23 @@
     back_down = by_row.T[:TILE] * (2 / SPAN)
     back_across = by_lane[:, :TILE] * (2 / SPAN)
 
-    def three(matrix):
+    def three(matrix, width=512):
         high, low = as_halves(matrix)
-        rest = np.zeros((matrix.shape[0], 512 - 3 * SPAN), bf16)
+        rest = np.zeros((matrix.shape[0], width - 3 * matrix.shape[1]), bf16)
         return np.concatenate([high, high, low, rest], axis=1)
 
-    same = np.zeros((SPAN, TILE), np.float32)
-    cross = np.zeros((SPAN, TILE), np.float32)
+    same = np.zeros((SPAN + 8, TAPS))
+    cross = np.zeros((SPAN + 8, TAPS))
     same[spot, :KSIZE] = same[spot + 4, :KSIZE] = cosine[:, :KSIZE]
     cross[spot, :KSIZE], cross[spot + 4, :KSIZE] = sine[:, :KSIZE], -sine[:, :KSIZE]
     along = np.zeros((TILE, 2 * TILE), np.float32)
     along[:KSIZE, :HALF], along[:KSIZE, TILE:TILE + HALF] = cosine[:, :KSIZE].T, -sine[:, :KSIZE].T
     return (
-        np.stack(as_halves(across)),
+        np.concatenate(as_halves(across), axis=0),
         three(down),
         three(back_down),
         np.concatenate(as_halves(back_across), axis=1),
-        np.stack([same, cross]),
+        np.concatenate([three(same, 256), three(cross, 256)], axis=0),
         along,
     )
 
@@ -182,8 +183,17 @@
 
 def filter_bank():
     taps = lax.broadcasted_iota(jnp.int32, (1, TILE), 1)
-    rows = [value / jnp.sqrt(jnp.sum(value * value, axis=1, keepdims=True)) for value in profiles_at(taps)]
-    return jnp.concatenate(rows + [jnp.zeros((16 - NFILT, TILE), f32)], axis=0)
+    values = profiles_at(taps)
+    norms = [jnp.sqrt(jnp.sum(value * value, axis=1, keepdims=True)) for value in values]
+    rows = [value / norm for value, norm in zip(values, norms)]
+    wide = jnp.concatenate(rows + [jnp.zeros((16 - NFILT, TILE), f32)], axis=0)
+    lane = lax.broadcasted_iota(jnp.int32, (TAPS, TILE), 1)
+    tall = jnp.zeros((TAPS, TILE), f32)
+    for number, (value, norm) in enumerate(
+        zip(profiles_at(lax.broadcasted_iota(jnp.int32, (TAPS, TILE), 0)), norms)
+    ):
+        tall = jnp.where(lane == number, value / norm, tall)
+    return wide, tall
 
 
 def kernel_spectrum(filters, which, table_ref, down_taps_ref, along_ref):
@@ -192,23 +202,30 @@
     mixing = jnp.zeros((16, 16), f32)
     for number, (p, q) in enumerate(filter_terms()):
         mixing = jnp.where((first == p) & (second == q), table_ref[number, which], mixing)
-    across = exact_dot(mixing, exact_dot(filters, along_ref[...]))
-    return [
-        exact_dot(exact_dot(down_taps_ref[part], filters, ((1,), (1,))), across)
-        for part in range(2)
-    ]
+    wide, tall = filters
+    across = exact_dot(mixing, exact_dot(wide, along_ref[...]))
+    across = jnp.concatenate([across, jnp.zeros((TILE - 16, 2 * TILE), f32)], axis=0)
+    mixed = exact_dot(tall, across)
+    high = mixed.astype(bf16).astype(f32)
+    rest = jnp.zeros((256 - 3 * TAPS, 2 * TILE), f32)
+    mixed = jnp.concatenate([high, mixed - high, high, rest], axis=0).astype(bf16)
+    both = jnp.dot(down_taps_ref[...], mixed, preferred_element_type=f32)
+    return both[:SPAN], both[SPAN + 8:2 * SPAN + 8]
 
 
 def match_kernel(
     place_ref, index_hbm, table_hbm, image_hbm, var_hbm, bits_hbm, owner_hbm, slot_hbm,
     across_hbm, down_hbm, back_down_hbm, back_across_hbm, down_taps_hbm, along_hbm,
-    out_0, out_1, out_2, out_3,
-    index_ref, table_ref, image_ref, var_ref, bits_ref, owner_ref, slot_ref,
-    across_ref, down_ref, back_down_ref, back_across_ref, down_taps_ref, along_ref, sems, out_sems,
-    tail_ref, high_ref, low_ref, wave_ref, stack_ref, turn_ref, result_ref, rows_ref, factor_ref,
-    weight_ref, out_ref,
-    *, block,
+    *rest, block,
 ):
+    count = 4 if block == 0 else 1
+    outs = rest[:count]
+    (
+        index_ref, table_ref, image_ref, var_ref, bits_ref, owner_ref, slot_ref,
+        across_ref, down_ref, back_down_ref, back_across_ref, down_taps_ref, along_ref, sems,
+        out_sems, tail_ref, high_ref, low_ref, wave_ref, stack_ref, turn_ref, result_ref, rows_ref,
+        factor_ref, weight_ref, out_ref,
+    ) = rest[count:]
     copies = [
         pltpu.make_async_copy(source, goal, sems.at[number])
         for number, (source, goal) in enumerate((
@@ -239,9 +256,11 @@
         copy.wait()
 
     pair = 2 * TILE
-    forward = jnp.concatenate([across_ref[0], across_ref[0], across_ref[1]], axis=0)
+    forward = jnp.concatenate([across_ref[:pair], across_ref[...]], axis=0)
     backward = jnp.concatenate([back_across_ref[...], back_across_ref[...]], axis=0)
-    spots = [way_to(place_ref[0], piece) for piece in range(CHIPS)]
+    spots = range(CHIPS)
+    if block == 0:
+        spots = [way_to(place_ref[0], piece) for piece in range(CHIPS)]
 
     def halve():
         tail_ref[:PADDED, :PADDED - BLOCK] = image_ref[:, BLOCK:]
@@ -268,9 +287,8 @@
         factor_ref[0] = same.reshape(SPAN // 8, 8, pair)
         factor_ref[1] = cross.reshape(SPAN // 8, 8, pair)
         weight_ref[...] = exact_dot(cell_weights(var_ref[block], bits_ref[block]), spread)
-        if block == 0:
-            info = item_info(var_ref, bits_ref, owner_ref, slot_ref)
-            out_ref[:, TILES_BLK] = jnp.broadcast_to(info[None], (CHIPS, INFO, TILE))
+        info = item_info(var_ref, bits_ref, owner_ref, slot_ref)
+        out_ref[:, TILES_BLK] = jnp.broadcast_to(info[None], (CHIPS, INFO, TILE))
 
     def stack(tile):
         column, line = divmod(tile, SIDE)
@@ -322,12 +340,13 @@
         column, rest = divmod(step - 4, SIDE)
         if rest == SIDE - 1 and 0 <= column < SIDE:
             back_across(column)
+    each = CHIPS // count
     sends = [
-        pltpu.make_async_copy(out_ref.at[way * 4:way * 4 + 4], out_hbm, out_sems.at[way])
-        for way, out_hbm in enumerate((out_0, out_1, out_2, out_3))
+        pltpu.make_async_copy(out_ref.at[way * each:(way + 1) * each], out_hbm, out_sems.at[way])
+        for way, out_hbm in enumerate(outs)
     ]
-    for way in (3, 1, 2, 0):
-        sends[way].start()
+    for send in reversed(sends):
+        send.start()
     for send in sends:
         send.wait()
 
@@ -335,14 +354,15 @@
 def match_block(block, place, exposures, variance, bits, table, index, owner, slot):
     blocks = exposures.shape[1]
     items = blocks * TILES_BLK
-    groups = TILES_BLK + (1 if block == 0 else 0)
+    groups = TILES_BLK + 1
+    count = 4 if block == 0 else 1
     matrices = transforms()
     return pl.pallas_call(
         functools.partial(match_kernel, block=block),
-        out_shape=[jax.ShapeDtypeStruct((4, groups, PIECE, TILE), f32)] * 4,
+        out_shape=[jax.ShapeDtypeStruct((CHIPS // count, groups, PIECE, TILE), f32)] * count,
         in_specs=[pl.BlockSpec(memory_space=pltpu.SMEM)]
         + [pl.BlockSpec(memory_space=pltpu.HBM)] * (7 + len(matrices)),
-        out_specs=[pl.BlockSpec(memory_space=pltpu.HBM)] * 4,
+        out_specs=[pl.BlockSpec(memory_space=pltpu.HBM)] * count,
         scratch_shapes=[
             pltpu.SMEM((1, blocks), jnp.int32),
             pltpu.SMEM(table.shape, f32),
@@ -390,13 +410,16 @@
 
 
 def partial_kernel(place_ref, *refs):
-    first_refs, second_refs, (mine_ref, other_ref) = refs[:4], refs[4:8], refs[8:]
+    first_refs, second_ref, mine_ref, other_ref = refs[:4], *refs[4:]
     core = place_ref[0] % 2
     per_group = TILE // TILES_BLK
     lane = lax.broadcasted_iota(jnp.int32, (INFO, TILE), 1)
-    info = [first_refs[source // 4][source % 4, TILES_BLK * PIECE:] for source in range(CHIPS)]
+    infos = (
+        [first_refs[source // 4][source % 4, TILES_BLK * PIECE:, :] for source in range(CHIPS)],
+        [second_ref[source, TILES_BLK * PIECE:, :] for source in range(CHIPS)],
+    )
     tables = []
-    for block in range(2):
+    for block, info in enumerate(infos):
         rows = []
         for m in range(PER_TILE):
             groups = []
@@ -438,9 +461,9 @@
     for line in range(PIECE):
         total = None
         rows = pl.ds(line, TILES_BLK, PIECE)
-        for route, part_refs in zip(routes, (first_refs, second_refs)):
+        for route, part_refs in zip(routes, (first_refs, (second_ref,))):
             part = jnp.concatenate(
-                [part_ref[:, rows, :].reshape(items // 4, TILE) for part_ref in part_refs], axis=0
+                [part_ref[:, rows, :].reshape(-1, TILE) for part_ref in part_refs], axis=0
             )
             high, low = split(part)
             term = jnp.dot(
@@ -470,19 +493,34 @@
     out_ref[...] = total.reshape(owned * PIECE, TILE)
 
 
-def owner_kernel(place_ref, mine_ref, other_ref, part_ref, image_ref, chi_ref):
+def chi_kernel(place_ref, mine_ref, other_ref, part_ref, upper_ref, lower_ref):
     owned = VISITS * OWN_DEV // 2
-    rows = pl.ds(pl.multiple_of(owned * PIECE + (place_ref[0] // 2) * OWN_DEV, OWN_DEV), OWN_DEV)
+    first = owned * PIECE + (place_ref[0] // 2) * OWN_DEV
+    rows = pl.ds(pl.multiple_of(first, OWN_DEV), OWN_DEV)
     sums = mine_ref[rows, :] + other_ref[rows, :]
-    spread = [spread_cells(sums, cell_row) + prior_weight for cell_row in range(PER_TILE)]
+    per_cell = CELL // PIECE
+    for m in range(PER_TILE):
+        weight = spread_cells(sums, m) + prior_weight
+        weight = jnp.broadcast_to(weight[:, None, :], (OWN_DEV, PIECE, TILE))
+        part = part_ref[m * per_cell:(m + 1) * per_cell]
+        chi_ref = upper_ref if m < PER_TILE // 2 else lower_ref
+        place = m % (PER_TILE // 2) * per_cell
+        chi_ref[place:place + per_cell] = part * part * weight.reshape(1, OWN_DEV * PIECE, TILE)
+
+
+def image_kernel(part_ref, image_ref):
     for slot in range(OWN_DEV):
-        image = part_ref[:, slot * PIECE:(slot + 1) * PIECE, :].reshape(TILE, TILE)
-        image_ref[slot] = image
-        weight = jnp.concatenate(
-            [jnp.broadcast_to(spread[m][slot:slot + 1], (CELL, TILE)) for m in range(PER_TILE)],
-            axis=0,
-        )
-        chi_ref[slot] = image * image * weight
+        rows = slice(slot * PIECE, (slot + 1) * PIECE)
+        image_ref[slot] = part_ref[:, rows, :].reshape(TILE, TILE)
+
+
+def detection_kernel(upper_ref, more_upper_ref, lower_ref, more_lower_ref, out_ref):
+    for slot in range(OWN_DEV):
+        rows = slice(slot * PIECE, (slot + 1) * PIECE)
+        upper = upper_ref[:, rows, :] + more_upper_ref[:, rows, :]
+        lower = lower_ref[:, rows, :] + more_lower_ref[:, rows, :]
+        out_ref[slot, :TILE // 2] = upper.reshape(TILE // 2, TILE)
+        out_ref[slot, TILE // 2:] = lower.reshape(TILE // 2, TILE)
 
 
 def local(exposures, variance, mask_planes, kernel_table, kernel_index, tile_owner, tile_slot):
@@ -511,27 +549,29 @@
 
     table = kernel_table.T
     owner = tile_owner.reshape(tile_slot.shape)
-    parts = []
-    for block in range(exposures.shape[1]):
-        pieces = match_block(
-            block, place, exposures, variance, mask_planes, table, kernel_index, owner, tile_slot
-        )
-        own = pl.pallas_call(
-            keep_kernel,
-            out_shape=jax.ShapeDtypeStruct(pieces[0].shape, f32),
-            in_specs=[pl.BlockSpec(memory_space=pltpu.HBM)],
-            out_specs=vmem,
-            scratch_shapes=[pltpu.SemaphoreType.DMA],
-            compiler_params=params,
-            name="keep",
-        )(pieces[0])
-        parts.extend(exchange([own, *pieces[1:]]))
-    parts = [part.reshape(4, -1, TILE) for part in parts]
+    def spread_tiles(pieces):
+        return lax.all_to_all(pieces, "visit", 0, 0, axis_index_groups=same_core, tiled=True)
+
+    same_core = [list(range(core, VISITS, 2)) for core in range(2)]
+    operands = (place, exposures, variance, mask_planes, table, kernel_index, owner, tile_slot)
+    pieces = match_block(0, *operands)
+    own = pl.pallas_call(
+        keep_kernel,
+        out_shape=jax.ShapeDtypeStruct(pieces[0].shape, f32),
+        in_specs=[pl.BlockSpec(memory_space=pltpu.HBM)],
+        out_specs=vmem,
+        scratch_shapes=[pltpu.SemaphoreType.DMA],
+        compiler_params=params,
+        name="keep",
+    )(pieces[0])
+    parts = [part.reshape(4, -1, TILE) for part in exchange([own, *pieces[1:]])]
+    (pieces,) = match_block(1, *operands)
+    parts.append(spread_tiles(pieces.reshape(CHIPS, -1, TILE)))
 
     mine, other = pl.pallas_call(
         partial_kernel,
         out_shape=[jax.ShapeDtypeStruct((owned * (PIECE + 1), TILE), f32)] * 2,
-        in_specs=[smem] + [vmem] * 8,
+        in_specs=[smem] + [vmem] * 5,
         out_specs=[vmem, vmem],
         compiler_params=params,
         name="partial_sums",
@@ -545,31 +585,41 @@
         compiler_params=params,
         name="merge_cores",
     )(place, mine, other)
-    pieces = lax.all_to_all(
-        pieces.reshape(CHIPS, OWN_DEV * PIECE, TILE),
-        "visit",
-        0,
-        0,
-        axis_index_groups=[list(range(core, VISITS, 2)) for core in range(2)],
-        tiled=True,
-    )
-    image, chi = pl.pallas_call(
-        owner_kernel,
-        out_shape=[jax.ShapeDtypeStruct((OWN_DEV, TILE, TILE), f32)] * 2,
+    pieces = spread_tiles(pieces.reshape(CHIPS, OWN_DEV * PIECE, TILE))
+    halves = pl.pallas_call(
+        chi_kernel,
+        out_shape=[jax.ShapeDtypeStruct((CHIPS // 2, OWN_DEV * PIECE, TILE), f32)] * 2,
         in_specs=[smem, vmem, vmem, vmem],
         out_specs=[vmem, vmem],
         compiler_params=params,
-        name="own",
+        name="chi",
     )(place, mine, other, pieces)
+    tiles = jax.ShapeDtypeStruct((OWN_DEV, TILE, TILE), f32)
+    image = pl.pallas_call(
+        image_kernel,
+        out_shape=tiles,
+        in_specs=[vmem],
+        out_specs=vmem,
+        compiler_params=params,
+        name="image",
+    )(pieces)
 
     pairings = ([(0, 1), (1, 0), (2, 3), (3, 2)], [(0, 3), (3, 0), (1, 2), (2, 1)])
-    halves = [chi[:OWN_DEV // 2], chi[OWN_DEV // 2:]]
-    for turn in range(2):
-        halves = [
-            half + lax.ppermute(half, "band", pairings[(turn + number) % 2])
-            for number, half in enumerate(halves)
-        ]
-    return image[None], jnp.concatenate(halves, axis=0)
+    halves = [
+        half + lax.ppermute(half, "band", pairings[number]) for number, half in enumerate(halves)
+    ]
+    terms = []
+    for number, half in enumerate(halves):
+        terms.extend((half, lax.ppermute(half, "band", pairings[1 - number])))
+    detection = pl.pallas_call(
+        detection_kernel,
+        out_shape=tiles,
+        in_specs=[vmem] * 4,
+        out_specs=vmem,
+        compiler_params=params,
+        name="detection",
+    )(*terms)
+    return image[None], detection
 
 
 def solution(mesh):

time: 90.1 us -> 88 us (0.977)
  starting transfers between devices: 30.6 us -> 25.4 us
  waiting for transfers between devices: 22.9 us -> 26.6 us
    ppermute x12 -> x6, starting transfers between devices: 23.4 us -> 9.56 us  [exchange(): lax.ppermute(parts[way], 'visit', phase_partners(phase, way))]
    ppermute x12 -> x6, waiting for transfers between devices: 9.16 us -> 16.5 us  [exchange(): lax.ppermute(parts[way], 'visit', phase_partners(phase, way))]
    all_to_all x0 -> x1, starting transfers between devices: none -> 7.13 us  [spread_tiles(): lax.all_to_all(pieces, 'visit', 0, 0, axis_index_groups=same_core, tiled=...]
    ppermute x4, waiting for transfers between devices: 11.7 us -> 8.19 us  [the longest x2 5.51 us: local(): terms.extend((half, lax.ppermute(half, 'band', pairings[1 - number])))]
    ppermute x4, starting transfers between devices: 7.14 us -> 8.58 us  [the longest x2 4.52 us: local(): lax.ppermute(half, 'band', pairings[number])]
    pallas_call x1 -> x3, Pallas kernels: 1.06 us -> 2.03 us  [the longest x1 0.85 us: local(): pl.pallas_call(detection_kernel, out_shape=tiles, in_specs=[vmem] * 4, ou...]
  transfers between devices with their start and end apart: 17 -> 12, of which waited for: 8 -> 9; matrix products, arithmetic and copies ran while one was open for 0% -> 0% of each run, Pallas kernels for 8% -> 9%
where the time goes in v5:
time: 88 us; the launch traced here: 87.7 us
  waiting for transfers between devices  26.6 us (30%)
  starting transfers between devices  25.4 us (29%)
  Pallas kernels  17.3 us (20%)
  blocking collectives  16.7 us (19%)
  local copies, waits for them, and re-layouts  0.96 us (1%)
    all_to_all x1, blocking collectives, spread_tiles(): lax.all_to_all(pieces, 'visit', 0, 0, axis_index_groups=same_core, tiled=...  16.7 us
    ppermute x6, waiting for transfers between devices, exchange(): lax.ppermute(parts[way], 'visit', phase_partners(phase, way))  16.5 us
    pallas_call x2, Pallas kernels, match_block(): pl.pallas_call(functools.partial(match_kernel, block=block), out_shape=[j...  13.8 us
    ppermute x6, starting transfers between devices, exchange(): lax.ppermute(parts[way], 'visit', phase_partners(phase, way))  9.56 us
    all_to_all x1, starting transfers between devices, spread_tiles(): lax.all_to_all(pieces, 'visit', 0, 0, axis_index_groups=same_core, tiled=...  7.13 us
    ppermute x2, waiting for transfers between devices, local(): terms.extend((half, lax.ppermute(half, 'band', pairings[1 - number])))  5.51 us
    ppermute x2, starting transfers between devices, local(): lax.ppermute(half, 'band', pairings[number])  4.52 us
    ppermute x2, starting transfers between devices, local(): terms.extend((half, lax.ppermute(half, 'band', pairings[1 - number])))  4.06 us
  transfers between devices with their start and end apart: 12, of which 9 were waited for; matrix products, arithmetic and copies ran while one was open for 0% of the time, Pallas kernels for 9%

profile of v5, /device:TPU:0, one launch (start us, length us, event | category | flops | bytes accessed | tf_op | source)
XLA Modules:
  0.0 87.7 jit_solution(1165538320879023557)
XLA Ops:
  0.6 6.9 %match_block.3 = f32[16,17,8,128]{3,2,1,0:T(8,128)} custom-call(s32[1]{0:T(128)} %bitcast.place_ref, s32[1,2]{1,0:T(1,128)} %index_hbm.3, f32[27,64]{1,0:T(8,128)} %bitcast.17, f32[1,2,552,552]{3,2,1,0:T(8,128)} %image_hbm.3, f32[1,2,16,16]{3,2,1,0:T(8,128)} %var_hbm.3, s32[1,2,16,16]{3,2,1,0:T(8,128)} %bits_hbm.3, s32[1,32]{1,0:T(1,128)} %bitcast.19, ...), custom_call_target="tpu_custom_call" | custom-call | flops 5242880000 | bytes 3145728 | tf_op jit(solution)/shard_map/match_block/pallas_call | solution.py:360
  7.5 7.1 %all-to-all-start = ((f32[16,136,128]{2,1,0:T(8,128)}), f32[16,136,128]{2,1,0:T(8,128)S(1)}, u32[]{:S(2)}, u32[]{:S(2)}) async-start(f32[16,136,128]{2,1,0:T(8,128)} %bitcast.15), calls=%async_computation | async-start | bytes 2228224 | tf_op jit(solution)/shard_map/all_to_all | solution.py:553
  14.6 7.0 %match_block.2 = (f32[4,17,8,128]{3,2,1,0:T(8,128)}, f32[4,17,8,128]{3,2,1,0:T(8,128)}, f32[4,17,8,128]{3,2,1,0:T(8,128)}, f32[4,17,8,128]{3,2,1,0:T(8,128)}) custom-call(s32[1]{0:T(128)} %bitcast.place_ref, s32[1,2]{1,0:T(1,128)} %index_hbm.3, f32[27,64]{1,0:T(8,128)} %bitcast.18, f32[1,2,552,552]{3,2,1,0:T(8,128)} %image_hbm.3, f32[1,2,16,16]{3,2,1,0:T(8,128)} %var_hbm.3, ...), custom_call_target="tpu_custom_call" | custom-call | flops 5242880000 | bytes 3145728 | tf_op jit(solution)/shard_map/match_block/pallas_call | solution.py:360
  21.6 2.9 %collective-permute-start = (f32[4,17,8,128]{3,2,1,0:T(8,128)}, f32[4,17,8,128]{3,2,1,0:T(8,128)S(1)}, u32[]{:S(2)}, u32[]{:S(2)}) collective-permute-start(f32[4,17,8,128]{3,2,1,0:T(8,128)} %get-tuple-element.15), channel_id=1, source_target_pairs={{0,40},{4,124},{8,32},{12,116},{16,56},{20,108},{24,48},{28,100},{... | collective-permute-start | bytes 835592 | tf_op jit(solution)/shard_map/ppermute | solution.py:536
  24.5 0.6 collective-permute-start.1
  25.1 0.1 collective-permute-start.2
  25.2 1.0 %copy-done = f32[4,17,8,128]{3,2,1,0:T(8,128)S(1)} copy-done((f32[4,17,8,128]{3,2,1,0:T(8,128)S(1)}, f32[4,17,8,128]{3,2,1,0:T(8,128)}, u32[]{:S(2)}) %copy-start) | copy-done | bytes 278552
  26.2 6.6 %collective-permute-done.refs_1_ = f32[4,17,8,128]{3,2,1,0:T(8,128)S(1)} collective-permute-done((f32[4,17,8,128]{3,2,1,0:T(8,128)}, f32[4,17,8,128]{3,2,1,0:T(8,128)S(1)}, u32[]{:S(2)}, u32[]{:S(2)}) %collective-permute-start) | collective-permute-done | bytes 278560 | tf_op jit(solution)/shard_map/ppermute | solution.py:536
  32.8 2.9 %collective-permute-done.1.refs_2_ = f32[4,17,8,128]{3,2,1,0:T(8,128)S(1)} collective-permute-done((f32[4,17,8,128]{3,2,1,0:T(8,128)}, f32[4,17,8,128]{3,2,1,0:T(8,128)S(1)}, u32[]{:S(2)}, u32[]{:S(2)}) %collective-permute-start.1) | collective-permute-done | bytes 278560 | tf_op jit(solution)/shard_map/ppermute | solution.py:536
  35.7 0.1 turn.1
  35.8 3.8 %collective-permute-start.3 = (f32[4,17,8,128]{3,2,1,0:T(8,128)S(1)}, f32[4,17,8,128]{3,2,1,0:T(8,128)S(1)}, u32[]{:S(2)}, u32[]{:S(2)}) collective-permute-start(f32[4,17,8,128]{3,2,1,0:T(8,128)S(1)} %get-tuple-element.19), channel_id=1, source_target_pairs={{0,120},{4,44},{8,112},{12,36},{16,104},{20,60},{24,96},{28,52},{3... | collective-permute-start | bytes 835592 | tf_op jit(solution)/shard_map/ppermute | solution.py:536
  39.6 1.4 %collective-permute-start.4 = (f32[4,17,8,128]{3,2,1,0:T(8,128)S(1)}, f32[4,17,8,128]{3,2,1,0:T(8,128)S(1)}, u32[]{:S(2)}, u32[]{:S(2)}) collective-permute-start(f32[4,17,8,128]{3,2,1,0:T(8,128)S(1)} %get-tuple-element.20), channel_id=1, source_target_pairs={{0,24},{4,12},{8,16},{12,4},{16,8},{20,28},{24,0},{28,20},{32,56},... | collective-permute-start | bytes 835592 | tf_op jit(solution)/shard_map/ppermute | solution.py:536
  41.0 0.8 collective-permute-start.5
  41.7 4.0 %collective-permute-done.3 = f32[4,17,8,128]{3,2,1,0:T(8,128)S(1)} collective-permute-done((f32[4,17,8,128]{3,2,1,0:T(8,128)S(1)}, f32[4,17,8,128]{3,2,1,0:T(8,128)S(1)}, u32[]{:S(2)}, u32[]{:S(2)}) %collective-permute-start.3) | collective-permute-done | bytes 278560 | tf_op jit(solution)/shard_map/ppermute | solution.py:536
  45.7 2.8 %collective-permute-done.4 = f32[4,17,8,128]{3,2,1,0:T(8,128)S(1)} collective-permute-done((f32[4,17,8,128]{3,2,1,0:T(8,128)S(1)}, f32[4,17,8,128]{3,2,1,0:T(8,128)S(1)}, u32[]{:S(2)}, u32[]{:S(2)}) %collective-permute-start.4) | collective-permute-done | bytes 278560 | tf_op jit(solution)/shard_map/ppermute | solution.py:536
  48.5 0.3 collective-permute-done.5
  48.7 0.0 all-to-all-done.refs_4_
  48.7 1.0 %partial_sums.1 = (f32[1152,128]{1,0:T(8,128)S(1)}, f32[1152,128]{1,0:T(8,128)S(1)}) custom-call(s32[1]{0:T(128)} %bitcast.place_ref, f32[4,136,128]{2,1,0:T(8,128)S(1)} %bitcast.11, f32[4,136,128]{2,1,0:T(8,128)S(1)} %bitcast.12, f32[4,136,128]{2,1,0:T(8,128)S(1)} %bitcast.13, f32[4,136,128]{2,1,0:T(8,128)S(1)} %bitcast.14, ...), custom_call_target="tpu_custom_call" | custom-call | tf_op jit(solution)/shard_map/partial_sums/pallas_call | solution.py:571
  49.8 0.1 collective-permute-start.6
  49.8 2.0 %collective-permute-done.6.other_ref = f32[1152,128]{1,0:T(8,128)S(1)} collective-permute-done((f32[1152,128]{1,0:T(8,128)S(1)}, f32[1152,128]{1,0:T(8,128)S(1)}, u32[]{:S(2)}, u32[]{:S(2)}) %collective-permute-start.6) | collective-permute-done | bytes 589856 | tf_op jit(solution)/shard_map/ppermute | solution.py:579
  51.8 0.3 merge_cores.1
  52.1 16.7 %all_to_all.10.part_ref = f32[16,64,128]{2,1,0:T(8,128)S(1)} all-to-all(f32[16,64,128]{2,1,0:T(8,128)S(1)} %bitcast.10), channel_id=1, replica_groups={{0,8,16,24,32,40,48,56,64,72,80,88,96,104,112,120},{4,12,20,28,36,44,52..., dimensions={0} | all-to-all | bytes 1048576 | tf_op jit(solution)/shard_map/all_to_all | solution.py:553
  68.8 0.3 chi.1
  69.2 2.0 %collective-permute-start.7 = (f32[8,64,128]{2,1,0:T(8,128)S(1)}, f32[8,64,128]{2,1,0:T(8,128)S(1)}, u32[]{:S(2)}, u32[]{:S(2)}) collective-permute-start(f32[8,64,128]{2,1,0:T(8,128)S(1)} %get-tuple-element.24), channel_id=1, source_target_pairs={{0,1},{1,0},{2,3},{3,2},{4,5},{5,4},{6,7},{7,6},{8,9},{9,8},{10,11... | collective-permute-start | bytes 786440 | tf_op jit(solution)/shard_map/ppermute | solution.py:609
  71.2 2.5 %collective-permute-start.9 = (f32[8,64,128]{2,1,0:T(8,128)S(1)}, f32[8,64,128]{2,1,0:T(8,128)S(1)}, u32[]{:S(2)}, u32[]{:S(2)}) collective-permute-start(f32[8,64,128]{2,1,0:T(8,128)S(1)} %get-tuple-element.25), channel_id=1, source_target_pairs={{0,3},{3,0},{1,2},{2,1},{4,7},{7,4},{5,6},{6,5},{8,11},{11,8},{9,1... | collective-permute-start | bytes 786440 | tf_op jit(solution)/shard_map/ppermute | solution.py:609
  73.7 2.7 %collective-permute-done.7 = f32[8,64,128]{2,1,0:T(8,128)S(1)} collective-permute-done((f32[8,64,128]{2,1,0:T(8,128)S(1)}, f32[8,64,128]{2,1,0:T(8,128)S(1)}, u32[]{:S(2)}, u32[]{:S(2)}) %collective-permute-start.7) | collective-permute-done | bytes 262176 | tf_op jit(solution)/shard_map/ppermute | solution.py:609
  76.4 3.9 %collective-permute-start.8 = (f32[8,64,128]{2,1,0:T(8,128)S(1)}, f32[8,64,128]{2,1,0:T(8,128)S(1)}, u32[]{:S(2)}, u32[]{:S(2)}) collective-permute-start(f32[8,64,128]{2,1,0:T(8,128)S(1)} %add.6.upper_ref), channel_id=1, source_target_pairs={{0,3},{3,0},{1,2},{2,1},{4,7},{7,4},{5,6},{6,5},{8,11},{11,8},{9,1... | collective-permute-start | bytes 786440 | tf_op jit(solution)/shard_map/ppermute | solution.py:613
  80.4 0.1 collective-permute-start.10
  80.5 0.8 image.1
  81.3 3.4 %collective-permute-done.8.more_upper_ref = f32[8,64,128]{2,1,0:T(8,128)S(1)} collective-permute-done((f32[8,64,128]{2,1,0:T(8,128)S(1)}, f32[8,64,128]{2,1,0:T(8,128)S(1)}, u32[]{:S(2)}, u32[]{:S(2)}) %collective-permute-start.8) | collective-permute-done | bytes 262176 | tf_op jit(solution)/shard_map/ppermute | solution.py:613
  84.7 2.1 %collective-permute-done.10.more_lower_ref = f32[8,64,128]{2,1,0:T(8,128)S(1)} collective-permute-done((f32[8,64,128]{2,1,0:T(8,128)S(1)}, f32[8,64,128]{2,1,0:T(8,128)S(1)}, u32[]{:S(2)}, u32[]{:S(2)}) %collective-permute-start.10) | collective-permute-done | bytes 262176 | tf_op jit(solution)/shard_map/ppermute | solution.py:613
  86.9 0.9 detection.1
  (6 shorter events, 0.1 us)
Async XLA Ops:
  7.5 41.2 %all-to-all-start = ((f32[16,136,128]{2,1,0:T(8,128)}), f32[16,136,128]{2,1,0:T(8,128)S(1)}, u32[]{:S(2)}, u32[]{:S(2)}) async-start(f32[16,136,128]{2,1,0:T(8,128)} %bitcast.15), calls=%async_computation | async-start | bytes 2228224 | tf_op jit(solution)/shard_map/all_to_all | solution.py:553
  21.6 11.2 %collective-permute-start = (f32[4,17,8,128]{3,2,1,0:T(8,128)}, f32[4,17,8,128]{3,2,1,0:T(8,128)S(1)}, u32[]{:S(2)}, u32[]{:S(2)}) collective-permute-start(f32[4,17,8,128]{3,2,1,0:T(8,128)} %get-tuple-element.15), channel_id=1, source_target_pairs={{0,40},{4,124},{8,32},{12,116},{16,56},{20,108},{24,48},{28,100},{... | collective-permute-start | bytes 835592 | tf_op jit(solution)/shard_map/ppermute | solution.py:536
  24.5 11.1 %collective-permute-start.1 = (f32[4,17,8,128]{3,2,1,0:T(8,128)}, f32[4,17,8,128]{3,2,1,0:T(8,128)S(1)}, u32[]{:S(2)}, u32[]{:S(2)}) collective-permute-start(f32[4,17,8,128]{3,2,1,0:T(8,128)} %get-tuple-element.16), channel_id=1, source_target_pairs={{0,8},{4,28},{8,0},{12,20},{16,24},{20,12},{24,16},{28,4},{32,40},... | collective-permute-start | bytes 835592 | tf_op jit(solution)/shard_map/ppermute | solution.py:536
  25.1 10.6 %collective-permute-start.2 = (f32[4,17,8,128]{3,2,1,0:T(8,128)}, f32[4,17,8,128]{3,2,1,0:T(8,128)S(1)}, u32[]{:S(2)}, u32[]{:S(2)}) collective-permute-start(f32[4,17,8,128]{3,2,1,0:T(8,128)} %get-tuple-element.17), channel_id=1, source_target_pairs={{0,32},{4,100},{8,40},{12,108},{16,48},{20,116},{24,56},{28,124},{... | collective-permute-start | bytes 835592 | tf_op jit(solution)/shard_map/ppermute | solution.py:536
  25.2 1.0 %copy-start = (f32[4,17,8,128]{3,2,1,0:T(8,128)S(1)}, f32[4,17,8,128]{3,2,1,0:T(8,128)}, u32[]{:S(2)}) copy-start(f32[4,17,8,128]{3,2,1,0:T(8,128)} %get-tuple-element.14.part_hbm) | copy-start | bytes 835588
  35.8 9.9 %collective-permute-start.3 = (f32[4,17,8,128]{3,2,1,0:T(8,128)S(1)}, f32[4,17,8,128]{3,2,1,0:T(8,128)S(1)}, u32[]{:S(2)}, u32[]{:S(2)}) collective-permute-start(f32[4,17,8,128]{3,2,1,0:T(8,128)S(1)} %get-tuple-element.19), channel_id=1, source_target_pairs={{0,120},{4,44},{8,112},{12,36},{16,104},{20,60},{24,96},{28,52},{3... | collective-permute-start | bytes 835592 | tf_op jit(solution)/shard_map/ppermute | solution.py:536
  39.6 8.9 %collective-permute-start.4 = (f32[4,17,8,128]{3,2,1,0:T(8,128)S(1)}, f32[4,17,8,128]{3,2,1,0:T(8,128)S(1)}, u32[]{:S(2)}, u32[]{:S(2)}) collective-permute-start(f32[4,17,8,128]{3,2,1,0:T(8,128)S(1)} %get-tuple-element.20), channel_id=1, source_target_pairs={{0,24},{4,12},{8,16},{12,4},{16,8},{20,28},{24,0},{28,20},{32,56},... | collective-permute-start | bytes 835592 | tf_op jit(solution)/shard_map/ppermute | solution.py:536
  41.0 7.8 %collective-permute-start.5 = (f32[4,17,8,128]{3,2,1,0:T(8,128)S(1)}, f32[4,17,8,128]{3,2,1,0:T(8,128)S(1)}, u32[]{:S(2)}, u32[]{:S(2)}) collective-permute-start(f32[4,17,8,128]{3,2,1,0:T(8,128)S(1)} %get-tuple-element.21), channel_id=1, source_target_pairs={{0,96},{4,36},{8,104},{12,44},{16,112},{20,52},{24,120},{28,60},{3... | collective-permute-start | bytes 835592 | tf_op jit(solution)/shard_map/ppermute | solution.py:536
  49.8 2.1 %collective-permute-start.6 = (f32[1152,128]{1,0:T(8,128)S(1)}, f32[1152,128]{1,0:T(8,128)S(1)}, u32[]{:S(2)}, u32[]{:S(2)}) collective-permute-start(f32[1152,128]{1,0:T(8,128)S(1)} %get-tuple-element.23), channel_id=1, source_target_pairs={{0,4},{4,0},{8,12},{12,8},{16,20},{20,16},{24,28},{28,24},{32,36},... | collective-permute-start | bytes 1769480 | tf_op jit(solution)/shard_map/ppermute | solution.py:579
  69.2 7.2 %collective-permute-start.7 = (f32[8,64,128]{2,1,0:T(8,128)S(1)}, f32[8,64,128]{2,1,0:T(8,128)S(1)}, u32[]{:S(2)}, u32[]{:S(2)}) collective-permute-start(f32[8,64,128]{2,1,0:T(8,128)S(1)} %get-tuple-element.24), channel_id=1, source_target_pairs={{0,1},{1,0},{2,3},{3,2},{4,5},{5,4},{6,7},{7,6},{8,9},{9,8},{10,11... | collective-permute-start | bytes 786440 | tf_op jit(solution)/shard_map/ppermute | solution.py:609
  71.2 9.2 %collective-permute-start.9 = (f32[8,64,128]{2,1,0:T(8,128)S(1)}, f32[8,64,128]{2,1,0:T(8,128)S(1)}, u32[]{:S(2)}, u32[]{:S(2)}) collective-permute-start(f32[8,64,128]{2,1,0:T(8,128)S(1)} %get-tuple-element.25), channel_id=1, source_target_pairs={{0,3},{3,0},{1,2},{2,1},{4,7},{7,4},{5,6},{6,5},{8,11},{11,8},{9,1... | collective-permute-start | bytes 786440 | tf_op jit(solution)/shard_map/ppermute | solution.py:609
  76.4 8.3 %collective-permute-start.8 = (f32[8,64,128]{2,1,0:T(8,128)S(1)}, f32[8,64,128]{2,1,0:T(8,128)S(1)}, u32[]{:S(2)}, u32[]{:S(2)}) collective-permute-start(f32[8,64,128]{2,1,0:T(8,128)S(1)} %add.6.upper_ref), channel_id=1, source_target_pairs={{0,3},{3,0},{1,2},{2,1},{4,7},{7,4},{5,6},{6,5},{8,11},{11,8},{9,1... | collective-permute-start | bytes 786440 | tf_op jit(solution)/shard_map/ppermute | solution.py:613
  80.4 6.5 %collective-permute-start.10 = (f32[8,64,128]{2,1,0:T(8,128)S(1)}, f32[8,64,128]{2,1,0:T(8,128)S(1)}, u32[]{:S(2)}, u32[]{:S(2)}) collective-permute-start(f32[8,64,128]{2,1,0:T(8,128)S(1)} %add.7.lower_ref), channel_id=1, source_target_pairs={{0,1},{1,0},{2,3},{3,2},{4,5},{5,4},{6,7},{7,6},{8,9},{9,8},{10,11... | collective-permute-start | bytes 786440 | tf_op jit(solution)/shard_map/ppermute | solution.py:613

commit v6 on v5

--- a/solution.py
+++ b/solution.py
@@ -218,7 +218,7 @@
     across_hbm, down_hbm, back_down_hbm, back_across_hbm, down_taps_hbm, along_hbm,
     *rest, block,
 ):
-    count = 4 if block == 0 else 1
+    count = 4
     outs = rest[:count]
     (
         index_ref, table_ref, image_ref, var_ref, bits_ref, owner_ref, slot_ref,
@@ -258,9 +258,7 @@
     pair = 2 * TILE
     forward = jnp.concatenate([across_ref[:pair], across_ref[...]], axis=0)
     backward = jnp.concatenate([back_across_ref[...], back_across_ref[...]], axis=0)
-    spots = range(CHIPS)
-    if block == 0:
-        spots = [way_to(place_ref[0], piece) for piece in range(CHIPS)]
+    spots = [way_to(place_ref[0], piece) for piece in range(CHIPS)]
 
     def halve():
         tail_ref[:PADDED, :PADDED - BLOCK] = image_ref[:, BLOCK:]
@@ -355,7 +353,7 @@
     blocks = exposures.shape[1]
     items = blocks * TILES_BLK
     groups = TILES_BLK + 1
-    count = 4 if block == 0 else 1
+    count = 4
     matrices = transforms()
     return pl.pallas_call(
         functools.partial(match_kernel, block=block),
@@ -409,32 +407,28 @@
             out_ref[first] = part_ref[second]
 
 
-def partial_kernel(place_ref, *refs):
-    first_refs, second_ref, mine_ref, other_ref = refs[:4], *refs[4:]
+def partial_kernel(place_ref, *refs, block):
+    part_refs, before, (mine_ref, other_ref) = refs[:4], refs[4:-2], refs[-2:]
     core = place_ref[0] % 2
     per_group = TILE // TILES_BLK
     lane = lax.broadcasted_iota(jnp.int32, (INFO, TILE), 1)
-    infos = (
-        [first_refs[source // 4][source % 4, TILES_BLK * PIECE:, :] for source in range(CHIPS)],
-        [second_ref[source, TILES_BLK * PIECE:, :] for source in range(CHIPS)],
-    )
-    tables = []
-    for block, info in enumerate(infos):
-        rows = []
-        for m in range(PER_TILE):
-            groups = []
-            for group in range(CHIPS // per_group):
-                total = None
-                for member in range(per_group):
-                    goal = member * TILES_BLK
-                    shift = (goal - (m * 2 + block) * TILES_BLK) % TILE
-                    value = info[group * per_group + member]
-                    value = pltpu.roll(value, shift, 1) if shift else value
-                    here = (lane >= goal) & (lane < goal + TILES_BLK)
-                    total = value if total is None else jnp.where(here, value, total)
-                groups.append(total)
-            rows.append(jnp.concatenate(groups, axis=1))
-        tables.append(rows)
+    info = [
+        part_refs[source // 4][source % 4, TILES_BLK * PIECE:, :] for source in range(CHIPS)
+    ]
+    rows = []
+    for m in range(PER_TILE):
+        groups = []
+        for group in range(CHIPS // per_group):
+            total = None
+            for member in range(per_group):
+                goal = member * TILES_BLK
+                shift = (goal - (m * 2 + block) * TILES_BLK) % TILE
+                value = info[group * per_group + member]
+                value = pltpu.roll(value, shift, 1) if shift else value
+                here = (lane >= goal) & (lane < goal + TILES_BLK)
+                total = value if total is None else jnp.where(here, value, total)
+            groups.append(total)
+        rows.append(jnp.concatenate(groups, axis=1))
 
     targets = VISITS * OWN_DEV
     owned = targets // 2
@@ -443,36 +437,32 @@
     side = (row // owned + core) % 2
     inner = row % owned
     wanted = ((inner // OWN_DEV) * 2 + side) * OWN_DEV + inner % OWN_DEV
-    routes = []
-    sums = None
-    over_items = (((1,), (1,)), ((), ()))
-    for block in range(2):
-        target = tables[block][0][PER_TILE:PER_TILE + 1, :].astype(jnp.int32)
-        route = jnp.where(wanted == target, 1.0, 0.0).astype(bf16)
-        routes.append(route)
-        weights = jnp.concatenate(
-            tables[block] + [jnp.zeros((TILE - INFO * PER_TILE, items), f32)], axis=0
+    target = rows[0][PER_TILE:PER_TILE + 1, :].astype(jnp.int32)
+    route = jnp.where(wanted == target, 1.0, 0.0).astype(bf16)
+    weights = jnp.concatenate(rows + [jnp.zeros((TILE - INFO * PER_TILE, items), f32)], axis=0)
+
+    def store(spot, total):
+        for number, goal_ref in enumerate((mine_ref, other_ref)):
+            value = total[number * owned:(number + 1) * owned]
+            goal_ref[spot, :] = value + before[number][spot, :] if before else value
+
+    sums = 0.0
+    for half in split(weights):
+        sums = sums + lax.dot_general(
+            route, half, (((1,), (1,)), ((), ())), preferred_element_type=f32
         )
-        for half in split(weights):
-            term = lax.dot_general(route, half, over_items, preferred_element_type=f32)
-            sums = term if sums is None else sums + term
-    mine_ref[owned * PIECE:, :] = sums[:owned]
-    other_ref[owned * PIECE:, :] = sums[owned:]
+    store(pl.ds(owned * PIECE, owned), sums)
     for line in range(PIECE):
-        total = None
-        rows = pl.ds(line, TILES_BLK, PIECE)
-        for route, part_refs in zip(routes, (first_refs, (second_ref,))):
-            part = jnp.concatenate(
-                [part_ref[:, rows, :].reshape(-1, TILE) for part_ref in part_refs], axis=0
-            )
-            high, low = split(part)
-            term = jnp.dot(
-                route, jnp.concatenate([high, low], axis=1), preferred_element_type=f32
-            )
-            total = term if total is None else total + term
-        total = total[:, :TILE] + total[:, TILE:]
-        mine_ref[pl.ds(line, owned, PIECE), :] = total[:owned]
-        other_ref[pl.ds(line, owned, PIECE), :] = total[owned:]
+        part = jnp.concatenate(
+            [
+                part_ref[:, pl.ds(line, TILES_BLK, PIECE), :].reshape(items // 4, TILE)
+                for part_ref in part_refs
+            ],
+            axis=0,
+        )
+        high, low = split(part)
+        total = jnp.dot(route, jnp.concatenate([high, low], axis=1), preferred_element_type=f32)
+        store(pl.ds(line, owned, PIECE), total[:, :TILE] + total[:, TILE:])
 
 
 def spread_cells(sums, cell_row):
@@ -554,28 +544,28 @@
 
     same_core = [list(range(core, VISITS, 2)) for core in range(2)]
     operands = (place, exposures, variance, mask_planes, table, kernel_index, owner, tile_slot)
-    pieces = match_block(0, *operands)
-    own = pl.pallas_call(
-        keep_kernel,
-        out_shape=jax.ShapeDtypeStruct(pieces[0].shape, f32),
-        in_specs=[pl.BlockSpec(memory_space=pltpu.HBM)],
-        out_specs=vmem,
-        scratch_shapes=[pltpu.SemaphoreType.DMA],
-        compiler_params=params,
-        name="keep",
-    )(pieces[0])
-    parts = [part.reshape(4, -1, TILE) for part in exchange([own, *pieces[1:]])]
-    (pieces,) = match_block(1, *operands)
-    parts.append(spread_tiles(pieces.reshape(CHIPS, -1, TILE)))
-
-    mine, other = pl.pallas_call(
-        partial_kernel,
-        out_shape=[jax.ShapeDtypeStruct((owned * (PIECE + 1), TILE), f32)] * 2,
-        in_specs=[smem] + [vmem] * 5,
-        out_specs=[vmem, vmem],
-        compiler_params=params,
-        name="partial_sums",
-    )(place, *parts)
+    partial = ()
+    for block in range(exposures.shape[1]):
+        pieces = match_block(block, *operands)
+        own = pl.pallas_call(
+            keep_kernel,
+            out_shape=jax.ShapeDtypeStruct(pieces[0].shape, f32),
+            in_specs=[pl.BlockSpec(memory_space=pltpu.HBM)],
+            out_specs=vmem,
+            scratch_shapes=[pltpu.SemaphoreType.DMA],
+            compiler_params=params,
+            name="keep",
+        )(pieces[0])
+        parts = [part.reshape(4, -1, TILE) for part in exchange([own, *pieces[1:]])]
+        partial = pl.pallas_call(
+            functools.partial(partial_kernel, block=block),
+            out_shape=[jax.ShapeDtypeStruct((owned * (PIECE + 1), TILE), f32)] * 2,
+            in_specs=[smem] + [vmem] * (4 + len(partial)),
+            out_specs=[vmem, vmem],
+            compiler_params=params,
+            name="partial_sums",
+        )(place, *parts, *partial)
+    mine, other = partial
     other = lax.ppermute(other, "visit", [(device, device ^ 1) for device in range(VISITS)])
     pieces = pl.pallas_call(
         merge_kernel,

time: 88 us -> 86.9 us (0.988)
  waiting for transfers between devices: 26.6 us -> 19.2 us
  starting transfers between devices: 25.4 us -> 28.6 us
  blocking collectives: 16.7 us -> 19.1 us
    ppermute x6 -> x12, starting transfers between devices: 9.56 us -> 19.3 us  [exchange(): lax.ppermute(parts[way], 'visit', phase_partners(phase, way))]
    ppermute x6 -> x12, waiting for transfers between devices: 16.5 us -> 9.12 us  [exchange(): lax.ppermute(parts[way], 'visit', phase_partners(phase, way))]
    all_to_all x1 -> x0, starting transfers between devices: 7.13 us -> none  [spread_tiles(): lax.all_to_all(pieces, 'visit', 0, 0, axis_index_groups=same_core, tiled=...]
    all_to_all x1, blocking collectives: 16.7 us -> 19.1 us  [spread_tiles(): lax.all_to_all(pieces, 'visit', 0, 0, axis_index_groups=same_core, tiled=...]
  transfers between devices with their start and end apart: 12 -> 17, of which waited for: 9 -> 9; matrix products, arithmetic and copies ran while one was open for 0% -> 0% of each run, Pallas kernels for 9% -> 10%
where the time goes in v6:
time: 86.9 us; the launch traced here: 86.6 us
  starting transfers between devices  28.6 us (33%)
  waiting for transfers between devices  19.2 us (22%)
  blocking collectives  19.1 us (22%)
  Pallas kernels  17.9 us (21%)
  local copies, waits for them, and re-layouts  0.96 us (1%)
    ppermute x12, starting transfers between devices, exchange(): lax.ppermute(parts[way], 'visit', phase_partners(phase, way))  19.3 us
    all_to_all x1, blocking collectives, spread_tiles(): lax.all_to_all(pieces, 'visit', 0, 0, axis_index_groups=same_core, tiled=...  19.1 us
    pallas_call x2, Pallas kernels, match_block(): pl.pallas_call(functools.partial(match_kernel, block=block), out_shape=[j...  14 us
    ppermute x12, waiting for transfers between devices, exchange(): lax.ppermute(parts[way], 'visit', phase_partners(phase, way))  9.12 us
    ppermute x2, waiting for transfers between devices, local(): terms.extend((half, lax.ppermute(half, 'band', pairings[1 - number])))  5.53 us
    ppermute x2, starting transfers between devices, local(): lax.ppermute(half, 'band', pairings[number])  4.52 us
    ppermute x2, starting transfers between devices, local(): terms.extend((half, lax.ppermute(half, 'band', pairings[1 - number])))  4.03 us
    ppermute x2, waiting for transfers between devices, local(): lax.ppermute(half, 'band', pairings[number])  2.9 us
  transfers between devices with their start and end apart: 17, of which 9 were waited for; matrix products, arithmetic and copies ran while one was open for 0% of the time, Pallas kernels for 10%

profile of v6, /device:TPU:0, one launch (start us, length us, event | category | flops | bytes accessed | tf_op | source)
XLA Modules:
  0.0 86.6 jit_solution(2073445605761432663)
XLA Ops:
  0.6 7.0 %match_block.3 = (f32[4,17,8,128]{3,2,1,0:T(8,128)}, f32[4,17,8,128]{3,2,1,0:T(8,128)}, f32[4,17,8,128]{3,2,1,0:T(8,128)}, f32[4,17,8,128]{3,2,1,0:T(8,128)}) custom-call(s32[1]{0:T(128)} %bitcast.place_ref, s32[1,2]{1,0:T(1,128)} %index_hbm.3, f32[27,64]{1,0:T(8,128)} %bitcast.23, f32[1,2,552,552]{3,2,1,0:T(8,128)} %image_hbm.3, f32[1,2,16,16]{3,2,1,0:T(8,128)} %var_hbm.3, ...), custom_call_target="tpu_custom_call" | custom-call | flops 5242880000 | bytes 3145728 | tf_op jit(solution)/shard_map/match_block/pallas_call | solution.py:358
  7.7 2.7 %collective-permute-start.6 = (f32[4,17,8,128]{3,2,1,0:T(8,128)}, f32[4,17,8,128]{3,2,1,0:T(8,128)S(1)}, u32[]{:S(2)}, u32[]{:S(2)}) collective-permute-start(f32[4,17,8,128]{3,2,1,0:T(8,128)} %get-tuple-element.33), channel_id=1, source_target_pairs={{0,40},{4,124},{8,32},{12,116},{16,56},{20,108},{24,48},{28,100},{... | collective-permute-start | bytes 835592 | tf_op jit(solution)/shard_map/ppermute | solution.py:526
  10.4 0.5 collective-permute-start.7
  10.9 0.4 collective-permute-start.8
  11.3 7.0 %match_block.2 = (f32[4,17,8,128]{3,2,1,0:T(8,128)}, f32[4,17,8,128]{3,2,1,0:T(8,128)}, f32[4,17,8,128]{3,2,1,0:T(8,128)}, f32[4,17,8,128]{3,2,1,0:T(8,128)}) custom-call(s32[1]{0:T(128)} %bitcast.place_ref, s32[1,2]{1,0:T(1,128)} %index_hbm.3, f32[27,64]{1,0:T(8,128)} %bitcast.24, f32[1,2,552,552]{3,2,1,0:T(8,128)} %image_hbm.3, f32[1,2,16,16]{3,2,1,0:T(8,128)} %var_hbm.3, ...), custom_call_target="tpu_custom_call" | custom-call | flops 5242880000 | bytes 3145728 | tf_op jit(solution)/shard_map/match_block/pallas_call | solution.py:358
  18.2 2.7 %collective-permute-start = (f32[4,17,8,128]{3,2,1,0:T(8,128)}, f32[4,17,8,128]{3,2,1,0:T(8,128)S(1)}, u32[]{:S(2)}, u32[]{:S(2)}) collective-permute-start(f32[4,17,8,128]{3,2,1,0:T(8,128)} %get-tuple-element.25), channel_id=1, source_target_pairs={{0,40},{4,124},{8,32},{12,116},{16,56},{20,108},{24,48},{28,100},{... | collective-permute-start | bytes 835592 | tf_op jit(solution)/shard_map/ppermute | solution.py:526
  20.9 0.5 collective-permute-start.1
  21.4 0.4 collective-permute-start.2
  22.0 5.4 %collective-permute-start.9 = (f32[4,17,8,128]{3,2,1,0:T(8,128)S(1)}, f32[4,17,8,128]{3,2,1,0:T(8,128)S(1)}, u32[]{:S(2)}, u32[]{:S(2)}) collective-permute-start(f32[4,17,8,128]{3,2,1,0:T(8,128)S(1)} %get-tuple-element.37), channel_id=1, source_target_pairs={{0,120},{4,44},{8,112},{12,36},{16,104},{20,60},{24,96},{28,52},{3... | collective-permute-start | bytes 835592 | tf_op jit(solution)/shard_map/ppermute | solution.py:526
  27.3 1.0 %copy-done = f32[4,17,8,128]{3,2,1,0:T(8,128)S(1)} copy-done((f32[4,17,8,128]{3,2,1,0:T(8,128)S(1)}, f32[4,17,8,128]{3,2,1,0:T(8,128)}, u32[]{:S(2)}) %copy-start) | copy-done | bytes 278552
  28.4 0.6 collective-permute-start.10
  29.2 2.8 %collective-permute-done.1.refs_2_ = f32[4,17,8,128]{3,2,1,0:T(8,128)S(1)} collective-permute-done((f32[4,17,8,128]{3,2,1,0:T(8,128)}, f32[4,17,8,128]{3,2,1,0:T(8,128)S(1)}, u32[]{:S(2)}, u32[]{:S(2)}) %collective-permute-start.1) | collective-permute-done | bytes 278560 | tf_op jit(solution)/shard_map/ppermute | solution.py:526
  32.1 4.4 %collective-permute-start.3 = (f32[4,17,8,128]{3,2,1,0:T(8,128)S(1)}, f32[4,17,8,128]{3,2,1,0:T(8,128)S(1)}, u32[]{:S(2)}, u32[]{:S(2)}) collective-permute-start(f32[4,17,8,128]{3,2,1,0:T(8,128)S(1)} %get-tuple-element.29), channel_id=1, source_target_pairs={{0,120},{4,44},{8,112},{12,36},{16,104},{20,60},{24,96},{28,52},{3... | collective-permute-start | bytes 835592 | tf_op jit(solution)/shard_map/ppermute | solution.py:526
  36.5 0.5 collective-permute-start.4
  36.9 1.1 %collective-permute-start.5 = (f32[4,17,8,128]{3,2,1,0:T(8,128)S(1)}, f32[4,17,8,128]{3,2,1,0:T(8,128)S(1)}, u32[]{:S(2)}, u32[]{:S(2)}) collective-permute-start(f32[4,17,8,128]{3,2,1,0:T(8,128)S(1)} %get-tuple-element.31), channel_id=1, source_target_pairs={{0,96},{4,36},{8,104},{12,44},{16,112},{20,52},{24,120},{28,60},{3... | collective-permute-start | bytes 835592 | tf_op jit(solution)/shard_map/ppermute | solution.py:526
  38.2 0.6 partial_sums.2
  38.9 3.2 %collective-permute-done.3 = f32[4,17,8,128]{3,2,1,0:T(8,128)S(1)} collective-permute-done((f32[4,17,8,128]{3,2,1,0:T(8,128)S(1)}, f32[4,17,8,128]{3,2,1,0:T(8,128)S(1)}, u32[]{:S(2)}, u32[]{:S(2)}) %collective-permute-start.3) | collective-permute-done | bytes 278560 | tf_op jit(solution)/shard_map/ppermute | solution.py:526
  42.1 2.4 %collective-permute-done.4 = f32[4,17,8,128]{3,2,1,0:T(8,128)S(1)} collective-permute-done((f32[4,17,8,128]{3,2,1,0:T(8,128)S(1)}, f32[4,17,8,128]{3,2,1,0:T(8,128)S(1)}, u32[]{:S(2)}, u32[]{:S(2)}) %collective-permute-start.4) | collective-permute-done | bytes 278560 | tf_op jit(solution)/shard_map/ppermute | solution.py:526
  44.5 0.6 collective-permute-done.5
  45.0 0.7 partial_sums.3
  45.8 0.8 collective-permute-start.12
  46.5 1.6 %collective-permute-done.12.other_ref = f32[1152,128]{1,0:T(8,128)S(1)} collective-permute-done((f32[1152,128]{1,0:T(8,128)S(1)}, f32[1152,128]{1,0:T(8,128)S(1)}, u32[]{:S(2)}, u32[]{:S(2)}) %collective-permute-start.12) | collective-permute-done | bytes 589856 | tf_op jit(solution)/shard_map/ppermute | solution.py:569
  48.4 19.1 %all_to_all.5.part_ref = f32[16,64,128]{2,1,0:T(8,128)S(1)} all-to-all(f32[16,64,128]{2,1,0:T(8,128)S(1)} %bitcast.13), channel_id=1, replica_groups={{0,8,16,24,32,40,48,56,64,72,80,88,96,104,112,120},{4,12,20,28,36,44,52..., dimensions={0} | all-to-all | bytes 1048576 | tf_op jit(solution)/shard_map/all_to_all | solution.py:543
  67.5 0.3 chi.1
  67.9 2.0 %collective-permute-start.13 = (f32[8,64,128]{2,1,0:T(8,128)S(1)}, f32[8,64,128]{2,1,0:T(8,128)S(1)}, u32[]{:S(2)}, u32[]{:S(2)}) collective-permute-start(f32[8,64,128]{2,1,0:T(8,128)S(1)} %get-tuple-element.44), channel_id=1, source_target_pairs={{0,1},{1,0},{2,3},{3,2},{4,5},{5,4},{6,7},{7,6},{8,9},{9,8},{10,11... | collective-permute-start | bytes 786440 | tf_op jit(solution)/shard_map/ppermute | solution.py:599
  69.9 2.5 %collective-permute-start.15 = (f32[8,64,128]{2,1,0:T(8,128)S(1)}, f32[8,64,128]{2,1,0:T(8,128)S(1)}, u32[]{:S(2)}, u32[]{:S(2)}) collective-permute-start(f32[8,64,128]{2,1,0:T(8,128)S(1)} %get-tuple-element.45), channel_id=1, source_target_pairs={{0,3},{3,0},{1,2},{2,1},{4,7},{7,4},{5,6},{6,5},{8,11},{11,8},{9,1... | collective-permute-start | bytes 786440 | tf_op jit(solution)/shard_map/ppermute | solution.py:599
  72.4 2.9 %collective-permute-done.13 = f32[8,64,128]{2,1,0:T(8,128)S(1)} collective-permute-done((f32[8,64,128]{2,1,0:T(8,128)S(1)}, f32[8,64,128]{2,1,0:T(8,128)S(1)}, u32[]{:S(2)}, u32[]{:S(2)}) %collective-permute-start.13) | collective-permute-done | bytes 262176 | tf_op jit(solution)/shard_map/ppermute | solution.py:599
  75.3 3.9 %collective-permute-start.14 = (f32[8,64,128]{2,1,0:T(8,128)S(1)}, f32[8,64,128]{2,1,0:T(8,128)S(1)}, u32[]{:S(2)}, u32[]{:S(2)}) collective-permute-start(f32[8,64,128]{2,1,0:T(8,128)S(1)} %add.6.upper_ref), channel_id=1, source_target_pairs={{0,3},{3,0},{1,2},{2,1},{4,7},{7,4},{5,6},{6,5},{8,11},{11,8},{9,1... | collective-permute-start | bytes 786440 | tf_op jit(solution)/shard_map/ppermute | solution.py:603
  79.4 0.8 image.1
  80.2 3.5 %collective-permute-done.14.more_upper_ref = f32[8,64,128]{2,1,0:T(8,128)S(1)} collective-permute-done((f32[8,64,128]{2,1,0:T(8,128)S(1)}, f32[8,64,128]{2,1,0:T(8,128)S(1)}, u32[]{:S(2)}, u32[]{:S(2)}) %collective-permute-start.14) | collective-permute-done | bytes 262176 | tf_op jit(solution)/shard_map/ppermute | solution.py:603
  83.8 2.0 %collective-permute-done.16.more_lower_ref = f32[8,64,128]{2,1,0:T(8,128)S(1)} collective-permute-done((f32[8,64,128]{2,1,0:T(8,128)S(1)}, f32[8,64,128]{2,1,0:T(8,128)S(1)}, u32[]{:S(2)}, u32[]{:S(2)}) %collective-permute-start.16) | collective-permute-done | bytes 262176 | tf_op jit(solution)/shard_map/ppermute | solution.py:603
  85.8 0.9 detection.1
  (21 shorter events, 1.1 us)
Async XLA Ops:
  7.7 13.8 %collective-permute-start.6 = (f32[4,17,8,128]{3,2,1,0:T(8,128)}, f32[4,17,8,128]{3,2,1,0:T(8,128)S(1)}, u32[]{:S(2)}, u32[]{:S(2)}) collective-permute-start(f32[4,17,8,128]{3,2,1,0:T(8,128)} %get-tuple-element.33), channel_id=1, source_target_pairs={{0,40},{4,124},{8,32},{12,116},{16,56},{20,108},{24,48},{28,100},{... | collective-permute-start | bytes 835592 | tf_op jit(solution)/shard_map/ppermute | solution.py:526
  10.4 11.5 %collective-permute-start.7 = (f32[4,17,8,128]{3,2,1,0:T(8,128)}, f32[4,17,8,128]{3,2,1,0:T(8,128)S(1)}, u32[]{:S(2)}, u32[]{:S(2)}) collective-permute-start(f32[4,17,8,128]{3,2,1,0:T(8,128)} %get-tuple-element.34), channel_id=1, source_target_pairs={{0,8},{4,28},{8,0},{12,20},{16,24},{20,12},{24,16},{28,4},{32,40},... | collective-permute-start | bytes 835592 | tf_op jit(solution)/shard_map/ppermute | solution.py:526
  10.9 10.9 %copy-start.1 = (f32[4,17,8,128]{3,2,1,0:T(8,128)S(1)}, f32[4,17,8,128]{3,2,1,0:T(8,128)}, u32[]{:S(2)}) copy-start(f32[4,17,8,128]{3,2,1,0:T(8,128)} %get-tuple-element.32.part_hbm) | copy-start | bytes 835588
  10.9 11.0 %collective-permute-start.8 = (f32[4,17,8,128]{3,2,1,0:T(8,128)}, f32[4,17,8,128]{3,2,1,0:T(8,128)S(1)}, u32[]{:S(2)}, u32[]{:S(2)}) collective-permute-start(f32[4,17,8,128]{3,2,1,0:T(8,128)} %get-tuple-element.35), channel_id=1, source_target_pairs={{0,32},{4,100},{8,40},{12,108},{16,48},{20,116},{24,56},{28,124},{... | collective-permute-start | bytes 835592 | tf_op jit(solution)/shard_map/ppermute | solution.py:526
  18.2 10.7 %collective-permute-start = (f32[4,17,8,128]{3,2,1,0:T(8,128)}, f32[4,17,8,128]{3,2,1,0:T(8,128)S(1)}, u32[]{:S(2)}, u32[]{:S(2)}) collective-permute-start(f32[4,17,8,128]{3,2,1,0:T(8,128)} %get-tuple-element.25), channel_id=1, source_target_pairs={{0,40},{4,124},{8,32},{12,116},{16,56},{20,108},{24,48},{28,100},{... | collective-permute-start | bytes 835592 | tf_op jit(solution)/shard_map/ppermute | solution.py:526
  20.9 11.1 %collective-permute-start.1 = (f32[4,17,8,128]{3,2,1,0:T(8,128)}, f32[4,17,8,128]{3,2,1,0:T(8,128)S(1)}, u32[]{:S(2)}, u32[]{:S(2)}) collective-permute-start(f32[4,17,8,128]{3,2,1,0:T(8,128)} %get-tuple-element.26), channel_id=1, source_target_pairs={{0,8},{4,28},{8,0},{12,20},{16,24},{20,12},{24,16},{28,4},{32,40},... | collective-permute-start | bytes 835592 | tf_op jit(solution)/shard_map/ppermute | solution.py:526
  21.4 10.6 %collective-permute-start.2 = (f32[4,17,8,128]{3,2,1,0:T(8,128)}, f32[4,17,8,128]{3,2,1,0:T(8,128)S(1)}, u32[]{:S(2)}, u32[]{:S(2)}) collective-permute-start(f32[4,17,8,128]{3,2,1,0:T(8,128)} %get-tuple-element.27), channel_id=1, source_target_pairs={{0,32},{4,100},{8,40},{12,108},{16,48},{20,116},{24,56},{28,124},{... | collective-permute-start | bytes 835592 | tf_op jit(solution)/shard_map/ppermute | solution.py:526
  22.0 15.0 %collective-permute-start.9 = (f32[4,17,8,128]{3,2,1,0:T(8,128)S(1)}, f32[4,17,8,128]{3,2,1,0:T(8,128)S(1)}, u32[]{:S(2)}, u32[]{:S(2)}) collective-permute-start(f32[4,17,8,128]{3,2,1,0:T(8,128)S(1)} %get-tuple-element.37), channel_id=1, source_target_pairs={{0,120},{4,44},{8,112},{12,36},{16,104},{20,60},{24,96},{28,52},{3... | collective-permute-start | bytes 835592 | tf_op jit(solution)/shard_map/ppermute | solution.py:526
  27.3 1.0 %copy-start = (f32[4,17,8,128]{3,2,1,0:T(8,128)S(1)}, f32[4,17,8,128]{3,2,1,0:T(8,128)}, u32[]{:S(2)}) copy-start(f32[4,17,8,128]{3,2,1,0:T(8,128)} %get-tuple-element.24.part_hbm) | copy-start | bytes 835588
  28.4 9.9 %collective-permute-start.10 = (f32[4,17,8,128]{3,2,1,0:T(8,128)S(1)}, f32[4,17,8,128]{3,2,1,0:T(8,128)S(1)}, u32[]{:S(2)}, u32[]{:S(2)}) collective-permute-start(f32[4,17,8,128]{3,2,1,0:T(8,128)S(1)} %get-tuple-element.38), channel_id=1, source_target_pairs={{0,24},{4,12},{8,16},{12,4},{16,8},{20,28},{24,0},{28,20},{32,56},... | collective-permute-start | bytes 835592 | tf_op jit(solution)/shard_map/ppermute | solution.py:526
  28.9 9.3 %collective-permute-start.11 = (f32[4,17,8,128]{3,2,1,0:T(8,128)S(1)}, f32[4,17,8,128]{3,2,1,0:T(8,128)S(1)}, u32[]{:S(2)}, u32[]{:S(2)}) collective-permute-start(f32[4,17,8,128]{3,2,1,0:T(8,128)S(1)} %get-tuple-element.39), channel_id=1, source_target_pairs={{0,96},{4,36},{8,104},{12,44},{16,112},{20,52},{24,120},{28,60},{3... | collective-permute-start | bytes 835592 | tf_op jit(solution)/shard_map/ppermute | solution.py:526
  32.1 10.0 %collective-permute-start.3 = (f32[4,17,8,128]{3,2,1,0:T(8,128)S(1)}, f32[4,17,8,128]{3,2,1,0:T(8,128)S(1)}, u32[]{:S(2)}, u32[]{:S(2)}) collective-permute-start(f32[4,17,8,128]{3,2,1,0:T(8,128)S(1)} %get-tuple-element.29), channel_id=1, source_target_pairs={{0,120},{4,44},{8,112},{12,36},{16,104},{20,60},{24,96},{28,52},{3... | collective-permute-start | bytes 835592 | tf_op jit(solution)/shard_map/ppermute | solution.py:526
  36.5 8.0 %collective-permute-start.4 = (f32[4,17,8,128]{3,2,1,0:T(8,128)S(1)}, f32[4,17,8,128]{3,2,1,0:T(8,128)S(1)}, u32[]{:S(2)}, u32[]{:S(2)}) collective-permute-start(f32[4,17,8,128]{3,2,1,0:T(8,128)S(1)} %get-tuple-element.30), channel_id=1, source_target_pairs={{0,24},{4,12},{8,16},{12,4},{16,8},{20,28},{24,0},{28,20},{32,56},... | collective-permute-start | bytes 835592 | tf_op jit(solution)/shard_map/ppermute | solution.py:526
  36.9 8.1 %collective-permute-start.5 = (f32[4,17,8,128]{3,2,1,0:T(8,128)S(1)}, f32[4,17,8,128]{3,2,1,0:T(8,128)S(1)}, u32[]{:S(2)}, u32[]{:S(2)}) collective-permute-start(f32[4,17,8,128]{3,2,1,0:T(8,128)S(1)} %get-tuple-element.31), channel_id=1, source_target_pairs={{0,96},{4,36},{8,104},{12,44},{16,112},{20,52},{24,120},{28,60},{3... | collective-permute-start | bytes 835592 | tf_op jit(solution)/shard_map/ppermute | solution.py:526
  45.8 2.4 %collective-permute-start.12 = (f32[1152,128]{1,0:T(8,128)S(1)}, f32[1152,128]{1,0:T(8,128)S(1)}, u32[]{:S(2)}, u32[]{:S(2)}) collective-permute-start(f32[1152,128]{1,0:T(8,128)S(1)} %get-tuple-element.43), channel_id=1, source_target_pairs={{0,4},{4,0},{8,12},{12,8},{16,20},{20,16},{24,28},{28,24},{32,36},... | collective-permute-start | bytes 1769480 | tf_op jit(solution)/shard_map/ppermute | solution.py:569
  67.9 7.4 %collective-permute-start.13 = (f32[8,64,128]{2,1,0:T(8,128)S(1)}, f32[8,64,128]{2,1,0:T(8,128)S(1)}, u32[]{:S(2)}, u32[]{:S(2)}) collective-permute-start(f32[8,64,128]{2,1,0:T(8,128)S(1)} %get-tuple-element.44), channel_id=1, source_target_pairs={{0,1},{1,0},{2,3},{3,2},{4,5},{5,4},{6,7},{7,6},{8,9},{9,8},{10,11... | collective-permute-start | bytes 786440 | tf_op jit(solution)/shard_map/ppermute | solution.py:599
  69.9 9.4 %collective-permute-start.15 = (f32[8,64,128]{2,1,0:T(8,128)S(1)}, f32[8,64,128]{2,1,0:T(8,128)S(1)}, u32[]{:S(2)}, u32[]{:S(2)}) collective-permute-start(f32[8,64,128]{2,1,0:T(8,128)S(1)} %get-tuple-element.45), channel_id=1, source_target_pairs={{0,3},{3,0},{1,2},{2,1},{4,7},{7,4},{5,6},{6,5},{8,11},{11,8},{9,1... | collective-permute-start | bytes 786440 | tf_op jit(solution)/shard_map/ppermute | solution.py:599
  75.3 8.4 %collective-permute-start.14 = (f32[8,64,128]{2,1,0:T(8,128)S(1)}, f32[8,64,128]{2,1,0:T(8,128)S(1)}, u32[]{:S(2)}, u32[]{:S(2)}) collective-permute-start(f32[8,64,128]{2,1,0:T(8,128)S(1)} %add.6.upper_ref), channel_id=1, source_target_pairs={{0,3},{3,0},{1,2},{2,1},{4,7},{7,4},{5,6},{6,5},{8,11},{11,8},{9,1... | collective-permute-start | bytes 786440 | tf_op jit(solution)/shard_map/ppermute | solution.py:603
  79.3 6.5 %collective-permute-start.16 = (f32[8,64,128]{2,1,0:T(8,128)S(1)}, f32[8,64,128]{2,1,0:T(8,128)S(1)}, u32[]{:S(2)}, u32[]{:S(2)}) collective-permute-start(f32[8,64,128]{2,1,0:T(8,128)S(1)} %add.7.lower_ref), channel_id=1, source_target_pairs={{0,1},{1,0},{2,3},{3,2},{4,5},{5,4},{6,7},{7,6},{8,9},{9,8},{10,11... | collective-permute-start | bytes 786440 | tf_op jit(solution)/shard_map/ppermute | solution.py:603

commit v7 on v6

--- a/solution.py
+++ b/solution.py
@@ -14,7 +14,6 @@
 KSIZE = 41
 OWN_DEV = 8
 PADDED = BLOCK + KSIZE - 1
-WIDE = 640
 NFILT = 11
 VISITS = 32
 SIDE = BLOCK // TILE
@@ -28,6 +27,9 @@
 HALF = SPAN // 2
 TALL = 560
 TAPS = 48
+WIDTH = 256
+KEPT = 176
+WINDOWS = 3
 
 width_fractions = (0.075, 0.15, 0.3)
 family_degrees = (4, 2, 2)
@@ -44,24 +46,28 @@
     return high, low
 
 
+def waves(length):
+    angle = 2 * np.pi * (np.arange(length // 2) + 0.5) / length
+    phase = angle[:, None] * np.arange(length)
+    return np.cos(phase), np.sin(phase)
+
+
 def transforms():
+    cosine, sine = waves(WIDTH)
+    by_lane = np.concatenate([cosine, sine], axis=0)
+    back_across = np.zeros((WIDTH, WIDTH))
+    back_across[:, :KEPT] = by_lane[:, :KEPT] * (2 / WIDTH)
+    along = np.zeros((TILE, WIDTH), np.float32)
+    along[:KSIZE] = np.concatenate([cosine, -sine], axis=0)[:, :KSIZE].T
+
+    cosine, sine = waves(SPAN)
     number = np.arange(HALF)
-    angle = 2 * np.pi * (number + 0.5) / SPAN
-    taps = np.arange(SPAN)
-    cosine, sine = np.cos(angle[:, None] * taps), np.sin(angle[:, None] * taps)
     spot = 8 * (number // 4) + number % 4
-
     by_row = np.zeros((SPAN, SPAN))
     by_row[spot], by_row[spot + 4] = cosine, sine
-    by_lane = np.zeros((2 * TILE, SPAN))
-    by_lane[:HALF], by_lane[TILE:TILE + HALF] = cosine, sine
-
-    across = np.zeros((2 * TILE, 2 * TILE))
-    across[:SPAN] = by_lane.T
     down = np.zeros((SPAN + 8, SPAN))
     down[:SPAN] = by_row
     back_down = by_row.T[:TILE] * (2 / SPAN)
-    back_across = by_lane[:, :TILE] * (2 / SPAN)
 
     def three(matrix, width=512):
         high, low = as_halves(matrix)
@@ -72,13 +78,11 @@
     cross = np.zeros((SPAN + 8, TAPS))
     same[spot, :KSIZE] = same[spot + 4, :KSIZE] = cosine[:, :KSIZE]
     cross[spot, :KSIZE], cross[spot + 4, :KSIZE] = sine[:, :KSIZE], -sine[:, :KSIZE]
-    along = np.zeros((TILE, 2 * TILE), np.float32)
-    along[:KSIZE, :HALF], along[:KSIZE, TILE:TILE + HALF] = cosine[:, :KSIZE].T, -sine[:, :KSIZE].T
     return (
-        np.concatenate(as_halves(across), axis=0),
+        np.concatenate(as_halves(by_lane.T), axis=0),
         three(down),
         three(back_down),
-        np.concatenate(as_halves(back_across), axis=1),
+        np.concatenate(as_halves(back_across), axis=0),
         np.concatenate([three(same, 256), three(cross, 256)], axis=0),
         along,
     )
@@ -224,7 +228,7 @@
         index_ref, table_ref, image_ref, var_ref, bits_ref, owner_ref, slot_ref,
         across_ref, down_ref, back_down_ref, back_across_ref, down_taps_ref, along_ref, sems,
         out_sems, tail_ref, high_ref, low_ref, wave_ref, stack_ref, turn_ref, result_ref, rows_ref,
-        factor_ref, weight_ref, out_ref,
+        matched_ref, factor_ref, weight_ref, out_ref,
     ) = rest[count:]
     copies = [
         pltpu.make_async_copy(source, goal, sems.at[number])
@@ -257,24 +261,37 @@
 
     pair = 2 * TILE
     forward = jnp.concatenate([across_ref[:pair], across_ref[...]], axis=0)
-    backward = jnp.concatenate([back_across_ref[...], back_across_ref[...]], axis=0)
+    backward = jnp.concatenate([back_across_ref[:pair], back_across_ref[...]], axis=0)
     spots = [way_to(place_ref[0], piece) for piece in range(CHIPS)]
+
+    def windows(rows):
+        tiles = [image_ref[rows, place:place + TILE] for place in range(0, BLOCK, TILE)]
+        tiles.append(tail_ref[rows, :])
+        lane = lax.broadcasted_iota(jnp.int32, tiles[0].shape, 1)
+        second = [pltpu.roll(tile, 80, 1) for tile in tiles[1:4]]
+        third = [pltpu.roll(tile, 32, 1) for tile in tiles[2:5]]
+        return (
+            tiles[:2],
+            [jnp.where(lane < 80, second[spot], second[spot + 1]) for spot in range(2)],
+            [jnp.where(lane < 32, third[spot], third[spot + 1]) for spot in range(2)],
+        )
 
     def halve():
         tail_ref[:PADDED, :PADDED - BLOCK] = image_ref[:, BLOCK:]
         whole = TALL - 16
-        for first, width, source in ((0, BLOCK, image_ref), (BLOCK, TILE, tail_ref)):
-            lanes = slice(first, first + width)
-            high_ref[:whole, lanes], low_ref[:whole, lanes] = split(source[:whole, :width])
-            last = jnp.concatenate(
-                [source[whole:PADDED, :width], jnp.zeros((8, width), f32)], axis=0
-            )
-            high_ref[whole:, lanes], low_ref[whole:, lanes] = split(last)
-
-    def transform_across(column):
-        lanes = slice(column * TILE, column * TILE + pair)
-        high, low = high_ref[:, lanes], low_ref[:, lanes]
-        wave_ref[column] = jnp.dot(
+        for window, tiles in enumerate(windows(slice(0, whole))):
+            for spot, tile in enumerate(tiles):
+                lanes = slice(spot * TILE, (spot + 1) * TILE)
+                high_ref[window, :whole, lanes], low_ref[window, :whole, lanes] = split(tile)
+        for window, tiles in enumerate(windows(slice(whole, PADDED))):
+            for spot, tile in enumerate(tiles):
+                lanes = slice(spot * TILE, (spot + 1) * TILE)
+                last = jnp.concatenate([tile, jnp.zeros((8, TILE), f32)], axis=0)
+                high_ref[window, whole:, lanes], low_ref[window, whole:, lanes] = split(last)
+
+    def transform_across(window):
+        high, low = high_ref[window], low_ref[window]
+        wave_ref[window] = jnp.dot(
             jnp.concatenate([high, low, high], axis=1), forward, preferred_element_type=f32
         )
 
@@ -315,9 +332,34 @@
         rows_ref[column, line * TILE:(line + 1) * TILE, :pair] = high
         rows_ref[column, line * TILE:(line + 1) * TILE, pair:] = low
 
-    def back_across(column):
-        matched = jnp.dot(rows_ref[column], backward, preferred_element_type=f32)
-        matched = matched[:, :TILE] + matched[:, TILE:]
+    def back_across(window):
+        high, low = rows_ref[window, :, :pair], rows_ref[window, :, pair:]
+        matched_ref[window] = jnp.dot(
+            jnp.concatenate([high, low, high], axis=1), backward, preferred_element_type=f32
+        )
+        if window == 1:
+            finish(0)
+            finish(1)
+        if window == 2:
+            finish(2)
+            finish(3)
+
+    def finish(column):
+        lane = lax.broadcasted_iota(jnp.int32, (BLOCK, TILE), 1)
+
+        def part(window, spot, shift):
+            value = matched_ref[window, :, spot * TILE:(spot + 1) * TILE]
+            return pltpu.roll(value, shift, 1) if shift else value
+
+        if column == 0:
+            matched = part(0, 0, 0)
+        elif column == 1:
+            matched = jnp.where(lane < 48, part(0, 1, 0), part(1, 0, 48))
+        elif column == 2:
+            matched = jnp.where(lane < 96, part(1, 1, 48), part(2, 0, 96))
+            matched = jnp.where(lane < 48, part(1, 0, 48), matched)
+        else:
+            matched = jnp.where(lane < 96, part(2, 0, 96), part(2, 1, 96))
         weight = weight_ref[:, column * TILE:(column + 1) * TILE]
         weighted = matched.reshape(CELLS, CELL, TILE) * weight[:, None, :]
         weighted = weighted.reshape(SIDE, CHIPS, PIECE, TILE)
@@ -329,14 +371,15 @@
     halve()
     transform_across(0)
     prepare()
-    for step in range(TILES_BLK + 5):
-        if step % SIDE == 0 and step // SIDE + 1 < SIDE:
+    tiles = WINDOWS * SIDE
+    for step in range(tiles + 5):
+        if step % SIDE == 0 and step // SIDE + 1 < WINDOWS:
             transform_across(step // SIDE + 1)
         for delay, stage in enumerate((stack, transform_down, multiply, back_down)):
-            if 0 <= step - delay < TILES_BLK:
+            if 0 <= step - delay < tiles:
                 stage(step - delay)
         column, rest = divmod(step - 4, SIDE)
-        if rest == SIDE - 1 and 0 <= column < SIDE:
+        if rest == SIDE - 1 and 0 <= column < WINDOWS:
             back_across(column)
     each = CHIPS // count
     sends = [
@@ -373,13 +416,14 @@
             pltpu.SemaphoreType.DMA((7 + len(matrices),)),
             pltpu.SemaphoreType.DMA((4,)),
             pltpu.VMEM((TALL, TILE), f32),
-            pltpu.VMEM((TALL, WIDE), bf16),
-            pltpu.VMEM((TALL, WIDE), bf16),
-            pltpu.VMEM((SIDE, TALL, 2 * TILE), f32),
-            pltpu.VMEM((TILES_BLK, 2 * SPAN, 2 * TILE), bf16),
-            pltpu.VMEM((TILES_BLK, SPAN + 8, 2 * TILE), f32),
-            pltpu.VMEM((TILES_BLK, 2 * SPAN, 2 * TILE), bf16),
-            pltpu.VMEM((SIDE, BLOCK, 4 * TILE), bf16),
+            pltpu.VMEM((WINDOWS, TALL, WIDTH), bf16),
+            pltpu.VMEM((WINDOWS, TALL, WIDTH), bf16),
+            pltpu.VMEM((WINDOWS, TALL, WIDTH), f32),
+            pltpu.VMEM((WINDOWS * SIDE, 2 * SPAN, WIDTH), bf16),
+            pltpu.VMEM((WINDOWS * SIDE, SPAN + 8, WIDTH), f32),
+            pltpu.VMEM((WINDOWS * SIDE, 2 * SPAN, WIDTH), bf16),
+            pltpu.VMEM((WINDOWS, BLOCK, 2 * WIDTH), bf16),
+            pltpu.VMEM((WINDOWS, BLOCK, WIDTH), f32),
             pltpu.VMEM((2, SPAN // 8, 8, 2 * TILE), f32),
             pltpu.VMEM((CELLS, BLOCK), f32),
             pltpu.VMEM((CHIPS, groups, PIECE, TILE), f32),

time: 86.9 us -> 86.3 us (level)
  no operation moved by 1% of the time
where the time goes in v7:
time: 86.3 us; the launch traced here: 86 us
  starting transfers between devices  28.6 us (33%)
  waiting for transfers between devices  19.1 us (22%)
  blocking collectives  19.1 us (22%)
  Pallas kernels  17.4 us (20%)
  local copies, waits for them, and re-layouts  0.96 us (1%)
    ppermute x12, starting transfers between devices, exchange(): lax.ppermute(parts[way], 'visit', phase_partners(phase, way))  19.3 us
    all_to_all x1, blocking collectives, spread_tiles(): lax.all_to_all(pieces, 'visit', 0, 0, axis_index_groups=same_core, tiled=...  19.1 us
    pallas_call x2, Pallas kernels, match_block(): pl.pallas_call(functools.partial(match_kernel, block=block), out_shape=[j...  13.5 us
    ppermute x12, waiting for transfers between devices, exchange(): lax.ppermute(parts[way], 'visit', phase_partners(phase, way))  9.14 us
    ppermute x2, waiting for transfers between devices, local(): terms.extend((half, lax.ppermute(half, 'band', pairings[1 - number])))  5.53 us
    ppermute x2, starting transfers between devices, local(): lax.ppermute(half, 'band', pairings[number])  4.62 us
    ppermute x2, starting transfers between devices, local(): terms.extend((half, lax.ppermute(half, 'band', pairings[1 - number])))  4.01 us
    ppermute x2, waiting for transfers between devices, local(): lax.ppermute(half, 'band', pairings[number])  2.81 us
  transfers between devices with their start and end apart: 17, of which 9 were waited for; matrix products, arithmetic and copies ran while one was open for 0% of the time, Pallas kernels for 10%

profile of v7, /device:TPU:0, one launch (start us, length us, event | category | flops | bytes accessed | tf_op | source)
XLA Modules:
  0.0 86.0 jit_solution(16078703833519906776)
XLA Ops:
  0.6 6.8 %match_block.3 = (f32[4,17,8,128]{3,2,1,0:T(8,128)}, f32[4,17,8,128]{3,2,1,0:T(8,128)}, f32[4,17,8,128]{3,2,1,0:T(8,128)}, f32[4,17,8,128]{3,2,1,0:T(8,128)}) custom-call(s32[1]{0:T(128)} %bitcast.place_ref, s32[1,2]{1,0:T(1,128)} %index_hbm.3, f32[27,64]{1,0:T(8,128)} %bitcast.23, f32[1,2,552,552]{3,2,1,0:T(8,128)} %image_hbm.3, f32[1,2,16,16]{3,2,1,0:T(8,128)} %var_hbm.3, ...), custom_call_target="tpu_custom_call" | custom-call | flops 5242880000 | bytes 3145728 | tf_op jit(solution)/shard_map/match_block/pallas_call | solution.py:401
  7.4 2.7 %collective-permute-start.6 = (f32[4,17,8,128]{3,2,1,0:T(8,128)}, f32[4,17,8,128]{3,2,1,0:T(8,128)S(1)}, u32[]{:S(2)}, u32[]{:S(2)}) collective-permute-start(f32[4,17,8,128]{3,2,1,0:T(8,128)} %get-tuple-element.33), channel_id=1, source_target_pairs={{0,40},{4,124},{8,32},{12,116},{16,56},{20,108},{24,48},{28,100},{... | collective-permute-start | bytes 835592 | tf_op jit(solution)/shard_map/ppermute | solution.py:570
  10.1 0.5 collective-permute-start.7
  10.6 0.4 collective-permute-start.8
  11.0 6.7 %match_block.2 = (f32[4,17,8,128]{3,2,1,0:T(8,128)}, f32[4,17,8,128]{3,2,1,0:T(8,128)}, f32[4,17,8,128]{3,2,1,0:T(8,128)}, f32[4,17,8,128]{3,2,1,0:T(8,128)}) custom-call(s32[1]{0:T(128)} %bitcast.place_ref, s32[1,2]{1,0:T(1,128)} %index_hbm.3, f32[27,64]{1,0:T(8,128)} %bitcast.24, f32[1,2,552,552]{3,2,1,0:T(8,128)} %image_hbm.3, f32[1,2,16,16]{3,2,1,0:T(8,128)} %var_hbm.3, ...), custom_call_target="tpu_custom_call" | custom-call | flops 5242880000 | bytes 3145728 | tf_op jit(solution)/shard_map/match_block/pallas_call | solution.py:401
  17.7 2.7 %collective-permute-start = (f32[4,17,8,128]{3,2,1,0:T(8,128)}, f32[4,17,8,128]{3,2,1,0:T(8,128)S(1)}, u32[]{:S(2)}, u32[]{:S(2)}) collective-permute-start(f32[4,17,8,128]{3,2,1,0:T(8,128)} %get-tuple-element.25), channel_id=1, source_target_pairs={{0,40},{4,124},{8,32},{12,116},{16,56},{20,108},{24,48},{28,100},{... | collective-permute-start | bytes 835592 | tf_op jit(solution)/shard_map/ppermute | solution.py:570
  20.4 0.5 collective-permute-start.1
  20.9 0.4 collective-permute-start.2
  21.5 5.3 %collective-permute-start.9 = (f32[4,17,8,128]{3,2,1,0:T(8,128)S(1)}, f32[4,17,8,128]{3,2,1,0:T(8,128)S(1)}, u32[]{:S(2)}, u32[]{:S(2)}) collective-permute-start(f32[4,17,8,128]{3,2,1,0:T(8,128)S(1)} %get-tuple-element.37), channel_id=1, source_target_pairs={{0,120},{4,44},{8,112},{12,36},{16,104},{20,60},{24,96},{28,52},{3... | collective-permute-start | bytes 835592 | tf_op jit(solution)/shard_map/ppermute | solution.py:570
  26.8 1.0 %copy-done = f32[4,17,8,128]{3,2,1,0:T(8,128)S(1)} copy-done((f32[4,17,8,128]{3,2,1,0:T(8,128)S(1)}, f32[4,17,8,128]{3,2,1,0:T(8,128)}, u32[]{:S(2)}) %copy-start) | copy-done | bytes 278552
  27.8 0.5 collective-permute-start.10
  28.6 2.8 %collective-permute-done.1.refs_2_ = f32[4,17,8,128]{3,2,1,0:T(8,128)S(1)} collective-permute-done((f32[4,17,8,128]{3,2,1,0:T(8,128)}, f32[4,17,8,128]{3,2,1,0:T(8,128)S(1)}, u32[]{:S(2)}, u32[]{:S(2)}) %collective-permute-start.1) | collective-permute-done | bytes 278560 | tf_op jit(solution)/shard_map/ppermute | solution.py:570
  31.5 4.4 %collective-permute-start.3 = (f32[4,17,8,128]{3,2,1,0:T(8,128)S(1)}, f32[4,17,8,128]{3,2,1,0:T(8,128)S(1)}, u32[]{:S(2)}, u32[]{:S(2)}) collective-permute-start(f32[4,17,8,128]{3,2,1,0:T(8,128)S(1)} %get-tuple-element.29), channel_id=1, source_target_pairs={{0,120},{4,44},{8,112},{12,36},{16,104},{20,60},{24,96},{28,52},{3... | collective-permute-start | bytes 835592 | tf_op jit(solution)/shard_map/ppermute | solution.py:570
  35.9 0.4 collective-permute-start.4
  36.4 1.2 %collective-permute-start.5 = (f32[4,17,8,128]{3,2,1,0:T(8,128)S(1)}, f32[4,17,8,128]{3,2,1,0:T(8,128)S(1)}, u32[]{:S(2)}, u32[]{:S(2)}) collective-permute-start(f32[4,17,8,128]{3,2,1,0:T(8,128)S(1)} %get-tuple-element.31), channel_id=1, source_target_pairs={{0,96},{4,36},{8,104},{12,44},{16,112},{20,52},{24,120},{28,60},{3... | collective-permute-start | bytes 835592 | tf_op jit(solution)/shard_map/ppermute | solution.py:570
  37.6 0.6 partial_sums.2
  38.3 3.2 %collective-permute-done.3 = f32[4,17,8,128]{3,2,1,0:T(8,128)S(1)} collective-permute-done((f32[4,17,8,128]{3,2,1,0:T(8,128)S(1)}, f32[4,17,8,128]{3,2,1,0:T(8,128)S(1)}, u32[]{:S(2)}, u32[]{:S(2)}) %collective-permute-start.3) | collective-permute-done | bytes 278560 | tf_op jit(solution)/shard_map/ppermute | solution.py:570
  41.5 2.4 %collective-permute-done.4 = f32[4,17,8,128]{3,2,1,0:T(8,128)S(1)} collective-permute-done((f32[4,17,8,128]{3,2,1,0:T(8,128)S(1)}, f32[4,17,8,128]{3,2,1,0:T(8,128)S(1)}, u32[]{:S(2)}, u32[]{:S(2)}) %collective-permute-start.4) | collective-permute-done | bytes 278560 | tf_op jit(solution)/shard_map/ppermute | solution.py:570
  43.9 0.6 collective-permute-done.5
  44.5 0.7 partial_sums.3
  45.2 0.8 collective-permute-start.12
  46.0 1.6 %collective-permute-done.12.other_ref = f32[1152,128]{1,0:T(8,128)S(1)} collective-permute-done((f32[1152,128]{1,0:T(8,128)S(1)}, f32[1152,128]{1,0:T(8,128)S(1)}, u32[]{:S(2)}, u32[]{:S(2)}) %collective-permute-start.12) | collective-permute-done | bytes 589856 | tf_op jit(solution)/shard_map/ppermute | solution.py:613
  47.9 19.1 %all_to_all.5.part_ref = f32[16,64,128]{2,1,0:T(8,128)S(1)} all-to-all(f32[16,64,128]{2,1,0:T(8,128)S(1)} %bitcast.13), channel_id=1, replica_groups={{0,8,16,24,32,40,48,56,64,72,80,88,96,104,112,120},{4,12,20,28,36,44,52..., dimensions={0} | all-to-all | bytes 1048576 | tf_op jit(solution)/shard_map/all_to_all | solution.py:587
  66.9 0.3 chi.1
  67.3 2.0 %collective-permute-start.13 = (f32[8,64,128]{2,1,0:T(8,128)S(1)}, f32[8,64,128]{2,1,0:T(8,128)S(1)}, u32[]{:S(2)}, u32[]{:S(2)}) collective-permute-start(f32[8,64,128]{2,1,0:T(8,128)S(1)} %get-tuple-element.44), channel_id=1, source_target_pairs={{0,1},{1,0},{2,3},{3,2},{4,5},{5,4},{6,7},{7,6},{8,9},{9,8},{10,11... | collective-permute-start | bytes 786440 | tf_op jit(solution)/shard_map/ppermute | solution.py:643
  69.3 2.6 %collective-permute-start.15 = (f32[8,64,128]{2,1,0:T(8,128)S(1)}, f32[8,64,128]{2,1,0:T(8,128)S(1)}, u32[]{:S(2)}, u32[]{:S(2)}) collective-permute-start(f32[8,64,128]{2,1,0:T(8,128)S(1)} %get-tuple-element.45), channel_id=1, source_target_pairs={{0,3},{3,0},{1,2},{2,1},{4,7},{7,4},{5,6},{6,5},{8,11},{11,8},{9,1... | collective-permute-start | bytes 786440 | tf_op jit(solution)/shard_map/ppermute | solution.py:643
  71.9 2.8 %collective-permute-done.13 = f32[8,64,128]{2,1,0:T(8,128)S(1)} collective-permute-done((f32[8,64,128]{2,1,0:T(8,128)S(1)}, f32[8,64,128]{2,1,0:T(8,128)S(1)}, u32[]{:S(2)}, u32[]{:S(2)}) %collective-permute-start.13) | collective-permute-done | bytes 262176 | tf_op jit(solution)/shard_map/ppermute | solution.py:643
  74.7 3.9 %collective-permute-start.14 = (f32[8,64,128]{2,1,0:T(8,128)S(1)}, f32[8,64,128]{2,1,0:T(8,128)S(1)}, u32[]{:S(2)}, u32[]{:S(2)}) collective-permute-start(f32[8,64,128]{2,1,0:T(8,128)S(1)} %add.6.upper_ref), channel_id=1, source_target_pairs={{0,3},{3,0},{1,2},{2,1},{4,7},{7,4},{5,6},{6,5},{8,11},{11,8},{9,1... | collective-permute-start | bytes 786440 | tf_op jit(solution)/shard_map/ppermute | solution.py:647
  78.8 0.8 image.1
  79.6 3.5 %collective-permute-done.14.more_upper_ref = f32[8,64,128]{2,1,0:T(8,128)S(1)} collective-permute-done((f32[8,64,128]{2,1,0:T(8,128)S(1)}, f32[8,64,128]{2,1,0:T(8,128)S(1)}, u32[]{:S(2)}, u32[]{:S(2)}) %collective-permute-start.14) | collective-permute-done | bytes 262176 | tf_op jit(solution)/shard_map/ppermute | solution.py:647
  83.2 2.0 %collective-permute-done.16.more_lower_ref = f32[8,64,128]{2,1,0:T(8,128)S(1)} collective-permute-done((f32[8,64,128]{2,1,0:T(8,128)S(1)}, f32[8,64,128]{2,1,0:T(8,128)S(1)}, u32[]{:S(2)}, u32[]{:S(2)}) %collective-permute-start.16) | collective-permute-done | bytes 262176 | tf_op jit(solution)/shard_map/ppermute | solution.py:647
  85.2 0.9 detection.1
  (21 shorter events, 1.1 us)
Async XLA Ops:
  7.4 13.5 %collective-permute-start.6 = (f32[4,17,8,128]{3,2,1,0:T(8,128)}, f32[4,17,8,128]{3,2,1,0:T(8,128)S(1)}, u32[]{:S(2)}, u32[]{:S(2)}) collective-permute-start(f32[4,17,8,128]{3,2,1,0:T(8,128)} %get-tuple-element.33), channel_id=1, source_target_pairs={{0,40},{4,124},{8,32},{12,116},{16,56},{20,108},{24,48},{28,100},{... | collective-permute-start | bytes 835592 | tf_op jit(solution)/shard_map/ppermute | solution.py:570
  10.1 11.3 %collective-permute-start.7 = (f32[4,17,8,128]{3,2,1,0:T(8,128)}, f32[4,17,8,128]{3,2,1,0:T(8,128)S(1)}, u32[]{:S(2)}, u32[]{:S(2)}) collective-permute-start(f32[4,17,8,128]{3,2,1,0:T(8,128)} %get-tuple-element.34), channel_id=1, source_target_pairs={{0,8},{4,28},{8,0},{12,20},{16,24},{20,12},{24,16},{28,4},{32,40},... | collective-permute-start | bytes 835592 | tf_op jit(solution)/shard_map/ppermute | solution.py:570
  10.6 10.7 %copy-start.1 = (f32[4,17,8,128]{3,2,1,0:T(8,128)S(1)}, f32[4,17,8,128]{3,2,1,0:T(8,128)}, u32[]{:S(2)}) copy-start(f32[4,17,8,128]{3,2,1,0:T(8,128)} %get-tuple-element.32.part_hbm) | copy-start | bytes 835588
  10.6 10.7 %collective-permute-start.8 = (f32[4,17,8,128]{3,2,1,0:T(8,128)}, f32[4,17,8,128]{3,2,1,0:T(8,128)S(1)}, u32[]{:S(2)}, u32[]{:S(2)}) collective-permute-start(f32[4,17,8,128]{3,2,1,0:T(8,128)} %get-tuple-element.35), channel_id=1, source_target_pairs={{0,32},{4,100},{8,40},{12,108},{16,48},{20,116},{24,56},{28,124},{... | collective-permute-start | bytes 835592 | tf_op jit(solution)/shard_map/ppermute | solution.py:570
  17.7 10.6 %collective-permute-start = (f32[4,17,8,128]{3,2,1,0:T(8,128)}, f32[4,17,8,128]{3,2,1,0:T(8,128)S(1)}, u32[]{:S(2)}, u32[]{:S(2)}) collective-permute-start(f32[4,17,8,128]{3,2,1,0:T(8,128)} %get-tuple-element.25), channel_id=1, source_target_pairs={{0,40},{4,124},{8,32},{12,116},{16,56},{20,108},{24,48},{28,100},{... | collective-permute-start | bytes 835592 | tf_op jit(solution)/shard_map/ppermute | solution.py:570
  20.4 11.1 %collective-permute-start.1 = (f32[4,17,8,128]{3,2,1,0:T(8,128)}, f32[4,17,8,128]{3,2,1,0:T(8,128)S(1)}, u32[]{:S(2)}, u32[]{:S(2)}) collective-permute-start(f32[4,17,8,128]{3,2,1,0:T(8,128)} %get-tuple-element.26), channel_id=1, source_target_pairs={{0,8},{4,28},{8,0},{12,20},{16,24},{20,12},{24,16},{28,4},{32,40},... | collective-permute-start | bytes 835592 | tf_op jit(solution)/shard_map/ppermute | solution.py:570
  20.9 10.6 %collective-permute-start.2 = (f32[4,17,8,128]{3,2,1,0:T(8,128)}, f32[4,17,8,128]{3,2,1,0:T(8,128)S(1)}, u32[]{:S(2)}, u32[]{:S(2)}) collective-permute-start(f32[4,17,8,128]{3,2,1,0:T(8,128)} %get-tuple-element.27), channel_id=1, source_target_pairs={{0,32},{4,100},{8,40},{12,108},{16,48},{20,116},{24,56},{28,124},{... | collective-permute-start | bytes 835592 | tf_op jit(solution)/shard_map/ppermute | solution.py:570
  21.5 14.9 %collective-permute-start.9 = (f32[4,17,8,128]{3,2,1,0:T(8,128)S(1)}, f32[4,17,8,128]{3,2,1,0:T(8,128)S(1)}, u32[]{:S(2)}, u32[]{:S(2)}) collective-permute-start(f32[4,17,8,128]{3,2,1,0:T(8,128)S(1)} %get-tuple-element.37), channel_id=1, source_target_pairs={{0,120},{4,44},{8,112},{12,36},{16,104},{20,60},{24,96},{28,52},{3... | collective-permute-start | bytes 835592 | tf_op jit(solution)/shard_map/ppermute | solution.py:570
  26.8 1.0 %copy-start = (f32[4,17,8,128]{3,2,1,0:T(8,128)S(1)}, f32[4,17,8,128]{3,2,1,0:T(8,128)}, u32[]{:S(2)}) copy-start(f32[4,17,8,128]{3,2,1,0:T(8,128)} %get-tuple-element.24.part_hbm) | copy-start | bytes 835588
  27.8 9.8 %collective-permute-start.10 = (f32[4,17,8,128]{3,2,1,0:T(8,128)S(1)}, f32[4,17,8,128]{3,2,1,0:T(8,128)S(1)}, u32[]{:S(2)}, u32[]{:S(2)}) collective-permute-start(f32[4,17,8,128]{3,2,1,0:T(8,128)S(1)} %get-tuple-element.38), channel_id=1, source_target_pairs={{0,24},{4,12},{8,16},{12,4},{16,8},{20,28},{24,0},{28,20},{32,56},... | collective-permute-start | bytes 835592 | tf_op jit(solution)/shard_map/ppermute | solution.py:570
  28.3 9.3 %collective-permute-start.11 = (f32[4,17,8,128]{3,2,1,0:T(8,128)S(1)}, f32[4,17,8,128]{3,2,1,0:T(8,128)S(1)}, u32[]{:S(2)}, u32[]{:S(2)}) collective-permute-start(f32[4,17,8,128]{3,2,1,0:T(8,128)S(1)} %get-tuple-element.39), channel_id=1, source_target_pairs={{0,96},{4,36},{8,104},{12,44},{16,112},{20,52},{24,120},{28,60},{3... | collective-permute-start | bytes 835592 | tf_op jit(solution)/shard_map/ppermute | solution.py:570
  31.5 10.0 %collective-permute-start.3 = (f32[4,17,8,128]{3,2,1,0:T(8,128)S(1)}, f32[4,17,8,128]{3,2,1,0:T(8,128)S(1)}, u32[]{:S(2)}, u32[]{:S(2)}) collective-permute-start(f32[4,17,8,128]{3,2,1,0:T(8,128)S(1)} %get-tuple-element.29), channel_id=1, source_target_pairs={{0,120},{4,44},{8,112},{12,36},{16,104},{20,60},{24,96},{28,52},{3... | collective-permute-start | bytes 835592 | tf_op jit(solution)/shard_map/ppermute | solution.py:570
  35.9 7.9 %collective-permute-start.4 = (f32[4,17,8,128]{3,2,1,0:T(8,128)S(1)}, f32[4,17,8,128]{3,2,1,0:T(8,128)S(1)}, u32[]{:S(2)}, u32[]{:S(2)}) collective-permute-start(f32[4,17,8,128]{3,2,1,0:T(8,128)S(1)} %get-tuple-element.30), channel_id=1, source_target_pairs={{0,24},{4,12},{8,16},{12,4},{16,8},{20,28},{24,0},{28,20},{32,56},... | collective-permute-start | bytes 835592 | tf_op jit(solution)/shard_map/ppermute | solution.py:570
  36.4 8.1 %collective-permute-start.5 = (f32[4,17,8,128]{3,2,1,0:T(8,128)S(1)}, f32[4,17,8,128]{3,2,1,0:T(8,128)S(1)}, u32[]{:S(2)}, u32[]{:S(2)}) collective-permute-start(f32[4,17,8,128]{3,2,1,0:T(8,128)S(1)} %get-tuple-element.31), channel_id=1, source_target_pairs={{0,96},{4,36},{8,104},{12,44},{16,112},{20,52},{24,120},{28,60},{3... | collective-permute-start | bytes 835592 | tf_op jit(solution)/shard_map/ppermute | solution.py:570
  45.2 2.4 %collective-permute-start.12 = (f32[1152,128]{1,0:T(8,128)S(1)}, f32[1152,128]{1,0:T(8,128)S(1)}, u32[]{:S(2)}, u32[]{:S(2)}) collective-permute-start(f32[1152,128]{1,0:T(8,128)S(1)} %get-tuple-element.43), channel_id=1, source_target_pairs={{0,4},{4,0},{8,12},{12,8},{16,20},{20,16},{24,28},{28,24},{32,36},... | collective-permute-start | bytes 1769480 | tf_op jit(solution)/shard_map/ppermute | solution.py:613
  67.3 7.4 %collective-permute-start.13 = (f32[8,64,128]{2,1,0:T(8,128)S(1)}, f32[8,64,128]{2,1,0:T(8,128)S(1)}, u32[]{:S(2)}, u32[]{:S(2)}) collective-permute-start(f32[8,64,128]{2,1,0:T(8,128)S(1)} %get-tuple-element.44), channel_id=1, source_target_pairs={{0,1},{1,0},{2,3},{3,2},{4,5},{5,4},{6,7},{7,6},{8,9},{9,8},{10,11... | collective-permute-start | bytes 786440 | tf_op jit(solution)/shard_map/ppermute | solution.py:643
  69.3 9.4 %collective-permute-start.15 = (f32[8,64,128]{2,1,0:T(8,128)S(1)}, f32[8,64,128]{2,1,0:T(8,128)S(1)}, u32[]{:S(2)}, u32[]{:S(2)}) collective-permute-start(f32[8,64,128]{2,1,0:T(8,128)S(1)} %get-tuple-element.45), channel_id=1, source_target_pairs={{0,3},{3,0},{1,2},{2,1},{4,7},{7,4},{5,6},{6,5},{8,11},{11,8},{9,1... | collective-permute-start | bytes 786440 | tf_op jit(solution)/shard_map/ppermute | solution.py:643
  74.7 8.4 %collective-permute-start.14 = (f32[8,64,128]{2,1,0:T(8,128)S(1)}, f32[8,64,128]{2,1,0:T(8,128)S(1)}, u32[]{:S(2)}, u32[]{:S(2)}) collective-permute-start(f32[8,64,128]{2,1,0:T(8,128)S(1)} %add.6.upper_ref), channel_id=1, source_target_pairs={{0,3},{3,0},{1,2},{2,1},{4,7},{7,4},{5,6},{6,5},{8,11},{11,8},{9,1... | collective-permute-start | bytes 786440 | tf_op jit(solution)/shard_map/ppermute | solution.py:647
  78.7 6.5 %collective-permute-start.16 = (f32[8,64,128]{2,1,0:T(8,128)S(1)}, f32[8,64,128]{2,1,0:T(8,128)S(1)}, u32[]{:S(2)}, u32[]{:S(2)}) collective-permute-start(f32[8,64,128]{2,1,0:T(8,128)S(1)} %add.7.lower_ref), channel_id=1, source_target_pairs={{0,1},{1,0},{2,3},{3,2},{4,5},{5,4},{6,7},{7,6},{8,9},{9,8},{10,11... | collective-permute-start | bytes 786440 | tf_op jit(solution)/shard_map/ppermute | solution.py:647

commit v8 on v7

--- a/solution.py
+++ b/solution.py
@@ -57,7 +57,7 @@
     by_lane = np.concatenate([cosine, sine], axis=0)
     back_across = np.zeros((WIDTH, WIDTH))
     back_across[:, :KEPT] = by_lane[:, :KEPT] * (2 / WIDTH)
-    along = np.zeros((TILE, WIDTH), np.float32)
+    along = np.zeros((TILE, WIDTH))
     along[:KSIZE] = np.concatenate([cosine, -sine], axis=0)[:, :KSIZE].T
 
     cosine, sine = waves(SPAN)
@@ -84,7 +84,7 @@
         three(back_down),
         np.concatenate(as_halves(back_across), axis=0),
         np.concatenate([three(same, 256), three(cross, 256)], axis=0),
-        along,
+        np.concatenate([as_halves(along)[part] for part in (0, 0, 1)], axis=0),
     )
 
 
@@ -186,34 +186,29 @@
 
 
 def filter_bank():
-    taps = lax.broadcasted_iota(jnp.int32, (1, TILE), 1)
-    values = profiles_at(taps)
-    norms = [jnp.sqrt(jnp.sum(value * value, axis=1, keepdims=True)) for value in values]
-    rows = [value / norm for value, norm in zip(values, norms)]
-    wide = jnp.concatenate(rows + [jnp.zeros((16 - NFILT, TILE), f32)], axis=0)
-    lane = lax.broadcasted_iota(jnp.int32, (TAPS, TILE), 1)
-    tall = jnp.zeros((TAPS, TILE), f32)
-    for number, (value, norm) in enumerate(
-        zip(profiles_at(lax.broadcasted_iota(jnp.int32, (TAPS, TILE), 0)), norms)
-    ):
-        tall = jnp.where(lane == number, value / norm, tall)
-    return wide, tall
+    values = profiles_at(lax.broadcasted_iota(jnp.int32, (1, TILE), 1))
+    scales = [1.0 / jnp.sqrt(jnp.sum(value * value, axis=1, keepdims=True)) for value in values]
+    wide = [value * scale for value, scale in zip(values, scales)]
+    tall = profiles_at(lax.broadcasted_iota(jnp.int32, (TAPS, TILE), 0))
+    return wide, [value * scale for value, scale in zip(tall, scales)]
 
 
 def kernel_spectrum(filters, which, table_ref, down_taps_ref, along_ref):
-    first = lax.broadcasted_iota(jnp.int32, (16, 16), 0)
-    second = lax.broadcasted_iota(jnp.int32, (16, 16), 1)
-    mixing = jnp.zeros((16, 16), f32)
-    for number, (p, q) in enumerate(filter_terms()):
-        mixing = jnp.where((first == p) & (second == q), table_ref[number, which], mixing)
     wide, tall = filters
-    across = exact_dot(mixing, exact_dot(wide, along_ref[...]))
-    across = jnp.concatenate([across, jnp.zeros((TILE - 16, 2 * TILE), f32)], axis=0)
-    mixed = exact_dot(tall, across)
-    high = mixed.astype(bf16).astype(f32)
-    rest = jnp.zeros((256 - 3 * TAPS, 2 * TILE), f32)
-    mixed = jnp.concatenate([high, mixed - high, high, rest], axis=0).astype(bf16)
-    both = jnp.dot(down_taps_ref[...], mixed, preferred_element_type=f32)
+    mixed = [0.0] * NFILT
+    for number, (first, second) in enumerate(filter_terms()):
+        mixed[first] = mixed[first] + table_ref[number, which] * wide[second]
+    kernel = 0.0
+    for down, across in zip(tall, mixed):
+        kernel = kernel + down * across
+    high, low = split(kernel)
+    half_way = jnp.dot(
+        jnp.concatenate([high, low, high], axis=1), along_ref[...], preferred_element_type=f32
+    )
+    high = half_way.astype(bf16).astype(f32)
+    rest = jnp.zeros((256 - 3 * TAPS, WIDTH), f32)
+    half_way = jnp.concatenate([high, half_way - high, high, rest], axis=0).astype(bf16)
+    both = jnp.dot(down_taps_ref[...], half_way, preferred_element_type=f32)
     return both[:SPAN], both[SPAN + 8:2 * SPAN + 8]
 
 

time: 86.3 us -> 85.6 us (level)
  transfers between devices with their start and end apart: 17 -> 17, of which waited for: 9 -> 9; matrix products, arithmetic and copies ran while one was open for 0% -> 0% of each run, Pallas kernels for 10% -> 9%
where the time goes in v8:
time: 85.6 us; the launch traced here: 85.3 us
  starting transfers between devices  28.6 us (33%)
  waiting for transfers between devices  19.2 us (22%)
  blocking collectives  19.1 us (22%)
  Pallas kernels  16.6 us (19%)
  local copies, waits for them, and re-layouts  0.96 us (1%)
    ppermute x12, starting transfers between devices, exchange(): lax.ppermute(parts[way], 'visit', phase_partners(phase, way))  19.3 us
    all_to_all x1, blocking collectives, spread_tiles(): lax.all_to_all(pieces, 'visit', 0, 0, axis_index_groups=same_core, tiled=...  19.1 us
    pallas_call x2, Pallas kernels, match_block(): pl.pallas_call(functools.partial(match_kernel, block=block), out_shape=[j...  12.7 us
    ppermute x12, waiting for transfers between devices, exchange(): lax.ppermute(parts[way], 'visit', phase_partners(phase, way))  9.14 us
    ppermute x2, waiting for transfers between devices, local(): terms.extend((half, lax.ppermute(half, 'band', pairings[1 - number])))  5.53 us
    ppermute x2, starting transfers between devices, local(): lax.ppermute(half, 'band', pairings[number])  4.52 us
    ppermute x2, starting transfers between devices, local(): terms.extend((half, lax.ppermute(half, 'band', pairings[1 - number])))  4.02 us
    ppermute x2, waiting for transfers between devices, local(): lax.ppermute(half, 'band', pairings[number])  2.9 us
  transfers between devices with their start and end apart: 17, of which 9 were waited for; matrix products, arithmetic and copies ran while one was open for 0% of the time, Pallas kernels for 9%

profile of v8, /device:TPU:0, one launch (start us, length us, event | category | flops | bytes accessed | tf_op | source)
XLA Modules:
  0.0 85.3 jit_solution(14227809586124830899)
XLA Ops:
  0.6 6.4 %match_block.3 = (f32[4,17,8,128]{3,2,1,0:T(8,128)}, f32[4,17,8,128]{3,2,1,0:T(8,128)}, f32[4,17,8,128]{3,2,1,0:T(8,128)}, f32[4,17,8,128]{3,2,1,0:T(8,128)}) custom-call(s32[1]{0:T(128)} %bitcast.place_ref, s32[1,2]{1,0:T(1,128)} %index_hbm.3, f32[27,64]{1,0:T(8,128)} %bitcast.23, f32[1,2,552,552]{3,2,1,0:T(8,128)} %image_hbm.3, f32[1,2,16,16]{3,2,1,0:T(8,128)} %var_hbm.3, ...), custom_call_target="tpu_custom_call" | custom-call | flops 5242880000 | bytes 3145728 | tf_op jit(solution)/shard_map/match_block/pallas_call | solution.py:396
  7.0 2.7 %collective-permute-start.6 = (f32[4,17,8,128]{3,2,1,0:T(8,128)}, f32[4,17,8,128]{3,2,1,0:T(8,128)S(1)}, u32[]{:S(2)}, u32[]{:S(2)}) collective-permute-start(f32[4,17,8,128]{3,2,1,0:T(8,128)} %get-tuple-element.33), channel_id=1, source_target_pairs={{0,40},{4,124},{8,32},{12,116},{16,56},{20,108},{24,48},{28,100},{... | collective-permute-start | bytes 835592 | tf_op jit(solution)/shard_map/ppermute | solution.py:565
  9.7 0.5 collective-permute-start.7
  10.2 0.4 collective-permute-start.8
  10.6 6.3 %match_block.2 = (f32[4,17,8,128]{3,2,1,0:T(8,128)}, f32[4,17,8,128]{3,2,1,0:T(8,128)}, f32[4,17,8,128]{3,2,1,0:T(8,128)}, f32[4,17,8,128]{3,2,1,0:T(8,128)}) custom-call(s32[1]{0:T(128)} %bitcast.place_ref, s32[1,2]{1,0:T(1,128)} %index_hbm.3, f32[27,64]{1,0:T(8,128)} %bitcast.24, f32[1,2,552,552]{3,2,1,0:T(8,128)} %image_hbm.3, f32[1,2,16,16]{3,2,1,0:T(8,128)} %var_hbm.3, ...), custom_call_target="tpu_custom_call" | custom-call | flops 5242880000 | bytes 3145728 | tf_op jit(solution)/shard_map/match_block/pallas_call | solution.py:396
  16.9 2.7 %collective-permute-start = (f32[4,17,8,128]{3,2,1,0:T(8,128)}, f32[4,17,8,128]{3,2,1,0:T(8,128)S(1)}, u32[]{:S(2)}, u32[]{:S(2)}) collective-permute-start(f32[4,17,8,128]{3,2,1,0:T(8,128)} %get-tuple-element.25), channel_id=1, source_target_pairs={{0,40},{4,124},{8,32},{12,116},{16,56},{20,108},{24,48},{28,100},{... | collective-permute-start | bytes 835592 | tf_op jit(solution)/shard_map/ppermute | solution.py:565
  19.6 0.5 collective-permute-start.1
  20.1 0.4 collective-permute-start.2
  20.6 5.4 %collective-permute-start.9 = (f32[4,17,8,128]{3,2,1,0:T(8,128)S(1)}, f32[4,17,8,128]{3,2,1,0:T(8,128)S(1)}, u32[]{:S(2)}, u32[]{:S(2)}) collective-permute-start(f32[4,17,8,128]{3,2,1,0:T(8,128)S(1)} %get-tuple-element.37), channel_id=1, source_target_pairs={{0,120},{4,44},{8,112},{12,36},{16,104},{20,60},{24,96},{28,52},{3... | collective-permute-start | bytes 835592 | tf_op jit(solution)/shard_map/ppermute | solution.py:565
  26.0 1.0 %copy-done = f32[4,17,8,128]{3,2,1,0:T(8,128)S(1)} copy-done((f32[4,17,8,128]{3,2,1,0:T(8,128)S(1)}, f32[4,17,8,128]{3,2,1,0:T(8,128)}, u32[]{:S(2)}) %copy-start) | copy-done | bytes 278552
  27.0 0.6 collective-permute-start.10
  27.9 2.8 %collective-permute-done.1.refs_2_ = f32[4,17,8,128]{3,2,1,0:T(8,128)S(1)} collective-permute-done((f32[4,17,8,128]{3,2,1,0:T(8,128)}, f32[4,17,8,128]{3,2,1,0:T(8,128)S(1)}, u32[]{:S(2)}, u32[]{:S(2)}) %collective-permute-start.1) | collective-permute-done | bytes 278560 | tf_op jit(solution)/shard_map/ppermute | solution.py:565
  30.8 4.4 %collective-permute-start.3 = (f32[4,17,8,128]{3,2,1,0:T(8,128)S(1)}, f32[4,17,8,128]{3,2,1,0:T(8,128)S(1)}, u32[]{:S(2)}, u32[]{:S(2)}) collective-permute-start(f32[4,17,8,128]{3,2,1,0:T(8,128)S(1)} %get-tuple-element.29), channel_id=1, source_target_pairs={{0,120},{4,44},{8,112},{12,36},{16,104},{20,60},{24,96},{28,52},{3... | collective-permute-start | bytes 835592 | tf_op jit(solution)/shard_map/ppermute | solution.py:565
  35.2 0.5 collective-permute-start.4
  35.6 1.1 %collective-permute-start.5 = (f32[4,17,8,128]{3,2,1,0:T(8,128)S(1)}, f32[4,17,8,128]{3,2,1,0:T(8,128)S(1)}, u32[]{:S(2)}, u32[]{:S(2)}) collective-permute-start(f32[4,17,8,128]{3,2,1,0:T(8,128)S(1)} %get-tuple-element.31), channel_id=1, source_target_pairs={{0,96},{4,36},{8,104},{12,44},{16,112},{20,52},{24,120},{28,60},{3... | collective-permute-start | bytes 835592 | tf_op jit(solution)/shard_map/ppermute | solution.py:565
  36.9 0.6 partial_sums.2
  37.6 3.2 %collective-permute-done.3 = f32[4,17,8,128]{3,2,1,0:T(8,128)S(1)} collective-permute-done((f32[4,17,8,128]{3,2,1,0:T(8,128)S(1)}, f32[4,17,8,128]{3,2,1,0:T(8,128)S(1)}, u32[]{:S(2)}, u32[]{:S(2)}) %collective-permute-start.3) | collective-permute-done | bytes 278560 | tf_op jit(solution)/shard_map/ppermute | solution.py:565
  40.8 2.4 %collective-permute-done.4 = f32[4,17,8,128]{3,2,1,0:T(8,128)S(1)} collective-permute-done((f32[4,17,8,128]{3,2,1,0:T(8,128)S(1)}, f32[4,17,8,128]{3,2,1,0:T(8,128)S(1)}, u32[]{:S(2)}, u32[]{:S(2)}) %collective-permute-start.4) | collective-permute-done | bytes 278560 | tf_op jit(solution)/shard_map/ppermute | solution.py:565
  43.1 0.6 collective-permute-done.5
  43.7 0.7 partial_sums.3
  44.5 0.8 collective-permute-start.12
  45.2 1.6 %collective-permute-done.12.other_ref = f32[1152,128]{1,0:T(8,128)S(1)} collective-permute-done((f32[1152,128]{1,0:T(8,128)S(1)}, f32[1152,128]{1,0:T(8,128)S(1)}, u32[]{:S(2)}, u32[]{:S(2)}) %collective-permute-start.12) | collective-permute-done | bytes 589856 | tf_op jit(solution)/shard_map/ppermute | solution.py:608
  47.1 19.1 %all_to_all.5.part_ref = f32[16,64,128]{2,1,0:T(8,128)S(1)} all-to-all(f32[16,64,128]{2,1,0:T(8,128)S(1)} %bitcast.13), channel_id=1, replica_groups={{0,8,16,24,32,40,48,56,64,72,80,88,96,104,112,120},{4,12,20,28,36,44,52..., dimensions={0} | all-to-all | bytes 1048576 | tf_op jit(solution)/shard_map/all_to_all | solution.py:582
  66.2 0.3 chi.1
  66.6 2.0 %collective-permute-start.13 = (f32[8,64,128]{2,1,0:T(8,128)S(1)}, f32[8,64,128]{2,1,0:T(8,128)S(1)}, u32[]{:S(2)}, u32[]{:S(2)}) collective-permute-start(f32[8,64,128]{2,1,0:T(8,128)S(1)} %get-tuple-element.44), channel_id=1, source_target_pairs={{0,1},{1,0},{2,3},{3,2},{4,5},{5,4},{6,7},{7,6},{8,9},{9,8},{10,11... | collective-permute-start | bytes 786440 | tf_op jit(solution)/shard_map/ppermute | solution.py:638
  68.6 2.5 %collective-permute-start.15 = (f32[8,64,128]{2,1,0:T(8,128)S(1)}, f32[8,64,128]{2,1,0:T(8,128)S(1)}, u32[]{:S(2)}, u32[]{:S(2)}) collective-permute-start(f32[8,64,128]{2,1,0:T(8,128)S(1)} %get-tuple-element.45), channel_id=1, source_target_pairs={{0,3},{3,0},{1,2},{2,1},{4,7},{7,4},{5,6},{6,5},{8,11},{11,8},{9,1... | collective-permute-start | bytes 786440 | tf_op jit(solution)/shard_map/ppermute | solution.py:638
  71.1 2.9 %collective-permute-done.13 = f32[8,64,128]{2,1,0:T(8,128)S(1)} collective-permute-done((f32[8,64,128]{2,1,0:T(8,128)S(1)}, f32[8,64,128]{2,1,0:T(8,128)S(1)}, u32[]{:S(2)}, u32[]{:S(2)}) %collective-permute-start.13) | collective-permute-done | bytes 262176 | tf_op jit(solution)/shard_map/ppermute | solution.py:638
  74.0 3.9 %collective-permute-start.14 = (f32[8,64,128]{2,1,0:T(8,128)S(1)}, f32[8,64,128]{2,1,0:T(8,128)S(1)}, u32[]{:S(2)}, u32[]{:S(2)}) collective-permute-start(f32[8,64,128]{2,1,0:T(8,128)S(1)} %add.6.upper_ref), channel_id=1, source_target_pairs={{0,3},{3,0},{1,2},{2,1},{4,7},{7,4},{5,6},{6,5},{8,11},{11,8},{9,1... | collective-permute-start | bytes 786440 | tf_op jit(solution)/shard_map/ppermute | solution.py:642
  78.1 0.8 image.1
  78.9 3.5 %collective-permute-done.14.more_upper_ref = f32[8,64,128]{2,1,0:T(8,128)S(1)} collective-permute-done((f32[8,64,128]{2,1,0:T(8,128)S(1)}, f32[8,64,128]{2,1,0:T(8,128)S(1)}, u32[]{:S(2)}, u32[]{:S(2)}) %collective-permute-start.14) | collective-permute-done | bytes 262176 | tf_op jit(solution)/shard_map/ppermute | solution.py:642
  82.4 2.0 %collective-permute-done.16.more_lower_ref = f32[8,64,128]{2,1,0:T(8,128)S(1)} collective-permute-done((f32[8,64,128]{2,1,0:T(8,128)S(1)}, f32[8,64,128]{2,1,0:T(8,128)S(1)}, u32[]{:S(2)}, u32[]{:S(2)}) %collective-permute-start.16) | collective-permute-done | bytes 262176 | tf_op jit(solution)/shard_map/ppermute | solution.py:642
  84.5 0.9 %detection.1 = f32[8,128,128]{2,1,0:T(8,128)} custom-call(f32[8,64,128]{2,1,0:T(8,128)S(1)} %add.6.upper_ref, f32[8,64,128]{2,1,0:T(8,128)S(1)} %collective-permute-done.14.more_upper_ref, f32[8,64,128]{2,1,0:T(8,128)S(1)} %add.7.lower_ref, f32[8,64,128]{2,1,0:T(8,128)S(1)} %collective-permute-done.16.more_lower_ref), custom_call_target="tpu_custom_call" | custom-call | tf_op jit(solution)/shard_map/detection/pallas_call | solution.py:643
  (21 shorter events, 1.1 us)
Async XLA Ops:
  7.0 13.1 %collective-permute-start.6 = (f32[4,17,8,128]{3,2,1,0:T(8,128)}, f32[4,17,8,128]{3,2,1,0:T(8,128)S(1)}, u32[]{:S(2)}, u32[]{:S(2)}) collective-permute-start(f32[4,17,8,128]{3,2,1,0:T(8,128)} %get-tuple-element.33), channel_id=1, source_target_pairs={{0,40},{4,124},{8,32},{12,116},{16,56},{20,108},{24,48},{28,100},{... | collective-permute-start | bytes 835592 | tf_op jit(solution)/shard_map/ppermute | solution.py:565
  9.7 10.9 %collective-permute-start.7 = (f32[4,17,8,128]{3,2,1,0:T(8,128)}, f32[4,17,8,128]{3,2,1,0:T(8,128)S(1)}, u32[]{:S(2)}, u32[]{:S(2)}) collective-permute-start(f32[4,17,8,128]{3,2,1,0:T(8,128)} %get-tuple-element.34), channel_id=1, source_target_pairs={{0,8},{4,28},{8,0},{12,20},{16,24},{20,12},{24,16},{28,4},{32,40},... | collective-permute-start | bytes 835592 | tf_op jit(solution)/shard_map/ppermute | solution.py:565
  10.2 10.3 %copy-start.1 = (f32[4,17,8,128]{3,2,1,0:T(8,128)S(1)}, f32[4,17,8,128]{3,2,1,0:T(8,128)}, u32[]{:S(2)}) copy-start(f32[4,17,8,128]{3,2,1,0:T(8,128)} %get-tuple-element.32.part_hbm) | copy-start | bytes 835588
  10.2 10.3 %collective-permute-start.8 = (f32[4,17,8,128]{3,2,1,0:T(8,128)}, f32[4,17,8,128]{3,2,1,0:T(8,128)S(1)}, u32[]{:S(2)}, u32[]{:S(2)}) collective-permute-start(f32[4,17,8,128]{3,2,1,0:T(8,128)} %get-tuple-element.35), channel_id=1, source_target_pairs={{0,32},{4,100},{8,40},{12,108},{16,48},{20,116},{24,56},{28,124},{... | collective-permute-start | bytes 835592 | tf_op jit(solution)/shard_map/ppermute | solution.py:565
  16.9 10.7 %collective-permute-start = (f32[4,17,8,128]{3,2,1,0:T(8,128)}, f32[4,17,8,128]{3,2,1,0:T(8,128)S(1)}, u32[]{:S(2)}, u32[]{:S(2)}) collective-permute-start(f32[4,17,8,128]{3,2,1,0:T(8,128)} %get-tuple-element.25), channel_id=1, source_target_pairs={{0,40},{4,124},{8,32},{12,116},{16,56},{20,108},{24,48},{28,100},{... | collective-permute-start | bytes 835592 | tf_op jit(solution)/shard_map/ppermute | solution.py:565
  19.6 11.1 %collective-permute-start.1 = (f32[4,17,8,128]{3,2,1,0:T(8,128)}, f32[4,17,8,128]{3,2,1,0:T(8,128)S(1)}, u32[]{:S(2)}, u32[]{:S(2)}) collective-permute-start(f32[4,17,8,128]{3,2,1,0:T(8,128)} %get-tuple-element.26), channel_id=1, source_target_pairs={{0,8},{4,28},{8,0},{12,20},{16,24},{20,12},{24,16},{28,4},{32,40},... | collective-permute-start | bytes 835592 | tf_op jit(solution)/shard_map/ppermute | solution.py:565
  20.1 10.6 %collective-permute-start.2 = (f32[4,17,8,128]{3,2,1,0:T(8,128)}, f32[4,17,8,128]{3,2,1,0:T(8,128)S(1)}, u32[]{:S(2)}, u32[]{:S(2)}) collective-permute-start(f32[4,17,8,128]{3,2,1,0:T(8,128)} %get-tuple-element.27), channel_id=1, source_target_pairs={{0,32},{4,100},{8,40},{12,108},{16,48},{20,116},{24,56},{28,124},{... | collective-permute-start | bytes 835592 | tf_op jit(solution)/shard_map/ppermute | solution.py:565
  20.6 15.0 %collective-permute-start.9 = (f32[4,17,8,128]{3,2,1,0:T(8,128)S(1)}, f32[4,17,8,128]{3,2,1,0:T(8,128)S(1)}, u32[]{:S(2)}, u32[]{:S(2)}) collective-permute-start(f32[4,17,8,128]{3,2,1,0:T(8,128)S(1)} %get-tuple-element.37), channel_id=1, source_target_pairs={{0,120},{4,44},{8,112},{12,36},{16,104},{20,60},{24,96},{28,52},{3... | collective-permute-start | bytes 835592 | tf_op jit(solution)/shard_map/ppermute | solution.py:565
  26.0 1.0 %copy-start = (f32[4,17,8,128]{3,2,1,0:T(8,128)S(1)}, f32[4,17,8,128]{3,2,1,0:T(8,128)}, u32[]{:S(2)}) copy-start(f32[4,17,8,128]{3,2,1,0:T(8,128)} %get-tuple-element.24.part_hbm) | copy-start | bytes 835588
  27.0 9.9 %collective-permute-start.10 = (f32[4,17,8,128]{3,2,1,0:T(8,128)S(1)}, f32[4,17,8,128]{3,2,1,0:T(8,128)S(1)}, u32[]{:S(2)}, u32[]{:S(2)}) collective-permute-start(f32[4,17,8,128]{3,2,1,0:T(8,128)S(1)} %get-tuple-element.38), channel_id=1, source_target_pairs={{0,24},{4,12},{8,16},{12,4},{16,8},{20,28},{24,0},{28,20},{32,56},... | collective-permute-start | bytes 835592 | tf_op jit(solution)/shard_map/ppermute | solution.py:565
  27.6 9.3 %collective-permute-start.11 = (f32[4,17,8,128]{3,2,1,0:T(8,128)S(1)}, f32[4,17,8,128]{3,2,1,0:T(8,128)S(1)}, u32[]{:S(2)}, u32[]{:S(2)}) collective-permute-start(f32[4,17,8,128]{3,2,1,0:T(8,128)S(1)} %get-tuple-element.39), channel_id=1, source_target_pairs={{0,96},{4,36},{8,104},{12,44},{16,112},{20,52},{24,120},{28,60},{3... | collective-permute-start | bytes 835592 | tf_op jit(solution)/shard_map/ppermute | solution.py:565
  30.8 10.0 %collective-permute-start.3 = (f32[4,17,8,128]{3,2,1,0:T(8,128)S(1)}, f32[4,17,8,128]{3,2,1,0:T(8,128)S(1)}, u32[]{:S(2)}, u32[]{:S(2)}) collective-permute-start(f32[4,17,8,128]{3,2,1,0:T(8,128)S(1)} %get-tuple-element.29), channel_id=1, source_target_pairs={{0,120},{4,44},{8,112},{12,36},{16,104},{20,60},{24,96},{28,52},{3... | collective-permute-start | bytes 835592 | tf_op jit(solution)/shard_map/ppermute | solution.py:565
  35.2 8.0 %collective-permute-start.4 = (f32[4,17,8,128]{3,2,1,0:T(8,128)S(1)}, f32[4,17,8,128]{3,2,1,0:T(8,128)S(1)}, u32[]{:S(2)}, u32[]{:S(2)}) collective-permute-start(f32[4,17,8,128]{3,2,1,0:T(8,128)S(1)} %get-tuple-element.30), channel_id=1, source_target_pairs={{0,24},{4,12},{8,16},{12,4},{16,8},{20,28},{24,0},{28,20},{32,56},... | collective-permute-start | bytes 835592 | tf_op jit(solution)/shard_map/ppermute | solution.py:565
  35.6 8.1 %collective-permute-start.5 = (f32[4,17,8,128]{3,2,1,0:T(8,128)S(1)}, f32[4,17,8,128]{3,2,1,0:T(8,128)S(1)}, u32[]{:S(2)}, u32[]{:S(2)}) collective-permute-start(f32[4,17,8,128]{3,2,1,0:T(8,128)S(1)} %get-tuple-element.31), channel_id=1, source_target_pairs={{0,96},{4,36},{8,104},{12,44},{16,112},{20,52},{24,120},{28,60},{3... | collective-permute-start | bytes 835592 | tf_op jit(solution)/shard_map/ppermute | solution.py:565
  44.5 2.4 %collective-permute-start.12 = (f32[1152,128]{1,0:T(8,128)S(1)}, f32[1152,128]{1,0:T(8,128)S(1)}, u32[]{:S(2)}, u32[]{:S(2)}) collective-permute-start(f32[1152,128]{1,0:T(8,128)S(1)} %get-tuple-element.43), channel_id=1, source_target_pairs={{0,4},{4,0},{8,12},{12,8},{16,20},{20,16},{24,28},{28,24},{32,36},... | collective-permute-start | bytes 1769480 | tf_op jit(solution)/shard_map/ppermute | solution.py:608
  66.6 7.4 %collective-permute-start.13 = (f32[8,64,128]{2,1,0:T(8,128)S(1)}, f32[8,64,128]{2,1,0:T(8,128)S(1)}, u32[]{:S(2)}, u32[]{:S(2)}) collective-permute-start(f32[8,64,128]{2,1,0:T(8,128)S(1)} %get-tuple-element.44), channel_id=1, source_target_pairs={{0,1},{1,0},{2,3},{3,2},{4,5},{5,4},{6,7},{7,6},{8,9},{9,8},{10,11... | collective-permute-start | bytes 786440 | tf_op jit(solution)/shard_map/ppermute | solution.py:638
  68.6 9.4 %collective-permute-start.15 = (f32[8,64,128]{2,1,0:T(8,128)S(1)}, f32[8,64,128]{2,1,0:T(8,128)S(1)}, u32[]{:S(2)}, u32[]{:S(2)}) collective-permute-start(f32[8,64,128]{2,1,0:T(8,128)S(1)} %get-tuple-element.45), channel_id=1, source_target_pairs={{0,3},{3,0},{1,2},{2,1},{4,7},{7,4},{5,6},{6,5},{8,11},{11,8},{9,1... | collective-permute-start | bytes 786440 | tf_op jit(solution)/shard_map/ppermute | solution.py:638
  74.0 8.4 %collective-permute-start.14 = (f32[8,64,128]{2,1,0:T(8,128)S(1)}, f32[8,64,128]{2,1,0:T(8,128)S(1)}, u32[]{:S(2)}, u32[]{:S(2)}) collective-permute-start(f32[8,64,128]{2,1,0:T(8,128)S(1)} %add.6.upper_ref), channel_id=1, source_target_pairs={{0,3},{3,0},{1,2},{2,1},{4,7},{7,4},{5,6},{6,5},{8,11},{11,8},{9,1... | collective-permute-start | bytes 786440 | tf_op jit(solution)/shard_map/ppermute | solution.py:642
  78.0 6.5 %collective-permute-start.16 = (f32[8,64,128]{2,1,0:T(8,128)S(1)}, f32[8,64,128]{2,1,0:T(8,128)S(1)}, u32[]{:S(2)}, u32[]{:S(2)}) collective-permute-start(f32[8,64,128]{2,1,0:T(8,128)S(1)} %add.7.lower_ref), channel_id=1, source_target_pairs={{0,1},{1,0},{2,3},{3,2},{4,5},{5,4},{6,7},{7,6},{8,9},{9,8},{10,11... | collective-permute-start | bytes 786440 | tf_op jit(solution)/shard_map/ppermute | solution.py:642

commit v9 on v8

--- a/solution.py
+++ b/solution.py
@@ -122,20 +122,17 @@
     return usable / variance
 
 
-def item_info(var_ref, bits_ref, owner_ref, slot_ref):
+def item_info(block, var_ref, bits_ref, owner_ref, slot_ref):
     exact = lax.Precision.HIGHEST
     lane = lax.broadcasted_iota(jnp.int32, (1, TILE), 1)
     row = lax.broadcasted_iota(jnp.int32, (CELLS, TILE), 0)
     item = lane % TILES_BLK
     cell_row = (item // SIDE) * PER_TILE + lane // (2 * TILES_BLK)
-    columns = None
-    for block in range(2):
-        picked = ((row == cell_row) & ((lane // TILES_BLK) % 2 == block)).astype(f32)
-        term = lax.dot_general(
-            cell_weights(var_ref[block], bits_ref[block]), picked,
-            (((0,), (0,)), ((), ())), precision=exact, preferred_element_type=f32,
-        )
-        columns = term if columns is None else columns + term
+    picked = (row == cell_row).astype(f32)
+    columns = lax.dot_general(
+        cell_weights(var_ref[block], bits_ref[block]), picked,
+        (((0,), (0,)), ((), ())), precision=exact, preferred_element_type=f32,
+    )
     rows = []
     for n in range(PER_TILE):
         chosen = row == (item % SIDE) * PER_TILE + n
@@ -259,30 +256,28 @@
     backward = jnp.concatenate([back_across_ref[:pair], back_across_ref[...]], axis=0)
     spots = [way_to(place_ref[0], piece) for piece in range(CHIPS)]
 
-    def windows(rows):
-        tiles = [image_ref[rows, place:place + TILE] for place in range(0, BLOCK, TILE)]
-        tiles.append(tail_ref[rows, :])
+    def window_of(window, rows):
+        first, shift = ((0, 0), (1, 80), (2, 32))[window]
+        tiles = []
+        for spot in range(first, first + (3 if shift else 2)):
+            tile = tail_ref[rows, :] if spot == SIDE else image_ref[rows, spot * TILE:(spot + 1) * TILE]
+            tiles.append(pltpu.roll(tile, shift, 1) if shift else tile)
+        if not shift:
+            return tiles
         lane = lax.broadcasted_iota(jnp.int32, tiles[0].shape, 1)
-        second = [pltpu.roll(tile, 80, 1) for tile in tiles[1:4]]
-        third = [pltpu.roll(tile, 32, 1) for tile in tiles[2:5]]
-        return (
-            tiles[:2],
-            [jnp.where(lane < 80, second[spot], second[spot + 1]) for spot in range(2)],
-            [jnp.where(lane < 32, third[spot], third[spot + 1]) for spot in range(2)],
-        )
-
-    def halve():
-        tail_ref[:PADDED, :PADDED - BLOCK] = image_ref[:, BLOCK:]
+        return [jnp.where(lane < shift, tiles[spot], tiles[spot + 1]) for spot in range(2)]
+
+    def halve(window):
+        if window == WINDOWS - 1:
+            tail_ref[:PADDED, :PADDED - BLOCK] = image_ref[:, BLOCK:]
         whole = TALL - 16
-        for window, tiles in enumerate(windows(slice(0, whole))):
-            for spot, tile in enumerate(tiles):
-                lanes = slice(spot * TILE, (spot + 1) * TILE)
-                high_ref[window, :whole, lanes], low_ref[window, :whole, lanes] = split(tile)
-        for window, tiles in enumerate(windows(slice(whole, PADDED))):
-            for spot, tile in enumerate(tiles):
-                lanes = slice(spot * TILE, (spot + 1) * TILE)
-                last = jnp.concatenate([tile, jnp.zeros((8, TILE), f32)], axis=0)
-                high_ref[window, whole:, lanes], low_ref[window, whole:, lanes] = split(last)
+        for spot, tile in enumerate(window_of(window, slice(0, whole))):
+            lanes = slice(spot * TILE, (spot + 1) * TILE)
+            high_ref[window, :whole, lanes], low_ref[window, :whole, lanes] = split(tile)
+        for spot, tile in enumerate(window_of(window, slice(whole, PADDED))):
+            lanes = slice(spot * TILE, (spot + 1) * TILE)
+            last = jnp.concatenate([tile, jnp.zeros((8, TILE), f32)], axis=0)
+            high_ref[window, whole:, lanes], low_ref[window, whole:, lanes] = split(last)
 
     def transform_across(window):
         high, low = high_ref[window], low_ref[window]
@@ -297,7 +292,7 @@
         factor_ref[0] = same.reshape(SPAN // 8, 8, pair)
         factor_ref[1] = cross.reshape(SPAN // 8, 8, pair)
         weight_ref[...] = exact_dot(cell_weights(var_ref[block], bits_ref[block]), spread)
-        info = item_info(var_ref, bits_ref, owner_ref, slot_ref)
+        info = item_info(block, var_ref, bits_ref, owner_ref, slot_ref)
         out_ref[:, TILES_BLK] = jnp.broadcast_to(info[None], (CHIPS, INFO, TILE))
 
     def stack(tile):
@@ -363,9 +358,11 @@
             for piece in range(CHIPS):
                 out_ref[spots[piece], item] = weighted[line, piece]
 
-    halve()
+    halve(0)
     transform_across(0)
     prepare()
+    halve(1)
+    halve(2)
     tiles = WINDOWS * SIDE
     for step in range(tiles + 5):
         if step % SIDE == 0 and step // SIDE + 1 < WINDOWS:

time: 85.6 us -> 86.4 us (level)
  Pallas kernels: 16.6 us -> 17.5 us
  transfers between devices with their start and end apart: 17 -> 17, of which waited for: 9 -> 9; matrix products, arithmetic and copies ran while one was open for 0% -> 0% of each run, Pallas kernels for 9% -> 10%
where the time goes in v9:
time: 86.4 us; the launch traced here: 86.1 us
  starting transfers between devices  28.6 us (33%)
  waiting for transfers between devices  19.2 us (22%)
  blocking collectives  19.1 us (22%)
  Pallas kernels  17.5 us (20%)
  local copies, waits for them, and re-layouts  0.96 us (1%)
    ppermute x12, starting transfers between devices, exchange(): lax.ppermute(parts[way], 'visit', phase_partners(phase, way))  19.3 us
    all_to_all x1, blocking collectives, spread_tiles(): lax.all_to_all(pieces, 'visit', 0, 0, axis_index_groups=same_core, tiled=...  19.1 us
    pallas_call x2, Pallas kernels, match_block(): pl.pallas_call(functools.partial(match_kernel, block=block), out_shape=[j...  13.5 us
    ppermute x12, waiting for transfers between devices, exchange(): lax.ppermute(parts[way], 'visit', phase_partners(phase, way))  9.14 us
    ppermute x2, waiting for transfers between devices, local(): terms.extend((half, lax.ppermute(half, 'band', pairings[1 - number])))  5.53 us
    ppermute x2, starting transfers between devices, local(): lax.ppermute(half, 'band', pairings[number])  4.53 us
    ppermute x2, starting transfers between devices, local(): terms.extend((half, lax.ppermute(half, 'band', pairings[1 - number])))  4.03 us
    ppermute x2, waiting for transfers between devices, local(): lax.ppermute(half, 'band', pairings[number])  2.88 us
  transfers between devices with their start and end apart: 17, of which 9 were waited for; matrix products, arithmetic and copies ran while one was open for 0% of the time, Pallas kernels for 10%

profile of v9, /device:TPU:0, one launch (start us, length us, event | category | flops | bytes accessed | tf_op | source)
XLA Modules:
  0.0 86.1 jit_solution(1246531320211264128)
XLA Ops:
  0.6 6.8 %match_block.3 = (f32[4,17,8,128]{3,2,1,0:T(8,128)}, f32[4,17,8,128]{3,2,1,0:T(8,128)}, f32[4,17,8,128]{3,2,1,0:T(8,128)}, f32[4,17,8,128]{3,2,1,0:T(8,128)}) custom-call(s32[1]{0:T(128)} %bitcast.place_ref, s32[1,2]{1,0:T(1,128)} %index_hbm.3, f32[27,64]{1,0:T(8,128)} %bitcast.23, f32[1,2,552,552]{3,2,1,0:T(8,128)} %image_hbm.3, f32[1,2,16,16]{3,2,1,0:T(8,128)} %var_hbm.3, ...), custom_call_target="tpu_custom_call" | custom-call | flops 5242880000 | bytes 3145728 | tf_op jit(solution)/shard_map/match_block/pallas_call | solution.py:393
  7.4 2.7 %collective-permute-start.6 = (f32[4,17,8,128]{3,2,1,0:T(8,128)}, f32[4,17,8,128]{3,2,1,0:T(8,128)S(1)}, u32[]{:S(2)}, u32[]{:S(2)}) collective-permute-start(f32[4,17,8,128]{3,2,1,0:T(8,128)} %get-tuple-element.33), channel_id=1, source_target_pairs={{0,40},{4,124},{8,32},{12,116},{16,56},{20,108},{24,48},{28,100},{... | collective-permute-start | bytes 835592 | tf_op jit(solution)/shard_map/ppermute | solution.py:562
  10.1 0.5 collective-permute-start.7
  10.7 0.4 collective-permute-start.8
  11.0 6.7 %match_block.2 = (f32[4,17,8,128]{3,2,1,0:T(8,128)}, f32[4,17,8,128]{3,2,1,0:T(8,128)}, f32[4,17,8,128]{3,2,1,0:T(8,128)}, f32[4,17,8,128]{3,2,1,0:T(8,128)}) custom-call(s32[1]{0:T(128)} %bitcast.place_ref, s32[1,2]{1,0:T(1,128)} %index_hbm.3, f32[27,64]{1,0:T(8,128)} %bitcast.24, f32[1,2,552,552]{3,2,1,0:T(8,128)} %image_hbm.3, f32[1,2,16,16]{3,2,1,0:T(8,128)} %var_hbm.3, ...), custom_call_target="tpu_custom_call" | custom-call | flops 5242880000 | bytes 3145728 | tf_op jit(solution)/shard_map/match_block/pallas_call | solution.py:393
  17.8 2.7 %collective-permute-start = (f32[4,17,8,128]{3,2,1,0:T(8,128)}, f32[4,17,8,128]{3,2,1,0:T(8,128)S(1)}, u32[]{:S(2)}, u32[]{:S(2)}) collective-permute-start(f32[4,17,8,128]{3,2,1,0:T(8,128)} %get-tuple-element.25), channel_id=1, source_target_pairs={{0,40},{4,124},{8,32},{12,116},{16,56},{20,108},{24,48},{28,100},{... | collective-permute-start | bytes 835592 | tf_op jit(solution)/shard_map/ppermute | solution.py:562
  20.4 0.5 collective-permute-start.1
  21.0 0.4 collective-permute-start.2
  21.5 5.4 %collective-permute-start.9 = (f32[4,17,8,128]{3,2,1,0:T(8,128)S(1)}, f32[4,17,8,128]{3,2,1,0:T(8,128)S(1)}, u32[]{:S(2)}, u32[]{:S(2)}) collective-permute-start(f32[4,17,8,128]{3,2,1,0:T(8,128)S(1)} %get-tuple-element.37), channel_id=1, source_target_pairs={{0,120},{4,44},{8,112},{12,36},{16,104},{20,60},{24,96},{28,52},{3... | collective-permute-start | bytes 835592 | tf_op jit(solution)/shard_map/ppermute | solution.py:562
  26.9 1.0 %copy-done = f32[4,17,8,128]{3,2,1,0:T(8,128)S(1)} copy-done((f32[4,17,8,128]{3,2,1,0:T(8,128)S(1)}, f32[4,17,8,128]{3,2,1,0:T(8,128)}, u32[]{:S(2)}) %copy-start) | copy-done | bytes 278552
  27.9 0.6 collective-permute-start.10
  28.7 2.8 %collective-permute-done.1.refs_2_ = f32[4,17,8,128]{3,2,1,0:T(8,128)S(1)} collective-permute-done((f32[4,17,8,128]{3,2,1,0:T(8,128)}, f32[4,17,8,128]{3,2,1,0:T(8,128)S(1)}, u32[]{:S(2)}, u32[]{:S(2)}) %collective-permute-start.1) | collective-permute-done | bytes 278560 | tf_op jit(solution)/shard_map/ppermute | solution.py:562
  31.6 4.4 %collective-permute-start.3 = (f32[4,17,8,128]{3,2,1,0:T(8,128)S(1)}, f32[4,17,8,128]{3,2,1,0:T(8,128)S(1)}, u32[]{:S(2)}, u32[]{:S(2)}) collective-permute-start(f32[4,17,8,128]{3,2,1,0:T(8,128)S(1)} %get-tuple-element.29), channel_id=1, source_target_pairs={{0,120},{4,44},{8,112},{12,36},{16,104},{20,60},{24,96},{28,52},{3... | collective-permute-start | bytes 835592 | tf_op jit(solution)/shard_map/ppermute | solution.py:562
  36.0 0.5 collective-permute-start.4
  36.5 1.1 %collective-permute-start.5 = (f32[4,17,8,128]{3,2,1,0:T(8,128)S(1)}, f32[4,17,8,128]{3,2,1,0:T(8,128)S(1)}, u32[]{:S(2)}, u32[]{:S(2)}) collective-permute-start(f32[4,17,8,128]{3,2,1,0:T(8,128)S(1)} %get-tuple-element.31), channel_id=1, source_target_pairs={{0,96},{4,36},{8,104},{12,44},{16,112},{20,52},{24,120},{28,60},{3... | collective-permute-start | bytes 835592 | tf_op jit(solution)/shard_map/ppermute | solution.py:562
  37.7 0.6 partial_sums.2
  38.4 3.2 %collective-permute-done.3 = f32[4,17,8,128]{3,2,1,0:T(8,128)S(1)} collective-permute-done((f32[4,17,8,128]{3,2,1,0:T(8,128)S(1)}, f32[4,17,8,128]{3,2,1,0:T(8,128)S(1)}, u32[]{:S(2)}, u32[]{:S(2)}) %collective-permute-start.3) | collective-permute-done | bytes 278560 | tf_op jit(solution)/shard_map/ppermute | solution.py:562
  41.6 2.4 %collective-permute-done.4 = f32[4,17,8,128]{3,2,1,0:T(8,128)S(1)} collective-permute-done((f32[4,17,8,128]{3,2,1,0:T(8,128)S(1)}, f32[4,17,8,128]{3,2,1,0:T(8,128)S(1)}, u32[]{:S(2)}, u32[]{:S(2)}) %collective-permute-start.4) | collective-permute-done | bytes 278560 | tf_op jit(solution)/shard_map/ppermute | solution.py:562
  44.0 0.6 collective-permute-done.5
  44.5 0.7 partial_sums.3
  45.3 0.8 collective-permute-start.12
  46.1 1.6 %collective-permute-done.12.other_ref = f32[1152,128]{1,0:T(8,128)S(1)} collective-permute-done((f32[1152,128]{1,0:T(8,128)S(1)}, f32[1152,128]{1,0:T(8,128)S(1)}, u32[]{:S(2)}, u32[]{:S(2)}) %collective-permute-start.12) | collective-permute-done | bytes 589856 | tf_op jit(solution)/shard_map/ppermute | solution.py:605
  48.0 19.1 %all_to_all.5.part_ref = f32[16,64,128]{2,1,0:T(8,128)S(1)} all-to-all(f32[16,64,128]{2,1,0:T(8,128)S(1)} %bitcast.13), channel_id=1, replica_groups={{0,8,16,24,32,40,48,56,64,72,80,88,96,104,112,120},{4,12,20,28,36,44,52..., dimensions={0} | all-to-all | bytes 1048576 | tf_op jit(solution)/shard_map/all_to_all | solution.py:579
  67.0 0.3 chi.1
  67.4 2.0 %collective-permute-start.13 = (f32[8,64,128]{2,1,0:T(8,128)S(1)}, f32[8,64,128]{2,1,0:T(8,128)S(1)}, u32[]{:S(2)}, u32[]{:S(2)}) collective-permute-start(f32[8,64,128]{2,1,0:T(8,128)S(1)} %get-tuple-element.44), channel_id=1, source_target_pairs={{0,1},{1,0},{2,3},{3,2},{4,5},{5,4},{6,7},{7,6},{8,9},{9,8},{10,11... | collective-permute-start | bytes 786440 | tf_op jit(solution)/shard_map/ppermute | solution.py:635
  69.4 2.5 %collective-permute-start.15 = (f32[8,64,128]{2,1,0:T(8,128)S(1)}, f32[8,64,128]{2,1,0:T(8,128)S(1)}, u32[]{:S(2)}, u32[]{:S(2)}) collective-permute-start(f32[8,64,128]{2,1,0:T(8,128)S(1)} %get-tuple-element.45), channel_id=1, source_target_pairs={{0,3},{3,0},{1,2},{2,1},{4,7},{7,4},{5,6},{6,5},{8,11},{11,8},{9,1... | collective-permute-start | bytes 786440 | tf_op jit(solution)/shard_map/ppermute | solution.py:635
  71.9 2.9 %collective-permute-done.13 = f32[8,64,128]{2,1,0:T(8,128)S(1)} collective-permute-done((f32[8,64,128]{2,1,0:T(8,128)S(1)}, f32[8,64,128]{2,1,0:T(8,128)S(1)}, u32[]{:S(2)}, u32[]{:S(2)}) %collective-permute-start.13) | collective-permute-done | bytes 262176 | tf_op jit(solution)/shard_map/ppermute | solution.py:635
  74.8 3.9 %collective-permute-start.14 = (f32[8,64,128]{2,1,0:T(8,128)S(1)}, f32[8,64,128]{2,1,0:T(8,128)S(1)}, u32[]{:S(2)}, u32[]{:S(2)}) collective-permute-start(f32[8,64,128]{2,1,0:T(8,128)S(1)} %add.6.upper_ref), channel_id=1, source_target_pairs={{0,3},{3,0},{1,2},{2,1},{4,7},{7,4},{5,6},{6,5},{8,11},{11,8},{9,1... | collective-permute-start | bytes 786440 | tf_op jit(solution)/shard_map/ppermute | solution.py:639
  78.9 0.8 image.1
  79.7 3.5 %collective-permute-done.14.more_upper_ref = f32[8,64,128]{2,1,0:T(8,128)S(1)} collective-permute-done((f32[8,64,128]{2,1,0:T(8,128)S(1)}, f32[8,64,128]{2,1,0:T(8,128)S(1)}, u32[]{:S(2)}, u32[]{:S(2)}) %collective-permute-start.14) | collective-permute-done | bytes 262176 | tf_op jit(solution)/shard_map/ppermute | solution.py:639
  83.3 2.0 %collective-permute-done.16.more_lower_ref = f32[8,64,128]{2,1,0:T(8,128)S(1)} collective-permute-done((f32[8,64,128]{2,1,0:T(8,128)S(1)}, f32[8,64,128]{2,1,0:T(8,128)S(1)}, u32[]{:S(2)}, u32[]{:S(2)}) %collective-permute-start.16) | collective-permute-done | bytes 262176 | tf_op jit(solution)/shard_map/ppermute | solution.py:639
  85.3 0.9 detection.1
  (21 shorter events, 1.1 us)
Async XLA Ops:
  7.4 13.5 %collective-permute-start.6 = (f32[4,17,8,128]{3,2,1,0:T(8,128)}, f32[4,17,8,128]{3,2,1,0:T(8,128)S(1)}, u32[]{:S(2)}, u32[]{:S(2)}) collective-permute-start(f32[4,17,8,128]{3,2,1,0:T(8,128)} %get-tuple-element.33), channel_id=1, source_target_pairs={{0,40},{4,124},{8,32},{12,116},{16,56},{20,108},{24,48},{28,100},{... | collective-permute-start | bytes 835592 | tf_op jit(solution)/shard_map/ppermute | solution.py:562
  10.1 11.3 %collective-permute-start.7 = (f32[4,17,8,128]{3,2,1,0:T(8,128)}, f32[4,17,8,128]{3,2,1,0:T(8,128)S(1)}, u32[]{:S(2)}, u32[]{:S(2)}) collective-permute-start(f32[4,17,8,128]{3,2,1,0:T(8,128)} %get-tuple-element.34), channel_id=1, source_target_pairs={{0,8},{4,28},{8,0},{12,20},{16,24},{20,12},{24,16},{28,4},{32,40},... | collective-permute-start | bytes 835592 | tf_op jit(solution)/shard_map/ppermute | solution.py:562
  10.7 10.7 %copy-start.1 = (f32[4,17,8,128]{3,2,1,0:T(8,128)S(1)}, f32[4,17,8,128]{3,2,1,0:T(8,128)}, u32[]{:S(2)}) copy-start(f32[4,17,8,128]{3,2,1,0:T(8,128)} %get-tuple-element.32.part_hbm) | copy-start | bytes 835588
  10.7 10.7 %collective-permute-start.8 = (f32[4,17,8,128]{3,2,1,0:T(8,128)}, f32[4,17,8,128]{3,2,1,0:T(8,128)S(1)}, u32[]{:S(2)}, u32[]{:S(2)}) collective-permute-start(f32[4,17,8,128]{3,2,1,0:T(8,128)} %get-tuple-element.35), channel_id=1, source_target_pairs={{0,32},{4,100},{8,40},{12,108},{16,48},{20,116},{24,56},{28,124},{... | collective-permute-start | bytes 835592 | tf_op jit(solution)/shard_map/ppermute | solution.py:562
  17.8 10.7 %collective-permute-start = (f32[4,17,8,128]{3,2,1,0:T(8,128)}, f32[4,17,8,128]{3,2,1,0:T(8,128)S(1)}, u32[]{:S(2)}, u32[]{:S(2)}) collective-permute-start(f32[4,17,8,128]{3,2,1,0:T(8,128)} %get-tuple-element.25), channel_id=1, source_target_pairs={{0,40},{4,124},{8,32},{12,116},{16,56},{20,108},{24,48},{28,100},{... | collective-permute-start | bytes 835592 | tf_op jit(solution)/shard_map/ppermute | solution.py:562
  20.4 11.1 %collective-permute-start.1 = (f32[4,17,8,128]{3,2,1,0:T(8,128)}, f32[4,17,8,128]{3,2,1,0:T(8,128)S(1)}, u32[]{:S(2)}, u32[]{:S(2)}) collective-permute-start(f32[4,17,8,128]{3,2,1,0:T(8,128)} %get-tuple-element.26), channel_id=1, source_target_pairs={{0,8},{4,28},{8,0},{12,20},{16,24},{20,12},{24,16},{28,4},{32,40},... | collective-permute-start | bytes 835592 | tf_op jit(solution)/shard_map/ppermute | solution.py:562
  21.0 10.6 %collective-permute-start.2 = (f32[4,17,8,128]{3,2,1,0:T(8,128)}, f32[4,17,8,128]{3,2,1,0:T(8,128)S(1)}, u32[]{:S(2)}, u32[]{:S(2)}) collective-permute-start(f32[4,17,8,128]{3,2,1,0:T(8,128)} %get-tuple-element.27), channel_id=1, source_target_pairs={{0,32},{4,100},{8,40},{12,108},{16,48},{20,116},{24,56},{28,124},{... | collective-permute-start | bytes 835592 | tf_op jit(solution)/shard_map/ppermute | solution.py:562
  21.5 15.0 %collective-permute-start.9 = (f32[4,17,8,128]{3,2,1,0:T(8,128)S(1)}, f32[4,17,8,128]{3,2,1,0:T(8,128)S(1)}, u32[]{:S(2)}, u32[]{:S(2)}) collective-permute-start(f32[4,17,8,128]{3,2,1,0:T(8,128)S(1)} %get-tuple-element.37), channel_id=1, source_target_pairs={{0,120},{4,44},{8,112},{12,36},{16,104},{20,60},{24,96},{28,52},{3... | collective-permute-start | bytes 835592 | tf_op jit(solution)/shard_map/ppermute | solution.py:562
  26.9 1.0 %copy-start = (f32[4,17,8,128]{3,2,1,0:T(8,128)S(1)}, f32[4,17,8,128]{3,2,1,0:T(8,128)}, u32[]{:S(2)}) copy-start(f32[4,17,8,128]{3,2,1,0:T(8,128)} %get-tuple-element.24.part_hbm) | copy-start | bytes 835588
  27.9 9.9 %collective-permute-start.10 = (f32[4,17,8,128]{3,2,1,0:T(8,128)S(1)}, f32[4,17,8,128]{3,2,1,0:T(8,128)S(1)}, u32[]{:S(2)}, u32[]{:S(2)}) collective-permute-start(f32[4,17,8,128]{3,2,1,0:T(8,128)S(1)} %get-tuple-element.38), channel_id=1, source_target_pairs={{0,24},{4,12},{8,16},{12,4},{16,8},{20,28},{24,0},{28,20},{32,56},... | collective-permute-start | bytes 835592 | tf_op jit(solution)/shard_map/ppermute | solution.py:562
  28.4 9.3 %collective-permute-start.11 = (f32[4,17,8,128]{3,2,1,0:T(8,128)S(1)}, f32[4,17,8,128]{3,2,1,0:T(8,128)S(1)}, u32[]{:S(2)}, u32[]{:S(2)}) collective-permute-start(f32[4,17,8,128]{3,2,1,0:T(8,128)S(1)} %get-tuple-element.39), channel_id=1, source_target_pairs={{0,96},{4,36},{8,104},{12,44},{16,112},{20,52},{24,120},{28,60},{3... | collective-permute-start | bytes 835592 | tf_op jit(solution)/shard_map/ppermute | solution.py:562
  31.6 10.0 %collective-permute-start.3 = (f32[4,17,8,128]{3,2,1,0:T(8,128)S(1)}, f32[4,17,8,128]{3,2,1,0:T(8,128)S(1)}, u32[]{:S(2)}, u32[]{:S(2)}) collective-permute-start(f32[4,17,8,128]{3,2,1,0:T(8,128)S(1)} %get-tuple-element.29), channel_id=1, source_target_pairs={{0,120},{4,44},{8,112},{12,36},{16,104},{20,60},{24,96},{28,52},{3... | collective-permute-start | bytes 835592 | tf_op jit(solution)/shard_map/ppermute | solution.py:562
  36.0 8.0 %collective-permute-start.4 = (f32[4,17,8,128]{3,2,1,0:T(8,128)S(1)}, f32[4,17,8,128]{3,2,1,0:T(8,128)S(1)}, u32[]{:S(2)}, u32[]{:S(2)}) collective-permute-start(f32[4,17,8,128]{3,2,1,0:T(8,128)S(1)} %get-tuple-element.30), channel_id=1, source_target_pairs={{0,24},{4,12},{8,16},{12,4},{16,8},{20,28},{24,0},{28,20},{32,56},... | collective-permute-start | bytes 835592 | tf_op jit(solution)/shard_map/ppermute | solution.py:562
  36.5 8.1 %collective-permute-start.5 = (f32[4,17,8,128]{3,2,1,0:T(8,128)S(1)}, f32[4,17,8,128]{3,2,1,0:T(8,128)S(1)}, u32[]{:S(2)}, u32[]{:S(2)}) collective-permute-start(f32[4,17,8,128]{3,2,1,0:T(8,128)S(1)} %get-tuple-element.31), channel_id=1, source_target_pairs={{0,96},{4,36},{8,104},{12,44},{16,112},{20,52},{24,120},{28,60},{3... | collective-permute-start | bytes 835592 | tf_op jit(solution)/shard_map/ppermute | solution.py:562
  45.3 2.4 %collective-permute-start.12 = (f32[1152,128]{1,0:T(8,128)S(1)}, f32[1152,128]{1,0:T(8,128)S(1)}, u32[]{:S(2)}, u32[]{:S(2)}) collective-permute-start(f32[1152,128]{1,0:T(8,128)S(1)} %get-tuple-element.43), channel_id=1, source_target_pairs={{0,4},{4,0},{8,12},{12,8},{16,20},{20,16},{24,28},{28,24},{32,36},... | collective-permute-start | bytes 1769480 | tf_op jit(solution)/shard_map/ppermute | solution.py:605
  67.4 7.4 %collective-permute-start.13 = (f32[8,64,128]{2,1,0:T(8,128)S(1)}, f32[8,64,128]{2,1,0:T(8,128)S(1)}, u32[]{:S(2)}, u32[]{:S(2)}) collective-permute-start(f32[8,64,128]{2,1,0:T(8,128)S(1)} %get-tuple-element.44), channel_id=1, source_target_pairs={{0,1},{1,0},{2,3},{3,2},{4,5},{5,4},{6,7},{7,6},{8,9},{9,8},{10,11... | collective-permute-start | bytes 786440 | tf_op jit(solution)/shard_map/ppermute | solution.py:635
  69.4 9.4 %collective-permute-start.15 = (f32[8,64,128]{2,1,0:T(8,128)S(1)}, f32[8,64,128]{2,1,0:T(8,128)S(1)}, u32[]{:S(2)}, u32[]{:S(2)}) collective-permute-start(f32[8,64,128]{2,1,0:T(8,128)S(1)} %get-tuple-element.45), channel_id=1, source_target_pairs={{0,3},{3,0},{1,2},{2,1},{4,7},{7,4},{5,6},{6,5},{8,11},{11,8},{9,1... | collective-permute-start | bytes 786440 | tf_op jit(solution)/shard_map/ppermute | solution.py:635
  74.8 8.4 %collective-permute-start.14 = (f32[8,64,128]{2,1,0:T(8,128)S(1)}, f32[8,64,128]{2,1,0:T(8,128)S(1)}, u32[]{:S(2)}, u32[]{:S(2)}) collective-permute-start(f32[8,64,128]{2,1,0:T(8,128)S(1)} %add.6.upper_ref), channel_id=1, source_target_pairs={{0,3},{3,0},{1,2},{2,1},{4,7},{7,4},{5,6},{6,5},{8,11},{11,8},{9,1... | collective-permute-start | bytes 786440 | tf_op jit(solution)/shard_map/ppermute | solution.py:639
  78.8 6.5 %collective-permute-start.16 = (f32[8,64,128]{2,1,0:T(8,128)S(1)}, f32[8,64,128]{2,1,0:T(8,128)S(1)}, u32[]{:S(2)}, u32[]{:S(2)}) collective-permute-start(f32[8,64,128]{2,1,0:T(8,128)S(1)} %add.7.lower_ref), channel_id=1, source_target_pairs={{0,1},{1,0},{2,3},{3,2},{4,5},{5,4},{6,7},{7,6},{8,9},{9,8},{10,11... | collective-permute-start | bytes 786440 | tf_op jit(solution)/shard_map/ppermute | solution.py:639

commit v10 on v8

--- a/solution.py
+++ b/solution.py
@@ -69,7 +69,7 @@
     down[:SPAN] = by_row
     back_down = by_row.T[:TILE] * (2 / SPAN)
 
-    def three(matrix, width=512):
+    def three(matrix, width):
         high, low = as_halves(matrix)
         rest = np.zeros((matrix.shape[0], width - 3 * matrix.shape[1]), bf16)
         return np.concatenate([high, high, low, rest], axis=1)
@@ -78,10 +78,15 @@
     cross = np.zeros((SPAN + 8, TAPS))
     same[spot, :KSIZE] = same[spot + 4, :KSIZE] = cosine[:, :KSIZE]
     cross[spot, :KSIZE], cross[spot + 4, :KSIZE] = sine[:, :KSIZE], -sine[:, :KSIZE]
+    def against(matrix):
+        high, low = as_halves(matrix)
+        zeros = np.zeros((matrix.shape[0], 8), bf16)
+        return np.concatenate([high, low[:, SPAN - 8:], high, zeros, low[:, :SPAN - 8]], axis=1)
+
     return (
         np.concatenate(as_halves(by_lane.T), axis=0),
-        three(down),
-        three(back_down),
+        against(down),
+        against(back_down),
         np.concatenate(as_halves(back_across), axis=0),
         np.concatenate([three(same, 256), three(cross, 256)], axis=0),
         np.concatenate([as_halves(along)[part] for part in (0, 0, 1)], axis=0),
@@ -175,13 +180,18 @@
     )
 
 
-def stacked_halves(value):
+def store_halves(halves_ref, tile, first, value):
     high = value.astype(bf16).astype(f32)
-    return jnp.concatenate([high, value - high], axis=0).astype(bf16)
+    low = value - high
+    if value.shape[0] < 16:
+        high = jnp.concatenate([high, high], axis=0)
+        low = jnp.concatenate([low, jnp.zeros_like(low)], axis=0)
+    halves_ref[tile, first:first + 16, :] = high.astype(bf16)
+    halves_ref[tile, SPAN + 8 + first:SPAN + 8 + first + 16, :] = low.astype(bf16)
 
 
 def against_halves(matrix, halves_ref):
-    rows = jnp.concatenate([halves_ref[...], halves_ref[:SPAN + 8, :]], axis=0)
+    rows = jnp.concatenate([halves_ref[...], halves_ref[:SPAN - 8, :]], axis=0)
     return jnp.dot(matrix, rows, preferred_element_type=f32)
 
 
@@ -274,10 +284,12 @@
     def halve():
         tail_ref[:PADDED, :PADDED - BLOCK] = image_ref[:, BLOCK:]
         whole = TALL - 16
-        for window, tiles in enumerate(windows(slice(0, whole))):
-            for spot, tile in enumerate(tiles):
-                lanes = slice(spot * TILE, (spot + 1) * TILE)
-                high_ref[window, :whole, lanes], low_ref[window, :whole, lanes] = split(tile)
+        for first in range(0, whole, 32):
+            rows = slice(first, first + 32)
+            for window, tiles in enumerate(windows(rows)):
+                for spot, tile in enumerate(tiles):
+                    lanes = slice(spot * TILE, (spot + 1) * TILE)
+                    high_ref[window, rows, lanes], low_ref[window, rows, lanes] = split(tile)
         for window, tiles in enumerate(windows(slice(whole, PADDED))):
             for spot, tile in enumerate(tiles):
                 lanes = slice(spot * TILE, (spot + 1) * TILE)
@@ -301,25 +313,30 @@
         out_ref[:, TILES_BLK] = jnp.broadcast_to(info[None], (CHIPS, INFO, TILE))
 
     def stack(tile):
-        column, line = divmod(tile, SIDE)
-        stack_ref[tile] = stacked_halves(wave_ref[column, line * TILE:line * TILE + SPAN, :])
+        window, line = divmod(tile, SIDE)
+        for first in range(0, SPAN, 16):
+            begin, end = line * TILE + first, line * TILE + min(first + 16, SPAN)
+            store_halves(stack_ref, tile, first, wave_ref[window, begin:end, :])
 
     def transform_down(tile):
         turn_ref[tile] = against_halves(down_ref[...], stack_ref.at[tile])
 
     def multiply(tile):
-        wave = turn_ref[tile, :SPAN].reshape(SPAN // 8, 8, pair)
-        turned = pltpu.roll(wave, 4, 1)
-        wave_c, wave_s = wave[..., :TILE], wave[..., TILE:]
-        turned_c, turned_s = turned[..., :TILE], turned[..., TILE:]
-        same_c, same_s = factor_ref[0, :, :, :TILE], factor_ref[0, :, :, TILE:]
-        cross_c, cross_s = factor_ref[1, :, :, :TILE], factor_ref[1, :, :, TILE:]
-        result_c = wave_c * same_c + turned_c * cross_c - wave_s * same_s - turned_s * cross_s
-        result_s = wave_s * same_c + turned_s * cross_c + wave_c * same_s + turned_c * cross_s
-        result = jnp.concatenate(
-            [result_c.reshape(SPAN, TILE), result_s.reshape(SPAN, TILE)], axis=1
-        )
-        result_ref[tile] = stacked_halves(result)
+        for first in range(0, SPAN, 16):
+            end = min(first + 16, SPAN)
+            groups = slice(first // 8, end // 8)
+            wave = turn_ref[tile, first:end, :].reshape((end - first) // 8, 8, pair)
+            turned = pltpu.roll(wave, 4, 1)
+            wave_c, wave_s = wave[..., :TILE], wave[..., TILE:]
+            turned_c, turned_s = turned[..., :TILE], turned[..., TILE:]
+            same_c, same_s = factor_ref[0, groups, :, :TILE], factor_ref[0, groups, :, TILE:]
+            cross_c, cross_s = factor_ref[1, groups, :, :TILE], factor_ref[1, groups, :, TILE:]
+            result_c = wave_c * same_c + turned_c * cross_c - wave_s * same_s - turned_s * cross_s
+            result_s = wave_s * same_c + turned_s * cross_c + wave_c * same_s + turned_c * cross_s
+            result = jnp.concatenate(
+                [result_c.reshape(end - first, TILE), result_s.reshape(end - first, TILE)], axis=1
+            )
+            store_halves(result_ref, tile, first, result)
 
     def back_down(tile):
         column, line = divmod(tile, SIDE)
@@ -414,9 +431,9 @@
             pltpu.VMEM((WINDOWS, TALL, WIDTH), bf16),
             pltpu.VMEM((WINDOWS, TALL, WIDTH), bf16),
             pltpu.VMEM((WINDOWS, TALL, WIDTH), f32),
-            pltpu.VMEM((WINDOWS * SIDE, 2 * SPAN, WIDTH), bf16),
+            pltpu.VMEM((WINDOWS * SIDE, 2 * SPAN + 16, WIDTH), bf16),
             pltpu.VMEM((WINDOWS * SIDE, SPAN + 8, WIDTH), f32),
-            pltpu.VMEM((WINDOWS * SIDE, 2 * SPAN, WIDTH), bf16),
+            pltpu.VMEM((WINDOWS * SIDE, 2 * SPAN + 16, WIDTH), bf16),
             pltpu.VMEM((WINDOWS, BLOCK, 2 * WIDTH), bf16),
             pltpu.VMEM((WINDOWS, BLOCK, WIDTH), f32),
             pltpu.VMEM((2, SPAN // 8, 8, 2 * TILE), f32),

time: 85.6 us -> 85.5 us (level)
  no operation moved by 1% of the time
where the time goes in v10:
time: 85.5 us; the launch traced here: 85.3 us
  starting transfers between devices  28.6 us (33%)
  waiting for transfers between devices  19.2 us (22%)
  blocking collectives  19.1 us (22%)
  Pallas kernels  16.6 us (19%)
  local copies, waits for them, and re-layouts  0.96 us (1%)
    ppermute x12, starting transfers between devices, exchange(): lax.ppermute(parts[way], 'visit', phase_partners(phase, way))  19.3 us
    all_to_all x1, blocking collectives, spread_tiles(): lax.all_to_all(pieces, 'visit', 0, 0, axis_index_groups=same_core, tiled=...  19.1 us
    pallas_call x2, Pallas kernels, match_block(): pl.pallas_call(functools.partial(match_kernel, block=block), out_shape=[j...  12.7 us
    ppermute x12, waiting for transfers between devices, exchange(): lax.ppermute(parts[way], 'visit', phase_partners(phase, way))  9.13 us
    ppermute x2, waiting for transfers between devices, local(): terms.extend((half, lax.ppermute(half, 'band', pairings[1 - number])))  5.53 us
    ppermute x2, starting transfers between devices, local(): lax.ppermute(half, 'band', pairings[number])  4.52 us
    ppermute x2, starting transfers between devices, local(): terms.extend((half, lax.ppermute(half, 'band', pairings[1 - number])))  4.03 us
    ppermute x2, waiting for transfers between devices, local(): lax.ppermute(half, 'band', pairings[number])  2.89 us
  transfers between devices with their start and end apart: 17, of which 9 were waited for; matrix products, arithmetic and copies ran while one was open for 0% of the time, Pallas kernels for 9%

profile of v10, /device:TPU:0, one launch (start us, length us, event | category | flops | bytes accessed | tf_op | source)
XLA Modules:
  0.0 85.3 jit_solution(2104474790995342775)
XLA Ops:
  0.6 6.4 %match_block.3 = (f32[4,17,8,128]{3,2,1,0:T(8,128)}, f32[4,17,8,128]{3,2,1,0:T(8,128)}, f32[4,17,8,128]{3,2,1,0:T(8,128)}, f32[4,17,8,128]{3,2,1,0:T(8,128)}) custom-call(s32[1]{0:T(128)} %bitcast.place_ref, s32[1,2]{1,0:T(1,128)} %index_hbm.3, f32[27,64]{1,0:T(8,128)} %bitcast.23, f32[1,2,552,552]{3,2,1,0:T(8,128)} %image_hbm.3, f32[1,2,16,16]{3,2,1,0:T(8,128)} %var_hbm.3, ...), custom_call_target="tpu_custom_call" | custom-call | flops 5242880000 | bytes 3145728 | tf_op jit(solution)/shard_map/match_block/pallas_call | solution.py:413
  7.0 2.7 %collective-permute-start.6 = (f32[4,17,8,128]{3,2,1,0:T(8,128)}, f32[4,17,8,128]{3,2,1,0:T(8,128)S(1)}, u32[]{:S(2)}, u32[]{:S(2)}) collective-permute-start(f32[4,17,8,128]{3,2,1,0:T(8,128)} %get-tuple-element.33), channel_id=1, source_target_pairs={{0,40},{4,124},{8,32},{12,116},{16,56},{20,108},{24,48},{28,100},{... | collective-permute-start | bytes 835592 | tf_op jit(solution)/shard_map/ppermute | solution.py:582
  9.7 0.5 collective-permute-start.7
  10.2 0.4 collective-permute-start.8
  10.6 6.3 %match_block.2 = (f32[4,17,8,128]{3,2,1,0:T(8,128)}, f32[4,17,8,128]{3,2,1,0:T(8,128)}, f32[4,17,8,128]{3,2,1,0:T(8,128)}, f32[4,17,8,128]{3,2,1,0:T(8,128)}) custom-call(s32[1]{0:T(128)} %bitcast.place_ref, s32[1,2]{1,0:T(1,128)} %index_hbm.3, f32[27,64]{1,0:T(8,128)} %bitcast.24, f32[1,2,552,552]{3,2,1,0:T(8,128)} %image_hbm.3, f32[1,2,16,16]{3,2,1,0:T(8,128)} %var_hbm.3, ...), custom_call_target="tpu_custom_call" | custom-call | flops 5242880000 | bytes 3145728 | tf_op jit(solution)/shard_map/match_block/pallas_call | solution.py:413
  16.9 2.7 %collective-permute-start = (f32[4,17,8,128]{3,2,1,0:T(8,128)}, f32[4,17,8,128]{3,2,1,0:T(8,128)S(1)}, u32[]{:S(2)}, u32[]{:S(2)}) collective-permute-start(f32[4,17,8,128]{3,2,1,0:T(8,128)} %get-tuple-element.25), channel_id=1, source_target_pairs={{0,40},{4,124},{8,32},{12,116},{16,56},{20,108},{24,48},{28,100},{... | collective-permute-start | bytes 835592 | tf_op jit(solution)/shard_map/ppermute | solution.py:582
  19.6 0.5 collective-permute-start.1
  20.1 0.4 collective-permute-start.2
  20.6 5.4 %collective-permute-start.9 = (f32[4,17,8,128]{3,2,1,0:T(8,128)S(1)}, f32[4,17,8,128]{3,2,1,0:T(8,128)S(1)}, u32[]{:S(2)}, u32[]{:S(2)}) collective-permute-start(f32[4,17,8,128]{3,2,1,0:T(8,128)S(1)} %get-tuple-element.37), channel_id=1, source_target_pairs={{0,120},{4,44},{8,112},{12,36},{16,104},{20,60},{24,96},{28,52},{3... | collective-permute-start | bytes 835592 | tf_op jit(solution)/shard_map/ppermute | solution.py:582
  26.0 1.0 %copy-done = f32[4,17,8,128]{3,2,1,0:T(8,128)S(1)} copy-done((f32[4,17,8,128]{3,2,1,0:T(8,128)S(1)}, f32[4,17,8,128]{3,2,1,0:T(8,128)}, u32[]{:S(2)}) %copy-start) | copy-done | bytes 278552
  27.0 0.6 collective-permute-start.10
  27.8 2.8 %collective-permute-done.1.refs_2_ = f32[4,17,8,128]{3,2,1,0:T(8,128)S(1)} collective-permute-done((f32[4,17,8,128]{3,2,1,0:T(8,128)}, f32[4,17,8,128]{3,2,1,0:T(8,128)S(1)}, u32[]{:S(2)}, u32[]{:S(2)}) %collective-permute-start.1) | collective-permute-done | bytes 278560 | tf_op jit(solution)/shard_map/ppermute | solution.py:582
  30.8 4.4 %collective-permute-start.3 = (f32[4,17,8,128]{3,2,1,0:T(8,128)S(1)}, f32[4,17,8,128]{3,2,1,0:T(8,128)S(1)}, u32[]{:S(2)}, u32[]{:S(2)}) collective-permute-start(f32[4,17,8,128]{3,2,1,0:T(8,128)S(1)} %get-tuple-element.29), channel_id=1, source_target_pairs={{0,120},{4,44},{8,112},{12,36},{16,104},{20,60},{24,96},{28,52},{3... | collective-permute-start | bytes 835592 | tf_op jit(solution)/shard_map/ppermute | solution.py:582
  35.1 0.5 collective-permute-start.4
  35.6 1.1 %collective-permute-start.5 = (f32[4,17,8,128]{3,2,1,0:T(8,128)S(1)}, f32[4,17,8,128]{3,2,1,0:T(8,128)S(1)}, u32[]{:S(2)}, u32[]{:S(2)}) collective-permute-start(f32[4,17,8,128]{3,2,1,0:T(8,128)S(1)} %get-tuple-element.31), channel_id=1, source_target_pairs={{0,96},{4,36},{8,104},{12,44},{16,112},{20,52},{24,120},{28,60},{3... | collective-permute-start | bytes 835592 | tf_op jit(solution)/shard_map/ppermute | solution.py:582
  36.9 0.6 partial_sums.2
  37.5 3.2 %collective-permute-done.3 = f32[4,17,8,128]{3,2,1,0:T(8,128)S(1)} collective-permute-done((f32[4,17,8,128]{3,2,1,0:T(8,128)S(1)}, f32[4,17,8,128]{3,2,1,0:T(8,128)S(1)}, u32[]{:S(2)}, u32[]{:S(2)}) %collective-permute-start.3) | collective-permute-done | bytes 278560 | tf_op jit(solution)/shard_map/ppermute | solution.py:582
  40.7 2.4 %collective-permute-done.4 = f32[4,17,8,128]{3,2,1,0:T(8,128)S(1)} collective-permute-done((f32[4,17,8,128]{3,2,1,0:T(8,128)S(1)}, f32[4,17,8,128]{3,2,1,0:T(8,128)S(1)}, u32[]{:S(2)}, u32[]{:S(2)}) %collective-permute-start.4) | collective-permute-done | bytes 278560 | tf_op jit(solution)/shard_map/ppermute | solution.py:582
  43.1 0.6 collective-permute-done.5
  43.7 0.7 partial_sums.3
  44.4 0.8 collective-permute-start.12
  45.2 1.6 %collective-permute-done.12.other_ref = f32[1152,128]{1,0:T(8,128)S(1)} collective-permute-done((f32[1152,128]{1,0:T(8,128)S(1)}, f32[1152,128]{1,0:T(8,128)S(1)}, u32[]{:S(2)}, u32[]{:S(2)}) %collective-permute-start.12) | collective-permute-done | bytes 589856 | tf_op jit(solution)/shard_map/ppermute | solution.py:625
  47.1 19.1 %all_to_all.5.part_ref = f32[16,64,128]{2,1,0:T(8,128)S(1)} all-to-all(f32[16,64,128]{2,1,0:T(8,128)S(1)} %bitcast.13), channel_id=1, replica_groups={{0,8,16,24,32,40,48,56,64,72,80,88,96,104,112,120},{4,12,20,28,36,44,52..., dimensions={0} | all-to-all | bytes 1048576 | tf_op jit(solution)/shard_map/all_to_all | solution.py:599
  66.2 0.3 chi.1
  66.6 2.0 %collective-permute-start.13 = (f32[8,64,128]{2,1,0:T(8,128)S(1)}, f32[8,64,128]{2,1,0:T(8,128)S(1)}, u32[]{:S(2)}, u32[]{:S(2)}) collective-permute-start(f32[8,64,128]{2,1,0:T(8,128)S(1)} %get-tuple-element.44), channel_id=1, source_target_pairs={{0,1},{1,0},{2,3},{3,2},{4,5},{5,4},{6,7},{7,6},{8,9},{9,8},{10,11... | collective-permute-start | bytes 786440 | tf_op jit(solution)/shard_map/ppermute | solution.py:655
  68.5 2.5 %collective-permute-start.15 = (f32[8,64,128]{2,1,0:T(8,128)S(1)}, f32[8,64,128]{2,1,0:T(8,128)S(1)}, u32[]{:S(2)}, u32[]{:S(2)}) collective-permute-start(f32[8,64,128]{2,1,0:T(8,128)S(1)} %get-tuple-element.45), channel_id=1, source_target_pairs={{0,3},{3,0},{1,2},{2,1},{4,7},{7,4},{5,6},{6,5},{8,11},{11,8},{9,1... | collective-permute-start | bytes 786440 | tf_op jit(solution)/shard_map/ppermute | solution.py:655
  71.1 2.9 %collective-permute-done.13 = f32[8,64,128]{2,1,0:T(8,128)S(1)} collective-permute-done((f32[8,64,128]{2,1,0:T(8,128)S(1)}, f32[8,64,128]{2,1,0:T(8,128)S(1)}, u32[]{:S(2)}, u32[]{:S(2)}) %collective-permute-start.13) | collective-permute-done | bytes 262176 | tf_op jit(solution)/shard_map/ppermute | solution.py:655
  74.0 3.9 %collective-permute-start.14 = (f32[8,64,128]{2,1,0:T(8,128)S(1)}, f32[8,64,128]{2,1,0:T(8,128)S(1)}, u32[]{:S(2)}, u32[]{:S(2)}) collective-permute-start(f32[8,64,128]{2,1,0:T(8,128)S(1)} %add.6.upper_ref), channel_id=1, source_target_pairs={{0,3},{3,0},{1,2},{2,1},{4,7},{7,4},{5,6},{6,5},{8,11},{11,8},{9,1... | collective-permute-start | bytes 786440 | tf_op jit(solution)/shard_map/ppermute | solution.py:659
  78.1 0.8 image.1
  78.9 3.5 %collective-permute-done.14.more_upper_ref = f32[8,64,128]{2,1,0:T(8,128)S(1)} collective-permute-done((f32[8,64,128]{2,1,0:T(8,128)S(1)}, f32[8,64,128]{2,1,0:T(8,128)S(1)}, u32[]{:S(2)}, u32[]{:S(2)}) %collective-permute-start.14) | collective-permute-done | bytes 262176 | tf_op jit(solution)/shard_map/ppermute | solution.py:659
  82.4 2.0 %collective-permute-done.16.more_lower_ref = f32[8,64,128]{2,1,0:T(8,128)S(1)} collective-permute-done((f32[8,64,128]{2,1,0:T(8,128)S(1)}, f32[8,64,128]{2,1,0:T(8,128)S(1)}, u32[]{:S(2)}, u32[]{:S(2)}) %collective-permute-start.16) | collective-permute-done | bytes 262176 | tf_op jit(solution)/shard_map/ppermute | solution.py:659
  84.4 0.9 %detection.1 = f32[8,128,128]{2,1,0:T(8,128)} custom-call(f32[8,64,128]{2,1,0:T(8,128)S(1)} %add.6.upper_ref, f32[8,64,128]{2,1,0:T(8,128)S(1)} %collective-permute-done.14.more_upper_ref, f32[8,64,128]{2,1,0:T(8,128)S(1)} %add.7.lower_ref, f32[8,64,128]{2,1,0:T(8,128)S(1)} %collective-permute-done.16.more_lower_ref), custom_call_target="tpu_custom_call" | custom-call | tf_op jit(solution)/shard_map/detection/pallas_call | solution.py:660
  (21 shorter events, 1.1 us)
Async XLA Ops:
  7.0 13.1 %collective-permute-start.6 = (f32[4,17,8,128]{3,2,1,0:T(8,128)}, f32[4,17,8,128]{3,2,1,0:T(8,128)S(1)}, u32[]{:S(2)}, u32[]{:S(2)}) collective-permute-start(f32[4,17,8,128]{3,2,1,0:T(8,128)} %get-tuple-element.33), channel_id=1, source_target_pairs={{0,40},{4,124},{8,32},{12,116},{16,56},{20,108},{24,48},{28,100},{... | collective-permute-start | bytes 835592 | tf_op jit(solution)/shard_map/ppermute | solution.py:582
  9.7 10.9 %collective-permute-start.7 = (f32[4,17,8,128]{3,2,1,0:T(8,128)}, f32[4,17,8,128]{3,2,1,0:T(8,128)S(1)}, u32[]{:S(2)}, u32[]{:S(2)}) collective-permute-start(f32[4,17,8,128]{3,2,1,0:T(8,128)} %get-tuple-element.34), channel_id=1, source_target_pairs={{0,8},{4,28},{8,0},{12,20},{16,24},{20,12},{24,16},{28,4},{32,40},... | collective-permute-start | bytes 835592 | tf_op jit(solution)/shard_map/ppermute | solution.py:582
  10.2 10.3 %copy-start.1 = (f32[4,17,8,128]{3,2,1,0:T(8,128)S(1)}, f32[4,17,8,128]{3,2,1,0:T(8,128)}, u32[]{:S(2)}) copy-start(f32[4,17,8,128]{3,2,1,0:T(8,128)} %get-tuple-element.32.part_hbm) | copy-start | bytes 835588
  10.2 10.3 %collective-permute-start.8 = (f32[4,17,8,128]{3,2,1,0:T(8,128)}, f32[4,17,8,128]{3,2,1,0:T(8,128)S(1)}, u32[]{:S(2)}, u32[]{:S(2)}) collective-permute-start(f32[4,17,8,128]{3,2,1,0:T(8,128)} %get-tuple-element.35), channel_id=1, source_target_pairs={{0,32},{4,100},{8,40},{12,108},{16,48},{20,116},{24,56},{28,124},{... | collective-permute-start | bytes 835592 | tf_op jit(solution)/shard_map/ppermute | solution.py:582
  16.9 10.7 %collective-permute-start = (f32[4,17,8,128]{3,2,1,0:T(8,128)}, f32[4,17,8,128]{3,2,1,0:T(8,128)S(1)}, u32[]{:S(2)}, u32[]{:S(2)}) collective-permute-start(f32[4,17,8,128]{3,2,1,0:T(8,128)} %get-tuple-element.25), channel_id=1, source_target_pairs={{0,40},{4,124},{8,32},{12,116},{16,56},{20,108},{24,48},{28,100},{... | collective-permute-start | bytes 835592 | tf_op jit(solution)/shard_map/ppermute | solution.py:582
  19.6 11.1 %collective-permute-start.1 = (f32[4,17,8,128]{3,2,1,0:T(8,128)}, f32[4,17,8,128]{3,2,1,0:T(8,128)S(1)}, u32[]{:S(2)}, u32[]{:S(2)}) collective-permute-start(f32[4,17,8,128]{3,2,1,0:T(8,128)} %get-tuple-element.26), channel_id=1, source_target_pairs={{0,8},{4,28},{8,0},{12,20},{16,24},{20,12},{24,16},{28,4},{32,40},... | collective-permute-start | bytes 835592 | tf_op jit(solution)/shard_map/ppermute | solution.py:582
  20.1 10.6 %collective-permute-start.2 = (f32[4,17,8,128]{3,2,1,0:T(8,128)}, f32[4,17,8,128]{3,2,1,0:T(8,128)S(1)}, u32[]{:S(2)}, u32[]{:S(2)}) collective-permute-start(f32[4,17,8,128]{3,2,1,0:T(8,128)} %get-tuple-element.27), channel_id=1, source_target_pairs={{0,32},{4,100},{8,40},{12,108},{16,48},{20,116},{24,56},{28,124},{... | collective-permute-start | bytes 835592 | tf_op jit(solution)/shard_map/ppermute | solution.py:582
  20.6 15.0 %collective-permute-start.9 = (f32[4,17,8,128]{3,2,1,0:T(8,128)S(1)}, f32[4,17,8,128]{3,2,1,0:T(8,128)S(1)}, u32[]{:S(2)}, u32[]{:S(2)}) collective-permute-start(f32[4,17,8,128]{3,2,1,0:T(8,128)S(1)} %get-tuple-element.37), channel_id=1, source_target_pairs={{0,120},{4,44},{8,112},{12,36},{16,104},{20,60},{24,96},{28,52},{3... | collective-permute-start | bytes 835592 | tf_op jit(solution)/shard_map/ppermute | solution.py:582
  26.0 1.0 %copy-start = (f32[4,17,8,128]{3,2,1,0:T(8,128)S(1)}, f32[4,17,8,128]{3,2,1,0:T(8,128)}, u32[]{:S(2)}) copy-start(f32[4,17,8,128]{3,2,1,0:T(8,128)} %get-tuple-element.24.part_hbm) | copy-start | bytes 835588
  27.0 9.9 %collective-permute-start.10 = (f32[4,17,8,128]{3,2,1,0:T(8,128)S(1)}, f32[4,17,8,128]{3,2,1,0:T(8,128)S(1)}, u32[]{:S(2)}, u32[]{:S(2)}) collective-permute-start(f32[4,17,8,128]{3,2,1,0:T(8,128)S(1)} %get-tuple-element.38), channel_id=1, source_target_pairs={{0,24},{4,12},{8,16},{12,4},{16,8},{20,28},{24,0},{28,20},{32,56},... | collective-permute-start | bytes 835592 | tf_op jit(solution)/shard_map/ppermute | solution.py:582
  27.6 9.3 %collective-permute-start.11 = (f32[4,17,8,128]{3,2,1,0:T(8,128)S(1)}, f32[4,17,8,128]{3,2,1,0:T(8,128)S(1)}, u32[]{:S(2)}, u32[]{:S(2)}) collective-permute-start(f32[4,17,8,128]{3,2,1,0:T(8,128)S(1)} %get-tuple-element.39), channel_id=1, source_target_pairs={{0,96},{4,36},{8,104},{12,44},{16,112},{20,52},{24,120},{28,60},{3... | collective-permute-start | bytes 835592 | tf_op jit(solution)/shard_map/ppermute | solution.py:582
  30.8 10.0 %collective-permute-start.3 = (f32[4,17,8,128]{3,2,1,0:T(8,128)S(1)}, f32[4,17,8,128]{3,2,1,0:T(8,128)S(1)}, u32[]{:S(2)}, u32[]{:S(2)}) collective-permute-start(f32[4,17,8,128]{3,2,1,0:T(8,128)S(1)} %get-tuple-element.29), channel_id=1, source_target_pairs={{0,120},{4,44},{8,112},{12,36},{16,104},{20,60},{24,96},{28,52},{3... | collective-permute-start | bytes 835592 | tf_op jit(solution)/shard_map/ppermute | solution.py:582
  35.1 8.0 %collective-permute-start.4 = (f32[4,17,8,128]{3,2,1,0:T(8,128)S(1)}, f32[4,17,8,128]{3,2,1,0:T(8,128)S(1)}, u32[]{:S(2)}, u32[]{:S(2)}) collective-permute-start(f32[4,17,8,128]{3,2,1,0:T(8,128)S(1)} %get-tuple-element.30), channel_id=1, source_target_pairs={{0,24},{4,12},{8,16},{12,4},{16,8},{20,28},{24,0},{28,20},{32,56},... | collective-permute-start | bytes 835592 | tf_op jit(solution)/shard_map/ppermute | solution.py:582
  35.6 8.1 %collective-permute-start.5 = (f32[4,17,8,128]{3,2,1,0:T(8,128)S(1)}, f32[4,17,8,128]{3,2,1,0:T(8,128)S(1)}, u32[]{:S(2)}, u32[]{:S(2)}) collective-permute-start(f32[4,17,8,128]{3,2,1,0:T(8,128)S(1)} %get-tuple-element.31), channel_id=1, source_target_pairs={{0,96},{4,36},{8,104},{12,44},{16,112},{20,52},{24,120},{28,60},{3... | collective-permute-start | bytes 835592 | tf_op jit(solution)/shard_map/ppermute | solution.py:582
  44.4 2.4 %collective-permute-start.12 = (f32[1152,128]{1,0:T(8,128)S(1)}, f32[1152,128]{1,0:T(8,128)S(1)}, u32[]{:S(2)}, u32[]{:S(2)}) collective-permute-start(f32[1152,128]{1,0:T(8,128)S(1)} %get-tuple-element.43), channel_id=1, source_target_pairs={{0,4},{4,0},{8,12},{12,8},{16,20},{20,16},{24,28},{28,24},{32,36},... | collective-permute-start | bytes 1769480 | tf_op jit(solution)/shard_map/ppermute | solution.py:625
  66.6 7.4 %collective-permute-start.13 = (f32[8,64,128]{2,1,0:T(8,128)S(1)}, f32[8,64,128]{2,1,0:T(8,128)S(1)}, u32[]{:S(2)}, u32[]{:S(2)}) collective-permute-start(f32[8,64,128]{2,1,0:T(8,128)S(1)} %get-tuple-element.44), channel_id=1, source_target_pairs={{0,1},{1,0},{2,3},{3,2},{4,5},{5,4},{6,7},{7,6},{8,9},{9,8},{10,11... | collective-permute-start | bytes 786440 | tf_op jit(solution)/shard_map/ppermute | solution.py:655
  68.5 9.4 %collective-permute-start.15 = (f32[8,64,128]{2,1,0:T(8,128)S(1)}, f32[8,64,128]{2,1,0:T(8,128)S(1)}, u32[]{:S(2)}, u32[]{:S(2)}) collective-permute-start(f32[8,64,128]{2,1,0:T(8,128)S(1)} %get-tuple-element.45), channel_id=1, source_target_pairs={{0,3},{3,0},{1,2},{2,1},{4,7},{7,4},{5,6},{6,5},{8,11},{11,8},{9,1... | collective-permute-start | bytes 786440 | tf_op jit(solution)/shard_map/ppermute | solution.py:655
  74.0 8.4 %collective-permute-start.14 = (f32[8,64,128]{2,1,0:T(8,128)S(1)}, f32[8,64,128]{2,1,0:T(8,128)S(1)}, u32[]{:S(2)}, u32[]{:S(2)}) collective-permute-start(f32[8,64,128]{2,1,0:T(8,128)S(1)} %add.6.upper_ref), channel_id=1, source_target_pairs={{0,3},{3,0},{1,2},{2,1},{4,7},{7,4},{5,6},{6,5},{8,11},{11,8},{9,1... | collective-permute-start | bytes 786440 | tf_op jit(solution)/shard_map/ppermute | solution.py:659
  78.0 6.5 %collective-permute-start.16 = (f32[8,64,128]{2,1,0:T(8,128)S(1)}, f32[8,64,128]{2,1,0:T(8,128)S(1)}, u32[]{:S(2)}, u32[]{:S(2)}) collective-permute-start(f32[8,64,128]{2,1,0:T(8,128)S(1)} %add.7.lower_ref), channel_id=1, source_target_pairs={{0,1},{1,0},{2,3},{3,2},{4,5},{5,4},{6,7},{7,6},{8,9},{9,8},{10,11... | collective-permute-start | bytes 786440 | tf_op jit(solution)/shard_map/ppermute | solution.py:659

commit v11 on v10

--- a/solution.py
+++ b/solution.py
@@ -238,12 +238,12 @@
     copies = [
         pltpu.make_async_copy(source, goal, sems.at[number])
         for number, (source, goal) in enumerate((
+            (image_hbm.at[0, block], image_ref),
+            (across_hbm, across_ref),
             (index_hbm, index_ref),
             (table_hbm, table_ref),
             (down_taps_hbm, down_taps_ref),
             (along_hbm, along_ref),
-            (image_hbm.at[0, block], image_ref),
-            (across_hbm, across_ref),
             (var_hbm.at[0], var_ref),
             (bits_hbm.at[0], bits_ref),
             (owner_hbm, owner_ref),
@@ -261,12 +261,11 @@
         lax.broadcasted_iota(jnp.int32, (CELLS, BLOCK), 1) // CELL
         == lax.broadcasted_iota(jnp.int32, (CELLS, BLOCK), 0)
     ).astype(f32)
-    for copy in copies:
+    for copy in copies[:2]:
         copy.wait()
 
     pair = 2 * TILE
     forward = jnp.concatenate([across_ref[:pair], across_ref[...]], axis=0)
-    backward = jnp.concatenate([back_across_ref[:pair], back_across_ref[...]], axis=0)
     spots = [way_to(place_ref[0], piece) for piece in range(CHIPS)]
 
     def windows(rows):
@@ -382,6 +381,9 @@
 
     halve()
     transform_across(0)
+    for copy in copies[2:]:
+        copy.wait()
+    backward = jnp.concatenate([back_across_ref[:pair], back_across_ref[...]], axis=0)
     prepare()
     tiles = WINDOWS * SIDE
     for step in range(tiles + 5):

time: 85.5 us -> 85.7 us (level)
  no operation moved by 1% of the time
where the time goes in v11:
time: 85.7 us; the launch traced here: 85.4 us
  starting transfers between devices  28.6 us (33%)
  waiting for transfers between devices  19.2 us (22%)
  blocking collectives  19.1 us (22%)
  Pallas kernels  16.8 us (20%)
  local copies, waits for them, and re-layouts  0.96 us (1%)
    ppermute x12, starting transfers between devices, exchange(): lax.ppermute(parts[way], 'visit', phase_partners(phase, way))  19.3 us
    all_to_all x1, blocking collectives, spread_tiles(): lax.all_to_all(pieces, 'visit', 0, 0, axis_index_groups=same_core, tiled=...  19.1 us
    pallas_call x2, Pallas kernels, match_block(): pl.pallas_call(functools.partial(match_kernel, block=block), out_shape=[j...  12.8 us
    ppermute x12, waiting for transfers between devices, exchange(): lax.ppermute(parts[way], 'visit', phase_partners(phase, way))  9.12 us
    ppermute x2, waiting for transfers between devices, local(): terms.extend((half, lax.ppermute(half, 'band', pairings[1 - number])))  5.53 us
    ppermute x2, starting transfers between devices, local(): lax.ppermute(half, 'band', pairings[number])  4.52 us
    ppermute x2, starting transfers between devices, local(): terms.extend((half, lax.ppermute(half, 'band', pairings[1 - number])))  4.03 us
    ppermute x2, waiting for transfers between devices, local(): lax.ppermute(half, 'band', pairings[number])  2.88 us
  transfers between devices with their start and end apart: 17, of which 9 were waited for; matrix products, arithmetic and copies ran while one was open for 0% of the time, Pallas kernels for 9%

profile of v11, /device:TPU:0, one launch (start us, length us, event | category | flops | bytes accessed | tf_op | source)
XLA Modules:
  0.0 85.4 jit_solution(7720249488928537336)
XLA Ops:
  0.6 6.4 %match_block.3 = (f32[4,17,8,128]{3,2,1,0:T(8,128)}, f32[4,17,8,128]{3,2,1,0:T(8,128)}, f32[4,17,8,128]{3,2,1,0:T(8,128)}, f32[4,17,8,128]{3,2,1,0:T(8,128)}) custom-call(s32[1]{0:T(128)} %bitcast.place_ref, s32[1,2]{1,0:T(1,128)} %index_hbm.3, f32[27,64]{1,0:T(8,128)} %bitcast.23, f32[1,2,552,552]{3,2,1,0:T(8,128)} %image_hbm.3, f32[1,2,16,16]{3,2,1,0:T(8,128)} %var_hbm.3, ...), custom_call_target="tpu_custom_call" | custom-call | flops 5242880000 | bytes 3145728 | tf_op jit(solution)/shard_map/match_block/pallas_call | solution.py:415
  7.1 2.7 %collective-permute-start.6 = (f32[4,17,8,128]{3,2,1,0:T(8,128)}, f32[4,17,8,128]{3,2,1,0:T(8,128)S(1)}, u32[]{:S(2)}, u32[]{:S(2)}) collective-permute-start(f32[4,17,8,128]{3,2,1,0:T(8,128)} %get-tuple-element.33), channel_id=1, source_target_pairs={{0,40},{4,124},{8,32},{12,116},{16,56},{20,108},{24,48},{28,100},{... | collective-permute-start | bytes 835592 | tf_op jit(solution)/shard_map/ppermute | solution.py:584
  9.8 0.5 collective-permute-start.7
  10.3 0.4 collective-permute-start.8
  10.7 6.4 %match_block.2 = (f32[4,17,8,128]{3,2,1,0:T(8,128)}, f32[4,17,8,128]{3,2,1,0:T(8,128)}, f32[4,17,8,128]{3,2,1,0:T(8,128)}, f32[4,17,8,128]{3,2,1,0:T(8,128)}) custom-call(s32[1]{0:T(128)} %bitcast.place_ref, s32[1,2]{1,0:T(1,128)} %index_hbm.3, f32[27,64]{1,0:T(8,128)} %bitcast.24, f32[1,2,552,552]{3,2,1,0:T(8,128)} %image_hbm.3, f32[1,2,16,16]{3,2,1,0:T(8,128)} %var_hbm.3, ...), custom_call_target="tpu_custom_call" | custom-call | flops 5242880000 | bytes 3145728 | tf_op jit(solution)/shard_map/match_block/pallas_call | solution.py:415
  17.0 2.7 %collective-permute-start = (f32[4,17,8,128]{3,2,1,0:T(8,128)}, f32[4,17,8,128]{3,2,1,0:T(8,128)S(1)}, u32[]{:S(2)}, u32[]{:S(2)}) collective-permute-start(f32[4,17,8,128]{3,2,1,0:T(8,128)} %get-tuple-element.25), channel_id=1, source_target_pairs={{0,40},{4,124},{8,32},{12,116},{16,56},{20,108},{24,48},{28,100},{... | collective-permute-start | bytes 835592 | tf_op jit(solution)/shard_map/ppermute | solution.py:584
  19.7 0.5 collective-permute-start.1
  20.2 0.4 collective-permute-start.2
  20.8 5.4 %collective-permute-start.9 = (f32[4,17,8,128]{3,2,1,0:T(8,128)S(1)}, f32[4,17,8,128]{3,2,1,0:T(8,128)S(1)}, u32[]{:S(2)}, u32[]{:S(2)}) collective-permute-start(f32[4,17,8,128]{3,2,1,0:T(8,128)S(1)} %get-tuple-element.37), channel_id=1, source_target_pairs={{0,120},{4,44},{8,112},{12,36},{16,104},{20,60},{24,96},{28,52},{3... | collective-permute-start | bytes 835592 | tf_op jit(solution)/shard_map/ppermute | solution.py:584
  26.1 1.0 %copy-done = f32[4,17,8,128]{3,2,1,0:T(8,128)S(1)} copy-done((f32[4,17,8,128]{3,2,1,0:T(8,128)S(1)}, f32[4,17,8,128]{3,2,1,0:T(8,128)}, u32[]{:S(2)}) %copy-start) | copy-done | bytes 278552
  27.2 0.6 collective-permute-start.10
  28.0 2.8 %collective-permute-done.1.refs_2_ = f32[4,17,8,128]{3,2,1,0:T(8,128)S(1)} collective-permute-done((f32[4,17,8,128]{3,2,1,0:T(8,128)}, f32[4,17,8,128]{3,2,1,0:T(8,128)S(1)}, u32[]{:S(2)}, u32[]{:S(2)}) %collective-permute-start.1) | collective-permute-done | bytes 278560 | tf_op jit(solution)/shard_map/ppermute | solution.py:584
  30.9 4.4 %collective-permute-start.3 = (f32[4,17,8,128]{3,2,1,0:T(8,128)S(1)}, f32[4,17,8,128]{3,2,1,0:T(8,128)S(1)}, u32[]{:S(2)}, u32[]{:S(2)}) collective-permute-start(f32[4,17,8,128]{3,2,1,0:T(8,128)S(1)} %get-tuple-element.29), channel_id=1, source_target_pairs={{0,120},{4,44},{8,112},{12,36},{16,104},{20,60},{24,96},{28,52},{3... | collective-permute-start | bytes 835592 | tf_op jit(solution)/shard_map/ppermute | solution.py:584
  35.3 0.5 collective-permute-start.4
  35.7 1.1 %collective-permute-start.5 = (f32[4,17,8,128]{3,2,1,0:T(8,128)S(1)}, f32[4,17,8,128]{3,2,1,0:T(8,128)S(1)}, u32[]{:S(2)}, u32[]{:S(2)}) collective-permute-start(f32[4,17,8,128]{3,2,1,0:T(8,128)S(1)} %get-tuple-element.31), channel_id=1, source_target_pairs={{0,96},{4,36},{8,104},{12,44},{16,112},{20,52},{24,120},{28,60},{3... | collective-permute-start | bytes 835592 | tf_op jit(solution)/shard_map/ppermute | solution.py:584
  37.0 0.6 partial_sums.2
  37.7 3.2 %collective-permute-done.3 = f32[4,17,8,128]{3,2,1,0:T(8,128)S(1)} collective-permute-done((f32[4,17,8,128]{3,2,1,0:T(8,128)S(1)}, f32[4,17,8,128]{3,2,1,0:T(8,128)S(1)}, u32[]{:S(2)}, u32[]{:S(2)}) %collective-permute-start.3) | collective-permute-done | bytes 278560 | tf_op jit(solution)/shard_map/ppermute | solution.py:584
  40.9 2.4 %collective-permute-done.4 = f32[4,17,8,128]{3,2,1,0:T(8,128)S(1)} collective-permute-done((f32[4,17,8,128]{3,2,1,0:T(8,128)S(1)}, f32[4,17,8,128]{3,2,1,0:T(8,128)S(1)}, u32[]{:S(2)}, u32[]{:S(2)}) %collective-permute-start.4) | collective-permute-done | bytes 278560 | tf_op jit(solution)/shard_map/ppermute | solution.py:584
  43.3 0.6 collective-permute-done.5
  43.8 0.7 partial_sums.3
  44.6 0.8 collective-permute-start.12
  45.3 1.6 %collective-permute-done.12.other_ref = f32[1152,128]{1,0:T(8,128)S(1)} collective-permute-done((f32[1152,128]{1,0:T(8,128)S(1)}, f32[1152,128]{1,0:T(8,128)S(1)}, u32[]{:S(2)}, u32[]{:S(2)}) %collective-permute-start.12) | collective-permute-done | bytes 589856 | tf_op jit(solution)/shard_map/ppermute | solution.py:627
  47.3 19.1 %all_to_all.5.part_ref = f32[16,64,128]{2,1,0:T(8,128)S(1)} all-to-all(f32[16,64,128]{2,1,0:T(8,128)S(1)} %bitcast.13), channel_id=1, replica_groups={{0,8,16,24,32,40,48,56,64,72,80,88,96,104,112,120},{4,12,20,28,36,44,52..., dimensions={0} | all-to-all | bytes 1048576 | tf_op jit(solution)/shard_map/all_to_all | solution.py:601
  66.3 0.3 chi.1
  66.7 2.0 %collective-permute-start.13 = (f32[8,64,128]{2,1,0:T(8,128)S(1)}, f32[8,64,128]{2,1,0:T(8,128)S(1)}, u32[]{:S(2)}, u32[]{:S(2)}) collective-permute-start(f32[8,64,128]{2,1,0:T(8,128)S(1)} %get-tuple-element.44), channel_id=1, source_target_pairs={{0,1},{1,0},{2,3},{3,2},{4,5},{5,4},{6,7},{7,6},{8,9},{9,8},{10,11... | collective-permute-start | bytes 786440 | tf_op jit(solution)/shard_map/ppermute | solution.py:657
  68.7 2.5 %collective-permute-start.15 = (f32[8,64,128]{2,1,0:T(8,128)S(1)}, f32[8,64,128]{2,1,0:T(8,128)S(1)}, u32[]{:S(2)}, u32[]{:S(2)}) collective-permute-start(f32[8,64,128]{2,1,0:T(8,128)S(1)} %get-tuple-element.45), channel_id=1, source_target_pairs={{0,3},{3,0},{1,2},{2,1},{4,7},{7,4},{5,6},{6,5},{8,11},{11,8},{9,1... | collective-permute-start | bytes 786440 | tf_op jit(solution)/shard_map/ppermute | solution.py:657
  71.2 2.9 %collective-permute-done.13 = f32[8,64,128]{2,1,0:T(8,128)S(1)} collective-permute-done((f32[8,64,128]{2,1,0:T(8,128)S(1)}, f32[8,64,128]{2,1,0:T(8,128)S(1)}, u32[]{:S(2)}, u32[]{:S(2)}) %collective-permute-start.13) | collective-permute-done | bytes 262176 | tf_op jit(solution)/shard_map/ppermute | solution.py:657
  74.1 3.9 %collective-permute-start.14 = (f32[8,64,128]{2,1,0:T(8,128)S(1)}, f32[8,64,128]{2,1,0:T(8,128)S(1)}, u32[]{:S(2)}, u32[]{:S(2)}) collective-permute-start(f32[8,64,128]{2,1,0:T(8,128)S(1)} %add.6.upper_ref), channel_id=1, source_target_pairs={{0,3},{3,0},{1,2},{2,1},{4,7},{7,4},{5,6},{6,5},{8,11},{11,8},{9,1... | collective-permute-start | bytes 786440 | tf_op jit(solution)/shard_map/ppermute | solution.py:661
  78.2 0.8 image.1
  79.0 3.5 %collective-permute-done.14.more_upper_ref = f32[8,64,128]{2,1,0:T(8,128)S(1)} collective-permute-done((f32[8,64,128]{2,1,0:T(8,128)S(1)}, f32[8,64,128]{2,1,0:T(8,128)S(1)}, u32[]{:S(2)}, u32[]{:S(2)}) %collective-permute-start.14) | collective-permute-done | bytes 262176 | tf_op jit(solution)/shard_map/ppermute | solution.py:661
  82.6 2.0 %collective-permute-done.16.more_lower_ref = f32[8,64,128]{2,1,0:T(8,128)S(1)} collective-permute-done((f32[8,64,128]{2,1,0:T(8,128)S(1)}, f32[8,64,128]{2,1,0:T(8,128)S(1)}, u32[]{:S(2)}, u32[]{:S(2)}) %collective-permute-start.16) | collective-permute-done | bytes 262176 | tf_op jit(solution)/shard_map/ppermute | solution.py:661
  84.6 0.9 %detection.1 = f32[8,128,128]{2,1,0:T(8,128)} custom-call(f32[8,64,128]{2,1,0:T(8,128)S(1)} %add.6.upper_ref, f32[8,64,128]{2,1,0:T(8,128)S(1)} %collective-permute-done.14.more_upper_ref, f32[8,64,128]{2,1,0:T(8,128)S(1)} %add.7.lower_ref, f32[8,64,128]{2,1,0:T(8,128)S(1)} %collective-permute-done.16.more_lower_ref), custom_call_target="tpu_custom_call" | custom-call | tf_op jit(solution)/shard_map/detection/pallas_call | solution.py:662
  (21 shorter events, 1.1 us)
Async XLA Ops:
  7.1 13.2 %collective-permute-start.6 = (f32[4,17,8,128]{3,2,1,0:T(8,128)}, f32[4,17,8,128]{3,2,1,0:T(8,128)S(1)}, u32[]{:S(2)}, u32[]{:S(2)}) collective-permute-start(f32[4,17,8,128]{3,2,1,0:T(8,128)} %get-tuple-element.33), channel_id=1, source_target_pairs={{0,40},{4,124},{8,32},{12,116},{16,56},{20,108},{24,48},{28,100},{... | collective-permute-start | bytes 835592 | tf_op jit(solution)/shard_map/ppermute | solution.py:584
  9.8 10.9 %collective-permute-start.7 = (f32[4,17,8,128]{3,2,1,0:T(8,128)}, f32[4,17,8,128]{3,2,1,0:T(8,128)S(1)}, u32[]{:S(2)}, u32[]{:S(2)}) collective-permute-start(f32[4,17,8,128]{3,2,1,0:T(8,128)} %get-tuple-element.34), channel_id=1, source_target_pairs={{0,8},{4,28},{8,0},{12,20},{16,24},{20,12},{24,16},{28,4},{32,40},... | collective-permute-start | bytes 835592 | tf_op jit(solution)/shard_map/ppermute | solution.py:584
  10.3 10.3 %copy-start.1 = (f32[4,17,8,128]{3,2,1,0:T(8,128)S(1)}, f32[4,17,8,128]{3,2,1,0:T(8,128)}, u32[]{:S(2)}) copy-start(f32[4,17,8,128]{3,2,1,0:T(8,128)} %get-tuple-element.32.part_hbm) | copy-start | bytes 835588
  10.3 10.4 %collective-permute-start.8 = (f32[4,17,8,128]{3,2,1,0:T(8,128)}, f32[4,17,8,128]{3,2,1,0:T(8,128)S(1)}, u32[]{:S(2)}, u32[]{:S(2)}) collective-permute-start(f32[4,17,8,128]{3,2,1,0:T(8,128)} %get-tuple-element.35), channel_id=1, source_target_pairs={{0,32},{4,100},{8,40},{12,108},{16,48},{20,116},{24,56},{28,124},{... | collective-permute-start | bytes 835592 | tf_op jit(solution)/shard_map/ppermute | solution.py:584
  17.0 10.7 %collective-permute-start = (f32[4,17,8,128]{3,2,1,0:T(8,128)}, f32[4,17,8,128]{3,2,1,0:T(8,128)S(1)}, u32[]{:S(2)}, u32[]{:S(2)}) collective-permute-start(f32[4,17,8,128]{3,2,1,0:T(8,128)} %get-tuple-element.25), channel_id=1, source_target_pairs={{0,40},{4,124},{8,32},{12,116},{16,56},{20,108},{24,48},{28,100},{... | collective-permute-start | bytes 835592 | tf_op jit(solution)/shard_map/ppermute | solution.py:584
  19.7 11.1 %collective-permute-start.1 = (f32[4,17,8,128]{3,2,1,0:T(8,128)}, f32[4,17,8,128]{3,2,1,0:T(8,128)S(1)}, u32[]{:S(2)}, u32[]{:S(2)}) collective-permute-start(f32[4,17,8,128]{3,2,1,0:T(8,128)} %get-tuple-element.26), channel_id=1, source_target_pairs={{0,8},{4,28},{8,0},{12,20},{16,24},{20,12},{24,16},{28,4},{32,40},... | collective-permute-start | bytes 835592 | tf_op jit(solution)/shard_map/ppermute | solution.py:584
  20.2 10.6 %collective-permute-start.2 = (f32[4,17,8,128]{3,2,1,0:T(8,128)}, f32[4,17,8,128]{3,2,1,0:T(8,128)S(1)}, u32[]{:S(2)}, u32[]{:S(2)}) collective-permute-start(f32[4,17,8,128]{3,2,1,0:T(8,128)} %get-tuple-element.27), channel_id=1, source_target_pairs={{0,32},{4,100},{8,40},{12,108},{16,48},{20,116},{24,56},{28,124},{... | collective-permute-start | bytes 835592 | tf_op jit(solution)/shard_map/ppermute | solution.py:584
  20.8 15.0 %collective-permute-start.9 = (f32[4,17,8,128]{3,2,1,0:T(8,128)S(1)}, f32[4,17,8,128]{3,2,1,0:T(8,128)S(1)}, u32[]{:S(2)}, u32[]{:S(2)}) collective-permute-start(f32[4,17,8,128]{3,2,1,0:T(8,128)S(1)} %get-tuple-element.37), channel_id=1, source_target_pairs={{0,120},{4,44},{8,112},{12,36},{16,104},{20,60},{24,96},{28,52},{3... | collective-permute-start | bytes 835592 | tf_op jit(solution)/shard_map/ppermute | solution.py:584
  26.1 1.0 %copy-start = (f32[4,17,8,128]{3,2,1,0:T(8,128)S(1)}, f32[4,17,8,128]{3,2,1,0:T(8,128)}, u32[]{:S(2)}) copy-start(f32[4,17,8,128]{3,2,1,0:T(8,128)} %get-tuple-element.24.part_hbm) | copy-start | bytes 835588
  27.2 9.9 %collective-permute-start.10 = (f32[4,17,8,128]{3,2,1,0:T(8,128)S(1)}, f32[4,17,8,128]{3,2,1,0:T(8,128)S(1)}, u32[]{:S(2)}, u32[]{:S(2)}) collective-permute-start(f32[4,17,8,128]{3,2,1,0:T(8,128)S(1)} %get-tuple-element.38), channel_id=1, source_target_pairs={{0,24},{4,12},{8,16},{12,4},{16,8},{20,28},{24,0},{28,20},{32,56},... | collective-permute-start | bytes 835592 | tf_op jit(solution)/shard_map/ppermute | solution.py:584
  27.7 9.3 %collective-permute-start.11 = (f32[4,17,8,128]{3,2,1,0:T(8,128)S(1)}, f32[4,17,8,128]{3,2,1,0:T(8,128)S(1)}, u32[]{:S(2)}, u32[]{:S(2)}) collective-permute-start(f32[4,17,8,128]{3,2,1,0:T(8,128)S(1)} %get-tuple-element.39), channel_id=1, source_target_pairs={{0,96},{4,36},{8,104},{12,44},{16,112},{20,52},{24,120},{28,60},{3... | collective-permute-start | bytes 835592 | tf_op jit(solution)/shard_map/ppermute | solution.py:584
  30.9 10.0 %collective-permute-start.3 = (f32[4,17,8,128]{3,2,1,0:T(8,128)S(1)}, f32[4,17,8,128]{3,2,1,0:T(8,128)S(1)}, u32[]{:S(2)}, u32[]{:S(2)}) collective-permute-start(f32[4,17,8,128]{3,2,1,0:T(8,128)S(1)} %get-tuple-element.29), channel_id=1, source_target_pairs={{0,120},{4,44},{8,112},{12,36},{16,104},{20,60},{24,96},{28,52},{3... | collective-permute-start | bytes 835592 | tf_op jit(solution)/shard_map/ppermute | solution.py:584
  35.3 8.0 %collective-permute-start.4 = (f32[4,17,8,128]{3,2,1,0:T(8,128)S(1)}, f32[4,17,8,128]{3,2,1,0:T(8,128)S(1)}, u32[]{:S(2)}, u32[]{:S(2)}) collective-permute-start(f32[4,17,8,128]{3,2,1,0:T(8,128)S(1)} %get-tuple-element.30), channel_id=1, source_target_pairs={{0,24},{4,12},{8,16},{12,4},{16,8},{20,28},{24,0},{28,20},{32,56},... | collective-permute-start | bytes 835592 | tf_op jit(solution)/shard_map/ppermute | solution.py:584
  35.7 8.1 %collective-permute-start.5 = (f32[4,17,8,128]{3,2,1,0:T(8,128)S(1)}, f32[4,17,8,128]{3,2,1,0:T(8,128)S(1)}, u32[]{:S(2)}, u32[]{:S(2)}) collective-permute-start(f32[4,17,8,128]{3,2,1,0:T(8,128)S(1)} %get-tuple-element.31), channel_id=1, source_target_pairs={{0,96},{4,36},{8,104},{12,44},{16,112},{20,52},{24,120},{28,60},{3... | collective-permute-start | bytes 835592 | tf_op jit(solution)/shard_map/ppermute | solution.py:584
  44.6 2.4 %collective-permute-start.12 = (f32[1152,128]{1,0:T(8,128)S(1)}, f32[1152,128]{1,0:T(8,128)S(1)}, u32[]{:S(2)}, u32[]{:S(2)}) collective-permute-start(f32[1152,128]{1,0:T(8,128)S(1)} %get-tuple-element.43), channel_id=1, source_target_pairs={{0,4},{4,0},{8,12},{12,8},{16,20},{20,16},{24,28},{28,24},{32,36},... | collective-permute-start | bytes 1769480 | tf_op jit(solution)/shard_map/ppermute | solution.py:627
  66.7 7.4 %collective-permute-start.13 = (f32[8,64,128]{2,1,0:T(8,128)S(1)}, f32[8,64,128]{2,1,0:T(8,128)S(1)}, u32[]{:S(2)}, u32[]{:S(2)}) collective-permute-start(f32[8,64,128]{2,1,0:T(8,128)S(1)} %get-tuple-element.44), channel_id=1, source_target_pairs={{0,1},{1,0},{2,3},{3,2},{4,5},{5,4},{6,7},{7,6},{8,9},{9,8},{10,11... | collective-permute-start | bytes 786440 | tf_op jit(solution)/shard_map/ppermute | solution.py:657
  68.7 9.4 %collective-permute-start.15 = (f32[8,64,128]{2,1,0:T(8,128)S(1)}, f32[8,64,128]{2,1,0:T(8,128)S(1)}, u32[]{:S(2)}, u32[]{:S(2)}) collective-permute-start(f32[8,64,128]{2,1,0:T(8,128)S(1)} %get-tuple-element.45), channel_id=1, source_target_pairs={{0,3},{3,0},{1,2},{2,1},{4,7},{7,4},{5,6},{6,5},{8,11},{11,8},{9,1... | collective-permute-start | bytes 786440 | tf_op jit(solution)/shard_map/ppermute | solution.py:657
  74.1 8.4 %collective-permute-start.14 = (f32[8,64,128]{2,1,0:T(8,128)S(1)}, f32[8,64,128]{2,1,0:T(8,128)S(1)}, u32[]{:S(2)}, u32[]{:S(2)}) collective-permute-start(f32[8,64,128]{2,1,0:T(8,128)S(1)} %add.6.upper_ref), channel_id=1, source_target_pairs={{0,3},{3,0},{1,2},{2,1},{4,7},{7,4},{5,6},{6,5},{8,11},{11,8},{9,1... | collective-permute-start | bytes 786440 | tf_op jit(solution)/shard_map/ppermute | solution.py:661
  78.1 6.5 %collective-permute-start.16 = (f32[8,64,128]{2,1,0:T(8,128)S(1)}, f32[8,64,128]{2,1,0:T(8,128)S(1)}, u32[]{:S(2)}, u32[]{:S(2)}) collective-permute-start(f32[8,64,128]{2,1,0:T(8,128)S(1)} %add.7.lower_ref), channel_id=1, source_target_pairs={{0,1},{1,0},{2,3},{3,2},{4,5},{5,4},{6,7},{7,6},{8,9},{9,8},{10,11... | collective-permute-start | bytes 786440 | tf_op jit(solution)/shard_map/ppermute | solution.py:661
